TPU v7x, 32 devices: a whole 2x2x4 slice. The times are simulated.
32 devices in a mesh: seq: 16 (over z, y, x), exp: 2 (over core).
Axes of the slice: x: 2, y: 2, z: 4, core: 2. Of those that a mesh axis runs over, the one named last changes fastest.
Arguments:
- x_in: bfloat16 [1024, 8192], P('seq', 'exp'), may hold values from -6 to 6
- z_gate: bfloat16 [1024, 8192], P('seq', 'exp'), may hold values from -6 to 6
- dt_low: bfloat16 [1024, 256], P('seq'), may hold values from -6 to 6
- dt_weight: bfloat16 [256, 8192], P(None, 'exp'), may hold values from -0.375 to 0.375
- dt_bias: float32 [8192], P('exp'), may hold values from -9 to -1
- a_log: float32 [16, 8192], P(None, 'exp'), may hold values from -4 to 0
- conv_weight: float32 [4, 8192], P(None, 'exp'), may hold values from -3 to 3
- conv_bias: float32 [8192], P('exp'), may hold values from -0.5 to 0.5
- d_skip: float32 [8192], P('exp'), may hold values from 0.5 to 1.5
- b_and_c: float32 [2, 16, 1024], P(None, None, 'seq'), may hold values from -6 to 6
- hidden: bfloat16 [1024, 4096], P('seq', 'exp'), may hold values from -6 to 6
- router: bfloat16 [4096, 8], P('exp'), may hold values from -0.09375 to 0.09375
- expert_ids: int32 [1024, 2], P('seq'), may hold values from 0 to 7, all different within a row; in each aligned block of 64 rows (0 to 63, 64 to 127, ...) at most 18 rows name the same one
- w_gate: bfloat16 [4096, 98304], P('exp', 'seq'), may hold values from -0.09375 to 0.09375
- w_down: bfloat16 [98304, 4096], P('seq', 'exp'), may hold values from -0.0546875 to 0.0546875
Outputs:
- mamba_out: bfloat16 [1024, 8192], P('seq', 'exp')
- moe_out: bfloat16 [1024, 4096], P('seq', 'exp')
Inputs may be any that keep to these rules, and one draw needn't show every extreme that they name: `expert_ids`: each token names 2 different experts; among the 64 tokens of one block no expert is named more than 18 times, a bound that some expert reaches in every block.
All inputs are finite; a program needn't handle non-finite values.
Results may differ from a plain program's by a relative error of at most 0.018.
Values may be sent and summed in bfloat16 or wider, within the bound.
No kernel may reach another device: no remote copies, remote signals or barrier semaphores. Data moves between devices by JAX's collectives and lax.ppermute only.
A program may use at most 128 MiB of HBM per device.

v0:
```python
import jax
import jax.numpy as jnp
from jax import lax
from jax.sharding import PartitionSpec as P

CAP = 18


def passed_along(value, axis, steps):
    count = lax.axis_size(axis)
    first, last = (max(0, -steps), min(count, count - steps))
    return lax.ppermute(value, axis, [(source, source + steps) for source in range(first, last)])


def carried_in(array, axis, join, neutral):
    place = lax.axis_index(axis)
    gathered = jax.tree.map(
        lambda a, kind: lax.all_gather(a.astype(kind), axis), array, (jnp.bfloat16, jnp.bfloat16)
    )
    state = jax.tree.map(lambda a, e: jnp.zeros_like(a) + jnp.asarray(e, a.dtype), array, neutral)

    def one(lap, state):
        return join(
            state,
            jax.tree.map(
                lambda a, own: lax.dynamic_index_in_dim(a, lap, 0, False).astype(own.dtype),
                gathered,
                array,
            ),
        )

    return lax.fori_loop(0, place, one, state)


def link_pairs(earlier, later):
    return (earlier[0] * later[0], later[0] * earlier[1] + later[1])


def mixer_scan(delta, activated, b_rows, c_rows, rates, start_state):
    token_count, channels = delta.shape
    block_len = 16
    block_count = token_count // block_len

    def regroup(values):
        return values.reshape((block_count, block_len) + values.shape[1:])

    def advance(carry, inputs):
        running, product = carry
        step_delta, step_x, step_b, step_c = inputs
        reads = []
        for position in range(block_len):
            factor = jnp.exp(step_delta[position][None, :] * rates)
            running = (
                factor * running
                + step_b[position][:, None] * (step_delta[position] * step_x[position])[None, :]
            )
            product = factor * product
            reads.append(jnp.sum(step_c[position][:, None] * running, axis=0))
        return ((running, product), (jnp.stack(reads),))

    initial = (start_state, jnp.ones(rates.shape, jnp.float32))
    finals, outputs = lax.scan(
        advance, initial, (regroup(delta), regroup(activated), regroup(b_rows), regroup(c_rows))
    )
    readout = outputs[0].reshape(token_count, channels)
    weighted_all = None
    return (readout, weighted_all, finals[0], finals[1])


def local(
    x_in,
    z_gate,
    dt_low,
    dt_weight,
    dt_bias,
    a_log,
    conv_weight,
    conv_bias,
    d_skip,
    b_and_c,
    hidden,
    router,
    expert_ids,
    w_gate,
    w_down,
):
    tok_rows = x_in.shape[0]
    kernel_taps = conv_weight.shape[0]
    edge_rows = passed_along(x_in[tok_rows - (kernel_taps - 1) :], "seq", 1)
    padded = jnp.concatenate([edge_rows, x_in], axis=0).astype(jnp.float32)
    convolved = jnp.zeros(x_in.shape, jnp.float32) + conv_bias[None, :]
    for offset in range(kernel_taps):
        convolved = convolved + conv_weight[offset][None, :] * padded[offset : offset + tok_rows]
    activated = jax.nn.silu(convolved)
    delta = jax.nn.softplus(
        jnp.dot(dt_low, dt_weight, preferred_element_type=jnp.float32) + dt_bias[None, :]
    )
    rates = -jnp.exp(a_log)
    b_rows = b_and_c[0].T
    c_rows = b_and_c[1].T
    zero_state = jnp.zeros(rates.shape, jnp.float32)
    readout, weighted_all, end_state, end_product = mixer_scan(
        delta, activated, b_rows, c_rows, rates, zero_state
    )
    identity = (jnp.ones(rates.shape, jnp.float32), jnp.zeros(rates.shape, jnp.float32))
    carried = carried_in((end_product, end_state), "seq", link_pairs, identity)
    entering = carried[1]
    readout = mixer_scan(delta, activated, b_rows, c_rows, rates, entering)[0]
    mamba_out = (
        (readout + d_skip[None, :] * activated) * jax.nn.silu(z_gate.astype(jnp.float32))
    ).astype(jnp.bfloat16)
    experts = router.shape[1]
    picks = expert_ids.shape[1]
    feature_width = hidden.shape[1]
    group_size = lax.axis_size("seq") // experts
    logits = lax.psum(jnp.dot(hidden, router, preferred_element_type=jnp.float32), "exp")
    expert_iota = lax.broadcasted_iota(jnp.int32, (1, 1, experts), 2)
    chosen = expert_ids[:, :, None] == expert_iota
    picked = jnp.sum(jnp.where(chosen, logits[:, None, :], 0.0), axis=2)
    gates = jax.nn.sigmoid(picked - picked[:, ::-1])
    flat_hits = chosen.reshape(tok_rows * picks, experts).astype(jnp.int32)
    earlier_hits = jnp.cumsum(flat_hits, axis=0) - flat_hits
    slots = jnp.sum(earlier_hits * flat_hits, axis=1).reshape(tok_rows, picks)
    slot_keys = expert_ids * CAP + slots
    slot_iota = lax.broadcasted_iota(jnp.int32, (experts * CAP, 1, 1), 0)
    matches = slot_keys[None] == slot_iota
    selector = jnp.sum(matches.astype(jnp.float32), axis=2).astype(jnp.bfloat16)
    blending = jnp.sum(jnp.where(matches, gates[None], 0.0), axis=2)
    packed = jnp.dot(selector, hidden, preferred_element_type=jnp.float32).astype(jnp.bfloat16)
    outgoing = jnp.broadcast_to(
        packed.reshape(experts, 1, CAP, feature_width), (experts, group_size, CAP, feature_width)
    )
    outgoing = outgoing.reshape(experts * group_size, CAP, feature_width)
    arrived = lax.all_to_all(outgoing, "seq", split_axis=0, concat_axis=0, tiled=True)
    sources, entries, features = arrived.shape
    routed = arrived.reshape(sources * entries, features)
    partial_value = jnp.dot(routed, w_gate, preferred_element_type=jnp.float32)
    summed = lax.psum(partial_value.astype(jnp.bfloat16), "exp").astype(jnp.float32)
    acted = jax.nn.silu(summed).astype(jnp.bfloat16)
    produced = jnp.dot(acted, w_down, preferred_element_type=jnp.float32)
    produced = produced.reshape(sources, entries, features)
    returned = lax.all_to_all(
        produced.astype(jnp.bfloat16), "seq", split_axis=0, concat_axis=0, tiled=True
    ).astype(produced.dtype)
    combined = jnp.sum(returned.reshape(experts, group_size, CAP, feature_width), axis=1).reshape(
        experts * CAP, feature_width
    )
    moe_out = jnp.einsum("rt,rd->td", blending, combined, precision=lax.Precision.HIGHEST)
    return (mamba_out, moe_out.astype(jnp.bfloat16))


def solution(mesh):
    return jax.shard_map(
        local,
        mesh=mesh,
        in_specs=(
            P("seq", "exp"),
            P("seq", "exp"),
            P("seq", None),
            P(None, "exp"),
            P("exp"),
            P(None, "exp"),
            P(None, "exp"),
            P("exp"),
            P("exp"),
            P(None, None, "seq"),
            P("seq", "exp"),
            P("exp", None),
            P("seq", None),
            P("exp", "seq"),
            P("seq", "exp"),
        ),
        out_specs=(P("seq", "exp"), P("seq", "exp")),
        check_vma=False,
    )
```

profile of v0, /device:TPU:0, one launch (start us, length us, event | category | flops | bytes accessed | tf_op | source)
XLA Modules:
  0.0 275.1 jit_solution(1637284257543302867)
XLA Ops:
  9.1 4.8 %collective-permute-start = (bf16[3,4096]{1,0:T(4,128)(2,1)S(1)}, bf16[3,4096]{1,0:T(4,128)(2,1)S(1)}, u32[]{:S(2)}, u32[]{:S(2)}) collective-permute-start(bf16[3,4096]{1,0:T(4,128)(2,1)S(1)} %slice.515), channel_id=1, source_target_pairs={{0,2},{2,4},{4,6},{6,8},{8,10},{10,12},{12,14},{14,16},{16,18},{18... | collective-permute-start | bytes 73736 | tf_op jit(solution)/shard_map/ppermute | solution.py:12
  16.1 2.6 compare_select_fusion
  19.7 29.2 %while.39 = (s32[]{:T(128)}, f32[16,4096]{1,0:T(8,128)}, f32[16,4096]{1,0:T(8,128)}, f32[4,16,4096]{2,1,0:T(8,128)}, f32[16,4096]{1,0:T(8,128)S(1)}, /*index=5*/...) while((s32[]{:T(128)}, f32[16,4096]{1,0:T(8,128)}, ...), condition=%wide.region_1.2_spmd.clone, body=%wide.region_0.1_spmd.clone.sunk | while | flops 6488082 | bytes 4197908 | solution.py:62
  19.7 2.8 %constant_dynamic-slice_fusion.115 = (f32[1,1,4096]{2,1,0:T(1,128)S(1)}, f32[1,1,4096]{2,1,0:T(1,128)S(1)}, f32[1,1,4096]{2,1,0:T(1,128)S(1)}, f32[1,1,4096]{2,1...) fusion(f32[4,16,4096]{2,1,0:T(8,128)S(1)} %get-tuple-element.82, ...), kind=kLoop, calls=%fused_computation.217.clone.1 | loop fusion | bytes 1048640 | tf_op jit(solution)/shard_map/while/body/eval_jaxpr/slice | solution.py:55
  25.8 2.7 constant_dynamic-slice_fusion.115
  31.1 2.6 multiply_add_fusion.23
  38.6 2.6 multiply_add_fusion.23
  41.2 2.6 constant_dynamic-slice_fusion.115
  46.3 2.6 multiply_add_fusion.23
  51.7 2.5 psum.14
  58.7 6.0 %all-to-all-start = ((bf16[16,18,2048]{2,1,0:T(8,128)(2,1)}), bf16[16,18,2048]{2,1,0:T(8,128)(2,1)}, u32[]{:S(2)}, u32[]{:S(2)}) async-start(bf16[16,18,2048]{2,1,0:T(8,128)(2,1)} %bitcast.431), calls=%async_computation | async-start | bytes 3145728 | tf_op jit(solution)/shard_map/all_to_all | solution.py:134
  67.1 37.7 %all-to-all-done = bf16[16,18,2048]{2,1,0:T(8,128)(2,1)} async-done(((bf16[16,18,2048]{2,1,0:T(8,128)(2,1)}), bf16[16,18,2048]{2,1,0:T(8,128)(2,1)}, u32[]{:S(2)}, u32[]{:S(2)}) %all-to-all-start) | async-done | bytes 1179680 | tf_op jit(solution)/shard_map/all_to_all | solution.py:134
  107.2 14.0 %convolution_convert_fusion = bf16[288,6144]{1,0:T(8,128)(2,1)} fusion(bf16[288,2048]{1,0:T(8,128)(2,1)} %reshape.657, bf16[2048,6144]{1,0:T(8,128)(2,1)} %param.34), kind=kOutput, calls=%fused_computation.255 | convolution fusion | flops 7249526784 | bytes 29884416 | tf_op jit(solution)/shard_map/dot_general | solution.py:137
  121.2 5.1 %all-gather.5.cloned.1.call-done = bf16[256,4096]{1,0:T(8,128)(2,1)} async-done(((bf16[16,4096]{1,0:T(8,128)(2,1)}), bf16[256,4096]{1,0:T(8,128)(2,1)}) %all-gather.5.cloned.1.call-update) | async-done | bytes 2097168 | tf_op jit(solution)/shard_map/all_gather | solution.py:18
  126.3 62.7 %all-gather.7.cloned.1.call-done = bf16[256,4096]{1,0:T(8,128)(2,1)} async-done(((bf16[16,4096]{1,0:T(8,128)(2,1)}), bf16[256,4096]{1,0:T(8,128)(2,1)}) %all-gather.7.cloned.1.call-update) | async-done | bytes 2097168 | tf_op jit(solution)/shard_map/all_gather | solution.py:18
  189.3 14.4 %fusion.94 = bf16[288,2048]{1,0:T(8,128)(2,1)} fusion(bf16[6144,2048]{1,0:T(8,128)(2,1)} %param.35, bf16[288,6144]{1,0:T(8,128)(2,1)} %all-reduce.2.cloned.1.call-done), kind=kOutput, calls=%fused_computation.265 | convolution fusion | flops 7258963968 | bytes 29884416 | tf_op jit(solution)/shard_map/dot_general | solution.py:140
  203.7 2.4 convert_element_type.73
  206.1 20.6 %all-to-all-start.1 = ((bf16[16,18,2048]{2,1,0:T(8,128)(2,1)}), bf16[16,18,2048]{2,1,0:T(8,128)(2,1)}, u32[]{:S(2)}, u32[]{:S(2)}) async-start(bf16[16,18,2048]{2,1,0:T(8,128)(2,1)} %convert_element_type.73), calls=%async_computation.1 | async-start | bytes 3145728 | tf_op jit(solution)/shard_map/all_to_all | solution.py:142
  226.7 31.6 %while.38 = (s32[]{:T(128)}, f32[16,4096]{1,0:T(8,128)S(1)}, f32[4,16,4096]{2,1,0:T(8,128)}, f32[4,16,4096]{2,1,0:T(8,128)}, f32[16,4096]{1,0:T(8,128)S(1)}, /*i...) while((s32[]{:T(128)}, f32[16,4096]{1,0:T(8,128)S(1)}, ...), condition=%wide.region_21.22_spmd, body=%wide.region_4.21_spmd.sunk | while | flops 9437201 | bytes 7741201 | solution.py:62
  226.7 2.8 %constant_dynamic-slice_fusion.114 = (f32[1,1,4096]{2,1,0:T(1,128)S(1)}, f32[1,1,4096]{2,1,0:T(1,128)S(1)}, f32[1,1,4096]{2,1,0:T(1,128)S(1)}, f32[1,1,4096]{2,1...) fusion(f32[4,16,4096]{2,1,0:T(8,128)S(1)} %get-tuple-element.92, ...), kind=kLoop, calls=%fused_computation.78.clone.1 | loop fusion | bytes 1048640 | tf_op jit(solution)/shard_map/while/body/eval_jaxpr/slice | solution.py:55
  234.8 2.7 constant_dynamic-slice_fusion.114
  250.5 2.5 constant_dynamic-slice_fusion.114
  258.3 3.2 %fusion.105 = bf16[64,4096]{1,0:T(8,128)(2,1)} fusion(bf16[64,4096]{1,0:T(8,128)(2,1)} %param.22, f32[4,16,4096]{2,1,0:T(8,128)} %get-tuple-element.129, f32[4096]{0:T(1024)} %param.29, f32[67,4096]{1,0:T(8,128)S(1)} %maximum_convert_fusion, f32[4096]{0:T(1024)} %bitcast.544, f32[4096]{0:T(1024)} %bitcast.546, f32[4096]{0:T(1024)} %bitcast.542, ...), kind=kLoop, calls=%fused_computation.284 | loop fusion | flops 5505024 | bytes 6389760 | tf_op jit(solution)/shard_map/convert_element_type | solution.py:111
  261.5 3.2 %convert_reduce_fusion = f32[8,18,2048]{2,1,0:T(8,128)} fusion(bf16[16,18,2048]{2,1,0:T(8,128)(2,1)} %all-to-all-done.1), kind=kLoop, calls=%fused_computation.263 | loop fusion | flops 884736 | bytes 2359296 | tf_op jit(solution)/shard_map/reduce_sum | solution.py:145
  (240 shorter events, 55.1 us)
Async XLA Ops:
  8.0 8.1 %copy-start = (bf16[256,4096]{1,0:T(8,128)(2,1)S(1)}, bf16[256,4096]{1,0:T(8,128)(2,1)}, u32[]{:S(2)}) copy-start(bf16[256,4096]{1,0:T(8,128)(2,1)} %param.24) | copy-start | bytes 6291460
  8.0 118.3 %all-gather.5.cloned.1.call-start = ((), (), s32[]{:S(2)}) async-start(), calls=%async_computation.3 | async-start | bytes 2228224 | tf_op jit(solution)/shard_map/all_gather | solution.py:18
  9.1 9.7 %collective-permute-start = (bf16[3,4096]{1,0:T(4,128)(2,1)S(1)}, bf16[3,4096]{1,0:T(4,128)(2,1)S(1)}, u32[]{:S(2)}, u32[]{:S(2)}) collective-permute-start(bf16[3,4096]{1,0:T(4,128)(2,1)S(1)} %slice.515), channel_id=1, source_target_pairs={{0,2},{2,4},{4,6},{6,8},{8,10},{10,12},{12,14},{14,16},{16,18},{18... | collective-permute-start | bytes 73736 | tf_op jit(solution)/shard_map/ppermute | solution.py:12
  15.0 4.0 %copy-start.5 = (f32[1,4096]{1,0:T(1,128)}, f32[1,4096]{1,0:T(1,128)S(1)}, u32[]{:S(2)}) copy-start(f32[1,4096]{1,0:T(1,128)S(1)} %get-tuple-element.376) | copy-start | bytes 49156
  15.0 4.0 %copy-start.6 = (f32[1,4096]{1,0:T(1,128)}, f32[1,4096]{1,0:T(1,128)S(1)}, u32[]{:S(2)}) copy-start(f32[1,4096]{1,0:T(1,128)S(1)} %get-tuple-element.377) | copy-start | bytes 49156
  15.0 4.0 %copy-start.7 = (f32[1,4096]{1,0:T(1,128)}, f32[1,4096]{1,0:T(1,128)S(1)}, u32[]{:S(2)}) copy-start(f32[1,4096]{1,0:T(1,128)S(1)} %get-tuple-element.378) | copy-start | bytes 49156
  15.0 4.0 %copy-start.8 = (f32[1,4096]{1,0:T(1,128)}, f32[1,4096]{1,0:T(1,128)S(1)}, u32[]{:S(2)}) copy-start(f32[1,4096]{1,0:T(1,128)S(1)} %get-tuple-element.379) | copy-start | bytes 49156
  15.0 3.7 %copy-start.11 = (f32[2,16,64]{2,1,0:T(8,128)S(1)}, f32[2,16,64]{2,1,0:T(8,128)}, u32[]{:S(2)}) copy-start(f32[2,16,64]{2,1,0:T(8,128)} %param.30) | copy-start | bytes 24580
  15.0 3.8 %copy-start.3 = (bf16[64,4096]{1,0:T(8,128)(2,1)S(1)}, bf16[64,4096]{1,0:T(8,128)(2,1)}, u32[]{:S(2)}) copy-start(bf16[64,4096]{1,0:T(8,128)(2,1)} %param.21) | copy-start | bytes 1572868
  16.1 2.9 %copy-start.9 = (f32[4096]{0:T(1024)S(1)}, f32[4096]{0:T(1024)}, u32[]{:S(2)}) copy-start(f32[4096]{0:T(1024)} %param.28) | copy-start | bytes 49156
  19.7 30.9 %copy-start.12 = (s32[64,2]{0,1:T(2,128)S(1)}, s32[64,2]{0,1:T(2,128)}, u32[]{:S(2)}) copy-start(s32[64,2]{0,1:T(2,128)} %param.33) | copy-start | bytes 1540
  19.7 31.8 %copy-start.2 = (bf16[64,2048]{1,0:T(8,128)(2,1)S(1)}, bf16[64,2048]{1,0:T(8,128)(2,1)}, u32[]{:S(2)}) copy-start(bf16[64,2048]{1,0:T(8,128)(2,1)} %param.31) | copy-start | bytes 786436
  19.7 31.8 %copy-start.10 = (bf16[2048,8]{0,1:T(8,128)(2,1)S(1)}, bf16[2048,8]{0,1:T(8,128)(2,1)}, u32[]{:S(2)}) copy-start(bf16[2048,8]{0,1:T(8,128)(2,1)} %param.32) | copy-start | bytes 98308
  58.7 46.1 %all-to-all-start = ((bf16[16,18,2048]{2,1,0:T(8,128)(2,1)}), bf16[16,18,2048]{2,1,0:T(8,128)(2,1)}, u32[]{:S(2)}, u32[]{:S(2)}) async-start(bf16[16,18,2048]{2,1,0:T(8,128)(2,1)} %bitcast.431), calls=%async_computation | async-start | bytes 3145728 | tf_op jit(solution)/shard_map/all_to_all | solution.py:134
  64.7 124.4 %all-gather.7.cloned.1.call-start = ((), (), s32[]{:S(2)}) async-start(), calls=%async_computation.4 | async-start | bytes 2228224 | tf_op jit(solution)/shard_map/all_gather | solution.py:18
  66.4 122.9 %all-reduce.2.cloned.1.call-start = ((), (), s32[]{:S(2)}) async-start(), calls=%async_computation.2 | async-start | bytes 7077888 | tf_op jit(solution)/shard_map/psum | solution.py:138
  206.1 55.4 %all-to-all-start.1 = ((bf16[16,18,2048]{2,1,0:T(8,128)(2,1)}), bf16[16,18,2048]{2,1,0:T(8,128)(2,1)}, u32[]{:S(2)}, u32[]{:S(2)}) async-start(bf16[16,18,2048]{2,1,0:T(8,128)(2,1)} %convert_element_type.73), calls=%async_computation.1 | async-start | bytes 3145728 | tf_op jit(solution)/shard_map/all_to_all | solution.py:142
  261.5 6.2 %copy-start.1 = (bf16[256,4096]{1,0:T(8,128)(2,1)S(1)}, bf16[256,4096]{1,0:T(8,128)(2,1)}, u32[]{:S(2)}) copy-start(bf16[256,4096]{1,0:T(8,128)(2,1)} %param.24) | copy-start | bytes 6291460
  264.6 1.6 copy-start.4
Sparse Core Ops, SparseCore 0:
  50.7 75.5 all-gather.4
  129.6 59.3 all-gather.6
Sparse Core Ops, SparseCore 1:
  121.3 26.5 all-reduce.1
where the time goes:
time: 278 us; the launch traced here: 275 us
  waiting for transfers between devices  106 us (38%)
  local copies, waits for them, and re-layouts  42.6 us (15%)
  other arithmetic  41.9 us (15%)
  matrix products  33.8 us (12%)
  starting transfers between devices  31.6 us (11%)
  between operations  15.8 us (6%)
    all_gather x2, waiting for transfers between devices, carried_in(): lax.all_gather(a.astype(kind), axis)  67.8 us
    all_to_all x1, waiting for transfers between devices, local(): lax.all_to_all(outgoing, 'seq', split_axis=0, concat_axis=0, tiled=True)  37.7 us
    slice x8, local copies, waits for them, and re-layouts, advance(): step_x[position]  20.9 us
    all_to_all x1, starting transfers between devices, local(): lax.all_to_all(produced.astype(jnp.bfloat16), 'seq', split_axis=0, concat...  20.6 us
    dot_general x1, matrix products, local(): produced = jnp.dot(acted, w_down, preferred_element_type=jnp.float32)  14.4 us
    dot_general x1, matrix products, local(): partial_value = jnp.dot(routed, w_gate, preferred_element_type=jnp.float32)  14 us
    reduce_sum x20, other arithmetic, advance(): reads.append(jnp.sum(step_c[position][:, None] * running, axis=0))  11.1 us
    add x4, other arithmetic, advance(): factor * running  9.49 us
  transfers between devices with their start and end apart: 6, of which 3 were waited for; matrix products, arithmetic and copies ran while one was open for 23% of the time, Pallas kernels for 0%

commit v1 on v0

v1 whole, which is shorter than its diff:
```python
import functools
import math

import jax
import jax.numpy as jnp
from jax import lax
from jax.experimental import pallas as pl
from jax.experimental.pallas import tpu as pltpu
from jax.sharding import PartitionSpec as P

CAP = 18
MIB = 1 << 20
LOG2E = math.log2(math.e)
F32 = jnp.float32
BF16 = jnp.bfloat16
GATE_PARTS = 2


def params(limit):
    return pltpu.CompilerParams(vmem_limit_bytes=limit * MIB)


def cost(flops, moved, transcendentals=0):
    return pl.CostEstimate(
        flops=int(flops), bytes_accessed=int(moved), transcendentals=int(transcendentals)
    )


def iota(shape, dim):
    return lax.broadcasted_iota(jnp.int32, shape, dim)


def dot(a, b):
    return jnp.dot(a, b, preferred_element_type=F32)


def dot_nt(a, b):
    return lax.dot_general(a, b, (((1,), (1,)), ((), ())), preferred_element_type=F32)


def packing(features):
    main = CAP // 16 * 16
    extra = CAP - main
    cuts = main // extra if extra and main % extra == 0 else 0
    if cuts and features % (cuts * 128) == 0:
        return main, extra, cuts, features // cuts
    return -(-CAP // 16) * 16, 0, 0, 0


def hits_and_slots(ids, experts):
    tokens = ids.shape[1]
    of = iota((experts, tokens), 0)
    hits = [(of == ids[k : k + 1]).astype(F32) for k in range(2)]
    before = (iota((tokens, tokens), 0) < iota((tokens, tokens), 1)).astype(BF16)
    earlier = dot((hits[0] + hits[1]).astype(BF16), before)
    slots = [jnp.sum(h * earlier, axis=0, keepdims=True).astype(jnp.int32) for h in hits]
    return hits, slots


def route_kernel(pack, ids_ref, hidden_ref, router_ref, out_ref, logits_ref):
    main, extra, cuts, width = pack
    experts, copies = out_ref.shape[:2]
    tokens, features = hidden_ref.shape
    ids = ids_ref[...]
    _, slots = hits_and_slots(ids, experts)
    hidden = hidden_ref[...]
    row = iota((experts * main, tokens), 0)
    picked = None
    for k in range(2):
        key = jnp.where(slots[k] < main, ids[k : k + 1] * main + slots[k], -1)
        hit = row == key
        picked = hit if picked is None else picked | hit
    packed = dot(picked.astype(BF16), hidden).astype(BF16)
    for e in range(experts):
        for m in range(copies):
            out_ref[e, m, :, :features] = packed[e * main : (e + 1) * main]
    if extra:
        picked = None
        for k in range(2):
            key = jnp.where(slots[k] >= main, ids[k : k + 1] * extra + slots[k] - main, -1)
            hit = row // cuts == key
            picked = hit if picked is None else picked | hit
        total = None
        for c in range(cuts):
            chosen = (picked & (row % cuts == c)).astype(BF16)
            part = dot(chosen, hidden[:, c * width : (c + 1) * width])
            total = part if total is None else total + part
        total = total.astype(BF16)
        for e in range(experts):
            for m in range(copies):
                out_ref[e, m, :, features:] = total[e * main : (e + 1) * main]
    logits_ref[...] = dot_nt(hidden, router_ref[...])


def route(ids, hidden, router, copies, pack):
    main, _, _, width = pack
    tokens, features = hidden.shape
    experts = router.shape[0]
    return pl.pallas_call(
        functools.partial(route_kernel, pack),
        out_shape=(
            jax.ShapeDtypeStruct((experts, copies, main, features + width), BF16),
            jax.ShapeDtypeStruct((tokens, experts), F32),
        ),
        compiler_params=params(40),
        cost_estimate=cost(2 * tokens * experts * main * features * 2, hidden.size * 8),
        name="route",
    )(ids, hidden, router)


def weights_kernel(pack, copies, ids_ref, logits_ref, main_ref, extra_ref, gates_ref):
    main, extra, cuts, _ = pack
    tokens, experts = logits_ref.shape
    ids = ids_ref[...]
    hits, slots = hits_and_slots(ids, experts)
    eye = (iota((tokens, tokens), 0) == iota((tokens, tokens), 1)).astype(BF16)
    logits = logits_ref[...]
    columns = [dot_nt(eye, h.astype(BF16)) for h in hits]
    picked = [jnp.sum(c * logits, axis=1, keepdims=True) for c in columns]
    expert = iota((tokens, experts), 1).astype(F32)
    total = experts * copies * main
    col = iota((tokens, total), 1)
    for k in range(2):
        gate = jax.nn.sigmoid(picked[k] - picked[1 - k])
        gates_ref[k] = jnp.broadcast_to(gate, gates_ref.shape[1:])
        named = jnp.sum(columns[k] * expert, axis=1, keepdims=True).astype(jnp.int32)
        wide = jnp.broadcast_to(slots[k].astype(F32), (8, tokens)).astype(BF16)
        slot = dot_nt(eye, wide)[:, :1].astype(jnp.int32)
        mine = col // (copies * main) == named
        main_ref[k] = (mine & (col % main == slot)).astype(BF16)
        if extra:
            place = (col % main) // cuts + main
            extra_ref[k] = (mine & (place == slot)).astype(BF16)
        else:
            extra_ref[k] = jnp.zeros(extra_ref.shape[1:], BF16)


def blend_weights(ids, logits, copies, pack):
    tokens, experts = logits.shape
    total = experts * copies * pack[0]
    return pl.pallas_call(
        functools.partial(weights_kernel, pack, copies),
        out_shape=(
            jax.ShapeDtypeStruct((2, tokens, total), BF16),
            jax.ShapeDtypeStruct((2, tokens, total), BF16),
            jax.ShapeDtypeStruct((2, tokens, 128), F32),
        ),
        compiler_params=params(40),
        cost_estimate=cost(2 * tokens * total * 16, tokens * total * 8),
        name="blend_weights",
    )(ids, logits)


def gate_kernel(pack, arrived_ref, w_ref, out_ref, x_ref):
    main, extra, cuts, width = pack
    sources = arrived_ref.shape[0]
    features = x_ref.shape[1]

    @pl.when(pl.program_id(0) == 0)
    def _():
        x_ref[: sources * main] = arrived_ref[:, :, :features].reshape(sources * main, features)
        if extra:
            folded = arrived_ref[:, :, features:].reshape(sources * main, width)
            shape = (sources * extra, sources * main)
            for c in range(cuts):
                pick = (iota(shape, 1) == iota(shape, 0) * cuts + c).astype(BF16)
                x_ref[sources * main :, c * width : (c + 1) * width] = dot(pick, folded).astype(BF16)

    out_ref[...] = dot(x_ref[...], w_ref[...]).astype(BF16)


def gate_part(arrived, w_gate, first, amount, pack):
    main, extra, _, _ = pack
    sources = arrived.shape[0]
    rows = sources * (main + extra)
    features = w_gate.shape[0]
    block = math.gcd(512, amount)
    start = first // block
    return pl.pallas_call(
        functools.partial(gate_kernel, pack),
        grid=(amount // block,),
        in_specs=[
            pl.BlockSpec(arrived.shape, lambda i: (0, 0, 0)),
            pl.BlockSpec((features, block), lambda i: (0, i + start)),
        ],
        out_specs=pl.BlockSpec((rows, block), lambda i: (0, i)),
        out_shape=jax.ShapeDtypeStruct((rows, amount), BF16),
        scratch_shapes=[pltpu.VMEM((rows, features), BF16)],
        compiler_params=params(40),
        cost_estimate=cost(2 * rows * features * amount, features * amount * 2),
        name="gate",
    )(arrived, w_gate)


def down_kernel(pack, sums, last, *refs):
    main, extra, cuts, width = pack
    part_refs, w_ref = refs[:sums], refs[sums]
    out_ref, acc_ref = refs[-2], refs[-1]
    before_ref = refs[sums + 1] if len(refs) == sums + 4 else None
    step = pl.program_id(0)
    total = part_refs[0][...].astype(F32)
    for ref in part_refs[1:]:
        total = total + ref[...].astype(F32)
    acted = (total * jax.nn.sigmoid(total)).astype(BF16)
    product = dot(acted, w_ref[...])

    @pl.when(step == 0)
    def _():
        acc_ref[...] = product if before_ref is None else product + before_ref[...]

    @pl.when(step > 0)
    def _():
        acc_ref[...] += product

    @pl.when(step == pl.num_programs(0) - 1)
    def _():
        if not last:
            out_ref[...] = acc_ref[...]
            return
        sources = out_ref.shape[0]
        features = acc_ref.shape[1]
        made = acc_ref[: sources * main].astype(BF16)
        out_ref[:, :, :features] = made.reshape(sources, main, features)
        if extra:
            shape = (sources * main, sources * extra)
            folded = None
            for c in range(cuts):
                piece = acc_ref[sources * main :, c * width : (c + 1) * width].astype(BF16)
                pick = (iota(shape, 0) == iota(shape, 1) * cuts + c).astype(BF16)
                part = dot(pick, piece)
                folded = part if folded is None else folded + part
            out_ref[:, :, features:] = folded.astype(BF16).reshape(sources, main, width)


def down_part(parts, w_down, first, before, last, sources, pack):
    main, extra, _, width = pack
    rows, amount = parts[0].shape
    features = w_down.shape[1]
    block = math.gcd(512, amount)
    start = first // block
    in_specs = [pl.BlockSpec((rows, block), lambda i: (0, i)) for _ in parts]
    in_specs.append(pl.BlockSpec((block, features), lambda i: (i + start, 0)))
    args = [*parts, w_down]
    if before is not None:
        in_specs.append(pl.BlockSpec((rows, features), lambda i: (0, 0)))
        args.append(before)
    if last:
        shape = jax.ShapeDtypeStruct((sources, main, features + width), BF16)
    else:
        shape = jax.ShapeDtypeStruct((rows, features), F32)
    zeros = (0,) * len(shape.shape)
    return pl.pallas_call(
        functools.partial(down_kernel, pack, len(parts), last),
        grid=(amount // block,),
        in_specs=in_specs,
        out_specs=pl.BlockSpec(shape.shape, lambda i: zeros),
        out_shape=shape,
        scratch_shapes=[pltpu.VMEM((rows, features), F32)],
        compiler_params=params(48),
        cost_estimate=cost(2 * rows * features * amount, features * amount * 2),
        name="down",
    )(*args)


def combine_kernel(pack, back_ref, main_ref, extra_ref, gates_ref, out_ref):
    main, extra, cuts, width = pack
    sources = back_ref.shape[0]
    tokens, features = out_ref.shape
    piece = width if extra else features
    back = back_ref[:, :, :features].reshape(sources * main, features)
    folded = back_ref[:, :, features:].reshape(sources * main, width) if extra else None
    total = None
    for k in range(2):
        rows = dot(main_ref[k], back)
        if extra:
            chosen = extra_ref[k]
            at = iota(chosen.shape, 1) % cuts
            pieces = [
                dot(jnp.where(at == c, chosen, jnp.zeros_like(chosen)), folded) for c in range(cuts)
            ]
            rows = rows + jnp.concatenate(pieces, axis=1)
        weighed = rows * gates_ref[k][:, :1]
        total = weighed if total is None else total + weighed
    out_ref[...] = total.astype(BF16)


def combine(back, weights, tokens, features, pack):
    return pl.pallas_call(
        functools.partial(combine_kernel, pack),
        out_shape=jax.ShapeDtypeStruct((tokens, features), BF16),
        compiler_params=params(40),
        cost_estimate=cost(4 * tokens * back.size, back.size * 2),
        name="combine",
    )(back, *weights)


def spread_states(bc, place, spread_ref):
    for t in range(spread_ref.shape[0]):
        spread_ref[t] = jnp.broadcast_to(bc[place][:, t : t + 1], spread_ref.shape[1:])


def tiled_lanes(value, lanes):
    return jnp.concatenate([value] * (lanes // value.shape[1]), axis=1)


def scan_kernel(
    x_ref, edge_ref, low_ref, dtw_ref, dtb_ref, alog_ref, cw_ref, cb_ref, skip_ref, bc_ref,
    read_ref, cum_ref, ends_ref, padded, delta_ref, fed_ref, b_ref, c_ref,
):
    tokens, lanes = x_ref.shape
    taps = cw_ref.shape[0]
    states = alog_ref.shape[0]

    @pl.when(pl.program_id(0) == 0)
    def _():
        spread_states(bc_ref, 0, b_ref)
        spread_states(bc_ref, 1, c_ref)

    padded[8:] = x_ref[...].astype(F32)
    padded[8 - (taps - 1) : 8] = edge_ref[...].astype(F32)
    conv = jnp.broadcast_to(cb_ref[...], (tokens, lanes))
    for k in range(taps):
        at = 8 - (taps - 1) + k
        conv = conv + cw_ref[k : k + 1] * padded[at : at + tokens]
    act = conv * jax.nn.sigmoid(conv)
    raw = dot(low_ref[...], dtw_ref[...]) + dtb_ref[...]
    delta = jnp.maximum(raw, 0.0) + jnp.log1p(jnp.exp(-jnp.abs(raw)))
    delta_ref[...] = delta
    fed_ref[...] = delta * act
    read_ref[...] = skip_ref[...] * act
    rates = -jnp.exp(alog_ref[...]) * LOG2E

    def eight(g, carry):
        state, running = carry
        at = pl.multiple_of(g * 8, 8)
        delta8 = delta_ref[pl.ds(at, 8)]
        fed8 = fed_ref[pl.ds(at, 8)]
        reads, sums = [], []
        for i in range(8):
            step = delta8[i : i + 1]
            running = running + step
            factor = jnp.exp2(rates * step)
            state = factor * state + tiled_lanes(b_ref[at + i], lanes) * fed8[i : i + 1]
            reads.append(jnp.sum(tiled_lanes(c_ref[at + i], lanes) * state, axis=0, keepdims=True))
            sums.append(running)
        read_ref[pl.ds(at, 8)] += jnp.concatenate(reads, axis=0)
        cum_ref[pl.ds(at, 8)] = jnp.concatenate(sums, axis=0)
        return state, running

    state, running = lax.fori_loop(
        0, tokens // 8, eight, (jnp.zeros((states, lanes), F32), jnp.zeros((1, lanes), F32))
    )
    ends_ref[:states] = state.astype(BF16)
    ends_ref[states:] = jnp.exp2(rates * running).astype(BF16)


def scan(x_in, edge, dt_low, dt_weight, dt_bias, a_log, conv_weight, conv_bias, d_skip, b_and_c):
    tokens, channels = x_in.shape
    states = a_log.shape[0]
    lanes = math.gcd(512, channels)

    def cut(rows):
        return pl.BlockSpec((rows, lanes), lambda i: (0, i))

    def whole(a):
        zeros = (0,) * a.ndim
        return pl.BlockSpec(a.shape, lambda i: zeros)

    return pl.pallas_call(
        scan_kernel,
        grid=(channels // lanes,),
        in_specs=[
            cut(tokens), cut(edge.shape[0]), whole(dt_low), cut(dt_weight.shape[0]), cut(1),
            cut(states), cut(conv_weight.shape[0]), cut(1), cut(1), whole(b_and_c),
        ],
        out_specs=(cut(tokens), cut(tokens), cut(2 * states)),
        out_shape=(
            jax.ShapeDtypeStruct((tokens, channels), F32),
            jax.ShapeDtypeStruct((tokens, channels), F32),
            jax.ShapeDtypeStruct((2 * states, channels), BF16),
        ),
        scratch_shapes=[
            pltpu.VMEM((tokens + 8, lanes), F32),
            pltpu.VMEM((tokens, lanes), F32),
            pltpu.VMEM((tokens, lanes), F32),
            pltpu.VMEM((tokens, states, 128), F32),
            pltpu.VMEM((tokens, states, 128), F32),
        ],
        compiler_params=params(40),
        cost_estimate=cost(
            tokens * channels * states * 8, tokens * channels * 12, tokens * channels * states
        ),
        name="scan",
    )(
        x_in, edge, dt_low, dt_weight, dt_bias[None], a_log, conv_weight, conv_bias[None],
        d_skip[None], b_and_c,
    )


def prefix_kernel(ends_ref, out_ref):
    blocks, states, lanes = out_ref.shape
    entering = jnp.zeros((states, lanes), F32)
    for i in range(blocks):
        out_ref[i] = entering.astype(BF16)
        entering = (
            ends_ref[i, states:].astype(F32) * entering + ends_ref[i, :states].astype(F32)
        )


def prefix(ends):
    blocks, both, lanes = ends.shape
    return pl.pallas_call(
        prefix_kernel,
        out_shape=jax.ShapeDtypeStruct((blocks, both // 2, lanes), BF16),
        compiler_params=params(16),
        cost_estimate=cost(ends.size, ends.size * 3),
        name="prefix",
    )(ends)


def finish_kernel(read_ref, cum_ref, z_ref, enter_ref, alog_ref, bc_ref, out_ref, sum_ref, c_ref):
    tokens, lanes = z_ref.shape

    @pl.when(pl.program_id(0) == 0)
    def _():
        spread_states(bc_ref, 1, c_ref)

    rates = -jnp.exp(alog_ref[...]) * LOG2E
    entering = enter_ref[...].astype(F32)

    def eight(g, carry):
        at = pl.multiple_of(g * 8, 8)
        cum8 = cum_ref[pl.ds(at, 8)]
        reads = []
        for i in range(8):
            kept = jnp.exp2(rates * cum8[i : i + 1]) * entering
            reads.append(jnp.sum(tiled_lanes(c_ref[at + i], lanes) * kept, axis=0, keepdims=True))
        sum_ref[pl.ds(at, 8)] = jnp.concatenate(reads, axis=0)
        return carry

    lax.fori_loop(0, tokens // 8, eight, 0)
    z = z_ref[...].astype(F32)
    out_ref[...] = ((read_ref[...] + sum_ref[...]) * (z * jax.nn.sigmoid(z))).astype(BF16)


def finish(read, cum, z_gate, entering, a_log, b_and_c):
    tokens, channels = z_gate.shape
    states = a_log.shape[0]
    lanes = math.gcd(512, channels)

    def cut(rows):
        return pl.BlockSpec((rows, lanes), lambda i: (0, i))

    return pl.pallas_call(
        finish_kernel,
        grid=(channels // lanes,),
        in_specs=[
            cut(tokens), cut(tokens), cut(tokens), cut(states), cut(states),
            pl.BlockSpec(b_and_c.shape, lambda i: (0, 0, 0)),
        ],
        out_specs=cut(tokens),
        out_shape=jax.ShapeDtypeStruct((tokens, channels), BF16),
        scratch_shapes=[
            pltpu.VMEM((tokens, lanes), F32),
            pltpu.VMEM((tokens, states, 128), F32),
        ],
        compiler_params=params(40),
        cost_estimate=cost(
            tokens * channels * states * 5, tokens * channels * 12, tokens * channels * states
        ),
        name="finish",
    )(read, cum, z_gate, entering, a_log, b_and_c)


def turned(value, axis, by):
    count = lax.axis_size(axis)
    return lax.ppermute(value, axis, [(i, (i + by) % count) for i in range(count)])


def local(
    x_in,
    z_gate,
    dt_low,
    dt_weight,
    dt_bias,
    a_log,
    conv_weight,
    conv_bias,
    d_skip,
    b_and_c,
    hidden,
    router,
    expert_ids,
    w_gate,
    w_down,
):
    blocks = lax.axis_size("seq")
    feature_parts = lax.axis_size("exp")
    tokens, features = hidden.shape
    experts = router.shape[1]
    copies = blocks // experts
    pack = packing(features)
    ids = expert_ids.T

    outgoing, logits = route(ids, hidden, router.T, copies, pack)
    outgoing = outgoing.reshape((blocks,) + outgoing.shape[2:])
    arrived = lax.all_to_all(outgoing, "seq", split_axis=0, concat_axis=0, tiled=True)

    edge, _ = lax.optimization_barrier((x_in[tokens - (conv_weight.shape[0] - 1) :], logits))
    edge = lax.ppermute(edge, "seq", [(i, i + 1) for i in range(blocks - 1)])
    logits = lax.psum(logits, "exp")
    weights = blend_weights(ids, logits, copies, pack)

    read, cum, ends = scan(
        x_in, edge, dt_low, dt_weight, dt_bias, a_log, conv_weight, conv_bias, d_skip, b_and_c
    )
    both, channels = ends.shape
    ends = lax.all_to_all(
        ends.reshape(both, blocks, channels // blocks).transpose(1, 0, 2),
        "seq", split_axis=0, concat_axis=0, tiled=True,
    )
    entering = lax.all_to_all(prefix(ends), "seq", split_axis=0, concat_axis=0, tiled=True)
    entering = entering.transpose(1, 0, 2).reshape(both // 2, channels)
    mamba_out = finish(read, cum, z_gate, entering, a_log, b_and_c)

    amount = w_gate.shape[1] // GATE_PARTS
    halves = []
    for q in range(GATE_PARTS):
        own = gate_part(arrived, w_gate, q * amount, amount, pack)
        halves.append([own] + [turned(own, "exp", d) for d in range(1, feature_parts)])
    produced = None
    for q in range(GATE_PARTS):
        produced = down_part(
            halves[q], w_down, q * amount, produced, q == GATE_PARTS - 1, blocks, pack
        )
    back = lax.all_to_all(produced, "seq", split_axis=0, concat_axis=0, tiled=True)
    moe_out = combine(back, weights, tokens, features, pack)
    return mamba_out, moe_out


def solution(mesh):
    return jax.shard_map(
        local,
        mesh=mesh,
        in_specs=(
            P("seq", "exp"),
            P("seq", "exp"),
            P("seq", None),
            P(None, "exp"),
            P("exp"),
            P(None, "exp"),
            P(None, "exp"),
            P("exp"),
            P("exp"),
            P(None, None, "seq"),
            P("seq", "exp"),
            P("exp", None),
            P("seq", None),
            P("exp", "seq"),
            P("seq", "exp"),
        ),
        out_specs=(P("seq", "exp"), P("seq", "exp")),
        check_vma=False,
    )
```

time: 278 us -> 155 us (0.56)
  waiting for transfers between devices: 106 us -> 13.9 us
  Pallas kernels: 0 us -> 58.8 us
  blocking collectives: 2.46 us -> 56.8 us
  other arithmetic: 41.9 us -> 0 us
  matrix products: 33.8 us -> 0 us
  local copies, waits for them, and re-layouts: 42.6 us -> 9.25 us
  starting transfers between devices: 31.6 us -> 14.1 us
  between operations: 15.8 us -> 0.97 us
    all_gather x2 -> x0, waiting for transfers between devices: 67.8 us -> none  [carried_in(): lax.all_gather(a.astype(kind), axis)]
    pallas_call x0 -> x10, Pallas kernels: none -> 58.8 us  [the longest x2 21.6 us: down_part(): pl.pallas_call(functools.partial(down_kernel, pack, len(parts), last), gr...]
    all_to_all x0 -> x2, blocking collectives: none -> 53.4 us  [the longest x1 38.1 us: local(): lax.all_to_all(outgoing, 'seq', split_axis=0, concat_axis=0, tiled=True)]
    dot_general x6 -> x0, matrix products: 33.8 us -> none  [the longest x1 14.4 us: local(): produced = jnp.dot(acted, w_down, preferred_element_type=jnp.float32)]
    all_to_all x2, waiting for transfers between devices: 37.7 us -> 12.3 us  [the longest x1 12.3 us: local(): lax.all_to_all(produced, 'seq', split_axis=0, concat_axis=0, tiled=True)]
    slice x10 -> x1, local copies, waits for them, and re-layouts: 22.9 us -> 0.02 us  [local(): x_in[tokens - (conv_weight.shape[0] - 1):]]
    all_to_all x2, starting transfers between devices: 26.6 us -> 11.1 us  [the longest x1 6.98 us: local(): lax.all_to_all(produced, 'seq', split_axis=0, concat_axis=0, tiled=True)]
    reduce_sum x24 -> x0, other arithmetic: 15.1 us -> none  [the longest x20 11.1 us: advance(): reads.append(jnp.sum(step_c[position][:, None] * running, axis=0))]
  transfers between devices with their start and end apart: 6 -> 5, of which waited for: 3 -> 2; matrix products, arithmetic and copies ran while one was open for 23% -> 1% of each run, Pallas kernels for 0% -> 31%
where the time goes in v1:
time: 155 us; the launch traced here: 154 us
  Pallas kernels  58.8 us (38%)
  blocking collectives  56.8 us (37%)
  starting transfers between devices  14.1 us (9%)
  waiting for transfers between devices  13.9 us (9%)
  local copies, waits for them, and re-layouts  9.25 us (6%)
    all_to_all x1, blocking collectives, local(): lax.all_to_all(outgoing, 'seq', split_axis=0, concat_axis=0, tiled=True)  38.1 us
    pallas_call x2, Pallas kernels, down_part(): pl.pallas_call(functools.partial(down_kernel, pack, len(parts), last), gr...  21.6 us
    pallas_call x2, Pallas kernels, gate_part(): pl.pallas_call(functools.partial(gate_kernel, pack), grid=(amount // bloc...  17.4 us
    all_to_all x1, blocking collectives, local(): lax.all_to_all(ends.reshape(both, blocks, channels // blocks).transpose(1...  15.3 us
    all_to_all x1, waiting for transfers between devices, local(): lax.all_to_all(produced, 'seq', split_axis=0, concat_axis=0, tiled=True)  12.3 us
    pallas_call x1, Pallas kernels, scan(): pl.pallas_call(scan_kernel, grid=(channels // lanes,), in_specs=[cut(toke...  10.6 us
    unnamed x46, local copies, waits for them, and re-layouts  8.29 us
    all_to_all x1, starting transfers between devices, local(): lax.all_to_all(produced, 'seq', split_axis=0, concat_axis=0, tiled=True)  6.98 us
  transfers between devices with their start and end apart: 5, of which 2 were waited for; matrix products, arithmetic and copies ran while one was open for 1% of the time, Pallas kernels for 31%

profile of v1, /device:TPU:0, one launch (start us, length us, event | category | flops | bytes accessed | tf_op | source)
XLA Modules:
  0.0 153.9 jit_solution(3730871453673869550)
XLA Ops:
  0.6 0.9 copy-done.2
  1.6 0.8 copy-done.3
  2.3 0.7 copy-done.6
  4.3 38.1 %all_to_all.20.arrived_ref = bf16[16,16,2304]{2,1,0:T(8,128)(2,1)S(1)} all-to-all(bf16[16,16,2304]{2,1,0:T(8,128)(2,1)S(1)} %bitcast.16), channel_id=1, replica_groups=mesh['seq'=16,'exp'=2] {'seq'}, dimensions={0} | all-to-all | bytes 2359296 | tf_op jit(solution)/shard_map/all_to_all | solution.py:507
  42.3 8.6 %gate.3.refs_0_ = bf16[288,3072]{1,0:T(8,128)(2,1)S(1)} custom-call(bf16[16,16,2304]{2,1,0:T(8,128)(2,1)S(1)} %all_to_all.20.arrived_ref, bf16[2048,6144]{1,0:T(8,128)(2,1)} %w_ref.3), custom_call_target="tpu_custom_call" | custom-call | flops 3623878656 | bytes 12582912 | tf_op jit(solution)/shard_map/gate/pallas_call | solution.py:179
  51.1 8.8 %gate.2.refs_0_ = bf16[288,3072]{1,0:T(8,128)(2,1)S(1)} custom-call(bf16[16,16,2304]{2,1,0:T(8,128)(2,1)S(1)} %all_to_all.20.arrived_ref, bf16[2048,6144]{1,0:T(8,128)(2,1)} %w_ref.3), custom_call_target="tpu_custom_call" | custom-call | flops 3623878656 | bytes 12582912 | tf_op jit(solution)/shard_map/gate/pallas_call | solution.py:179
  60.4 2.5 %collective-permute-start = (bf16[3,4096]{1,0:T(4,128)(2,1)S(1)}, bf16[3,4096]{1,0:T(4,128)(2,1)S(1)}, u32[]{:S(2)}, u32[]{:S(2)}) collective-permute-start(bf16[3,4096]{1,0:T(4,128)(2,1)S(1)} %slice.3), channel_id=1, source_target_pairs={{0,2},{2,4},{4,6},{6,8},{8,10},{10,12},{12,14},{14,16},{16,18},{18... | collective-permute-start | bytes 73736 | tf_op jit(solution)/shard_map/ppermute | solution.py:510
  62.8 1.6 %collective-permute-done.edge_ref = bf16[3,4096]{1,0:T(4,128)(2,1)S(1)} collective-permute-done((bf16[3,4096]{1,0:T(4,128)(2,1)S(1)}, bf16[3,4096]{1,0:T(4,128)(2,1)S(1)}, u32[]{:S(2)}, u32[]{:S(2)}) %collective-permute-start) | collective-permute-done | bytes 24608 | tf_op jit(solution)/shard_map/ppermute | solution.py:510
  64.5 10.6 %scan.1 = (f32[64,4096]{1,0:T(8,128)S(1)}, f32[64,4096]{1,0:T(8,128)S(1)}, bf16[32,4096]{1,0:T(8,128)(2,1)S(1)}) custom-call(bf16[64,4096]{1,0:T(8,128)(2,1)S(1)} %copy-done.8, bf16[3,4096]{1,0:T(4,128)(2,1)S(1)} %collective-permute-done.edge_ref, bf16[64,256]{1,0:T(8,128)(2,1)S(1)} %copy-done.14, bf16[256,4096]{1,0:T(8,128)(2,1)S(1)} %copy-done.9, ...), custom_call_target="tpu_custom_call" | custom-call | flops 33554432 | bytes 3145728 | tf_op jit(solution)/shard_map/scan/pallas_call | solution.py:369
  75.1 1.0 copy-done.19
  76.1 0.9 copy-done.21
  77.0 15.3 %all_to_all.21.ends_ref = bf16[16,32,256]{2,1,0:T(8,128)(2,1)S(1)} all-to-all(bf16[16,32,256]{2,1,0:T(8,128)(2,1)S(1)} %bitcast.25), channel_id=1, replica_groups=mesh['seq'=16,'exp'=2] {'seq'}, dimensions={0} | all-to-all | bytes 524288 | tf_op jit(solution)/shard_map/all_to_all | solution.py:518
  92.4 0.6 copy-done.1
  93.1 4.2 %all-to-all-start.1 = ((bf16[16,16,256]{2,1,0:T(8,128)(2,1)}), bf16[16,16,256]{2,1,0:T(8,128)(2,1)}, u32[]{:S(2)}, u32[]{:S(2)}) async-start(bf16[16,16,256]{2,1,0:T(8,128)(2,1)} %copy-done.1), calls=%async_computation.1 | async-start | bytes 262144 | tf_op jit(solution)/shard_map/all_to_all | solution.py:522
  97.3 9.6 %down.2.refs_3_ = f32[288,2048]{1,0:T(8,128)S(1)} custom-call(bf16[288,3072]{1,0:T(8,128)(2,1)S(1)} %gate.3.refs_0_, bf16[288,3072]{1,0:T(8,128)(2,1)} %collective-permute-done.2.refs_1_, bf16[6144,2048]{1,0:T(8,128)(2,1)} %refs_2_.3), custom_call_target="tpu_custom_call" | custom-call | flops 3623878656 | bytes 12582912 | tf_op jit(solution)/shard_map/down/pallas_call | solution.py:252
  106.9 1.4 copy-done
  108.3 11.9 %down.3 = bf16[16,16,2304]{2,1,0:T(8,128)(2,1)} custom-call(bf16[288,3072]{1,0:T(8,128)(2,1)S(1)} %gate.2.refs_0_, bf16[288,3072]{1,0:T(8,128)(2,1)} %collective-permute-done.1.refs_1_, bf16[6144,2048]{1,0:T(8,128)(2,1)} %refs_2_.3, f32[288,2048]{1,0:T(8,128)} %copy-done), custom_call_target="tpu_custom_call" | custom-call | flops 3623878656 | bytes 12582912 | tf_op jit(solution)/shard_map/down/pallas_call | solution.py:252
  120.3 7.0 %all-to-all-start.3 = ((bf16[16,16,2304]{2,1,0:T(8,128)(2,1)}), bf16[16,16,2304]{2,1,0:T(8,128)(2,1)S(1)}, u32[]{:S(2)}, u32[]{:S(2)}) async-start(bf16[16,16,2304]{2,1,0:T(8,128)(2,1)} %down.3), calls=%async_computation.3 | async-start | bytes 2359296 | tf_op jit(solution)/shard_map/all_to_all | solution.py:536
  127.3 3.4 %psum.7.logits_ref = f32[64,8]{1,0:T(8,128)S(1)} all-reduce(f32[64,8]{1,0:T(8,128)S(1)} %copy-done.5), channel_id=1, replica_groups=mesh['seq'=16,'exp'=2] {'exp'}, use_global_device_ids=true, to_apply=%region_0.0 | all-reduce | flops 512 | bytes 4096 | tf_op jit(solution)/shard_map/psum | solution.py:511
  131.1 0.9 copy.21
  132.1 1.2 copy-done.22
  133.3 6.7 %finish.1 = bf16[64,4096]{1,0:T(8,128)(2,1)} custom-call(f32[64,4096]{1,0:T(8,128)S(1)} %copy-done.20, f32[64,4096]{1,0:T(8,128)S(1)} %copy-done.22, bf16[64,4096]{1,0:T(8,128)(2,1)S(1)} %copy-done.10, bf16[16,4096]{1,0:T(8,128)(2,1)S(1)} %bitcast.18, f32[16,4096]{1,0:T(8,128)S(1)} %copy-done.12, f32[2,16,64]{2,1,0:T(8,128)S(1)} %copy-done.18), custom_call_target="tpu_custom_call" | custom-call | flops 20971520 | bytes 3145728 | tf_op jit(solution)/shard_map/finish/pallas_call | solution.py:454
  140.0 12.3 %all-to-all-done.3.back_ref = bf16[16,16,2304]{2,1,0:T(8,128)(2,1)S(1)} async-done(((bf16[16,16,2304]{2,1,0:T(8,128)(2,1)}), bf16[16,16,2304]{2,1,0:T(8,128)(2,1)S(1)}, u32[]{:S(2)}, u32[]{:S(2)}) %all-to-all-start.3) | async-done | bytes 1179680 | tf_op jit(solution)/shard_map/all_to_all | solution.py:536
  152.3 1.5 %combine.1 = bf16[64,2048]{1,0:T(8,128)(2,1)} custom-call(bf16[16,16,2304]{2,1,0:T(8,128)(2,1)S(1)} %all-to-all-done.3.back_ref, bf16[2,64,256]{2,1,0:T(8,128)(2,1)S(1)} %get-tuple-element.17.main_ref, bf16[2,64,256]{2,1,0:T(8,128)(2,1)S(1)} %get-tuple-element.18.extra_ref, f32[2,64,128]{2,1,0:T(8,128)S(1)} %get-tuple-element.19.gates_ref), custom_call_target="tpu_custom_call" | custom-call | flops 150994944 | bytes 1179648 | tf_op jit(solution)/shard_map/combine/pallas_call | solution.py:288
  (48 shorter events, 2.3 us)
Async XLA Ops:
  0.6 1.0 copy-start.2
  51.0 9.4 %copy-start.8 = (bf16[64,4096]{1,0:T(8,128)(2,1)S(1)}, bf16[64,4096]{1,0:T(8,128)(2,1)}, u32[]{:S(2)}) copy-start(bf16[64,4096]{1,0:T(8,128)(2,1)} %x_ref.1) | copy-start | bytes 1572868
  51.0 13.4 %copy-start.9 = (bf16[256,4096]{1,0:T(8,128)(2,1)S(1)}, bf16[256,4096]{1,0:T(8,128)(2,1)}, u32[]{:S(2)}) copy-start(bf16[256,4096]{1,0:T(8,128)(2,1)} %dtw_ref.1) | copy-start | bytes 6291460
  51.0 13.4 %copy-start.11 = (f32[16,4096]{1,0:T(8,128)S(1)}, f32[16,4096]{1,0:T(8,128)}, u32[]{:S(2)}) copy-start(f32[16,4096]{1,0:T(8,128)} %alog_ref.3) | copy-start | bytes 786436
  51.0 13.4 %copy-start.13 = (f32[4,4096]{1,0:T(4,128)S(1)}, f32[4,4096]{1,0:T(4,128)}, u32[]{:S(2)}) copy-start(f32[4,4096]{1,0:T(4,128)} %cw_ref.1) | copy-start | bytes 196612
  51.0 13.4 %copy-start.14 = (bf16[64,256]{1,0:T(8,128)(2,1)S(1)}, bf16[64,256]{1,0:T(8,128)(2,1)}, u32[]{:S(2)}) copy-start(bf16[64,256]{1,0:T(8,128)(2,1)} %low_ref.1) | copy-start | bytes 98308
  51.0 13.4 %copy-start.15 = (f32[4096]{0:T(1024)S(1)}, f32[4096]{0:T(1024)}, u32[]{:S(2)}) copy-start(f32[4096]{0:T(1024)} %param.19) | copy-start | bytes 49156
  51.0 13.4 %copy-start.16 = (f32[4096]{0:T(1024)S(1)}, f32[4096]{0:T(1024)}, u32[]{:S(2)}) copy-start(f32[4096]{0:T(1024)} %param.22) | copy-start | bytes 49156
  51.0 13.4 %copy-start.17 = (f32[4096]{0:T(1024)S(1)}, f32[4096]{0:T(1024)}, u32[]{:S(2)}) copy-start(f32[4096]{0:T(1024)} %param.23) | copy-start | bytes 49156
  51.1 13.4 %copy-start.18 = (f32[2,16,64]{2,1,0:T(8,128)S(1)}, f32[2,16,64]{2,1,0:T(8,128)}, u32[]{:S(2)}) copy-start(f32[2,16,64]{2,1,0:T(8,128)} %bc_ref.3) | copy-start | bytes 24580
  51.1 46.2 %collective-permute-start.2 = (bf16[288,3072]{1,0:T(8,128)(2,1)S(1)}, bf16[288,3072]{1,0:T(8,128)(2,1)}, u32[]{:S(2)}, u32[]{:S(2)}) collective-permute-start(bf16[288,3072]{1,0:T(8,128)(2,1)S(1)} %gate.3.refs_0_), channel_id=1, source_target_pairs={{0,1},{1,0},{2,3},{3,2},{4,5},{5,4},{6,7},{7,6},{8,9},{9,8},{10,11... | collective-permute-start | bytes 5308424 | tf_op jit(solution)/shard_map/ppermute | solution.py:477
  59.9 48.4 %collective-permute-start.1 = (bf16[288,3072]{1,0:T(8,128)(2,1)S(1)}, bf16[288,3072]{1,0:T(8,128)(2,1)}, u32[]{:S(2)}, u32[]{:S(2)}) collective-permute-start(bf16[288,3072]{1,0:T(8,128)(2,1)S(1)} %gate.2.refs_0_), channel_id=1, source_target_pairs={{0,1},{1,0},{2,3},{3,2},{4,5},{5,4},{6,7},{7,6},{8,9},{9,8},{10,11... | collective-permute-start | bytes 5308424 | tf_op jit(solution)/shard_map/ppermute | solution.py:477
  60.4 4.1 %collective-permute-start = (bf16[3,4096]{1,0:T(4,128)(2,1)S(1)}, bf16[3,4096]{1,0:T(4,128)(2,1)S(1)}, u32[]{:S(2)}, u32[]{:S(2)}) collective-permute-start(bf16[3,4096]{1,0:T(4,128)(2,1)S(1)} %slice.3), channel_id=1, source_target_pairs={{0,2},{2,4},{4,6},{6,8},{8,10},{10,12},{12,14},{14,16},{16,18},{18... | collective-permute-start | bytes 73736 | tf_op jit(solution)/shard_map/ppermute | solution.py:510
  75.1 1.0 copy-start.19
  76.0 1.0 copy-start.21
  93.1 27.2 %all-to-all-start.1 = ((bf16[16,16,256]{2,1,0:T(8,128)(2,1)}), bf16[16,16,256]{2,1,0:T(8,128)(2,1)}, u32[]{:S(2)}, u32[]{:S(2)}) async-start(bf16[16,16,256]{2,1,0:T(8,128)(2,1)} %copy-done.1), calls=%async_computation.1 | async-start | bytes 262144 | tf_op jit(solution)/shard_map/all_to_all | solution.py:522
  106.9 1.4 copy-start
  120.2 7.0 %copy-start.5 = (f32[64,8]{1,0:T(8,128)S(1)}, f32[64,8]{1,0:T(8,128)}, u32[]{:S(2)}) copy-start(f32[64,8]{1,0:T(8,128)} %copy-done.4) | copy-start | bytes 6148
  120.2 10.4 %copy-start.7 = (s32[64,2]{0,1:T(2,128)S(1)}, s32[64,2]{0,1:T(2,128)}, u32[]{:S(2)}) copy-start(s32[64,2]{0,1:T(2,128)} %param.27) | copy-start | bytes 1540
  120.2 11.8 %copy-start.10 = (bf16[64,4096]{1,0:T(8,128)(2,1)S(1)}, bf16[64,4096]{1,0:T(8,128)(2,1)}, u32[]{:S(2)}) copy-start(bf16[64,4096]{1,0:T(8,128)(2,1)} %z_ref.1) | copy-start | bytes 1572868
  120.3 11.8 %copy-start.12 = (f32[16,4096]{1,0:T(8,128)S(1)}, f32[16,4096]{1,0:T(8,128)}, u32[]{:S(2)}) copy-start(f32[16,4096]{1,0:T(8,128)} %alog_ref.3) | copy-start | bytes 786436
  120.3 11.8 %copy-start.20 = (f32[64,4096]{1,0:T(8,128)S(1)}, f32[64,4096]{1,0:T(8,128)}, u32[]{:S(2)}) copy-start(f32[64,4096]{1,0:T(8,128)} %copy-done.19) | copy-start | bytes 3145732
  120.3 32.1 %all-to-all-start.3 = ((bf16[16,16,2304]{2,1,0:T(8,128)(2,1)}), bf16[16,16,2304]{2,1,0:T(8,128)(2,1)S(1)}, u32[]{:S(2)}, u32[]{:S(2)}) async-start(bf16[16,16,2304]{2,1,0:T(8,128)(2,1)} %down.3), calls=%async_computation.3 | async-start | bytes 2359296 | tf_op jit(solution)/shard_map/all_to_all | solution.py:536
  132.0 1.2 copy-start.22
  (4 other events, 2.7 us)

commit v2 on v1

--- a/solution.py
+++ b/solution.py
@@ -13,7 +13,6 @@
 LOG2E = math.log2(math.e)
 F32 = jnp.float32
 BF16 = jnp.bfloat16
-GATE_PARTS = 2
 
 
 def params(limit):
@@ -151,122 +150,73 @@
     )(ids, logits)
 
 
-def gate_kernel(pack, arrived_ref, w_ref, out_ref, x_ref):
+def unpack_kernel(pack, arrived_ref, out_ref):
     main, extra, cuts, width = pack
     sources = arrived_ref.shape[0]
-    features = x_ref.shape[1]
-
-    @pl.when(pl.program_id(0) == 0)
-    def _():
-        x_ref[: sources * main] = arrived_ref[:, :, :features].reshape(sources * main, features)
-        if extra:
-            folded = arrived_ref[:, :, features:].reshape(sources * main, width)
-            shape = (sources * extra, sources * main)
-            for c in range(cuts):
-                pick = (iota(shape, 1) == iota(shape, 0) * cuts + c).astype(BF16)
-                x_ref[sources * main :, c * width : (c + 1) * width] = dot(pick, folded).astype(BF16)
-
-    out_ref[...] = dot(x_ref[...], w_ref[...]).astype(BF16)
-
-
-def gate_part(arrived, w_gate, first, amount, pack):
+    features = out_ref.shape[1]
+    out_ref[: sources * main] = arrived_ref[:, :, :features].reshape(sources * main, features)
+    if extra:
+        folded = arrived_ref[:, :, features:].reshape(sources * main, width)
+        shape = (sources * extra, sources * main)
+        for c in range(cuts):
+            pick = (iota(shape, 1) == iota(shape, 0) * cuts + c).astype(BF16)
+            out_ref[sources * main :, c * width : (c + 1) * width] = dot(pick, folded).astype(BF16)
+
+
+def unpack(arrived, features, pack):
     main, extra, _, _ = pack
-    sources = arrived.shape[0]
-    rows = sources * (main + extra)
-    features = w_gate.shape[0]
-    block = math.gcd(512, amount)
-    start = first // block
-    return pl.pallas_call(
-        functools.partial(gate_kernel, pack),
-        grid=(amount // block,),
-        in_specs=[
-            pl.BlockSpec(arrived.shape, lambda i: (0, 0, 0)),
-            pl.BlockSpec((features, block), lambda i: (0, i + start)),
-        ],
-        out_specs=pl.BlockSpec((rows, block), lambda i: (0, i)),
-        out_shape=jax.ShapeDtypeStruct((rows, amount), BF16),
-        scratch_shapes=[pltpu.VMEM((rows, features), BF16)],
-        compiler_params=params(40),
-        cost_estimate=cost(2 * rows * features * amount, features * amount * 2),
-        name="gate",
-    )(arrived, w_gate)
-
-
-def down_kernel(pack, sums, last, *refs):
+    rows = arrived.shape[0] * (main + extra)
+    return pl.pallas_call(
+        functools.partial(unpack_kernel, pack),
+        out_shape=jax.ShapeDtypeStruct((rows, features), BF16),
+        compiler_params=params(24),
+        cost_estimate=cost(arrived.size * 16, arrived.size * 4),
+        name="unpack",
+    )(arrived)
+
+
+def pack_kernel(pack, *refs):
     main, extra, cuts, width = pack
-    part_refs, w_ref = refs[:sums], refs[sums]
-    out_ref, acc_ref = refs[-2], refs[-1]
-    before_ref = refs[sums + 1] if len(refs) == sums + 4 else None
-    step = pl.program_id(0)
-    total = part_refs[0][...].astype(F32)
-    for ref in part_refs[1:]:
-        total = total + ref[...].astype(F32)
-    acted = (total * jax.nn.sigmoid(total)).astype(BF16)
-    product = dot(acted, w_ref[...])
-
-    @pl.when(step == 0)
-    def _():
-        acc_ref[...] = product if before_ref is None else product + before_ref[...]
-
-    @pl.when(step > 0)
-    def _():
-        acc_ref[...] += product
-
-    @pl.when(step == pl.num_programs(0) - 1)
-    def _():
-        if not last:
-            out_ref[...] = acc_ref[...]
-            return
-        sources = out_ref.shape[0]
-        features = acc_ref.shape[1]
-        made = acc_ref[: sources * main].astype(BF16)
-        out_ref[:, :, :features] = made.reshape(sources, main, features)
-        if extra:
-            shape = (sources * main, sources * extra)
-            folded = None
-            for c in range(cuts):
-                piece = acc_ref[sources * main :, c * width : (c + 1) * width].astype(BF16)
-                pick = (iota(shape, 0) == iota(shape, 1) * cuts + c).astype(BF16)
-                part = dot(pick, piece)
-                folded = part if folded is None else folded + part
-            out_ref[:, :, features:] = folded.astype(BF16).reshape(sources, main, width)
-
-
-def down_part(parts, w_down, first, before, last, sources, pack):
-    main, extra, _, width = pack
-    rows, amount = parts[0].shape
-    features = w_down.shape[1]
-    block = math.gcd(512, amount)
-    start = first // block
-    in_specs = [pl.BlockSpec((rows, block), lambda i: (0, i)) for _ in parts]
-    in_specs.append(pl.BlockSpec((block, features), lambda i: (i + start, 0)))
-    args = [*parts, w_down]
-    if before is not None:
-        in_specs.append(pl.BlockSpec((rows, features), lambda i: (0, 0)))
-        args.append(before)
-    if last:
-        shape = jax.ShapeDtypeStruct((sources, main, features + width), BF16)
-    else:
-        shape = jax.ShapeDtypeStruct((rows, features), F32)
-    zeros = (0,) * len(shape.shape)
-    return pl.pallas_call(
-        functools.partial(down_kernel, pack, len(parts), last),
-        grid=(amount // block,),
-        in_specs=in_specs,
-        out_specs=pl.BlockSpec(shape.shape, lambda i: zeros),
-        out_shape=shape,
-        scratch_shapes=[pltpu.VMEM((rows, features), F32)],
-        compiler_params=params(48),
-        cost_estimate=cost(2 * rows * features * amount, features * amount * 2),
-        name="down",
-    )(*args)
+    part_refs, out_ref = refs[:-1], refs[-1]
+    sources = out_ref.shape[0]
+    features = part_refs[0].shape[1]
+    first = sources * main
+
+    def total(rows, columns):
+        value = part_refs[0][rows, columns].astype(F32)
+        for ref in part_refs[1:]:
+            value = value + ref[rows, columns].astype(F32)
+        return value.astype(BF16)
+
+    made = total(slice(0, first), slice(0, features))
+    out_ref[:, :, :features] = made.reshape(sources, main, features)
+    if extra:
+        shape = (sources * main, sources * extra)
+        folded = None
+        for c in range(cuts):
+            piece = total(slice(first, None), slice(c * width, (c + 1) * width))
+            pick = (iota(shape, 0) == iota(shape, 1) * cuts + c).astype(BF16)
+            part = dot(pick, piece)
+            folded = part if folded is None else folded + part
+        out_ref[:, :, features:] = folded.astype(BF16).reshape(sources, main, width)
+
+
+def pack_sum(parts, sources, pack):
+    main, _, _, width = pack
+    features = parts[0].shape[1]
+    return pl.pallas_call(
+        functools.partial(pack_kernel, pack),
+        out_shape=jax.ShapeDtypeStruct((sources, main, features + width), BF16),
+        compiler_params=params(24),
+        cost_estimate=cost(parts[0].size * 16, parts[0].size * 8),
+        name="pack_sum",
+    )(*parts)
 
 
 def combine_kernel(pack, back_ref, main_ref, extra_ref, gates_ref, out_ref):
     main, extra, cuts, width = pack
     sources = back_ref.shape[0]
     tokens, features = out_ref.shape
-    piece = width if extra else features
     back = back_ref[:, :, :features].reshape(sources * main, features)
     folded = back_ref[:, :, features:].reshape(sources * main, width) if extra else None
     total = None
@@ -477,6 +427,25 @@
     return lax.ppermute(value, axis, [(i, (i + by) % count) for i in range(count)])
 
 
+def turned_within(value, copies, by):
+    count = lax.axis_size("seq")
+    return lax.ppermute(
+        value, "seq", [(i, i // copies * copies + (i + by) % copies) for i in range(count)]
+    )
+
+
+def exchanged(value, copies):
+    count = lax.axis_size("seq")
+    groups = [list(range(m, count, copies)) for m in range(copies)]
+    return lax.all_to_all(
+        value, "seq", split_axis=0, concat_axis=0, tiled=True, axis_index_groups=groups
+    )
+
+
+def after(value, *others):
+    return lax.optimization_barrier((value, *others))[0]
+
+
 def local(
     x_in,
     z_gate,
@@ -502,38 +471,51 @@
     pack = packing(features)
     ids = expert_ids.T
 
-    outgoing, logits = route(ids, hidden, router.T, copies, pack)
-    outgoing = outgoing.reshape((blocks,) + outgoing.shape[2:])
-    arrived = lax.all_to_all(outgoing, "seq", split_axis=0, concat_axis=0, tiled=True)
-
-    edge, _ = lax.optimization_barrier((x_in[tokens - (conv_weight.shape[0] - 1) :], logits))
+    outgoing, logits = route(ids, hidden, router.T, 1, pack)
+    arrived = exchanged(outgoing.reshape((experts,) + outgoing.shape[2:]), copies)
+
+    edge = after(x_in[tokens - (conv_weight.shape[0] - 1) :], logits)
     edge = lax.ppermute(edge, "seq", [(i, i + 1) for i in range(blocks - 1)])
-    logits = lax.psum(logits, "exp")
-    weights = blend_weights(ids, logits, copies, pack)
-
     read, cum, ends = scan(
         x_in, edge, dt_low, dt_weight, dt_bias, a_log, conv_weight, conv_bias, d_skip, b_and_c
     )
+    logits = lax.psum(logits, "exp")
+    weights = blend_weights(ids, logits, 1, pack)
+
+    arrived = after(arrived, ends)
+    rows = [unpack(arrived, features, pack)]
+    for d in range(1, copies):
+        rows.append(turned_within(rows[0], copies, d))
+    gated = []
+    for part in rows:
+        if gated:
+            part = after(part, gated[-1][0])
+        own = jnp.dot(part, w_gate, preferred_element_type=F32).astype(BF16)
+        gated.append([own] + [turned(own, "exp", d) for d in range(1, feature_parts)])
+
     both, channels = ends.shape
+    ends = after(ends, gated[-1][0])
     ends = lax.all_to_all(
         ends.reshape(both, blocks, channels // blocks).transpose(1, 0, 2),
         "seq", split_axis=0, concat_axis=0, tiled=True,
     )
-    entering = lax.all_to_all(prefix(ends), "seq", split_axis=0, concat_axis=0, tiled=True)
+    entering = prefix(ends)
+
+    made = []
+    for parts in gated[1:] + gated[:1]:
+        total = sum(p.astype(F32) for p in parts)
+        acted = (total * jax.nn.sigmoid(total)).astype(BF16)
+        made.append(jnp.dot(acted, w_down, preferred_element_type=F32))
+    entering = after(entering, made[0])
+    sums = [made[-1]]
+    for d in range(1, copies):
+        sums.append(turned_within(made[d - 1].astype(BF16), copies, -d))
+
+    entering = lax.all_to_all(entering, "seq", split_axis=0, concat_axis=0, tiled=True)
     entering = entering.transpose(1, 0, 2).reshape(both // 2, channels)
     mamba_out = finish(read, cum, z_gate, entering, a_log, b_and_c)
 
-    amount = w_gate.shape[1] // GATE_PARTS
-    halves = []
-    for q in range(GATE_PARTS):
-        own = gate_part(arrived, w_gate, q * amount, amount, pack)
-        halves.append([own] + [turned(own, "exp", d) for d in range(1, feature_parts)])
-    produced = None
-    for q in range(GATE_PARTS):
-        produced = down_part(
-            halves[q], w_down, q * amount, produced, q == GATE_PARTS - 1, blocks, pack
-        )
-    back = lax.all_to_all(produced, "seq", split_axis=0, concat_axis=0, tiled=True)
+    back = exchanged(pack_sum(sums, experts, pack), copies)
     moe_out = combine(back, weights, tokens, features, pack)
     return mamba_out, moe_out
 

time: 155 us -> 147 us (0.948)
  blocking collectives: 56.8 us -> 3.39 us
  matrix products: 0 us -> 52 us
  Pallas kernels: 58.8 us -> 22.4 us
  starting transfers between devices: 14.1 us -> 38.4 us
  local copies, waits for them, and re-layouts: 9.25 us -> 15.2 us
    all_to_all x2 -> x0, blocking collectives: 53.4 us -> none  [the longest x1 38.1 us: local(): lax.all_to_all(outgoing, 'seq', split_axis=0, concat_axis=0, tiled=True)]
    dot_general x0 -> x4, matrix products: none -> 52 us  [the longest x2 26.5 us: local(): own = jnp.dot(part, w_gate, preferred_element_type=F32).astype(BF16)]
    pallas_call x4 -> x2, Pallas kernels: 38.9 us -> 1.44 us  [the longest x1 1.26 us: pack_sum(): pl.pallas_call(functools.partial(pack_kernel, pack), out_shape=jax.ShapeD...]
    all_to_all x2 -> x4, starting transfers between devices: 11.1 us -> 31.6 us  [the longest x1 14.2 us: local(): lax.all_to_all(ends.reshape(both, blocks, channels // blocks).transpose(1...]
    unnamed x46 -> x38, local copies, waits for them, and re-layouts: 8.29 us -> 12.7 us
    ppermute x0 -> x2, starting transfers between devices: none -> 3.12 us  [turned_within(): lax.ppermute(value, 'seq', [(i, i // copies * copies + (i + by) % copies)...]
    all_to_all x2 -> x4, waiting for transfers between devices: 12.3 us -> 12.2 us  [the longest x1 10.2 us: local(): lax.all_to_all(ends.reshape(both, blocks, channels // blocks).transpose(1...]
  transfers between devices with their start and end apart: 5 -> 9, of which waited for: 2 -> 3; matrix products, arithmetic and copies ran while one was open for 1% -> 28% of each run, Pallas kernels for 31% -> 13%
where the time goes in v2:
time: 147 us; the launch traced here: 146 us
  matrix products  52 us (35%)
  starting transfers between devices  38.4 us (26%)
  Pallas kernels  22.4 us (15%)
  local copies, waits for them, and re-layouts  15.2 us (10%)
  waiting for transfers between devices  13.8 us (9%)
  blocking collectives  3.39 us (2%)
    dot_general x2, matrix products, local(): own = jnp.dot(part, w_gate, preferred_element_type=F32).astype(BF16)  26.5 us
    dot_general x2, matrix products, local(): made.append(jnp.dot(acted, w_down, preferred_element_type=F32))  25.5 us
    all_to_all x1, starting transfers between devices, local(): lax.all_to_all(ends.reshape(both, blocks, channels // blocks).transpose(1...  14.2 us
    all_to_all x2, starting transfers between devices, exchanged(): lax.all_to_all(value, 'seq', split_axis=0, concat_axis=0, tiled=True, axi...  13.1 us
    unnamed x38, local copies, waits for them, and re-layouts  12.7 us
    pallas_call x1, Pallas kernels, scan(): pl.pallas_call(scan_kernel, grid=(channels // lanes,), in_specs=[cut(toke...  10.6 us
    all_to_all x1, waiting for transfers between devices, local(): lax.all_to_all(ends.reshape(both, blocks, channels // blocks).transpose(1...  10.2 us
    pallas_call x1, Pallas kernels, finish(): pl.pallas_call(finish_kernel, grid=(channels // lanes,), in_specs=[cut(to...  6.73 us
  transfers between devices with their start and end apart: 9, of which 3 were waited for; matrix products, arithmetic and copies ran while one was open for 28% of the time, Pallas kernels for 13%

profile of v2, /device:TPU:0, one launch (start us, length us, event | category | flops | bytes accessed | tf_op | source)
XLA Modules:
  0.0 146.0 jit_solution(8043911201780459235)
XLA Ops:
  3.0 1.5 %route.1 = (bf16[8,1,16,2304]{3,2,1,0:T(8,128)(2,1)}, f32[64,8]{1,0:T(8,128)S(1)}) custom-call(s32[2,64]{1,0:T(2,128)S(1)} %bitcast.25, bf16[64,2048]{1,0:T(8,128)(2,1)S(1)} %copy-done, bf16[8,2048]{1,0:T(8,128)(2,1)S(1)} %bitcast.24), custom_call_target="tpu_custom_call" | custom-call | flops 67108864 | bytes 1048576 | tf_op jit(solution)/shard_map/route/pallas_call | solution.py:98
  4.5 7.3 %all-to-all-start = ((bf16[8,16,2304]{2,1,0:T(8,128)(2,1)}), bf16[8,16,2304]{2,1,0:T(8,128)(2,1)S(1)}, u32[]{:S(2)}, u32[]{:S(2)}) async-start(bf16[8,16,2304]{2,1,0:T(8,128)(2,1)} %bitcast.5), calls=%async_computation | async-start | bytes 1179648 | tf_op jit(solution)/shard_map/all_to_all | solution.py:440
  12.6 3.4 %collective-permute-start = (bf16[3,4096]{1,0:T(4,128)(2,1)S(1)}, bf16[3,4096]{1,0:T(4,128)(2,1)S(1)}, u32[]{:S(2)}, u32[]{:S(2)}) collective-permute-start(bf16[3,4096]{1,0:T(4,128)(2,1)S(1)} %slice.3), channel_id=1, source_target_pairs={{0,2},{2,4},{4,6},{6,8},{8,10},{10,12},{12,14},{14,16},{16,18},{18... | collective-permute-start | bytes 73736 | tf_op jit(solution)/shard_map/ppermute | solution.py:478
  16.0 1.6 %collective-permute-done.edge_ref = bf16[3,4096]{1,0:T(4,128)(2,1)S(1)} collective-permute-done((bf16[3,4096]{1,0:T(4,128)(2,1)S(1)}, bf16[3,4096]{1,0:T(4,128)(2,1)S(1)}, u32[]{:S(2)}, u32[]{:S(2)}) %collective-permute-start) | collective-permute-done | bytes 24608 | tf_op jit(solution)/shard_map/ppermute | solution.py:478
  17.6 1.0 copy-done.4
  18.7 1.6 %copy-done.5 = bf16[256,4096]{1,0:T(8,128)(2,1)S(1)} copy-done((bf16[256,4096]{1,0:T(8,128)(2,1)S(1)}, bf16[256,4096]{1,0:T(8,128)(2,1)}, u32[]{:S(2)}) %copy-start.5) | copy-done | bytes 2097176
  20.2 0.9 copy-done.7
  25.7 10.6 %scan.1 = (f32[64,4096]{1,0:T(8,128)S(1)}, f32[64,4096]{1,0:T(8,128)S(1)}, bf16[32,4096]{1,0:T(8,128)(2,1)S(1)}) custom-call(bf16[64,4096]{1,0:T(8,128)(2,1)S(1)} %copy-done.4, bf16[3,4096]{1,0:T(4,128)(2,1)S(1)} %collective-permute-done.edge_ref, bf16[64,256]{1,0:T(8,128)(2,1)S(1)} %copy-done.10, bf16[256,4096]{1,0:T(8,128)(2,1)S(1)} %copy-done.5, ...), custom_call_target="tpu_custom_call" | custom-call | flops 33554432 | bytes 3145728 | tf_op jit(solution)/shard_map/scan/pallas_call | solution.py:319
  36.2 1.0 copy-done.16
  37.5 2.4 %collective-permute-start.1 = (bf16[144,2048]{1,0:T(8,128)(2,1)S(1)}, bf16[144,2048]{1,0:T(8,128)(2,1)S(1)}, u32[]{:S(2)}, u32[]{:S(2)}) collective-permute-start(bf16[144,2048]{1,0:T(8,128)(2,1)S(1)} %unpack.1), channel_id=1, source_target_pairs={{0,2},{2,0},{4,6},{6,4},{8,10},{10,8},{12,14},{14,12},{16,18},{18,... | collective-permute-start | bytes 1769480 | tf_op jit(solution)/shard_map/ppermute | solution.py:432
  39.8 13.2 %convolution_convert_fusion.1 = bf16[144,6144]{1,0:T(8,128)(2,1)} fusion(bf16[144,2048]{1,0:T(8,128)(2,1)S(1)} %unpack.1, bf16[2048,6144]{1,0:T(8,128)(2,1)} %param.28), kind=kOutput, calls=%fused_computation.1 | convolution fusion | flops 3624763392 | bytes 27525120 | tf_op jit(solution)/shard_map/dot_general | solution.py:493
  53.1 13.3 %convolution_convert_fusion = bf16[144,6144]{1,0:T(8,128)(2,1)} fusion(bf16[144,2048]{1,0:T(8,128)(2,1)S(1)} %collective-permute-done.1, bf16[2048,6144]{1,0:T(8,128)(2,1)} %param.28), kind=kOutput, calls=%fused_computation | convolution fusion | flops 3624763392 | bytes 27525120 | tf_op jit(solution)/shard_map/dot_general | solution.py:493
  67.0 14.2 %all-to-all-start.1 = ((bf16[16,32,256]{2,1,0:T(8,128)(2,1)}), bf16[16,32,256]{2,1,0:T(8,128)(2,1)S(1)}, u32[]{:S(2)}, u32[]{:S(2)}) async-start(bf16[16,32,256]{2,1,0:T(8,128)(2,1)} %bitcast.21), calls=%async_computation.1 | async-start | bytes 524288 | tf_op jit(solution)/shard_map/all_to_all | solution.py:498
  81.6 10.2 %all-to-all-done.1.ends_ref = bf16[16,32,256]{2,1,0:T(8,128)(2,1)S(1)} async-done(((bf16[16,32,256]{2,1,0:T(8,128)(2,1)}), bf16[16,32,256]{2,1,0:T(8,128)(2,1)S(1)}, u32[]{:S(2)}, u32[]{:S(2)}) %all-to-all-start.1) | async-done | bytes 262176 | tf_op jit(solution)/shard_map/all_to_all | solution.py:498
  92.5 14.4 %fusion = bf16[144,2048]{1,0:T(8,128)(2,1)} fusion(bf16[6144,2048]{1,0:T(8,128)(2,1)} %param.29, bf16[144,6144]{1,0:T(8,128)(2,1)} %collective-permute-done.2, bf16[144,6144]{1,0:T(8,128)(2,1)} %convolution_convert_fusion), kind=kOutput, calls=%fused_computation.4 | convolution fusion | flops 3630956544 | bytes 29294592 | tf_op jit(solution)/shard_map/dot_general | solution.py:508
  107.7 4.3 %all-to-all-start.2 = ((bf16[16,16,256]{2,1,0:T(8,128)(2,1)}), bf16[16,16,256]{2,1,0:T(8,128)(2,1)}, u32[]{:S(2)}, u32[]{:S(2)}) async-start(bf16[16,16,256]{2,1,0:T(8,128)(2,1)} %prefix.1), calls=%async_computation.2 | async-start | bytes 262144 | tf_op jit(solution)/shard_map/all_to_all | solution.py:514
  112.0 11.1 %fusion.1.refs_0_ = f32[144,2048]{1,0:T(8,128)S(1)} fusion(bf16[6144,2048]{1,0:T(8,128)(2,1)} %param.29, bf16[144,6144]{1,0:T(8,128)(2,1)} %collective-permute-done.3, bf16[144,6144]{1,0:T(8,128)(2,1)S(1)} %copy-done.18), kind=kOutput, calls=%fused_computation.5 | convolution fusion | flops 3630956544 | bytes 29884416 | tf_op jit(solution)/shard_map/dot_general | solution.py:508
  123.2 1.3 pack_sum.1
  124.4 5.9 %all-to-all-start.3 = ((bf16[8,16,2304]{2,1,0:T(8,128)(2,1)}), bf16[8,16,2304]{2,1,0:T(8,128)(2,1)S(1)}, u32[]{:S(2)}, u32[]{:S(2)}) async-start(bf16[8,16,2304]{2,1,0:T(8,128)(2,1)} %pack_sum.1), calls=%async_computation.3 | async-start | bytes 1179648 | tf_op jit(solution)/shard_map/all_to_all | solution.py:440
  130.3 3.4 %psum.7.logits_ref = f32[64,8]{1,0:T(8,128)S(1)} all-reduce(f32[64,8]{1,0:T(8,128)S(1)} %get-tuple-element.15), channel_id=1, replica_groups=mesh['seq'=16,'exp'=2] {'exp'}, use_global_device_ids=true, to_apply=%region_0.0 | all-reduce | flops 512 | bytes 4096 | tf_op jit(solution)/shard_map/psum | solution.py:482
  135.0 1.2 copy-done.17
  136.2 6.7 %finish.1 = bf16[64,4096]{1,0:T(8,128)(2,1)} custom-call(f32[64,4096]{1,0:T(8,128)S(1)} %get-tuple-element.17.read_ref, f32[64,4096]{1,0:T(8,128)S(1)} %copy-done.17, bf16[64,4096]{1,0:T(8,128)(2,1)S(1)} %copy-done.6, bf16[16,4096]{1,0:T(8,128)(2,1)S(1)} %bitcast.23, f32[16,4096]{1,0:T(8,128)S(1)} %copy-done.8, f32[2,16,64]{2,1,0:T(8,128)S(1)} %copy-done.15), custom_call_target="tpu_custom_call" | custom-call | flops 20971520 | bytes 3145728 | tf_op jit(solution)/shard_map/finish/pallas_call | solution.py:404
  143.0 1.9 %all-to-all-done.3.back_ref = bf16[8,16,2304]{2,1,0:T(8,128)(2,1)S(1)} async-done(((bf16[8,16,2304]{2,1,0:T(8,128)(2,1)}), bf16[8,16,2304]{2,1,0:T(8,128)(2,1)S(1)}, u32[]{:S(2)}, u32[]{:S(2)}) %all-to-all-start.3) | async-done | bytes 589856 | tf_op jit(solution)/shard_map/all_to_all | solution.py:440
  144.9 1.1 combine.1
  (48 shorter events, 11.7 us)
Async XLA Ops:
  0.6 1.0 copy-start
  1.6 0.8 copy-start.1
  4.5 32.8 %all-to-all-start = ((bf16[8,16,2304]{2,1,0:T(8,128)(2,1)}), bf16[8,16,2304]{2,1,0:T(8,128)(2,1)S(1)}, u32[]{:S(2)}, u32[]{:S(2)}) async-start(bf16[8,16,2304]{2,1,0:T(8,128)(2,1)} %bitcast.5), calls=%async_computation | async-start | bytes 1179648 | tf_op jit(solution)/shard_map/all_to_all | solution.py:440
  12.6 5.0 %collective-permute-start = (bf16[3,4096]{1,0:T(4,128)(2,1)S(1)}, bf16[3,4096]{1,0:T(4,128)(2,1)S(1)}, u32[]{:S(2)}, u32[]{:S(2)}) collective-permute-start(bf16[3,4096]{1,0:T(4,128)(2,1)S(1)} %slice.3), channel_id=1, source_target_pairs={{0,2},{2,4},{4,6},{6,8},{8,10},{10,12},{12,14},{14,16},{16,18},{18... | collective-permute-start | bytes 73736 | tf_op jit(solution)/shard_map/ppermute | solution.py:478
  17.6 1.0 copy-start.4
  18.7 1.6 %copy-start.5 = (bf16[256,4096]{1,0:T(8,128)(2,1)S(1)}, bf16[256,4096]{1,0:T(8,128)(2,1)}, u32[]{:S(2)}) copy-start(bf16[256,4096]{1,0:T(8,128)(2,1)} %dtw_ref.1) | copy-start | bytes 6291460
  20.2 0.9 copy-start.7
  21.2 0.8 copy-start.9
  22.0 0.8 copy-start.10
  22.8 0.7 copy-start.11
  36.2 1.0 copy-start.16
  37.5 15.6 %collective-permute-start.1 = (bf16[144,2048]{1,0:T(8,128)(2,1)S(1)}, bf16[144,2048]{1,0:T(8,128)(2,1)S(1)}, u32[]{:S(2)}, u32[]{:S(2)}) collective-permute-start(bf16[144,2048]{1,0:T(8,128)(2,1)S(1)} %unpack.1), channel_id=1, source_target_pairs={{0,2},{2,0},{4,6},{6,4},{8,10},{10,8},{12,14},{14,12},{16,18},{18,... | collective-permute-start | bytes 1769480 | tf_op jit(solution)/shard_map/ppermute | solution.py:432
  66.3 26.2 %collective-permute-start.2 = (bf16[144,6144]{1,0:T(8,128)(2,1)}, bf16[144,6144]{1,0:T(8,128)(2,1)}, u32[]{:S(2)}, u32[]{:S(2)}) collective-permute-start(bf16[144,6144]{1,0:T(8,128)(2,1)} %convolution_convert_fusion), channel_id=1, source_target_pairs={{0,1},{1,0},{2,3},{3,2},{4,5},{5,4},{6,7},{7,6},{8,9},{9,8},{10,11... | collective-permute-start | bytes 5308424 | tf_op jit(solution)/shard_map/ppermute | solution.py:427
  67.0 24.8 %all-to-all-start.1 = ((bf16[16,32,256]{2,1,0:T(8,128)(2,1)}), bf16[16,32,256]{2,1,0:T(8,128)(2,1)S(1)}, u32[]{:S(2)}, u32[]{:S(2)}) async-start(bf16[16,32,256]{2,1,0:T(8,128)(2,1)} %bitcast.21), calls=%async_computation.1 | async-start | bytes 524288 | tf_op jit(solution)/shard_map/all_to_all | solution.py:498
  81.3 30.7 %collective-permute-start.3 = (bf16[144,6144]{1,0:T(8,128)(2,1)}, bf16[144,6144]{1,0:T(8,128)(2,1)}, u32[]{:S(2)}, u32[]{:S(2)}) collective-permute-start(bf16[144,6144]{1,0:T(8,128)(2,1)} %convolution_convert_fusion.1), channel_id=1, source_target_pairs={{0,1},{1,0},{2,3},{3,2},{4,5},{5,4},{6,7},{7,6},{8,9},{9,8},{10,11... | collective-permute-start | bytes 5308424 | tf_op jit(solution)/shard_map/ppermute | solution.py:427
  92.5 19.5 %copy-start.18 = (bf16[144,6144]{1,0:T(8,128)(2,1)S(1)}, bf16[144,6144]{1,0:T(8,128)(2,1)}, u32[]{:S(2)}) copy-start(bf16[144,6144]{1,0:T(8,128)(2,1)} %convolution_convert_fusion.1) | copy-start | bytes 5308420
  106.9 16.2 %collective-permute-start.4 = (bf16[144,2048]{1,0:T(8,128)(2,1)}, bf16[144,2048]{1,0:T(8,128)(2,1)S(1)}, u32[]{:S(2)}, u32[]{:S(2)}) collective-permute-start(bf16[144,2048]{1,0:T(8,128)(2,1)} %fusion), channel_id=1, source_target_pairs={{0,2},{2,0},{4,6},{6,4},{8,10},{10,8},{12,14},{14,12},{16,18},{18,... | collective-permute-start | bytes 1769480 | tf_op jit(solution)/shard_map/ppermute | solution.py:432
  107.7 16.7 %all-to-all-start.2 = ((bf16[16,16,256]{2,1,0:T(8,128)(2,1)}), bf16[16,16,256]{2,1,0:T(8,128)(2,1)}, u32[]{:S(2)}, u32[]{:S(2)}) async-start(bf16[16,16,256]{2,1,0:T(8,128)(2,1)} %prefix.1), calls=%async_computation.2 | async-start | bytes 262144 | tf_op jit(solution)/shard_map/all_to_all | solution.py:514
  123.1 10.6 %copy-start.3 = (s32[64,2]{0,1:T(2,128)S(1)}, s32[64,2]{0,1:T(2,128)}, u32[]{:S(2)}) copy-start(s32[64,2]{0,1:T(2,128)} %param.27) | copy-start | bytes 1540
  123.1 11.9 %copy-start.6 = (bf16[64,4096]{1,0:T(8,128)(2,1)S(1)}, bf16[64,4096]{1,0:T(8,128)(2,1)}, u32[]{:S(2)}) copy-start(bf16[64,4096]{1,0:T(8,128)(2,1)} %z_ref.1) | copy-start | bytes 1572868
  123.1 11.9 %copy-start.8 = (f32[16,4096]{1,0:T(8,128)S(1)}, f32[16,4096]{1,0:T(8,128)}, u32[]{:S(2)}) copy-start(f32[16,4096]{1,0:T(8,128)} %alog_ref.3) | copy-start | bytes 786436
  123.1 11.9 %copy-start.15 = (f32[2,16,64]{2,1,0:T(8,128)S(1)}, f32[2,16,64]{2,1,0:T(8,128)}, u32[]{:S(2)}) copy-start(f32[2,16,64]{2,1,0:T(8,128)} %bc_ref.3) | copy-start | bytes 24580
  124.4 20.5 %all-to-all-start.3 = ((bf16[8,16,2304]{2,1,0:T(8,128)(2,1)}), bf16[8,16,2304]{2,1,0:T(8,128)(2,1)S(1)}, u32[]{:S(2)}, u32[]{:S(2)}) async-start(bf16[8,16,2304]{2,1,0:T(8,128)(2,1)} %pack_sum.1), calls=%async_computation.3 | async-start | bytes 1179648 | tf_op jit(solution)/shard_map/all_to_all | solution.py:440
  135.0 1.2 copy-start.17
  (4 other events, 2.8 us)

commit v3 on v2

--- a/solution.py
+++ b/solution.py
@@ -23,6 +23,10 @@
     return pl.CostEstimate(
         flops=int(flops), bytes_accessed=int(moved), transcendentals=int(transcendentals)
     )
+
+
+def in_hbm(*arrays):
+    return [pltpu.with_memory_space_constraint(a, pltpu.HBM) for a in arrays]
 
 
 def iota(shape, dim):
@@ -104,7 +108,7 @@
         compiler_params=params(40),
         cost_estimate=cost(2 * tokens * experts * main * features * 2, hidden.size * 8),
         name="route",
-    )(ids, hidden, router)
+    )(ids, *in_hbm(hidden, router))
 
 
 def weights_kernel(pack, copies, ids_ref, logits_ref, main_ref, extra_ref, gates_ref):
@@ -150,6 +154,110 @@
     )(ids, logits)
 
 
+ANYWHERE = pl.BlockSpec(memory_space=pl.ANY)
+INSIDE = pl.BlockSpec(memory_space=pltpu.VMEM)
+AHEAD = 4
+
+
+def streamed(from_ref, to_ref, sems, dim, chunk, use):
+    count = from_ref.shape[dim] // chunk
+
+    def copy(i):
+        at = pl.ds(pl.multiple_of(i * chunk, chunk), chunk)
+        part = (slice(None), at) if dim else (at, slice(None))
+        return pltpu.make_async_copy(from_ref.at[part], to_ref.at[part], sems.at[i])
+
+    for i in range(min(AHEAD, count)):
+        copy(i).start()
+
+    def step(i, carry):
+        copy(i).wait()
+
+        @pl.when(i + AHEAD < count)
+        def _():
+            copy(i + AHEAD).start()
+
+        use(i)
+        return carry
+
+    lax.fori_loop(0, count, step, 0)
+
+
+def gate_kernel(chunk, x_ref, w_ref, out_ref, held_ref, sems):
+    def use(i):
+        at = pl.ds(pl.multiple_of(i * chunk, chunk), chunk)
+        out_ref[:, at] = dot(x_ref[...], held_ref[:, at]).astype(BF16)
+
+    streamed(w_ref, held_ref, sems, 1, chunk, use)
+
+
+def gate(x, w_gate):
+    rows, features = x.shape
+    amount = w_gate.shape[1]
+    chunk = math.gcd(512, amount)
+    return pl.pallas_call(
+        functools.partial(gate_kernel, chunk),
+        in_specs=[INSIDE, ANYWHERE],
+        out_specs=INSIDE,
+        out_shape=jax.ShapeDtypeStruct((rows, amount), BF16),
+        scratch_shapes=[
+            pltpu.VMEM(w_gate.shape, BF16),
+            pltpu.SemaphoreType.DMA((amount // chunk,)),
+        ],
+        compiler_params=params(44),
+        cost_estimate=cost(2 * rows * features * amount, features * amount * 2),
+        name="gate",
+    )(x, *in_hbm(w_gate))
+
+
+def fill_acted(chunk, part_refs, acted_ref):
+    def piece(i):
+        at = pl.ds(pl.multiple_of(i * chunk, chunk), chunk)
+        total = part_refs[0][:, at].astype(F32)
+        for ref in part_refs[1:]:
+            total = total + ref[:, at].astype(F32)
+        acted_ref[:, at] = (total * jax.nn.sigmoid(total)).astype(BF16)
+
+    pl.loop(0, acted_ref.shape[1] // chunk)(piece)
+
+
+def down_kernel(chunk, *refs):
+    part_refs, w_ref, out_ref, acted_ref, acc_ref, held_ref, sems = refs[:-6], *refs[-6:]
+
+    def use(i):
+        @pl.when(i == 0)
+        def _():
+            fill_acted(chunk, part_refs, acted_ref)
+            acc_ref[...] = jnp.zeros_like(acc_ref)
+
+        at = pl.ds(pl.multiple_of(i * chunk, chunk), chunk)
+        acc_ref[...] += dot(acted_ref[:, at], held_ref[at])
+
+    streamed(w_ref, held_ref, sems, 0, chunk, use)
+    out_ref[...] = acc_ref[...].astype(out_ref.dtype)
+
+
+def down(parts, w_down, dtype):
+    rows, amount = parts[0].shape
+    features = w_down.shape[1]
+    chunk = math.gcd(512, amount)
+    return pl.pallas_call(
+        functools.partial(down_kernel, chunk),
+        in_specs=[INSIDE] * len(parts) + [ANYWHERE],
+        out_specs=INSIDE,
+        out_shape=jax.ShapeDtypeStruct((rows, features), dtype),
+        scratch_shapes=[
+            pltpu.VMEM((rows, amount), BF16),
+            pltpu.VMEM((rows, features), F32),
+            pltpu.VMEM(w_down.shape, BF16),
+            pltpu.SemaphoreType.DMA((amount // chunk,)),
+        ],
+        compiler_params=params(48),
+        cost_estimate=cost(2 * rows * features * amount, features * amount * 2),
+        name="down",
+    )(*parts, *in_hbm(w_down))
+
+
 def unpack_kernel(pack, arrived_ref, out_ref):
     main, extra, cuts, width = pack
     sources = arrived_ref.shape[0]
@@ -325,8 +433,8 @@
         ],
         out_specs=(cut(tokens), cut(tokens), cut(2 * states)),
         out_shape=(
-            jax.ShapeDtypeStruct((tokens, channels), F32),
-            jax.ShapeDtypeStruct((tokens, channels), F32),
+            pltpu.HBM((tokens, channels), F32),
+            pltpu.HBM((tokens, channels), F32),
             jax.ShapeDtypeStruct((2 * states, channels), BF16),
         ),
         scratch_shapes=[
@@ -342,8 +450,12 @@
         ),
         name="scan",
     )(
-        x_in, edge, dt_low, dt_weight, dt_bias[None], a_log, conv_weight, conv_bias[None],
-        d_skip[None], b_and_c,
+        *in_hbm(x_in),
+        edge,
+        *in_hbm(
+            dt_low, dt_weight, dt_bias[None], a_log, conv_weight, conv_bias[None], d_skip[None],
+            b_and_c,
+        ),
     )
 
 
@@ -419,7 +531,7 @@
             tokens * channels * states * 5, tokens * channels * 12, tokens * channels * states
         ),
         name="finish",
-    )(read, cum, z_gate, entering, a_log, b_and_c)
+    )(*in_hbm(read, cum, z_gate), entering, *in_hbm(a_log, b_and_c))
 
 
 def turned(value, axis, by):
@@ -490,7 +602,7 @@
     for part in rows:
         if gated:
             part = after(part, gated[-1][0])
-        own = jnp.dot(part, w_gate, preferred_element_type=F32).astype(BF16)
+        own = gate(part, w_gate)
         gated.append([own] + [turned(own, "exp", d) for d in range(1, feature_parts)])
 
     both, channels = ends.shape
@@ -503,13 +615,11 @@
 
     made = []
     for parts in gated[1:] + gated[:1]:
-        total = sum(p.astype(F32) for p in parts)
-        acted = (total * jax.nn.sigmoid(total)).astype(BF16)
-        made.append(jnp.dot(acted, w_down, preferred_element_type=F32))
+        made.append(down(parts, w_down, BF16 if len(made) < copies - 1 else F32))
     entering = after(entering, made[0])
     sums = [made[-1]]
     for d in range(1, copies):
-        sums.append(turned_within(made[d - 1].astype(BF16), copies, -d))
+        sums.append(turned_within(made[d - 1], copies, -d))
 
     entering = lax.all_to_all(entering, "seq", split_axis=0, concat_axis=0, tiled=True)
     entering = entering.transpose(1, 0, 2).reshape(both // 2, channels)

time: 147 us -> 126 us (0.86)
  matrix products: 52 us -> 0 us
  Pallas kernels: 22.4 us -> 68.2 us
  local copies, waits for them, and re-layouts: 15.2 us -> 3.61 us
  waiting for transfers between devices: 13.8 us -> 6.95 us
  starting transfers between devices: 38.4 us -> 42.3 us
    dot_general x4 -> x0, matrix products: 52 us -> none  [the longest x2 26.5 us: local(): own = jnp.dot(part, w_gate, preferred_element_type=F32).astype(BF16)]
    pallas_call x0 -> x4, Pallas kernels: none -> 40.6 us  [the longest x2 22.1 us: down(): pl.pallas_call(functools.partial(down_kernel, chunk), in_specs=[INSIDE] *...]
    unnamed x38 -> x12, local copies, waits for them, and re-layouts: 12.7 us -> 2.01 us
    all_to_all x1, waiting for transfers between devices: 10.2 us -> 0.01 us  [local(): lax.all_to_all(ends.reshape(both, blocks, channels // blocks).transpose(1...]
    ppermute x2, waiting for transfers between devices: 0.01 us -> 2.93 us  [turned_within(): lax.ppermute(value, 'seq', [(i, i // copies * copies + (i + by) % copies)...]
    pallas_call x1, Pallas kernels: 6.73 us -> 8.47 us  [finish(): pl.pallas_call(finish_kernel, grid=(channels // lanes,), in_specs=[cut(to...]
    pallas_call x1, Pallas kernels: 10.6 us -> 12.1 us  [scan(): pl.pallas_call(scan_kernel, grid=(channels // lanes,), in_specs=[cut(toke...]
  transfers between devices with their start and end apart: 9 -> 9, of which waited for: 3 -> 3; matrix products, arithmetic and copies ran while one was open for 28% -> 1% of each run, Pallas kernels for 13% -> 44%
where the time goes in v3:
time: 126 us; the launch traced here: 125 us
  Pallas kernels  68.2 us (54%)
  starting transfers between devices  42.3 us (34%)
  waiting for transfers between devices  6.95 us (6%)
  local copies, waits for them, and re-layouts  3.61 us (3%)
  blocking collectives  3.41 us (3%)
    pallas_call x2, Pallas kernels, down(): pl.pallas_call(functools.partial(down_kernel, chunk), in_specs=[INSIDE] *...  22.1 us
    pallas_call x2, Pallas kernels, gate(): pl.pallas_call(functools.partial(gate_kernel, chunk), in_specs=[INSIDE, A...  18.5 us
    all_to_all x1, starting transfers between devices, local(): lax.all_to_all(ends.reshape(both, blocks, channels // blocks).transpose(1...  15.3 us
    all_to_all x2, starting transfers between devices, exchanged(): lax.all_to_all(value, 'seq', split_axis=0, concat_axis=0, tiled=True, axi...  13.2 us
    pallas_call x1, Pallas kernels, scan(): pl.pallas_call(scan_kernel, grid=(channels // lanes,), in_specs=[cut(toke...  12.1 us
    pallas_call x1, Pallas kernels, finish(): pl.pallas_call(finish_kernel, grid=(channels // lanes,), in_specs=[cut(to...  8.47 us
    all_to_all x1, starting transfers between devices, local(): lax.all_to_all(entering, 'seq', split_axis=0, concat_axis=0, tiled=True)  5.56 us
    ppermute x2, starting transfers between devices, turned_within(): lax.ppermute(value, 'seq', [(i, i // copies * copies + (i + by) % copies)...  4.29 us
  transfers between devices with their start and end apart: 9, of which 3 were waited for; matrix products, arithmetic and copies ran while one was open for 1% of the time, Pallas kernels for 44%

profile of v3, /device:TPU:0, one launch (start us, length us, event | category | flops | bytes accessed | tf_op | source)
XLA Modules:
  0.0 125.2 jit_solution(11733456699358166641)
XLA Ops:
  1.3 2.4 %route.1 = (bf16[8,1,16,2304]{3,2,1,0:T(8,128)(2,1)}, f32[64,8]{1,0:T(8,128)S(1)}) custom-call(s32[2,64]{1,0:T(2,128)S(1)} %bitcast.18, bf16[64,2048]{1,0:T(8,128)(2,1)} %hidden_ref.1, bf16[8,2048]{1,0:T(8,128)(2,1)} %bitcast.22), custom_call_target="tpu_custom_call" | custom-call | flops 67108864 | bytes 1048576 | tf_op jit(solution)/shard_map/route/pallas_call | solution.py:102
  4.3 7.3 %all-to-all-start = ((bf16[8,16,2304]{2,1,0:T(8,128)(2,1)}), bf16[8,16,2304]{2,1,0:T(8,128)(2,1)S(1)}, u32[]{:S(2)}, u32[]{:S(2)}) async-start(bf16[8,16,2304]{2,1,0:T(8,128)(2,1)} %bitcast.5), calls=%async_computation | async-start | bytes 1179648 | tf_op jit(solution)/shard_map/all_to_all | solution.py:552
  11.6 0.9 slice.3
  12.5 3.4 %collective-permute-start = (bf16[3,4096]{1,0:T(4,128)(2,1)S(1)}, bf16[3,4096]{1,0:T(4,128)(2,1)S(1)}, u32[]{:S(2)}, u32[]{:S(2)}) collective-permute-start(bf16[3,4096]{1,0:T(4,128)(2,1)S(1)} %slice.3), channel_id=1, source_target_pairs={{0,2},{2,4},{4,6},{6,8},{8,10},{10,12},{12,14},{14,16},{16,18},{18... | collective-permute-start | bytes 73736 | tf_op jit(solution)/shard_map/ppermute | solution.py:590
  15.9 1.6 %collective-permute-done.edge_ref = bf16[3,4096]{1,0:T(4,128)(2,1)S(1)} collective-permute-done((bf16[3,4096]{1,0:T(4,128)(2,1)S(1)}, bf16[3,4096]{1,0:T(4,128)(2,1)S(1)}, u32[]{:S(2)}, u32[]{:S(2)}) %collective-permute-start) | collective-permute-done | bytes 24608 | tf_op jit(solution)/shard_map/ppermute | solution.py:590
  17.5 12.1 %scan.1 = (f32[64,4096]{1,0:T(8,128)}, f32[64,4096]{1,0:T(8,128)}, bf16[32,4096]{1,0:T(8,128)(2,1)S(1)}) custom-call(bf16[64,4096]{1,0:T(8,128)(2,1)} %x_ref.1, bf16[3,4096]{1,0:T(4,128)(2,1)S(1)} %collective-permute-done.edge_ref, bf16[64,256]{1,0:T(8,128)(2,1)} %low_ref.1, bf16[256,4096]{1,0:T(8,128)(2,1)} %dtw_ref.1, f32[1,4096]{1,0:T(1,128)} %bitcast.23, ...), custom_call_target="tpu_custom_call" | custom-call | flops 33554432 | bytes 3145728 | tf_op jit(solution)/shard_map/scan/pallas_call | solution.py:427
  29.6 0.7 copy-done
  30.5 2.4 %collective-permute-start.1 = (bf16[144,2048]{1,0:T(8,128)(2,1)S(1)}, bf16[144,2048]{1,0:T(8,128)(2,1)S(1)}, u32[]{:S(2)}, u32[]{:S(2)}) collective-permute-start(bf16[144,2048]{1,0:T(8,128)(2,1)S(1)} %unpack.1.x_ref), channel_id=1, source_target_pairs={{0,2},{2,0},{4,6},{6,4},{8,10},{10,8},{12,14},{14,12},{16,18},{18,... | collective-permute-start | bytes 1769480 | tf_op jit(solution)/shard_map/ppermute | solution.py:544
  32.8 9.2 %gate.2.refs_0_ = bf16[144,6144]{1,0:T(8,128)(2,1)S(1)} custom-call(bf16[144,2048]{1,0:T(8,128)(2,1)S(1)} %unpack.1.x_ref, bf16[2048,6144]{1,0:T(8,128)(2,1)} %w_ref.3), custom_call_target="tpu_custom_call" | custom-call | flops 3623878656 | bytes 25165824 | tf_op jit(solution)/shard_map/gate/pallas_call | solution.py:198
  42.1 2.9 %collective-permute-done.1.x_ref = bf16[144,2048]{1,0:T(8,128)(2,1)S(1)} collective-permute-done((bf16[144,2048]{1,0:T(8,128)(2,1)S(1)}, bf16[144,2048]{1,0:T(8,128)(2,1)S(1)}, u32[]{:S(2)}, u32[]{:S(2)}) %collective-permute-start.1) | collective-permute-done | bytes 589856 | tf_op jit(solution)/shard_map/ppermute | solution.py:544
  45.0 9.2 %gate.3.refs_0_ = bf16[144,6144]{1,0:T(8,128)(2,1)S(1)} custom-call(bf16[144,2048]{1,0:T(8,128)(2,1)S(1)} %collective-permute-done.1.x_ref, bf16[2048,6144]{1,0:T(8,128)(2,1)} %w_ref.3), custom_call_target="tpu_custom_call" | custom-call | flops 3623878656 | bytes 25165824 | tf_op jit(solution)/shard_map/gate/pallas_call | solution.py:198
  54.9 0.7 copy.23
  55.6 15.3 %all-to-all-start.1 = ((bf16[16,32,256]{2,1,0:T(8,128)(2,1)}), bf16[16,32,256]{2,1,0:T(8,128)(2,1)}, u32[]{:S(2)}, u32[]{:S(2)}) async-start(bf16[16,32,256]{2,1,0:T(8,128)(2,1)} %bitcast.20), calls=%async_computation.1 | async-start | bytes 524288 | tf_op jit(solution)/shard_map/all_to_all | solution.py:610
  70.9 11.4 %down.2 = bf16[144,2048]{1,0:T(8,128)(2,1)} custom-call(bf16[144,6144]{1,0:T(8,128)(2,1)S(1)} %gate.3.refs_0_, bf16[144,6144]{1,0:T(8,128)(2,1)} %collective-permute-done.2.refs_1_, bf16[6144,2048]{1,0:T(8,128)(2,1)} %refs_2_.3), custom_call_target="tpu_custom_call" | custom-call | flops 3623878656 | bytes 25165824 | tf_op jit(solution)/shard_map/down/pallas_call | solution.py:244
  82.4 1.9 %collective-permute-start.4 = (bf16[144,2048]{1,0:T(8,128)(2,1)}, bf16[144,2048]{1,0:T(8,128)(2,1)S(1)}, u32[]{:S(2)}, u32[]{:S(2)}) collective-permute-start(bf16[144,2048]{1,0:T(8,128)(2,1)} %down.2), channel_id=1, source_target_pairs={{0,2},{2,0},{4,6},{6,4},{8,10},{10,8},{12,14},{14,12},{16,18},{18,... | collective-permute-start | bytes 1769480 | tf_op jit(solution)/shard_map/ppermute | solution.py:544
  84.3 1.6 %prefix.1 = bf16[16,16,256]{2,1,0:T(8,128)(2,1)} custom-call(bf16[16,32,256]{2,1,0:T(8,128)(2,1)} %all-to-all-done.1.ends_ref), custom_call_target="tpu_custom_call" | custom-call | flops 131072 | bytes 393216 | tf_op jit(solution)/shard_map/prefix/pallas_call | solution.py:474
  85.9 5.6 %all-to-all-start.2 = ((bf16[16,16,256]{2,1,0:T(8,128)(2,1)}), bf16[16,16,256]{2,1,0:T(8,128)(2,1)S(1)}, u32[]{:S(2)}, u32[]{:S(2)}) async-start(bf16[16,16,256]{2,1,0:T(8,128)(2,1)} %prefix.1), calls=%async_computation.2 | async-start | bytes 262144 | tf_op jit(solution)/shard_map/all_to_all | solution.py:624
  91.5 10.6 %down.3.refs_0_ = f32[144,2048]{1,0:T(8,128)S(1)} custom-call(bf16[144,6144]{1,0:T(8,128)(2,1)S(1)} %gate.2.refs_0_, bf16[144,6144]{1,0:T(8,128)(2,1)} %collective-permute-done.3.refs_1_, bf16[6144,2048]{1,0:T(8,128)(2,1)} %refs_2_.3), custom_call_target="tpu_custom_call" | custom-call | flops 3623878656 | bytes 25165824 | tf_op jit(solution)/shard_map/down/pallas_call | solution.py:244
  102.2 1.2 pack_sum.1
  103.5 5.9 %all-to-all-start.3 = ((bf16[8,16,2304]{2,1,0:T(8,128)(2,1)}), bf16[8,16,2304]{2,1,0:T(8,128)(2,1)S(1)}, u32[]{:S(2)}, u32[]{:S(2)}) async-start(bf16[8,16,2304]{2,1,0:T(8,128)(2,1)} %pack_sum.1), calls=%async_computation.3 | async-start | bytes 1179648 | tf_op jit(solution)/shard_map/all_to_all | solution.py:552
  109.4 3.4 %psum.7.logits_ref = f32[64,8]{1,0:T(8,128)S(1)} all-reduce(f32[64,8]{1,0:T(8,128)S(1)} %copy-done.3), channel_id=1, replica_groups=mesh['seq'=16,'exp'=2] {'exp'}, use_global_device_ids=true, to_apply=%region_0.0 | all-reduce | flops 512 | bytes 4096 | tf_op jit(solution)/shard_map/psum | solution.py:594
  113.2 8.5 %finish.1 = bf16[64,4096]{1,0:T(8,128)(2,1)} custom-call(f32[64,4096]{1,0:T(8,128)} %get-tuple-element.17.read_ref, f32[64,4096]{1,0:T(8,128)} %get-tuple-element.18.cum_ref, bf16[64,4096]{1,0:T(8,128)(2,1)} %z_ref.1, bf16[16,4096]{1,0:T(8,128)(2,1)S(1)} %bitcast.17, f32[16,4096]{1,0:T(8,128)} %alog_ref.3, f32[2,16,64]{2,1,0:T(8,128)} %bc_ref.3), custom_call_target="tpu_custom_call" | custom-call | flops 20971520 | bytes 3145728 | tf_op jit(solution)/shard_map/finish/pallas_call | solution.py:516
  121.7 2.4 %all-to-all-done.3.back_ref = bf16[8,16,2304]{2,1,0:T(8,128)(2,1)S(1)} async-done(((bf16[8,16,2304]{2,1,0:T(8,128)(2,1)}), bf16[8,16,2304]{2,1,0:T(8,128)(2,1)S(1)}, u32[]{:S(2)}, u32[]{:S(2)}) %all-to-all-start.3) | async-done | bytes 589856 | tf_op jit(solution)/shard_map/all_to_all | solution.py:552
  124.1 1.1 combine.1
  (22 shorter events, 2.5 us)
Async XLA Ops:
  0.6 0.7 copy-start.4
  3.7 0.6 copy-start.2
  4.3 26.0 %all-to-all-start = ((bf16[8,16,2304]{2,1,0:T(8,128)(2,1)}), bf16[8,16,2304]{2,1,0:T(8,128)(2,1)S(1)}, u32[]{:S(2)}, u32[]{:S(2)}) async-start(bf16[8,16,2304]{2,1,0:T(8,128)(2,1)} %bitcast.5), calls=%async_computation | async-start | bytes 1179648 | tf_op jit(solution)/shard_map/all_to_all | solution.py:552
  12.5 5.0 %collective-permute-start = (bf16[3,4096]{1,0:T(4,128)(2,1)S(1)}, bf16[3,4096]{1,0:T(4,128)(2,1)S(1)}, u32[]{:S(2)}, u32[]{:S(2)}) collective-permute-start(bf16[3,4096]{1,0:T(4,128)(2,1)S(1)} %slice.3), channel_id=1, source_target_pairs={{0,2},{2,4},{4,6},{6,8},{8,10},{10,12},{12,14},{14,16},{16,18},{18... | collective-permute-start | bytes 73736 | tf_op jit(solution)/shard_map/ppermute | solution.py:590
  29.6 0.7 copy-start
  30.5 14.6 %collective-permute-start.1 = (bf16[144,2048]{1,0:T(8,128)(2,1)S(1)}, bf16[144,2048]{1,0:T(8,128)(2,1)S(1)}, u32[]{:S(2)}, u32[]{:S(2)}) collective-permute-start(bf16[144,2048]{1,0:T(8,128)(2,1)S(1)} %unpack.1.x_ref), channel_id=1, source_target_pairs={{0,2},{2,0},{4,6},{6,4},{8,10},{10,8},{12,14},{14,12},{16,18},{18,... | collective-permute-start | bytes 1769480 | tf_op jit(solution)/shard_map/ppermute | solution.py:544
  42.1 12.8 %copy-start.1 = (bf16[32,4096]{1,0:T(8,128)(2,1)S(1)}, bf16[32,4096]{1,0:T(8,128)(2,1)}, u32[]{:S(2)}) copy-start(bf16[32,4096]{1,0:T(8,128)(2,1)} %copy-done) | copy-start | bytes 786436
  54.3 16.6 %collective-permute-start.2 = (bf16[144,6144]{1,0:T(8,128)(2,1)S(1)}, bf16[144,6144]{1,0:T(8,128)(2,1)}, u32[]{:S(2)}, u32[]{:S(2)}) collective-permute-start(bf16[144,6144]{1,0:T(8,128)(2,1)S(1)} %gate.3.refs_0_), channel_id=1, source_target_pairs={{0,1},{1,0},{2,3},{3,2},{4,5},{5,4},{6,7},{7,6},{8,9},{9,8},{10,11... | collective-permute-start | bytes 5308424 | tf_op jit(solution)/shard_map/ppermute | solution.py:539
  54.4 37.1 %collective-permute-start.3 = (bf16[144,6144]{1,0:T(8,128)(2,1)S(1)}, bf16[144,6144]{1,0:T(8,128)(2,1)}, u32[]{:S(2)}, u32[]{:S(2)}) collective-permute-start(bf16[144,6144]{1,0:T(8,128)(2,1)S(1)} %gate.2.refs_0_), channel_id=1, source_target_pairs={{0,1},{1,0},{2,3},{3,2},{4,5},{5,4},{6,7},{7,6},{8,9},{9,8},{10,11... | collective-permute-start | bytes 5308424 | tf_op jit(solution)/shard_map/ppermute | solution.py:539
  55.6 28.7 %all-to-all-start.1 = ((bf16[16,32,256]{2,1,0:T(8,128)(2,1)}), bf16[16,32,256]{2,1,0:T(8,128)(2,1)}, u32[]{:S(2)}, u32[]{:S(2)}) async-start(bf16[16,32,256]{2,1,0:T(8,128)(2,1)} %bitcast.20), calls=%async_computation.1 | async-start | bytes 524288 | tf_op jit(solution)/shard_map/all_to_all | solution.py:610
  82.4 19.8 %collective-permute-start.4 = (bf16[144,2048]{1,0:T(8,128)(2,1)}, bf16[144,2048]{1,0:T(8,128)(2,1)S(1)}, u32[]{:S(2)}, u32[]{:S(2)}) collective-permute-start(bf16[144,2048]{1,0:T(8,128)(2,1)} %down.2), channel_id=1, source_target_pairs={{0,2},{2,0},{4,6},{6,4},{8,10},{10,8},{12,14},{14,12},{16,18},{18,... | collective-permute-start | bytes 1769480 | tf_op jit(solution)/shard_map/ppermute | solution.py:544
  85.9 17.5 %all-to-all-start.2 = ((bf16[16,16,256]{2,1,0:T(8,128)(2,1)}), bf16[16,16,256]{2,1,0:T(8,128)(2,1)S(1)}, u32[]{:S(2)}, u32[]{:S(2)}) async-start(bf16[16,16,256]{2,1,0:T(8,128)(2,1)} %prefix.1), calls=%async_computation.2 | async-start | bytes 262144 | tf_op jit(solution)/shard_map/all_to_all | solution.py:624
  102.2 7.2 %copy-start.3 = (f32[64,8]{1,0:T(8,128)S(1)}, f32[64,8]{1,0:T(8,128)}, u32[]{:S(2)}) copy-start(f32[64,8]{1,0:T(8,128)} %copy-done.2) | copy-start | bytes 6148
  102.2 10.6 %copy-start.5 = (s32[64,2]{0,1:T(2,128)S(1)}, s32[64,2]{0,1:T(2,128)}, u32[]{:S(2)}) copy-start(s32[64,2]{0,1:T(2,128)} %param.27) | copy-start | bytes 1540
  103.5 20.6 %all-to-all-start.3 = ((bf16[8,16,2304]{2,1,0:T(8,128)(2,1)}), bf16[8,16,2304]{2,1,0:T(8,128)(2,1)S(1)}, u32[]{:S(2)}, u32[]{:S(2)}) async-start(bf16[8,16,2304]{2,1,0:T(8,128)(2,1)} %pack_sum.1), calls=%async_computation.3 | async-start | bytes 1179648 | tf_op jit(solution)/shard_map/all_to_all | solution.py:552

commit v4 on v3

--- a/solution.py
+++ b/solution.py
@@ -156,10 +156,10 @@
 
 ANYWHERE = pl.BlockSpec(memory_space=pl.ANY)
 INSIDE = pl.BlockSpec(memory_space=pltpu.VMEM)
-AHEAD = 4
-
-
-def streamed(from_ref, to_ref, sems, dim, chunk, use):
+AHEAD = 6
+
+
+def streamed(from_ref, to_ref, sems, dim, chunk, use, begin=None):
     count = from_ref.shape[dim] // chunk
 
     def copy(i):
@@ -169,6 +169,8 @@
 
     for i in range(min(AHEAD, count)):
         copy(i).start()
+    if begin is not None:
+        begin()
 
     def step(i, carry):
         copy(i).wait()
@@ -194,7 +196,7 @@
 def gate(x, w_gate):
     rows, features = x.shape
     amount = w_gate.shape[1]
-    chunk = math.gcd(512, amount)
+    chunk = math.gcd(256, amount)
     return pl.pallas_call(
         functools.partial(gate_kernel, chunk),
         in_specs=[INSIDE, ANYWHERE],
@@ -222,25 +224,22 @@
 
 
 def down_kernel(chunk, *refs):
-    part_refs, w_ref, out_ref, acted_ref, acc_ref, held_ref, sems = refs[:-6], *refs[-6:]
+    part_refs, w_ref, out_ref, acted_ref, held_ref, sems = refs[:-5], *refs[-5:]
 
     def use(i):
-        @pl.when(i == 0)
-        def _():
-            fill_acted(chunk, part_refs, acted_ref)
-            acc_ref[...] = jnp.zeros_like(acc_ref)
-
         at = pl.ds(pl.multiple_of(i * chunk, chunk), chunk)
-        acc_ref[...] += dot(acted_ref[:, at], held_ref[at])
-
-    streamed(w_ref, held_ref, sems, 0, chunk, use)
-    out_ref[...] = acc_ref[...].astype(out_ref.dtype)
+        out_ref[:, at] = dot(acted_ref[...], held_ref[:, at]).astype(out_ref.dtype)
+
+    def begin():
+        fill_acted(math.gcd(512, acted_ref.shape[1]), part_refs, acted_ref)
+
+    streamed(w_ref, held_ref, sems, 1, chunk, use, begin)
 
 
 def down(parts, w_down, dtype):
     rows, amount = parts[0].shape
     features = w_down.shape[1]
-    chunk = math.gcd(512, amount)
+    chunk = math.gcd(256, features)
     return pl.pallas_call(
         functools.partial(down_kernel, chunk),
         in_specs=[INSIDE] * len(parts) + [ANYWHERE],
@@ -248,9 +247,8 @@
         out_shape=jax.ShapeDtypeStruct((rows, features), dtype),
         scratch_shapes=[
             pltpu.VMEM((rows, amount), BF16),
-            pltpu.VMEM((rows, features), F32),
             pltpu.VMEM(w_down.shape, BF16),
-            pltpu.SemaphoreType.DMA((amount // chunk,)),
+            pltpu.SemaphoreType.DMA((features // chunk,)),
         ],
         compiler_params=params(48),
         cost_estimate=cost(2 * rows * features * amount, features * amount * 2),
@@ -352,9 +350,29 @@
     )(back, *weights)
 
 
-def spread_states(bc, place, spread_ref):
+def spread_states(values, spread_ref):
     for t in range(spread_ref.shape[0]):
-        spread_ref[t] = jnp.broadcast_to(bc[place][:, t : t + 1], spread_ref.shape[1:])
+        spread_ref[t] = jnp.broadcast_to(values[:, t : t + 1], spread_ref.shape[1:])
+
+
+def fill_readers(values, readers_ref):
+    states, tokens = values.shape
+    shape = (states, 8 * states)
+    copy = (iota(shape, 1) % states == iota(shape, 0)).astype(BF16)
+    wide = (tokens, 8 * states)
+    own = iota(wide, 1) // states == iota(wide, 0) % 8
+    high = values.astype(BF16)
+    low = (values - high.astype(F32)).astype(BF16)
+    for place, part in enumerate((high, low)):
+        rows = lax.dot_general(part, copy, (((0,), (0,)), ((), ())), preferred_element_type=F32)
+        rows = jnp.where(own, rows, 0.0)
+        for g in range(tokens // 8):
+            readers_ref[g, place * 8 : place * 8 + 8] = rows[g * 8 : g * 8 + 8]
+
+
+def read_out(readers, stacked):
+    both = dot(readers.astype(BF16), jnp.concatenate(stacked, axis=0))
+    return both[:8] + both[8:]
 
 
 def tiled_lanes(value, lanes):
@@ -363,7 +381,7 @@
 
 def scan_kernel(
     x_ref, edge_ref, low_ref, dtw_ref, dtb_ref, alog_ref, cw_ref, cb_ref, skip_ref, bc_ref,
-    read_ref, cum_ref, ends_ref, padded, delta_ref, fed_ref, b_ref, c_ref,
+    read_ref, cum_ref, ends_ref, padded, delta_ref, fed_ref, b_ref, readers_ref,
 ):
     tokens, lanes = x_ref.shape
     taps = cw_ref.shape[0]
@@ -371,8 +389,8 @@
 
     @pl.when(pl.program_id(0) == 0)
     def _():
-        spread_states(bc_ref, 0, b_ref)
-        spread_states(bc_ref, 1, c_ref)
+        spread_states(bc_ref[0], b_ref)
+        fill_readers(bc_ref[1], readers_ref)
 
     padded[8:] = x_ref[...].astype(F32)
     padded[8 - (taps - 1) : 8] = edge_ref[...].astype(F32)
@@ -393,15 +411,15 @@
         at = pl.multiple_of(g * 8, 8)
         delta8 = delta_ref[pl.ds(at, 8)]
         fed8 = fed_ref[pl.ds(at, 8)]
-        reads, sums = [], []
+        stacked, sums = [], []
         for i in range(8):
             step = delta8[i : i + 1]
             running = running + step
             factor = jnp.exp2(rates * step)
             state = factor * state + tiled_lanes(b_ref[at + i], lanes) * fed8[i : i + 1]
-            reads.append(jnp.sum(tiled_lanes(c_ref[at + i], lanes) * state, axis=0, keepdims=True))
+            stacked.append(state.astype(BF16))
             sums.append(running)
-        read_ref[pl.ds(at, 8)] += jnp.concatenate(reads, axis=0)
+        read_ref[pl.ds(at, 8)] += read_out(readers_ref[g], stacked)
         cum_ref[pl.ds(at, 8)] = jnp.concatenate(sums, axis=0)
         return state, running
 
@@ -442,7 +460,7 @@
             pltpu.VMEM((tokens, lanes), F32),
             pltpu.VMEM((tokens, lanes), F32),
             pltpu.VMEM((tokens, states, 128), F32),
-            pltpu.VMEM((tokens, states, 128), F32),
+            pltpu.VMEM((tokens // 8, 16, 8 * states), F32),
         ],
         compiler_params=params(40),
         cost_estimate=cost(
@@ -480,12 +498,12 @@
     )(ends)
 
 
-def finish_kernel(read_ref, cum_ref, z_ref, enter_ref, alog_ref, bc_ref, out_ref, sum_ref, c_ref):
+def finish_kernel(read_ref, cum_ref, z_ref, enter_ref, alog_ref, bc_ref, out_ref, sum_ref, readers_ref):
     tokens, lanes = z_ref.shape
 
     @pl.when(pl.program_id(0) == 0)
     def _():
-        spread_states(bc_ref, 1, c_ref)
+        fill_readers(bc_ref[1], readers_ref)
 
     rates = -jnp.exp(alog_ref[...]) * LOG2E
     entering = enter_ref[...].astype(F32)
@@ -493,11 +511,10 @@
     def eight(g, carry):
         at = pl.multiple_of(g * 8, 8)
         cum8 = cum_ref[pl.ds(at, 8)]
-        reads = []
+        stacked = []
         for i in range(8):
-            kept = jnp.exp2(rates * cum8[i : i + 1]) * entering
-            reads.append(jnp.sum(tiled_lanes(c_ref[at + i], lanes) * kept, axis=0, keepdims=True))
-        sum_ref[pl.ds(at, 8)] = jnp.concatenate(reads, axis=0)
+            stacked.append((jnp.exp2(rates * cum8[i : i + 1]) * entering).astype(BF16))
+        sum_ref[pl.ds(at, 8)] = read_out(readers_ref[g], stacked)
         return carry
 
     lax.fori_loop(0, tokens // 8, eight, 0)
@@ -524,7 +541,7 @@
         out_shape=jax.ShapeDtypeStruct((tokens, channels), BF16),
         scratch_shapes=[
             pltpu.VMEM((tokens, lanes), F32),
-            pltpu.VMEM((tokens, states, 128), F32),
+            pltpu.VMEM((tokens // 8, 16, 8 * states), F32),
         ],
         compiler_params=params(40),
         cost_estimate=cost(
@@ -583,49 +600,51 @@
     pack = packing(features)
     ids = expert_ids.T
 
+    edge = x_in[tokens - (conv_weight.shape[0] - 1) :]
+    edge = lax.ppermute(edge, "seq", [(i, i + 1) for i in range(blocks - 1)])
     outgoing, logits = route(ids, hidden, router.T, 1, pack)
+    outgoing = after(outgoing, edge)
     arrived = exchanged(outgoing.reshape((experts,) + outgoing.shape[2:]), copies)
 
-    edge = after(x_in[tokens - (conv_weight.shape[0] - 1) :], logits)
-    edge = lax.ppermute(edge, "seq", [(i, i + 1) for i in range(blocks - 1)])
     read, cum, ends = scan(
         x_in, edge, dt_low, dt_weight, dt_bias, a_log, conv_weight, conv_bias, d_skip, b_and_c
     )
-    logits = lax.psum(logits, "exp")
-    weights = blend_weights(ids, logits, 1, pack)
-
+    both, channels = ends.shape
     arrived = after(arrived, ends)
+    ends = lax.all_to_all(
+        ends.reshape(both, blocks, channels // blocks).transpose(1, 0, 2),
+        "seq", split_axis=0, concat_axis=0, tiled=True,
+    )
+
     rows = [unpack(arrived, features, pack)]
     for d in range(1, copies):
         rows.append(turned_within(rows[0], copies, d))
     gated = []
     for part in rows:
-        if gated:
-            part = after(part, gated[-1][0])
+        if len(gated) == 1:
+            entering = prefix(after(ends, gated[0][0]))
+            part = after(part, entering)
+        else:
+            part = after(part, gated[-1][0] if gated else ends)
         own = gate(part, w_gate)
         gated.append([own] + [turned(own, "exp", d) for d in range(1, feature_parts)])
-
-    both, channels = ends.shape
-    ends = after(ends, gated[-1][0])
-    ends = lax.all_to_all(
-        ends.reshape(both, blocks, channels // blocks).transpose(1, 0, 2),
-        "seq", split_axis=0, concat_axis=0, tiled=True,
-    )
-    entering = prefix(ends)
+    entering = after(entering, gated[-1][0])
+    entering = lax.all_to_all(entering, "seq", split_axis=0, concat_axis=0, tiled=True)
+    gated[-1] = list(lax.optimization_barrier((*gated[-1], entering))[:-1])
 
     made = []
     for parts in gated[1:] + gated[:1]:
         made.append(down(parts, w_down, BF16 if len(made) < copies - 1 else F32))
-    entering = after(entering, made[0])
     sums = [made[-1]]
     for d in range(1, copies):
         sums.append(turned_within(made[d - 1], copies, -d))
-
-    entering = lax.all_to_all(entering, "seq", split_axis=0, concat_axis=0, tiled=True)
+    packed = pack_sum(sums, experts, pack)
+    back = exchanged(packed, copies)
+
+    logits = lax.psum(after(logits, packed), "exp")
+    weights = blend_weights(ids, logits, 1, pack)
     entering = entering.transpose(1, 0, 2).reshape(both // 2, channels)
-    mamba_out = finish(read, cum, z_gate, entering, a_log, b_and_c)
-
-    back = exchanged(pack_sum(sums, experts, pack), copies)
+    mamba_out = finish(read, cum, z_gate, after(entering, packed), a_log, b_and_c)
     moe_out = combine(back, weights, tokens, features, pack)
     return mamba_out, moe_out
 

time: 126 us -> 127 us (level)
  starting transfers between devices: 42.3 us -> 24.4 us
  blocking collectives: 3.41 us -> 14.9 us
  Pallas kernels: 68.2 us -> 73.9 us
  waiting for transfers between devices: 6.95 us -> 10 us
  local copies, waits for them, and re-layouts: 3.61 us -> 2.28 us
    all_to_all x0 -> x1, blocking collectives: none -> 11.5 us  [local(): lax.all_to_all(entering, 'seq', split_axis=0, concat_axis=0, tiled=True)]
    all_to_all x1, starting transfers between devices: 15.3 us -> 6.13 us  [local(): lax.all_to_all(ends.reshape(both, blocks, channels // blocks).transpose(1...]
    all_to_all x1, waiting for transfers between devices: 0.01 us -> 6.46 us  [local(): lax.all_to_all(ends.reshape(both, blocks, channels // blocks).transpose(1...]
    all_to_all x1 -> x0, starting transfers between devices: 5.56 us -> none  [local(): lax.all_to_all(entering, 'seq', split_axis=0, concat_axis=0, tiled=True)]
    pallas_call x1, Pallas kernels: 12.1 us -> 17 us  [scan(): pl.pallas_call(scan_kernel, grid=(channels // lanes,), in_specs=[cut(toke...]
    pallas_call x1, Pallas kernels: 8.47 us -> 12.8 us  [finish(): pl.pallas_call(finish_kernel, grid=(channels // lanes,), in_specs=[cut(to...]
    all_to_all x2, starting transfers between devices: 13.2 us -> 9.75 us  [exchanged(): lax.all_to_all(value, 'seq', split_axis=0, concat_axis=0, tiled=True, axi...]
    pallas_call x2, Pallas kernels: 22.1 us -> 18.7 us  [down(): pl.pallas_call(functools.partial(down_kernel, chunk), in_specs=[INSIDE] *...]
  transfers between devices with their start and end apart: 9 -> 8, of which waited for: 3 -> 2; matrix products, arithmetic and copies ran while one was open for 1% -> 1% of each run, Pallas kernels for 44% -> 49%
where the time goes in v4:
time: 127 us; the launch traced here: 126 us
  Pallas kernels  73.9 us (58%)
  starting transfers between devices  24.4 us (19%)
  blocking collectives  14.9 us (12%)
  waiting for transfers between devices  10 us (8%)
  local copies, waits for them, and re-layouts  2.28 us (2%)
    pallas_call x2, Pallas kernels, gate(): pl.pallas_call(functools.partial(gate_kernel, chunk), in_specs=[INSIDE, A...  20.1 us
    pallas_call x2, Pallas kernels, down(): pl.pallas_call(functools.partial(down_kernel, chunk), in_specs=[INSIDE] *...  18.7 us
    pallas_call x1, Pallas kernels, scan(): pl.pallas_call(scan_kernel, grid=(channels // lanes,), in_specs=[cut(toke...  17 us
    pallas_call x1, Pallas kernels, finish(): pl.pallas_call(finish_kernel, grid=(channels // lanes,), in_specs=[cut(to...  12.8 us
    all_to_all x1, blocking collectives, local(): lax.all_to_all(entering, 'seq', split_axis=0, concat_axis=0, tiled=True)  11.5 us
    all_to_all x2, starting transfers between devices, exchanged(): lax.all_to_all(value, 'seq', split_axis=0, concat_axis=0, tiled=True, axi...  9.75 us
    all_to_all x1, waiting for transfers between devices, local(): lax.all_to_all(ends.reshape(both, blocks, channels // blocks).transpose(1...  6.46 us
    all_to_all x1, starting transfers between devices, local(): lax.all_to_all(ends.reshape(both, blocks, channels // blocks).transpose(1...  6.13 us
  transfers between devices with their start and end apart: 8, of which 2 were waited for; matrix products, arithmetic and copies ran while one was open for 1% of the time, Pallas kernels for 49%

profile of v4, /device:TPU:0, one launch (start us, length us, event | category | flops | bytes accessed | tf_op | source)
XLA Modules:
  0.0 126.3 jit_solution(5271479123778959513)
XLA Ops:
  0.6 0.9 slice.3
  1.5 4.8 %collective-permute-start = (bf16[3,4096]{1,0:T(4,128)(2,1)S(1)}, bf16[3,4096]{1,0:T(4,128)(2,1)S(1)}, u32[]{:S(2)}, u32[]{:S(2)}) collective-permute-start(bf16[3,4096]{1,0:T(4,128)(2,1)S(1)} %slice.3), channel_id=1, source_target_pairs={{0,2},{2,4},{4,6},{6,8},{8,10},{10,12},{12,14},{14,16},{16,18},{18... | collective-permute-start | bytes 73736 | tf_op jit(solution)/shard_map/ppermute | solution.py:604
  6.4 0.7 copy-done
  7.0 2.4 %route.1 = (bf16[8,1,16,2304]{3,2,1,0:T(8,128)(2,1)}, f32[64,8]{1,0:T(8,128)S(1)}) custom-call(s32[2,64]{1,0:T(2,128)S(1)} %bitcast.18, bf16[64,2048]{1,0:T(8,128)(2,1)} %hidden_ref.1, bf16[8,2048]{1,0:T(8,128)(2,1)} %bitcast.21), custom_call_target="tpu_custom_call" | custom-call | flops 67108864 | bytes 1048576 | tf_op jit(solution)/shard_map/route/pallas_call | solution.py:102
  9.5 6.0 %all-to-all-start.1 = ((bf16[8,16,2304]{2,1,0:T(8,128)(2,1)}), bf16[8,16,2304]{2,1,0:T(8,128)(2,1)S(1)}, u32[]{:S(2)}, u32[]{:S(2)}) async-start(bf16[8,16,2304]{2,1,0:T(8,128)(2,1)} %bitcast.6), calls=%async_computation.1 | async-start | bytes 1179648 | tf_op jit(solution)/shard_map/all_to_all | solution.py:569
  15.5 17.0 %scan.1 = (f32[64,4096]{1,0:T(8,128)}, f32[64,4096]{1,0:T(8,128)}, bf16[32,4096]{1,0:T(8,128)(2,1)S(1)}) custom-call(bf16[64,4096]{1,0:T(8,128)(2,1)} %x_ref.1, bf16[3,4096]{1,0:T(4,128)(2,1)S(1)} %collective-permute-done.edge_ref, bf16[64,256]{1,0:T(8,128)(2,1)} %low_ref.1, bf16[256,4096]{1,0:T(8,128)(2,1)} %dtw_ref.1, f32[1,4096]{1,0:T(1,128)} %bitcast.22, ...), custom_call_target="tpu_custom_call" | custom-call | flops 33554432 | bytes 3145728 | tf_op jit(solution)/shard_map/scan/pallas_call | solution.py:445
  32.4 0.7 copy.23
  33.2 6.1 %all-to-all-start = ((bf16[16,32,256]{2,1,0:T(8,128)(2,1)}), bf16[16,32,256]{2,1,0:T(8,128)(2,1)S(1)}, u32[]{:S(2)}, u32[]{:S(2)}) async-start(bf16[16,32,256]{2,1,0:T(8,128)(2,1)} %bitcast.15), calls=%async_computation | async-start | bytes 524288 | tf_op jit(solution)/shard_map/all_to_all | solution.py:614
  39.5 2.0 %collective-permute-start.1 = (bf16[144,2048]{1,0:T(8,128)(2,1)S(1)}, bf16[144,2048]{1,0:T(8,128)(2,1)S(1)}, u32[]{:S(2)}, u32[]{:S(2)}) collective-permute-start(bf16[144,2048]{1,0:T(8,128)(2,1)S(1)} %unpack.1.x_ref), channel_id=1, source_target_pairs={{0,2},{2,0},{4,6},{6,4},{8,10},{10,8},{12,14},{14,12},{16,18},{18,... | collective-permute-start | bytes 1769480 | tf_op jit(solution)/shard_map/ppermute | solution.py:561
  41.5 6.5 %all-to-all-done.ends_ref = bf16[16,32,256]{2,1,0:T(8,128)(2,1)S(1)} async-done(((bf16[16,32,256]{2,1,0:T(8,128)(2,1)}), bf16[16,32,256]{2,1,0:T(8,128)(2,1)S(1)}, u32[]{:S(2)}, u32[]{:S(2)}) %all-to-all-start) | async-done | bytes 262176 | tf_op jit(solution)/shard_map/all_to_all | solution.py:614
  47.9 10.1 %gate.2.refs_0_ = bf16[144,6144]{1,0:T(8,128)(2,1)S(1)} custom-call(bf16[144,2048]{1,0:T(8,128)(2,1)S(1)} %unpack.1.x_ref, bf16[2048,6144]{1,0:T(8,128)(2,1)} %w_ref.3), custom_call_target="tpu_custom_call" | custom-call | flops 3623878656 | bytes 25165824 | tf_op jit(solution)/shard_map/gate/pallas_call | solution.py:200
  58.0 10.0 %gate.3.refs_0_ = bf16[144,6144]{1,0:T(8,128)(2,1)S(1)} custom-call(bf16[144,2048]{1,0:T(8,128)(2,1)S(1)} %collective-permute-done.1.x_ref, bf16[2048,6144]{1,0:T(8,128)(2,1)} %w_ref.3), custom_call_target="tpu_custom_call" | custom-call | flops 3623878656 | bytes 25165824 | tf_op jit(solution)/shard_map/gate/pallas_call | solution.py:200
  68.2 0.5 collective-permute-start.2
  68.7 11.5 %all_to_all.20 = bf16[16,16,256]{2,1,0:T(8,128)(2,1)S(1)} all-to-all(bf16[16,16,256]{2,1,0:T(8,128)(2,1)S(1)} %prefix.1), channel_id=1, replica_groups=mesh['seq'=16,'exp'=2] {'seq'}, dimensions={0} | all-to-all | bytes 262144 | tf_op jit(solution)/shard_map/all_to_all | solution.py:632
  80.2 9.3 %down.3 = bf16[144,2048]{1,0:T(8,128)(2,1)S(1)} custom-call(bf16[144,6144]{1,0:T(8,128)(2,1)S(1)} %gate.3.refs_0_, bf16[144,6144]{1,0:T(8,128)(2,1)S(1)} %collective-permute-done.3.refs_1_, bf16[6144,2048]{1,0:T(8,128)(2,1)} %refs_2_.3), custom_call_target="tpu_custom_call" | custom-call | flops 3623878656 | bytes 25165824 | tf_op jit(solution)/shard_map/down/pallas_call | solution.py:243
  89.6 1.1 collective-permute-start.4
  90.7 9.3 %down.2.refs_0_ = f32[144,2048]{1,0:T(8,128)S(1)} custom-call(bf16[144,6144]{1,0:T(8,128)(2,1)S(1)} %gate.2.refs_0_, bf16[144,6144]{1,0:T(8,128)(2,1)S(1)} %collective-permute-done.2.refs_1_, bf16[6144,2048]{1,0:T(8,128)(2,1)} %refs_2_.3), custom_call_target="tpu_custom_call" | custom-call | flops 3623878656 | bytes 25165824 | tf_op jit(solution)/shard_map/down/pallas_call | solution.py:243
  100.1 3.5 %collective-permute-done.4.refs_1_ = bf16[144,2048]{1,0:T(8,128)(2,1)S(1)} collective-permute-done((bf16[144,2048]{1,0:T(8,128)(2,1)S(1)}, bf16[144,2048]{1,0:T(8,128)(2,1)S(1)}, u32[]{:S(2)}, u32[]{:S(2)}) %collective-permute-start.4) | collective-permute-done | bytes 589856 | tf_op jit(solution)/shard_map/ppermute | solution.py:561
  103.6 1.3 pack_sum.1
  104.9 3.7 %all-to-all-start.3 = ((bf16[8,16,2304]{2,1,0:T(8,128)(2,1)}), bf16[8,16,2304]{2,1,0:T(8,128)(2,1)S(1)}, u32[]{:S(2)}, u32[]{:S(2)}) async-start(bf16[8,16,2304]{2,1,0:T(8,128)(2,1)} %pack_sum.1), calls=%async_computation.3 | async-start | bytes 1179648 | tf_op jit(solution)/shard_map/all_to_all | solution.py:569
  108.6 3.4 %psum.7.logits_ref = f32[64,8]{1,0:T(8,128)S(1)} all-reduce(f32[64,8]{1,0:T(8,128)S(1)} %get-tuple-element.34), channel_id=1, replica_groups=mesh['seq'=16,'exp'=2] {'exp'}, use_global_device_ids=true, to_apply=%region_0.0 | all-reduce | flops 512 | bytes 4096 | tf_op jit(solution)/shard_map/psum | solution.py:644
  112.0 0.4 blend_weights.1
  112.4 12.8 %finish.1 = bf16[64,4096]{1,0:T(8,128)(2,1)} custom-call(f32[64,4096]{1,0:T(8,128)} %get-tuple-element.20.read_ref, f32[64,4096]{1,0:T(8,128)} %get-tuple-element.21.cum_ref, bf16[64,4096]{1,0:T(8,128)(2,1)} %z_ref.1, bf16[16,4096]{1,0:T(8,128)(2,1)S(1)} %bitcast.17, f32[16,4096]{1,0:T(8,128)} %alog_ref.3, f32[2,16,64]{2,1,0:T(8,128)} %bc_ref.3), custom_call_target="tpu_custom_call" | custom-call | flops 20971520 | bytes 3145728 | tf_op jit(solution)/shard_map/finish/pallas_call | solution.py:533
  125.2 1.1 combine.1
  (13 shorter events, 0.3 us)
Async XLA Ops:
  1.5 8.0 %collective-permute-start = (bf16[3,4096]{1,0:T(4,128)(2,1)S(1)}, bf16[3,4096]{1,0:T(4,128)(2,1)S(1)}, u32[]{:S(2)}, u32[]{:S(2)}) collective-permute-start(bf16[3,4096]{1,0:T(4,128)(2,1)S(1)} %slice.3), channel_id=1, source_target_pairs={{0,2},{2,4},{4,6},{6,8},{8,10},{10,12},{12,14},{14,16},{16,18},{18... | collective-permute-start | bytes 73736 | tf_op jit(solution)/shard_map/ppermute | solution.py:604
  6.3 0.7 copy-start
  9.5 23.7 %all-to-all-start.1 = ((bf16[8,16,2304]{2,1,0:T(8,128)(2,1)}), bf16[8,16,2304]{2,1,0:T(8,128)(2,1)S(1)}, u32[]{:S(2)}, u32[]{:S(2)}) async-start(bf16[8,16,2304]{2,1,0:T(8,128)(2,1)} %bitcast.6), calls=%async_computation.1 | async-start | bytes 1179648 | tf_op jit(solution)/shard_map/all_to_all | solution.py:569
  33.2 14.7 %all-to-all-start = ((bf16[16,32,256]{2,1,0:T(8,128)(2,1)}), bf16[16,32,256]{2,1,0:T(8,128)(2,1)S(1)}, u32[]{:S(2)}, u32[]{:S(2)}) async-start(bf16[16,32,256]{2,1,0:T(8,128)(2,1)} %bitcast.15), calls=%async_computation | async-start | bytes 524288 | tf_op jit(solution)/shard_map/all_to_all | solution.py:614
  39.5 18.5 %collective-permute-start.1 = (bf16[144,2048]{1,0:T(8,128)(2,1)S(1)}, bf16[144,2048]{1,0:T(8,128)(2,1)S(1)}, u32[]{:S(2)}, u32[]{:S(2)}) collective-permute-start(bf16[144,2048]{1,0:T(8,128)(2,1)S(1)} %unpack.1.x_ref), channel_id=1, source_target_pairs={{0,2},{2,0},{4,6},{6,4},{8,10},{10,8},{12,14},{14,12},{16,18},{18,... | collective-permute-start | bytes 1769480 | tf_op jit(solution)/shard_map/ppermute | solution.py:561
  68.1 12.1 %collective-permute-start.3 = (bf16[144,6144]{1,0:T(8,128)(2,1)S(1)}, bf16[144,6144]{1,0:T(8,128)(2,1)S(1)}, u32[]{:S(2)}, u32[]{:S(2)}) collective-permute-start(bf16[144,6144]{1,0:T(8,128)(2,1)S(1)} %gate.3.refs_0_), channel_id=1, source_target_pairs={{0,1},{1,0},{2,3},{3,2},{4,5},{5,4},{6,7},{7,6},{8,9},{9,8},{10,11... | collective-permute-start | bytes 5308424 | tf_op jit(solution)/shard_map/ppermute | solution.py:556
  68.2 22.5 %collective-permute-start.2 = (bf16[144,6144]{1,0:T(8,128)(2,1)S(1)}, bf16[144,6144]{1,0:T(8,128)(2,1)S(1)}, u32[]{:S(2)}, u32[]{:S(2)}) collective-permute-start(bf16[144,6144]{1,0:T(8,128)(2,1)S(1)} %gate.2.refs_0_), channel_id=1, source_target_pairs={{0,1},{1,0},{2,3},{3,2},{4,5},{5,4},{6,7},{7,6},{8,9},{9,8},{10,11... | collective-permute-start | bytes 5308424 | tf_op jit(solution)/shard_map/ppermute | solution.py:556
  89.6 14.0 %collective-permute-start.4 = (bf16[144,2048]{1,0:T(8,128)(2,1)S(1)}, bf16[144,2048]{1,0:T(8,128)(2,1)S(1)}, u32[]{:S(2)}, u32[]{:S(2)}) collective-permute-start(bf16[144,2048]{1,0:T(8,128)(2,1)S(1)} %down.3), channel_id=1, source_target_pairs={{0,2},{2,0},{4,6},{6,4},{8,10},{10,8},{12,14},{14,12},{16,18},{18,... | collective-permute-start | bytes 1769480 | tf_op jit(solution)/shard_map/ppermute | solution.py:561
  100.1 11.9 %copy-start.1 = (s32[64,2]{0,1:T(2,128)S(1)}, s32[64,2]{0,1:T(2,128)}, u32[]{:S(2)}) copy-start(s32[64,2]{0,1:T(2,128)} %param.27) | copy-start | bytes 1540
  104.9 20.3 %all-to-all-start.3 = ((bf16[8,16,2304]{2,1,0:T(8,128)(2,1)}), bf16[8,16,2304]{2,1,0:T(8,128)(2,1)S(1)}, u32[]{:S(2)}, u32[]{:S(2)}) async-start(bf16[8,16,2304]{2,1,0:T(8,128)(2,1)} %pack_sum.1), calls=%async_computation.3 | async-start | bytes 1179648 | tf_op jit(solution)/shard_map/all_to_all | solution.py:569

commit v5 on v4

--- a/solution.py
+++ b/solution.py
@@ -108,16 +108,19 @@
         compiler_params=params(40),
         cost_estimate=cost(2 * tokens * experts * main * features * 2, hidden.size * 8),
         name="route",
-    )(ids, *in_hbm(hidden, router))
-
-
-def weights_kernel(pack, copies, ids_ref, logits_ref, main_ref, extra_ref, gates_ref):
+    )(*in_hbm(ids, hidden, router))
+
+
+def weights_kernel(pack, copies, ids_ref, *refs):
+    logits_refs, (main_ref, extra_ref, gates_ref) = refs[:-3], refs[-3:]
     main, extra, cuts, _ = pack
-    tokens, experts = logits_ref.shape
+    tokens, experts = logits_refs[0].shape
     ids = ids_ref[...]
     hits, slots = hits_and_slots(ids, experts)
     eye = (iota((tokens, tokens), 0) == iota((tokens, tokens), 1)).astype(BF16)
-    logits = logits_ref[...]
+    logits = logits_refs[0][...]
+    for ref in logits_refs[1:]:
+        logits = logits + ref[...]
     columns = [dot_nt(eye, h.astype(BF16)) for h in hits]
     picked = [jnp.sum(c * logits, axis=1, keepdims=True) for c in columns]
     expert = iota((tokens, experts), 1).astype(F32)
@@ -139,7 +142,7 @@
 
 
 def blend_weights(ids, logits, copies, pack):
-    tokens, experts = logits.shape
+    tokens, experts = logits[0].shape
     total = experts * copies * pack[0]
     return pl.pallas_call(
         functools.partial(weights_kernel, pack, copies),
@@ -151,7 +154,7 @@
         compiler_params=params(40),
         cost_estimate=cost(2 * tokens * total * 16, tokens * total * 8),
         name="blend_weights",
-    )(ids, logits)
+    )(*in_hbm(ids), *logits)
 
 
 ANYWHERE = pl.BlockSpec(memory_space=pl.ANY)
@@ -196,7 +199,7 @@
 def gate(x, w_gate):
     rows, features = x.shape
     amount = w_gate.shape[1]
-    chunk = math.gcd(256, amount)
+    chunk = math.gcd(512, amount)
     return pl.pallas_call(
         functools.partial(gate_kernel, chunk),
         in_specs=[INSIDE, ANYWHERE],
@@ -207,7 +210,7 @@
             pltpu.SemaphoreType.DMA((amount // chunk,)),
         ],
         compiler_params=params(44),
-        cost_estimate=cost(2 * rows * features * amount, features * amount * 2),
+        cost_estimate=cost(rows, rows),
         name="gate",
     )(x, *in_hbm(w_gate))
 
@@ -251,7 +254,7 @@
             pltpu.SemaphoreType.DMA((features // chunk,)),
         ],
         compiler_params=params(48),
-        cost_estimate=cost(2 * rows * features * amount, features * amount * 2),
+        cost_estimate=cost(rows, rows),
         name="down",
     )(*parts, *in_hbm(w_down))
 
@@ -355,24 +358,29 @@
         spread_ref[t] = jnp.broadcast_to(values[:, t : t + 1], spread_ref.shape[1:])
 
 
-def fill_readers(values, readers_ref):
-    states, tokens = values.shape
-    shape = (states, 8 * states)
-    copy = (iota(shape, 1) % states == iota(shape, 0)).astype(BF16)
-    wide = (tokens, 8 * states)
-    own = iota(wide, 1) // states == iota(wide, 0) % 8
-    high = values.astype(BF16)
-    low = (values - high.astype(F32)).astype(BF16)
-    for place, part in enumerate((high, low)):
-        rows = lax.dot_general(part, copy, (((0,), (0,)), ((), ())), preferred_element_type=F32)
-        rows = jnp.where(own, rows, 0.0)
-        for g in range(tokens // 8):
-            readers_ref[g, place * 8 : place * 8 + 8] = rows[g * 8 : g * 8 + 8]
-
-
-def read_out(readers, stacked):
-    both = dot(readers.astype(BF16), jnp.concatenate(stacked, axis=0))
-    return both[:8] + both[8:]
+def row_sums(parts):
+    place = iota(parts[0].shape, 0)
+    for stride in (4, 2, 1):
+        low = place & stride == 0
+        half = len(parts) // 2
+        joined = []
+        for a, b in zip(parts[:half], parts[half:]):
+            kept = jnp.where(low, a, b)
+            moved = jnp.where(low, b, a)
+            if stride == 4:
+                other = pltpu.roll(moved, 4, 0)
+            else:
+                other = jnp.where(low, pltpu.roll(moved, 8 - stride, 0), pltpu.roll(moved, stride, 0))
+            joined.append(kept + other)
+        parts = joined
+    return parts[0]
+
+
+def state_sum(value):
+    total = value[:8]
+    for at in range(8, value.shape[0], 8):
+        total = total + value[at : at + 8]
+    return total
 
 
 def tiled_lanes(value, lanes):
@@ -381,7 +389,7 @@
 
 def scan_kernel(
     x_ref, edge_ref, low_ref, dtw_ref, dtb_ref, alog_ref, cw_ref, cb_ref, skip_ref, bc_ref,
-    read_ref, cum_ref, ends_ref, padded, delta_ref, fed_ref, b_ref, readers_ref,
+    read_ref, cum_ref, ends_ref, padded, delta_ref, fed_ref, totals_ref, b_ref, c_ref,
 ):
     tokens, lanes = x_ref.shape
     taps = cw_ref.shape[0]
@@ -390,7 +398,8 @@
     @pl.when(pl.program_id(0) == 0)
     def _():
         spread_states(bc_ref[0], b_ref)
-        fill_readers(bc_ref[1], readers_ref)
+        spread_states(bc_ref[1], c_ref)
+        totals_ref[...] = jnp.zeros_like(totals_ref)
 
     padded[8:] = x_ref[...].astype(F32)
     padded[8 - (taps - 1) : 8] = edge_ref[...].astype(F32)
@@ -411,23 +420,30 @@
         at = pl.multiple_of(g * 8, 8)
         delta8 = delta_ref[pl.ds(at, 8)]
         fed8 = fed_ref[pl.ds(at, 8)]
-        stacked, sums = [], []
+        reads, sums = [], []
         for i in range(8):
             step = delta8[i : i + 1]
             running = running + step
             factor = jnp.exp2(rates * step)
             state = factor * state + tiled_lanes(b_ref[at + i], lanes) * fed8[i : i + 1]
-            stacked.append(state.astype(BF16))
+            reads.append(state_sum(tiled_lanes(c_ref[at + i], lanes) * state))
             sums.append(running)
-        read_ref[pl.ds(at, 8)] += read_out(readers_ref[g], stacked)
+        read_ref[pl.ds(at, 8)] += row_sums(reads)
         cum_ref[pl.ds(at, 8)] = jnp.concatenate(sums, axis=0)
         return state, running
 
     state, running = lax.fori_loop(
         0, tokens // 8, eight, (jnp.zeros((states, lanes), F32), jnp.zeros((1, lanes), F32))
     )
-    ends_ref[:states] = state.astype(BF16)
-    ends_ref[states:] = jnp.exp2(rates * running).astype(BF16)
+    step, steps = pl.program_id(0), pl.num_programs(0)
+    ends_ref[:, pl.ds(pl.multiple_of(step * lanes, lanes), lanes)] = state.astype(BF16)
+    high = running.astype(BF16).astype(F32)
+    totals_ref[pl.ds(step, 1)] = high
+    totals_ref[pl.ds(steps + step, 1)] = running - high
+
+    @pl.when(step == steps - 1)
+    def _():
+        ends_ref[:, ends_ref.shape[1] - lanes :] = totals_ref[...].astype(BF16)
 
 
 def scan(x_in, edge, dt_low, dt_weight, dt_bias, a_log, conv_weight, conv_bias, d_skip, b_and_c):
@@ -449,18 +465,23 @@
             cut(tokens), cut(edge.shape[0]), whole(dt_low), cut(dt_weight.shape[0]), cut(1),
             cut(states), cut(conv_weight.shape[0]), cut(1), cut(1), whole(b_and_c),
         ],
-        out_specs=(cut(tokens), cut(tokens), cut(2 * states)),
+        out_specs=(
+            cut(tokens),
+            cut(tokens),
+            pl.BlockSpec((states, channels + lanes), lambda i: (0, 0)),
+        ),
         out_shape=(
             pltpu.HBM((tokens, channels), F32),
             pltpu.HBM((tokens, channels), F32),
-            jax.ShapeDtypeStruct((2 * states, channels), BF16),
+            jax.ShapeDtypeStruct((states, channels + lanes), BF16),
         ),
         scratch_shapes=[
             pltpu.VMEM((tokens + 8, lanes), F32),
             pltpu.VMEM((tokens, lanes), F32),
             pltpu.VMEM((tokens, lanes), F32),
+            pltpu.VMEM((states, lanes), F32),
             pltpu.VMEM((tokens, states, 128), F32),
-            pltpu.VMEM((tokens // 8, 16, 8 * states), F32),
+            pltpu.VMEM((tokens, states, 128), F32),
         ],
         compiler_params=params(40),
         cost_estimate=cost(
@@ -477,44 +498,35 @@
     )
 
 
-def prefix_kernel(ends_ref, out_ref):
-    blocks, states, lanes = out_ref.shape
-    entering = jnp.zeros((states, lanes), F32)
-    for i in range(blocks):
-        out_ref[i] = entering.astype(BF16)
-        entering = (
-            ends_ref[i, states:].astype(F32) * entering + ends_ref[i, :states].astype(F32)
-        )
-
-
-def prefix(ends):
-    blocks, both, lanes = ends.shape
-    return pl.pallas_call(
-        prefix_kernel,
-        out_shape=jax.ShapeDtypeStruct((blocks, both // 2, lanes), BF16),
-        compiler_params=params(16),
-        cost_estimate=cost(ends.size, ends.size * 3),
-        name="prefix",
-    )(ends)
-
-
-def finish_kernel(read_ref, cum_ref, z_ref, enter_ref, alog_ref, bc_ref, out_ref, sum_ref, readers_ref):
+def finish_kernel(
+    read_ref, cum_ref, z_ref, ends_ref, totals_ref, alog_ref, bc_ref, out_ref, sum_ref, wide_ref, c_ref
+):
     tokens, lanes = z_ref.shape
-
-    @pl.when(pl.program_id(0) == 0)
+    states = alog_ref.shape[0]
+    step, steps = pl.program_id(0), pl.num_programs(0)
+
+    @pl.when(step == 0)
     def _():
-        fill_readers(bc_ref[1], readers_ref)
+        spread_states(bc_ref[1], c_ref)
+        wide_ref[...] = totals_ref[...].astype(F32)
 
     rates = -jnp.exp(alog_ref[...]) * LOG2E
-    entering = enter_ref[...].astype(F32)
+
+    def block(j, entering):
+        at = pl.multiple_of(j * states, states)
+        total = wide_ref[pl.ds(at + step, 1)] + wide_ref[pl.ds(at + steps + step, 1)]
+        return jnp.exp2(rates * total) * entering + ends_ref[pl.ds(at, states)].astype(F32)
+
+    entering = lax.fori_loop(0, lax.axis_index("seq"), block, jnp.zeros((states, lanes), F32))
 
     def eight(g, carry):
         at = pl.multiple_of(g * 8, 8)
         cum8 = cum_ref[pl.ds(at, 8)]
-        stacked = []
+        reads = []
         for i in range(8):
-            stacked.append((jnp.exp2(rates * cum8[i : i + 1]) * entering).astype(BF16))
-        sum_ref[pl.ds(at, 8)] = read_out(readers_ref[g], stacked)
+            kept = jnp.exp2(rates * cum8[i : i + 1]) * entering
+            reads.append(state_sum(tiled_lanes(c_ref[at + i], lanes) * kept))
+        sum_ref[pl.ds(at, 8)] = row_sums(reads)
         return carry
 
     lax.fori_loop(0, tokens // 8, eight, 0)
@@ -522,10 +534,11 @@
     out_ref[...] = ((read_ref[...] + sum_ref[...]) * (z * jax.nn.sigmoid(z))).astype(BF16)
 
 
-def finish(read, cum, z_gate, entering, a_log, b_and_c):
+def finish(read, cum, z_gate, ends, a_log, b_and_c):
     tokens, channels = z_gate.shape
     states = a_log.shape[0]
-    lanes = math.gcd(512, channels)
+    rows, width = ends.shape
+    lanes = width - channels
 
     def cut(rows):
         return pl.BlockSpec((rows, lanes), lambda i: (0, i))
@@ -534,21 +547,24 @@
         finish_kernel,
         grid=(channels // lanes,),
         in_specs=[
-            cut(tokens), cut(tokens), cut(tokens), cut(states), cut(states),
+            cut(tokens), cut(tokens), cut(tokens), cut(rows),
+            pl.BlockSpec((rows, lanes), lambda i: (0, channels // lanes)),
+            cut(states),
             pl.BlockSpec(b_and_c.shape, lambda i: (0, 0, 0)),
         ],
         out_specs=cut(tokens),
         out_shape=jax.ShapeDtypeStruct((tokens, channels), BF16),
         scratch_shapes=[
             pltpu.VMEM((tokens, lanes), F32),
-            pltpu.VMEM((tokens // 8, 16, 8 * states), F32),
+            pltpu.VMEM((rows, lanes), F32),
+            pltpu.VMEM((tokens, states, 128), F32),
         ],
         compiler_params=params(40),
         cost_estimate=cost(
             tokens * channels * states * 5, tokens * channels * 12, tokens * channels * states
         ),
         name="finish",
-    )(*in_hbm(read, cum, z_gate), entering, *in_hbm(a_log, b_and_c))
+    )(*in_hbm(read, cum, z_gate, ends, ends, a_log, b_and_c))
 
 
 def turned(value, axis, by):
@@ -609,29 +625,20 @@
     read, cum, ends = scan(
         x_in, edge, dt_low, dt_weight, dt_bias, a_log, conv_weight, conv_bias, d_skip, b_and_c
     )
-    both, channels = ends.shape
     arrived = after(arrived, ends)
-    ends = lax.all_to_all(
-        ends.reshape(both, blocks, channels // blocks).transpose(1, 0, 2),
-        "seq", split_axis=0, concat_axis=0, tiled=True,
-    )
+    ends = lax.all_gather(ends, "seq", tiled=True)
+    logits = [logits] + [turned(logits, "exp", d) for d in range(1, feature_parts)]
+    weights = blend_weights(ids, logits, 1, pack)
 
     rows = [unpack(arrived, features, pack)]
     for d in range(1, copies):
         rows.append(turned_within(rows[0], copies, d))
     gated = []
     for part in rows:
-        if len(gated) == 1:
-            entering = prefix(after(ends, gated[0][0]))
-            part = after(part, entering)
-        else:
-            part = after(part, gated[-1][0] if gated else ends)
+        if gated:
+            part = after(part, gated[-1][0])
         own = gate(part, w_gate)
         gated.append([own] + [turned(own, "exp", d) for d in range(1, feature_parts)])
-    entering = after(entering, gated[-1][0])
-    entering = lax.all_to_all(entering, "seq", split_axis=0, concat_axis=0, tiled=True)
-    gated[-1] = list(lax.optimization_barrier((*gated[-1], entering))[:-1])
-
     made = []
     for parts in gated[1:] + gated[:1]:
         made.append(down(parts, w_down, BF16 if len(made) < copies - 1 else F32))
@@ -641,10 +648,8 @@
     packed = pack_sum(sums, experts, pack)
     back = exchanged(packed, copies)
 
-    logits = lax.psum(after(logits, packed), "exp")
-    weights = blend_weights(ids, logits, 1, pack)
-    entering = entering.transpose(1, 0, 2).reshape(both // 2, channels)
-    mamba_out = finish(read, cum, z_gate, after(entering, packed), a_log, b_and_c)
+    mamba_out = finish(read, cum, z_gate, after(ends, packed), a_log, b_and_c)
+    back = after(back, mamba_out)
     moe_out = combine(back, weights, tokens, features, pack)
     return mamba_out, moe_out
 

time: 127 us -> 126 us (level)
  waiting for transfers between devices: 10 us -> 28.3 us
  blocking collectives: 14.9 us -> 0 us
  between operations: 0.76 us -> 14.1 us
  Pallas kernels: 73.9 us -> 64 us
  starting transfers between devices: 24.4 us -> 18.2 us
  local copies, waits for them, and re-layouts: 2.28 us -> 0.86 us
    ppermute x2, waiting for transfers between devices: 3.53 us -> 17.8 us  [turned_within(): lax.ppermute(value, 'seq', [(i, i // copies * copies + (i + by) % copies)...]
    all_to_all x1 -> x0, blocking collectives: 11.5 us -> none  [local(): lax.all_to_all(entering, 'seq', split_axis=0, concat_axis=0, tiled=True)]
    all_to_all x1 -> x0, waiting for transfers between devices: 6.46 us -> none  [local(): lax.all_to_all(ends.reshape(both, blocks, channels // blocks).transpose(1...]
    all_to_all x1 -> x0, starting transfers between devices: 6.13 us -> none  [local(): lax.all_to_all(ends.reshape(both, blocks, channels // blocks).transpose(1...]
    all_to_all x2, waiting for transfers between devices: 0.01 us -> 6.12 us  [exchanged(): lax.all_to_all(value, 'seq', split_axis=0, concat_axis=0, tiled=True, axi...]
    pallas_call x1, Pallas kernels: 17 us -> 11.5 us  [scan(): pl.pallas_call(scan_kernel, grid=(channels // lanes,), in_specs=[cut(toke...]
    ppermute x2 -> x3, waiting for transfers between devices: 0.01 us -> 4.38 us  [turned(): lax.ppermute(value, axis, [(i, (i + by) % count) for i in range(count)])]
    pallas_call x1, Pallas kernels: 12.8 us -> 8.79 us  [finish(): pl.pallas_call(finish_kernel, grid=(channels // lanes,), in_specs=[cut(to...]
  transfers between devices with their start and end apart: 8 -> 9, of which waited for: 2 -> 6; matrix products, arithmetic and copies ran while one was open for 1% -> 0% of each run, Pallas kernels for 49% -> 50%
where the time goes in v5:
time: 126 us; the launch traced here: 125 us
  Pallas kernels  64 us (51%)
  waiting for transfers between devices  28.3 us (22%)
  starting transfers between devices  18.2 us (14%)
  between operations  14.1 us (11%)
    pallas_call x2, Pallas kernels, down(): pl.pallas_call(functools.partial(down_kernel, chunk), in_specs=[INSIDE] *...  19.1 us
    pallas_call x2, Pallas kernels, gate(): pl.pallas_call(functools.partial(gate_kernel, chunk), in_specs=[INSIDE, A...  18.6 us
    ppermute x2, waiting for transfers between devices, turned_within(): lax.ppermute(value, 'seq', [(i, i // copies * copies + (i + by) % copies)...  17.8 us
    pallas_call x1, Pallas kernels, scan(): pl.pallas_call(scan_kernel, grid=(channels // lanes,), in_specs=[cut(toke...  11.5 us
    all_to_all x2, starting transfers between devices, exchanged(): lax.all_to_all(value, 'seq', split_axis=0, concat_axis=0, tiled=True, axi...  11.4 us
    pallas_call x1, Pallas kernels, finish(): pl.pallas_call(finish_kernel, grid=(channels // lanes,), in_specs=[cut(to...  8.79 us
    all_to_all x2, waiting for transfers between devices, exchanged(): lax.all_to_all(value, 'seq', split_axis=0, concat_axis=0, tiled=True, axi...  6.12 us
    ppermute x1, starting transfers between devices, local(): edge = lax.ppermute(edge, 'seq', [(i, i + 1) for i in range(blocks - 1)])  4.84 us
  transfers between devices with their start and end apart: 9, of which 6 were waited for; matrix products, arithmetic and copies ran while one was open for 0% of the time, Pallas kernels for 50%

profile of v5, /device:TPU:0, one launch (start us, length us, event | category | flops | bytes accessed | tf_op | source)
XLA Modules:
  0.0 125.5 jit_solution(5391920401111123672)
XLA Ops:
  7.2 0.9 slice.3
  8.0 4.8 %collective-permute-start = (bf16[3,4096]{1,0:T(4,128)(2,1)S(1)}, bf16[3,4096]{1,0:T(4,128)(2,1)S(1)}, u32[]{:S(2)}, u32[]{:S(2)}) collective-permute-start(bf16[3,4096]{1,0:T(4,128)(2,1)S(1)} %slice.3), channel_id=1, source_target_pairs={{0,2},{2,4},{4,6},{6,8},{8,10},{10,12},{12,14},{14,16},{16,18},{18... | collective-permute-start | bytes 73736 | tf_op jit(solution)/shard_map/ppermute | solution.py:620
  12.9 2.4 %route.1 = (bf16[8,1,16,2304]{3,2,1,0:T(8,128)(2,1)}, f32[64,8]{1,0:T(8,128)S(1)}) custom-call(s32[2,64]{1,0:T(2,128)} %bitcast.7, bf16[64,2048]{1,0:T(8,128)(2,1)} %hidden_ref.1, bf16[8,2048]{1,0:T(8,128)(2,1)} %bitcast.6), custom_call_target="tpu_custom_call" | custom-call | flops 67108864 | bytes 1048576 | tf_op jit(solution)/shard_map/route/pallas_call | solution.py:102
  15.3 6.7 %all-to-all-start = ((bf16[8,16,2304]{2,1,0:T(8,128)(2,1)}), bf16[8,16,2304]{2,1,0:T(8,128)(2,1)S(1)}, u32[]{:S(2)}, u32[]{:S(2)}) async-start(bf16[8,16,2304]{2,1,0:T(8,128)(2,1)} %bitcast.5), calls=%async_computation | async-start | bytes 1179648 | tf_op jit(solution)/shard_map/all_to_all | solution.py:585
  22.1 11.5 %scan.1 = (f32[64,4096]{1,0:T(8,128)}, f32[64,4096]{1,0:T(8,128)}, bf16[16,4608]{1,0:T(8,128)(2,1)}) custom-call(bf16[64,4096]{1,0:T(8,128)(2,1)} %x_ref.1, bf16[3,4096]{1,0:T(4,128)(2,1)S(1)} %collective-permute-done.edge_ref, bf16[64,256]{1,0:T(8,128)(2,1)} %low_ref.1, bf16[256,4096]{1,0:T(8,128)(2,1)} %dtw_ref.1, f32[1,4096]{1,0:T(1,128)} %bitcast.9, ...), custom_call_target="tpu_custom_call" | custom-call | flops 33554432 | bytes 3145728 | tf_op jit(solution)/shard_map/scan/pallas_call | solution.py:461
  33.6 3.2 %all-to-all-done.arrived_ref = bf16[8,16,2304]{2,1,0:T(8,128)(2,1)S(1)} async-done(((bf16[8,16,2304]{2,1,0:T(8,128)(2,1)}), bf16[8,16,2304]{2,1,0:T(8,128)(2,1)S(1)}, u32[]{:S(2)}, u32[]{:S(2)}) %all-to-all-start) | async-done | bytes 589856 | tf_op jit(solution)/shard_map/all_to_all | solution.py:585
  36.8 0.2 unpack.1.x_ref
  36.9 0.6 collective-permute-start.2
  37.6 9.3 %gate.2.refs_0_ = bf16[144,6144]{1,0:T(8,128)(2,1)S(1)} custom-call(bf16[144,2048]{1,0:T(8,128)(2,1)S(1)} %unpack.1.x_ref, bf16[2048,6144]{1,0:T(8,128)(2,1)} %w_ref.3), custom_call_target="tpu_custom_call" | custom-call | flops 144 | bytes 144 | tf_op jit(solution)/shard_map/gate/pallas_call | solution.py:203
  46.9 4.3 %collective-permute-done.2.x_ref = bf16[144,2048]{1,0:T(8,128)(2,1)S(1)} collective-permute-done((bf16[144,2048]{1,0:T(8,128)(2,1)S(1)}, bf16[144,2048]{1,0:T(8,128)(2,1)S(1)}, u32[]{:S(2)}, u32[]{:S(2)}) %collective-permute-start.2) | collective-permute-done | bytes 589856 | tf_op jit(solution)/shard_map/ppermute | solution.py:577
  51.2 9.2 %gate.3.refs_0_ = bf16[144,6144]{1,0:T(8,128)(2,1)S(1)} custom-call(bf16[144,2048]{1,0:T(8,128)(2,1)S(1)} %collective-permute-done.2.x_ref, bf16[2048,6144]{1,0:T(8,128)(2,1)} %w_ref.3), custom_call_target="tpu_custom_call" | custom-call | flops 144 | bytes 144 | tf_op jit(solution)/shard_map/gate/pallas_call | solution.py:203
  60.5 0.5 collective-permute-start.1
  61.0 3.2 %collective-permute-done.3.refs_1_ = bf16[144,6144]{1,0:T(8,128)(2,1)S(1)} collective-permute-done((bf16[144,6144]{1,0:T(8,128)(2,1)S(1)}, bf16[144,6144]{1,0:T(8,128)(2,1)S(1)}, u32[]{:S(2)}, u32[]{:S(2)}) %collective-permute-start.3) | collective-permute-done | bytes 1769504 | tf_op jit(solution)/shard_map/ppermute | solution.py:572
  64.2 9.4 %down.3 = bf16[144,2048]{1,0:T(8,128)(2,1)S(1)} custom-call(bf16[144,6144]{1,0:T(8,128)(2,1)S(1)} %gate.3.refs_0_, bf16[144,6144]{1,0:T(8,128)(2,1)S(1)} %collective-permute-done.3.refs_1_, bf16[6144,2048]{1,0:T(8,128)(2,1)} %refs_2_.3), custom_call_target="tpu_custom_call" | custom-call | flops 144 | bytes 144 | tf_op jit(solution)/shard_map/down/pallas_call | solution.py:246
  73.6 0.7 collective-permute-start.4
  74.3 9.7 %down.2.refs_0_ = f32[144,2048]{1,0:T(8,128)S(1)} custom-call(bf16[144,6144]{1,0:T(8,128)(2,1)S(1)} %gate.2.refs_0_, bf16[144,6144]{1,0:T(8,128)(2,1)S(1)} %collective-permute-done.1.refs_1_, bf16[6144,2048]{1,0:T(8,128)(2,1)} %refs_2_.3), custom_call_target="tpu_custom_call" | custom-call | flops 144 | bytes 144 | tf_op jit(solution)/shard_map/down/pallas_call | solution.py:246
  84.0 13.5 %collective-permute-done.4.refs_1_ = bf16[144,2048]{1,0:T(8,128)(2,1)S(1)} collective-permute-done((bf16[144,2048]{1,0:T(8,128)(2,1)S(1)}, bf16[144,2048]{1,0:T(8,128)(2,1)S(1)}, u32[]{:S(2)}, u32[]{:S(2)}) %collective-permute-start.4) | collective-permute-done | bytes 589856 | tf_op jit(solution)/shard_map/ppermute | solution.py:577
  97.5 1.3 %pack_sum.1 = bf16[8,16,2304]{2,1,0:T(8,128)(2,1)} custom-call(f32[144,2048]{1,0:T(8,128)S(1)} %down.2.refs_0_, bf16[144,2048]{1,0:T(8,128)(2,1)S(1)} %collective-permute-done.4.refs_1_), custom_call_target="tpu_custom_call" | custom-call | flops 4718592 | bytes 2359296 | tf_op jit(solution)/shard_map/pack_sum/pallas_call | solution.py:316
  98.7 4.7 %all-to-all-start.1 = ((bf16[8,16,2304]{2,1,0:T(8,128)(2,1)}), bf16[8,16,2304]{2,1,0:T(8,128)(2,1)S(1)}, u32[]{:S(2)}, u32[]{:S(2)}) async-start(bf16[8,16,2304]{2,1,0:T(8,128)(2,1)} %pack_sum.1), calls=%async_computation.1 | async-start | bytes 1179648 | tf_op jit(solution)/shard_map/all_to_all | solution.py:585
  103.4 1.2 collective-permute-done.5.refs_1_
  104.6 1.0 blend_weights.1
  105.7 8.8 %finish.1 = bf16[64,4096]{1,0:T(8,128)(2,1)} custom-call(f32[64,4096]{1,0:T(8,128)} %get-tuple-element.15.read_ref, f32[64,4096]{1,0:T(8,128)} %get-tuple-element.16.cum_ref, bf16[64,4096]{1,0:T(8,128)(2,1)} %z_ref.1, bf16[256,4608]{1,0:T(8,128)(2,1)} %all-gather.2.cloned.1.call-done.ends_ref.totals_ref, ...), custom_call_target="tpu_custom_call" | custom-call | flops 20971520 | bytes 3145728 | tf_op jit(solution)/shard_map/finish/pallas_call | solution.py:546
  114.5 3.0 %all-to-all-done.1.back_ref = bf16[8,16,2304]{2,1,0:T(8,128)(2,1)S(1)} async-done(((bf16[8,16,2304]{2,1,0:T(8,128)(2,1)}), bf16[8,16,2304]{2,1,0:T(8,128)(2,1)S(1)}, u32[]{:S(2)}, u32[]{:S(2)}) %all-to-all-start.1) | async-done | bytes 589856 | tf_op jit(solution)/shard_map/all_to_all | solution.py:585
  117.5 1.1 combine.1
  (7 shorter events, 0.2 us)
Async XLA Ops:
  8.0 7.3 %collective-permute-start = (bf16[3,4096]{1,0:T(4,128)(2,1)S(1)}, bf16[3,4096]{1,0:T(4,128)(2,1)S(1)}, u32[]{:S(2)}, u32[]{:S(2)}) collective-permute-start(bf16[3,4096]{1,0:T(4,128)(2,1)S(1)} %slice.3), channel_id=1, source_target_pairs={{0,2},{2,4},{4,6},{6,8},{8,10},{10,12},{12,14},{14,16},{16,18},{18... | collective-permute-start | bytes 73736 | tf_op jit(solution)/shard_map/ppermute | solution.py:620
  15.3 21.4 %all-to-all-start = ((bf16[8,16,2304]{2,1,0:T(8,128)(2,1)}), bf16[8,16,2304]{2,1,0:T(8,128)(2,1)S(1)}, u32[]{:S(2)}, u32[]{:S(2)}) async-start(bf16[8,16,2304]{2,1,0:T(8,128)(2,1)} %bitcast.5), calls=%async_computation | async-start | bytes 1179648 | tf_op jit(solution)/shard_map/all_to_all | solution.py:585
  22.0 83.7 %all-gather.2.cloned.1.call-start = ((), (), s32[]{:S(2)}) async-start(), calls=%async_computation.2 | async-start | bytes 2506752 | tf_op jit(solution)/shard_map/all_gather | solution.py:629
  36.9 14.3 %collective-permute-start.2 = (bf16[144,2048]{1,0:T(8,128)(2,1)S(1)}, bf16[144,2048]{1,0:T(8,128)(2,1)S(1)}, u32[]{:S(2)}, u32[]{:S(2)}) collective-permute-start(bf16[144,2048]{1,0:T(8,128)(2,1)S(1)} %unpack.1.x_ref), channel_id=1, source_target_pairs={{0,2},{2,0},{4,6},{6,4},{8,10},{10,8},{12,14},{14,12},{16,18},{18,... | collective-permute-start | bytes 1769480 | tf_op jit(solution)/shard_map/ppermute | solution.py:577
  60.4 3.8 %collective-permute-start.3 = (bf16[144,6144]{1,0:T(8,128)(2,1)S(1)}, bf16[144,6144]{1,0:T(8,128)(2,1)S(1)}, u32[]{:S(2)}, u32[]{:S(2)}) collective-permute-start(bf16[144,6144]{1,0:T(8,128)(2,1)S(1)} %gate.3.refs_0_), channel_id=1, source_target_pairs={{0,1},{1,0},{2,3},{3,2},{4,5},{5,4},{6,7},{7,6},{8,9},{9,8},{10,11... | collective-permute-start | bytes 5308424 | tf_op jit(solution)/shard_map/ppermute | solution.py:572
  60.5 13.8 %collective-permute-start.1 = (bf16[144,6144]{1,0:T(8,128)(2,1)S(1)}, bf16[144,6144]{1,0:T(8,128)(2,1)S(1)}, u32[]{:S(2)}, u32[]{:S(2)}) collective-permute-start(bf16[144,6144]{1,0:T(8,128)(2,1)S(1)} %gate.2.refs_0_), channel_id=1, source_target_pairs={{0,1},{1,0},{2,3},{3,2},{4,5},{5,4},{6,7},{7,6},{8,9},{9,8},{10,11... | collective-permute-start | bytes 5308424 | tf_op jit(solution)/shard_map/ppermute | solution.py:572
  73.6 23.9 %collective-permute-start.4 = (bf16[144,2048]{1,0:T(8,128)(2,1)S(1)}, bf16[144,2048]{1,0:T(8,128)(2,1)S(1)}, u32[]{:S(2)}, u32[]{:S(2)}) collective-permute-start(bf16[144,2048]{1,0:T(8,128)(2,1)S(1)} %down.3), channel_id=1, source_target_pairs={{0,2},{2,0},{4,6},{6,4},{8,10},{10,8},{12,14},{14,12},{16,18},{18,... | collective-permute-start | bytes 1769480 | tf_op jit(solution)/shard_map/ppermute | solution.py:577
  98.7 18.8 %all-to-all-start.1 = ((bf16[8,16,2304]{2,1,0:T(8,128)(2,1)}), bf16[8,16,2304]{2,1,0:T(8,128)(2,1)S(1)}, u32[]{:S(2)}, u32[]{:S(2)}) async-start(bf16[8,16,2304]{2,1,0:T(8,128)(2,1)} %pack_sum.1), calls=%async_computation.1 | async-start | bytes 1179648 | tf_op jit(solution)/shard_map/all_to_all | solution.py:585
  103.4 1.2 collective-permute-start.5
Sparse Core Ops, SparseCore 0:
  33.7 70.1 all-gather.1

commit v6 on v5

--- a/solution.py
+++ b/solution.py
@@ -210,7 +210,7 @@
             pltpu.SemaphoreType.DMA((amount // chunk,)),
         ],
         compiler_params=params(44),
-        cost_estimate=cost(rows, rows),
+        cost_estimate=cost(2 * rows * features * amount, features * amount * 2),
         name="gate",
     )(x, *in_hbm(w_gate))
 
@@ -254,7 +254,7 @@
             pltpu.SemaphoreType.DMA((features // chunk,)),
         ],
         compiler_params=params(48),
-        cost_estimate=cost(rows, rows),
+        cost_estimate=cost(2 * rows * features * amount, features * amount * 2),
         name="down",
     )(*parts, *in_hbm(w_down))
 
@@ -389,7 +389,7 @@
 
 def scan_kernel(
     x_ref, edge_ref, low_ref, dtw_ref, dtb_ref, alog_ref, cw_ref, cb_ref, skip_ref, bc_ref,
-    read_ref, cum_ref, ends_ref, padded, delta_ref, fed_ref, totals_ref, b_ref, c_ref,
+    read_ref, cum_ref, ends_ref, padded, delta_ref, fed_ref, b_ref, c_ref,
 ):
     tokens, lanes = x_ref.shape
     taps = cw_ref.shape[0]
@@ -399,7 +399,6 @@
     def _():
         spread_states(bc_ref[0], b_ref)
         spread_states(bc_ref[1], c_ref)
-        totals_ref[...] = jnp.zeros_like(totals_ref)
 
     padded[8:] = x_ref[...].astype(F32)
     padded[8 - (taps - 1) : 8] = edge_ref[...].astype(F32)
@@ -435,15 +434,8 @@
     state, running = lax.fori_loop(
         0, tokens // 8, eight, (jnp.zeros((states, lanes), F32), jnp.zeros((1, lanes), F32))
     )
-    step, steps = pl.program_id(0), pl.num_programs(0)
-    ends_ref[:, pl.ds(pl.multiple_of(step * lanes, lanes), lanes)] = state.astype(BF16)
-    high = running.astype(BF16).astype(F32)
-    totals_ref[pl.ds(step, 1)] = high
-    totals_ref[pl.ds(steps + step, 1)] = running - high
-
-    @pl.when(step == steps - 1)
-    def _():
-        ends_ref[:, ends_ref.shape[1] - lanes :] = totals_ref[...].astype(BF16)
+    ends_ref[:states] = state.astype(BF16)
+    ends_ref[states:] = jnp.exp2(rates * running).astype(BF16)
 
 
 def scan(x_in, edge, dt_low, dt_weight, dt_bias, a_log, conv_weight, conv_bias, d_skip, b_and_c):
@@ -465,21 +457,16 @@
             cut(tokens), cut(edge.shape[0]), whole(dt_low), cut(dt_weight.shape[0]), cut(1),
             cut(states), cut(conv_weight.shape[0]), cut(1), cut(1), whole(b_and_c),
         ],
-        out_specs=(
-            cut(tokens),
-            cut(tokens),
-            pl.BlockSpec((states, channels + lanes), lambda i: (0, 0)),
-        ),
+        out_specs=(cut(tokens), cut(tokens), cut(2 * states)),
         out_shape=(
             pltpu.HBM((tokens, channels), F32),
             pltpu.HBM((tokens, channels), F32),
-            jax.ShapeDtypeStruct((states, channels + lanes), BF16),
+            jax.ShapeDtypeStruct((2 * states, channels), BF16),
         ),
         scratch_shapes=[
             pltpu.VMEM((tokens + 8, lanes), F32),
             pltpu.VMEM((tokens, lanes), F32),
             pltpu.VMEM((tokens, lanes), F32),
-            pltpu.VMEM((states, lanes), F32),
             pltpu.VMEM((tokens, states, 128), F32),
             pltpu.VMEM((tokens, states, 128), F32),
         ],
@@ -498,26 +485,37 @@
     )
 
 
+def link_kernel(later_ref, earlier_ref, out_ref):
+    states = out_ref.shape[0] // 2
+    decay = later_ref[states:].astype(F32)
+    end = later_ref[:states].astype(F32) + decay * earlier_ref[:states].astype(F32)
+    out_ref[:states] = end.astype(BF16)
+    out_ref[states:] = (decay * earlier_ref[states:].astype(F32)).astype(BF16)
+
+
+def link(later, earlier):
+    return pl.pallas_call(
+        link_kernel,
+        out_shape=jax.ShapeDtypeStruct(later.shape, BF16),
+        compiler_params=params(16),
+        cost_estimate=cost(later.size * 2, later.size * 6),
+        name="link",
+    )(later, earlier)
+
+
 def finish_kernel(
-    read_ref, cum_ref, z_ref, ends_ref, totals_ref, alog_ref, bc_ref, out_ref, sum_ref, wide_ref, c_ref
+    read_ref, cum_ref, z_ref, later_ref, earlier_ref, alog_ref, bc_ref, out_ref, sum_ref, c_ref
 ):
     tokens, lanes = z_ref.shape
     states = alog_ref.shape[0]
-    step, steps = pl.program_id(0), pl.num_programs(0)
-
-    @pl.when(step == 0)
+
+    @pl.when(pl.program_id(0) == 0)
     def _():
         spread_states(bc_ref[1], c_ref)
-        wide_ref[...] = totals_ref[...].astype(F32)
 
     rates = -jnp.exp(alog_ref[...]) * LOG2E
-
-    def block(j, entering):
-        at = pl.multiple_of(j * states, states)
-        total = wide_ref[pl.ds(at + step, 1)] + wide_ref[pl.ds(at + steps + step, 1)]
-        return jnp.exp2(rates * total) * entering + ends_ref[pl.ds(at, states)].astype(F32)
-
-    entering = lax.fori_loop(0, lax.axis_index("seq"), block, jnp.zeros((states, lanes), F32))
+    entering = later_ref[:states].astype(F32)
+    entering = entering + later_ref[states:].astype(F32) * earlier_ref[...].astype(F32)
 
     def eight(g, carry):
         at = pl.multiple_of(g * 8, 8)
@@ -534,11 +532,10 @@
     out_ref[...] = ((read_ref[...] + sum_ref[...]) * (z * jax.nn.sigmoid(z))).astype(BF16)
 
 
-def finish(read, cum, z_gate, ends, a_log, b_and_c):
+def finish(read, cum, z_gate, later, earlier, a_log, b_and_c):
     tokens, channels = z_gate.shape
     states = a_log.shape[0]
-    rows, width = ends.shape
-    lanes = width - channels
+    lanes = math.gcd(512, channels)
 
     def cut(rows):
         return pl.BlockSpec((rows, lanes), lambda i: (0, i))
@@ -547,16 +544,13 @@
         finish_kernel,
         grid=(channels // lanes,),
         in_specs=[
-            cut(tokens), cut(tokens), cut(tokens), cut(rows),
-            pl.BlockSpec((rows, lanes), lambda i: (0, channels // lanes)),
-            cut(states),
+            cut(tokens), cut(tokens), cut(tokens), cut(2 * states), cut(states), cut(states),
             pl.BlockSpec(b_and_c.shape, lambda i: (0, 0, 0)),
         ],
         out_specs=cut(tokens),
         out_shape=jax.ShapeDtypeStruct((tokens, channels), BF16),
         scratch_shapes=[
             pltpu.VMEM((tokens, lanes), F32),
-            pltpu.VMEM((rows, lanes), F32),
             pltpu.VMEM((tokens, states, 128), F32),
         ],
         compiler_params=params(40),
@@ -564,7 +558,12 @@
             tokens * channels * states * 5, tokens * channels * 12, tokens * channels * states
         ),
         name="finish",
-    )(*in_hbm(read, cum, z_gate, ends, ends, a_log, b_and_c))
+    )(*in_hbm(read, cum, z_gate), later, earlier, *in_hbm(a_log, b_and_c))
+
+
+def shifted(value, by):
+    count = lax.axis_size("seq")
+    return lax.ppermute(value, "seq", [(i, i + by) for i in range(count - by)])
 
 
 def turned(value, axis, by):
@@ -588,7 +587,7 @@
 
 
 def after(value, *others):
-    return lax.optimization_barrier((value, *others))[0]
+    return lax.optimization_barrier((value, others))[0]
 
 
 def local(
@@ -616,8 +615,7 @@
     pack = packing(features)
     ids = expert_ids.T
 
-    edge = x_in[tokens - (conv_weight.shape[0] - 1) :]
-    edge = lax.ppermute(edge, "seq", [(i, i + 1) for i in range(blocks - 1)])
+    edge = shifted(x_in[tokens - (conv_weight.shape[0] - 1) :], 1)
     outgoing, logits = route(ids, hidden, router.T, 1, pack)
     outgoing = after(outgoing, edge)
     arrived = exchanged(outgoing.reshape((experts,) + outgoing.shape[2:]), copies)
@@ -626,9 +624,22 @@
         x_in, edge, dt_low, dt_weight, dt_bias, a_log, conv_weight, conv_bias, d_skip, b_and_c
     )
     arrived = after(arrived, ends)
-    ends = lax.all_gather(ends, "seq", tiled=True)
-    logits = [logits] + [turned(logits, "exp", d) for d in range(1, feature_parts)]
-    weights = blend_weights(ids, logits, 1, pack)
+
+    spans = [1, 2]
+    while spans[-1] * 2 < blocks:
+        spans.append(spans[-1] * 2)
+    state = ends
+    pending = [shifted(ends, by) for by in spans[:2]]
+    spans = spans[1:]
+
+    def linked(state, pending, spans, *marks):
+        if pending is None or not spans:
+            return state, pending, spans
+        state = link(*after(tuple(pending), *marks))
+        span, spans = spans[0], spans[1:]
+        if not spans:
+            return state, [shifted(state[: state.shape[0] // 2], span)], spans
+        return state, [state, shifted(state, span)], spans
 
     rows = [unpack(arrived, features, pack)]
     for d in range(1, copies):
@@ -636,19 +647,28 @@
     gated = []
     for part in rows:
         if gated:
-            part = after(part, gated[-1][0])
+            state, pending, spans = linked(state, pending, spans, gated[-1][0])
+            part = after(part, gated[-1][0], state)
         own = gate(part, w_gate)
         gated.append([own] + [turned(own, "exp", d) for d in range(1, feature_parts)])
     made = []
     for parts in gated[1:] + gated[:1]:
+        parts = lax.optimization_barrier((*parts, state))[:-1]
         made.append(down(parts, w_down, BF16 if len(made) < copies - 1 else F32))
-    sums = [made[-1]]
+        state, pending, spans = linked(state, pending, spans, made[-1])
+    while spans:
+        state, pending, spans = linked(state, pending, spans)
+
+    logits = after(logits, made[0])
+    logits = [logits] + [turned(logits, "exp", d) for d in range(1, feature_parts)]
+    weights = blend_weights(ids, logits, 1, pack)
+    sums = [after(made[-1], weights[2])]
     for d in range(1, copies):
         sums.append(turned_within(made[d - 1], copies, -d))
     packed = pack_sum(sums, experts, pack)
     back = exchanged(packed, copies)
 
-    mamba_out = finish(read, cum, z_gate, after(ends, packed), a_log, b_and_c)
+    mamba_out = finish(read, cum, z_gate, state, after(pending[0], packed), a_log, b_and_c)
     back = after(back, mamba_out)
     moe_out = combine(back, weights, tokens, features, pack)
     return mamba_out, moe_out

time: 126 us -> 129 us (1.024)
  starting transfers between devices: 18.2 us -> 42.5 us
  between operations: 14.1 us -> 0.79 us
  waiting for transfers between devices: 28.3 us -> 20.9 us
    ppermute x1 -> x6, starting transfers between devices: 4.84 us -> 29.1 us  [shifted(): return lax.ppermute(value, 'seq', [(i, i + by) for i in range(count - by)])]
    ppermute x2, waiting for transfers between devices: 17.8 us -> 3.88 us  [turned_within(): lax.ppermute(value, 'seq', [(i, i // copies * copies + (i + by) % copies)...]
    ppermute x1 -> x6, waiting for transfers between devices: 0.01 us -> 13.8 us  [shifted(): return lax.ppermute(value, 'seq', [(i, i + by) for i in range(count - by)])]
    ppermute x3, waiting for transfers between devices: 4.38 us -> 0.01 us  [turned(): lax.ppermute(value, axis, [(i, (i + by) % count) for i in range(count)])]
    all_to_all x2, waiting for transfers between devices: 6.12 us -> 3.24 us  [exchanged(): lax.all_to_all(value, 'seq', split_axis=0, concat_axis=0, tiled=True, axi...]
  transfers between devices with their start and end apart: 9 -> 13, of which waited for: 6 -> 5; matrix products, arithmetic and copies ran while one was open for 0% -> 0% of each run, Pallas kernels for 50% -> 40%
where the time goes in v6:
time: 129 us; the launch traced here: 128 us
  Pallas kernels  63.1 us (49%)
  starting transfers between devices  42.5 us (33%)
  waiting for transfers between devices  20.9 us (16%)
    ppermute x6, starting transfers between devices, shifted(): return lax.ppermute(value, 'seq', [(i, i + by) for i in range(count - by)])  29.1 us
    pallas_call x2, Pallas kernels, down(): pl.pallas_call(functools.partial(down_kernel, chunk), in_specs=[INSIDE] *...  18.7 us
    pallas_call x2, Pallas kernels, gate(): pl.pallas_call(functools.partial(gate_kernel, chunk), in_specs=[INSIDE, A...  18.4 us
    ppermute x6, waiting for transfers between devices, shifted(): return lax.ppermute(value, 'seq', [(i, i + by) for i in range(count - by)])  13.8 us
    pallas_call x1, Pallas kernels, scan(): pl.pallas_call(scan_kernel, grid=(channels // lanes,), in_specs=[cut(toke...  11.5 us
    all_to_all x2, starting transfers between devices, exchanged(): lax.all_to_all(value, 'seq', split_axis=0, concat_axis=0, tiled=True, axi...  11.5 us
    pallas_call x1, Pallas kernels, finish(): pl.pallas_call(finish_kernel, grid=(channels // lanes,), in_specs=[cut(to...  8.19 us
    ppermute x2, waiting for transfers between devices, turned_within(): lax.ppermute(value, 'seq', [(i, i // copies * copies + (i + by) % copies)...  3.88 us
  transfers between devices with their start and end apart: 13, of which 5 were waited for; matrix products, arithmetic and copies ran while one was open for 0% of the time, Pallas kernels for 40%

profile of v6, /device:TPU:0, one launch (start us, length us, event | category | flops | bytes accessed | tf_op | source)
XLA Modules:
  0.0 128.1 jit_solution(17929851959374279974)
XLA Ops:
  0.6 0.9 slice.6
  1.5 4.8 %collective-permute-start = (bf16[3,4096]{1,0:T(4,128)(2,1)S(1)}, bf16[3,4096]{1,0:T(4,128)(2,1)S(1)}, u32[]{:S(2)}, u32[]{:S(2)}) collective-permute-start(bf16[3,4096]{1,0:T(4,128)(2,1)S(1)} %slice.6), channel_id=1, source_target_pairs={{0,2},{2,4},{4,6},{6,8},{8,10},{10,12},{12,14},{14,16},{16,18},{18... | collective-permute-start | bytes 73736 | tf_op jit(solution)/shard_map/ppermute | solution.py:566
  6.3 2.4 %route.1 = (bf16[8,1,16,2304]{3,2,1,0:T(8,128)(2,1)}, f32[64,8]{1,0:T(8,128)S(1)}) custom-call(s32[2,64]{1,0:T(2,128)} %bitcast.7, bf16[64,2048]{1,0:T(8,128)(2,1)} %hidden_ref.1, bf16[8,2048]{1,0:T(8,128)(2,1)} %bitcast.6), custom_call_target="tpu_custom_call" | custom-call | flops 67108864 | bytes 1048576 | tf_op jit(solution)/shard_map/route/pallas_call | solution.py:102
  8.8 6.7 %all-to-all-start = ((bf16[8,16,2304]{2,1,0:T(8,128)(2,1)}), bf16[8,16,2304]{2,1,0:T(8,128)(2,1)S(1)}, u32[]{:S(2)}, u32[]{:S(2)}) async-start(bf16[8,16,2304]{2,1,0:T(8,128)(2,1)} %bitcast.5), calls=%async_computation | async-start | bytes 1179648 | tf_op jit(solution)/shard_map/all_to_all | solution.py:584
  15.5 11.5 %scan.1 = (f32[64,4096]{1,0:T(8,128)}, f32[64,4096]{1,0:T(8,128)}, bf16[32,4096]{1,0:T(8,128)(2,1)S(1)}) custom-call(bf16[64,4096]{1,0:T(8,128)(2,1)} %x_ref.1, bf16[3,4096]{1,0:T(4,128)(2,1)S(1)} %collective-permute-done.edge_ref, bf16[64,256]{1,0:T(8,128)(2,1)} %low_ref.1, bf16[256,4096]{1,0:T(8,128)(2,1)} %dtw_ref.1, f32[1,4096]{1,0:T(1,128)} %bitcast.9, ...), custom_call_target="tpu_custom_call" | custom-call | flops 33554432 | bytes 3145728 | tf_op jit(solution)/shard_map/scan/pallas_call | solution.py:453
  27.0 3.2 %all-to-all-done.arrived_ref = bf16[8,16,2304]{2,1,0:T(8,128)(2,1)S(1)} async-done(((bf16[8,16,2304]{2,1,0:T(8,128)(2,1)}), bf16[8,16,2304]{2,1,0:T(8,128)(2,1)S(1)}, u32[]{:S(2)}, u32[]{:S(2)}) %all-to-all-start) | async-done | bytes 589856 | tf_op jit(solution)/shard_map/all_to_all | solution.py:584
  31.1 3.3 %collective-permute-start.1 = (bf16[32,4096]{1,0:T(8,128)(2,1)S(1)}, bf16[32,4096]{1,0:T(8,128)(2,1)S(1)}, u32[]{:S(2)}, u32[]{:S(2)}) collective-permute-start(bf16[32,4096]{1,0:T(8,128)(2,1)S(1)} %get-tuple-element.29), channel_id=1, source_target_pairs={{0,2},{2,4},{4,6},{6,8},{8,10},{10,12},{12,14},{14,16},{16,18},{18... | collective-permute-start | bytes 786440 | tf_op jit(solution)/shard_map/ppermute | solution.py:566
  34.4 3.4 %collective-permute-start.2 = (bf16[32,4096]{1,0:T(8,128)(2,1)S(1)}, bf16[32,4096]{1,0:T(8,128)(2,1)S(1)}, u32[]{:S(2)}, u32[]{:S(2)}) collective-permute-start(bf16[32,4096]{1,0:T(8,128)(2,1)S(1)} %get-tuple-element.29), channel_id=1, source_target_pairs={{0,4},{2,6},{4,8},{6,10},{8,12},{10,14},{12,16},{14,18},{16,20},{1... | collective-permute-start | bytes 786440 | tf_op jit(solution)/shard_map/ppermute | solution.py:566
  37.8 9.2 %gate.2.refs_0_ = bf16[144,6144]{1,0:T(8,128)(2,1)S(1)} custom-call(bf16[144,2048]{1,0:T(8,128)(2,1)S(1)} %unpack.1.x_ref, bf16[2048,6144]{1,0:T(8,128)(2,1)} %w_ref.3), custom_call_target="tpu_custom_call" | custom-call | flops 3623878656 | bytes 25165824 | tf_op jit(solution)/shard_map/gate/pallas_call | solution.py:203
  47.5 9.2 %gate.3.refs_0_ = bf16[144,6144]{1,0:T(8,128)(2,1)S(1)} custom-call(bf16[144,2048]{1,0:T(8,128)(2,1)S(1)} %collective-permute-done.4.x_ref, bf16[2048,6144]{1,0:T(8,128)(2,1)} %w_ref.3), custom_call_target="tpu_custom_call" | custom-call | flops 3623878656 | bytes 25165824 | tf_op jit(solution)/shard_map/gate/pallas_call | solution.py:203
  57.3 5.3 %collective-permute-start.3 = (bf16[32,4096]{1,0:T(8,128)(2,1)S(1)}, bf16[32,4096]{1,0:T(8,128)(2,1)S(1)}, u32[]{:S(2)}, u32[]{:S(2)}) collective-permute-start(bf16[32,4096]{1,0:T(8,128)(2,1)S(1)} %link.3.later_ref), channel_id=1, source_target_pairs={{0,4},{2,6},{4,8},{6,10},{8,12},{10,14},{12,16},{14,18},{16,20},{1... | collective-permute-start | bytes 786440 | tf_op jit(solution)/shard_map/ppermute | solution.py:566
  62.5 9.3 %down.2 = bf16[144,2048]{1,0:T(8,128)(2,1)S(1)} custom-call(bf16[144,6144]{1,0:T(8,128)(2,1)S(1)} %gate.3.refs_0_, bf16[144,6144]{1,0:T(8,128)(2,1)S(1)} %collective-permute-done.5.refs_1_, bf16[6144,2048]{1,0:T(8,128)(2,1)} %refs_2_.3), custom_call_target="tpu_custom_call" | custom-call | flops 3623878656 | bytes 25165824 | tf_op jit(solution)/shard_map/down/pallas_call | solution.py:246
  71.9 0.7 collective-permute-start.10
  72.7 9.3 %down.3.refs_0_ = f32[144,2048]{1,0:T(8,128)S(1)} custom-call(bf16[144,6144]{1,0:T(8,128)(2,1)S(1)} %gate.2.refs_0_, bf16[144,6144]{1,0:T(8,128)(2,1)S(1)} %collective-permute-done.7.refs_1_, bf16[6144,2048]{1,0:T(8,128)(2,1)} %refs_2_.3), custom_call_target="tpu_custom_call" | custom-call | flops 3623878656 | bytes 25165824 | tf_op jit(solution)/shard_map/down/pallas_call | solution.py:246
  82.0 1.1 blend_weights.1
  83.1 3.9 %collective-permute-done.10.refs_1_ = bf16[144,2048]{1,0:T(8,128)(2,1)S(1)} collective-permute-done((bf16[144,2048]{1,0:T(8,128)(2,1)S(1)}, bf16[144,2048]{1,0:T(8,128)(2,1)S(1)}, u32[]{:S(2)}, u32[]{:S(2)}) %collective-permute-start.10) | collective-permute-done | bytes 589856 | tf_op jit(solution)/shard_map/ppermute | solution.py:576
  87.0 1.2 pack_sum.1
  88.2 4.7 %all-to-all-start.1 = ((bf16[8,16,2304]{2,1,0:T(8,128)(2,1)}), bf16[8,16,2304]{2,1,0:T(8,128)(2,1)S(1)}, u32[]{:S(2)}, u32[]{:S(2)}) async-start(bf16[8,16,2304]{2,1,0:T(8,128)(2,1)} %pack_sum.1), calls=%async_computation.1 | async-start | bytes 1179648 | tf_op jit(solution)/shard_map/all_to_all | solution.py:584
  93.0 3.9 %collective-permute-start.6 = (bf16[32,4096]{1,0:T(8,128)(2,1)S(1)}, bf16[32,4096]{1,0:T(8,128)(2,1)S(1)}, u32[]{:S(2)}, u32[]{:S(2)}) collective-permute-start(bf16[32,4096]{1,0:T(8,128)(2,1)S(1)} %link.4.later_ref), channel_id=1, source_target_pairs={{0,8},{2,10},{4,12},{6,14},{8,16},{10,18},{12,20},{14,22},{16,24},... | collective-permute-start | bytes 786440 | tf_op jit(solution)/shard_map/ppermute | solution.py:566
  96.9 10.9 %collective-permute-done.6.earlier_ref = bf16[32,4096]{1,0:T(8,128)(2,1)S(1)} collective-permute-done((bf16[32,4096]{1,0:T(8,128)(2,1)S(1)}, bf16[32,4096]{1,0:T(8,128)(2,1)S(1)}, u32[]{:S(2)}, u32[]{:S(2)}) %collective-permute-start.6) | collective-permute-done | bytes 262176 | tf_op jit(solution)/shard_map/ppermute | solution.py:566
  107.9 8.4 %collective-permute-start.8 = (bf16[16,4096]{1,0:T(8,128)(2,1)S(1)}, bf16[16,4096]{1,0:T(8,128)(2,1)S(1)}, u32[]{:S(2)}, u32[]{:S(2)}) collective-permute-start(bf16[16,4096]{1,0:T(8,128)(2,1)S(1)} %slice.8), channel_id=1, source_target_pairs={{0,16},{2,18},{4,20},{6,22},{8,24},{10,26},{12,28},{14,30},{1,17},... | collective-permute-start | bytes 393224 | tf_op jit(solution)/shard_map/ppermute | solution.py:566
  116.3 2.5 %collective-permute-done.8.earlier_ref = bf16[16,4096]{1,0:T(8,128)(2,1)S(1)} collective-permute-done((bf16[16,4096]{1,0:T(8,128)(2,1)S(1)}, bf16[16,4096]{1,0:T(8,128)(2,1)S(1)}, u32[]{:S(2)}, u32[]{:S(2)}) %collective-permute-start.8) | collective-permute-done | bytes 131104 | tf_op jit(solution)/shard_map/ppermute | solution.py:566
  118.7 8.2 %finish.1 = bf16[64,4096]{1,0:T(8,128)(2,1)} custom-call(f32[64,4096]{1,0:T(8,128)} %get-tuple-element.27.read_ref, f32[64,4096]{1,0:T(8,128)} %get-tuple-element.28.cum_ref, bf16[64,4096]{1,0:T(8,128)(2,1)} %z_ref.1, bf16[32,4096]{1,0:T(8,128)(2,1)S(1)} %link.5.later_ref, bf16[16,4096]{1,0:T(8,128)(2,1)S(1)} %collective-permute-done.8.earlier_ref, ...), custom_call_target="tpu_custom_call" | custom-call | flops 20971520 | bytes 3145728 | tf_op jit(solution)/shard_map/finish/pallas_call | solution.py:543
  126.9 1.1 combine.1
  (18 shorter events, 2.0 us)
Async XLA Ops:
  1.5 7.3 %collective-permute-start = (bf16[3,4096]{1,0:T(4,128)(2,1)S(1)}, bf16[3,4096]{1,0:T(4,128)(2,1)S(1)}, u32[]{:S(2)}, u32[]{:S(2)}) collective-permute-start(bf16[3,4096]{1,0:T(4,128)(2,1)S(1)} %slice.6), channel_id=1, source_target_pairs={{0,2},{2,4},{4,6},{6,8},{8,10},{10,12},{12,14},{14,16},{16,18},{18... | collective-permute-start | bytes 73736 | tf_op jit(solution)/shard_map/ppermute | solution.py:566
  8.8 21.5 %all-to-all-start = ((bf16[8,16,2304]{2,1,0:T(8,128)(2,1)}), bf16[8,16,2304]{2,1,0:T(8,128)(2,1)S(1)}, u32[]{:S(2)}, u32[]{:S(2)}) async-start(bf16[8,16,2304]{2,1,0:T(8,128)(2,1)} %bitcast.5), calls=%async_computation | async-start | bytes 1179648 | tf_op jit(solution)/shard_map/all_to_all | solution.py:584
  30.4 17.1 %collective-permute-start.4 = (bf16[144,2048]{1,0:T(8,128)(2,1)S(1)}, bf16[144,2048]{1,0:T(8,128)(2,1)S(1)}, u32[]{:S(2)}, u32[]{:S(2)}) collective-permute-start(bf16[144,2048]{1,0:T(8,128)(2,1)S(1)} %unpack.1.x_ref), channel_id=1, source_target_pairs={{0,2},{2,0},{4,6},{6,4},{8,10},{10,8},{12,14},{14,12},{16,18},{18,... | collective-permute-start | bytes 1769480 | tf_op jit(solution)/shard_map/ppermute | solution.py:576
  31.1 16.3 %collective-permute-start.1 = (bf16[32,4096]{1,0:T(8,128)(2,1)S(1)}, bf16[32,4096]{1,0:T(8,128)(2,1)S(1)}, u32[]{:S(2)}, u32[]{:S(2)}) collective-permute-start(bf16[32,4096]{1,0:T(8,128)(2,1)S(1)} %get-tuple-element.29), channel_id=1, source_target_pairs={{0,2},{2,4},{4,6},{6,8},{8,10},{10,12},{12,14},{14,16},{16,18},{18... | collective-permute-start | bytes 786440 | tf_op jit(solution)/shard_map/ppermute | solution.py:566
  34.4 13.0 %collective-permute-start.2 = (bf16[32,4096]{1,0:T(8,128)(2,1)S(1)}, bf16[32,4096]{1,0:T(8,128)(2,1)S(1)}, u32[]{:S(2)}, u32[]{:S(2)}) collective-permute-start(bf16[32,4096]{1,0:T(8,128)(2,1)S(1)} %get-tuple-element.29), channel_id=1, source_target_pairs={{0,4},{2,6},{4,8},{6,10},{8,12},{10,14},{12,16},{14,18},{16,20},{1... | collective-permute-start | bytes 786440 | tf_op jit(solution)/shard_map/ppermute | solution.py:566
  56.7 5.8 %collective-permute-start.5 = (bf16[144,6144]{1,0:T(8,128)(2,1)S(1)}, bf16[144,6144]{1,0:T(8,128)(2,1)S(1)}, u32[]{:S(2)}, u32[]{:S(2)}) collective-permute-start(bf16[144,6144]{1,0:T(8,128)(2,1)S(1)} %gate.3.refs_0_), channel_id=1, source_target_pairs={{0,1},{1,0},{2,3},{3,2},{4,5},{5,4},{6,7},{7,6},{8,9},{9,8},{10,11... | collective-permute-start | bytes 5308424 | tf_op jit(solution)/shard_map/ppermute | solution.py:571
  56.8 15.9 %collective-permute-start.7 = (bf16[144,6144]{1,0:T(8,128)(2,1)S(1)}, bf16[144,6144]{1,0:T(8,128)(2,1)S(1)}, u32[]{:S(2)}, u32[]{:S(2)}) collective-permute-start(bf16[144,6144]{1,0:T(8,128)(2,1)S(1)} %gate.2.refs_0_), channel_id=1, source_target_pairs={{0,1},{1,0},{2,3},{3,2},{4,5},{5,4},{6,7},{7,6},{8,9},{9,8},{10,11... | collective-permute-start | bytes 5308424 | tf_op jit(solution)/shard_map/ppermute | solution.py:571
  57.3 15.3 %collective-permute-start.3 = (bf16[32,4096]{1,0:T(8,128)(2,1)S(1)}, bf16[32,4096]{1,0:T(8,128)(2,1)S(1)}, u32[]{:S(2)}, u32[]{:S(2)}) collective-permute-start(bf16[32,4096]{1,0:T(8,128)(2,1)S(1)} %link.3.later_ref), channel_id=1, source_target_pairs={{0,4},{2,6},{4,8},{6,10},{8,12},{10,14},{12,16},{14,18},{16,20},{1... | collective-permute-start | bytes 786440 | tf_op jit(solution)/shard_map/ppermute | solution.py:566
  71.9 15.1 %collective-permute-start.10 = (bf16[144,2048]{1,0:T(8,128)(2,1)S(1)}, bf16[144,2048]{1,0:T(8,128)(2,1)S(1)}, u32[]{:S(2)}, u32[]{:S(2)}) collective-permute-start(bf16[144,2048]{1,0:T(8,128)(2,1)S(1)} %down.2), channel_id=1, source_target_pairs={{0,2},{2,0},{4,6},{6,4},{8,10},{10,8},{12,14},{14,12},{16,18},{18,... | collective-permute-start | bytes 1769480 | tf_op jit(solution)/shard_map/ppermute | solution.py:576
  72.6 9.5 %collective-permute-start.9 = (f32[64,8]{1,0:T(8,128)S(1)}, f32[64,8]{1,0:T(8,128)S(1)}, u32[]{:S(2)}, u32[]{:S(2)}) collective-permute-start(f32[64,8]{1,0:T(8,128)S(1)} %get-tuple-element.45.refs_0_), channel_id=1, source_target_pairs={{0,1},{1,0},{2,3},{3,2},{4,5},{5,4},{6,7},{7,6},{8,9},{9,8},{10,11... | collective-permute-start | bytes 6152 | tf_op jit(solution)/shard_map/ppermute | solution.py:571
  88.2 38.7 %all-to-all-start.1 = ((bf16[8,16,2304]{2,1,0:T(8,128)(2,1)}), bf16[8,16,2304]{2,1,0:T(8,128)(2,1)S(1)}, u32[]{:S(2)}, u32[]{:S(2)}) async-start(bf16[8,16,2304]{2,1,0:T(8,128)(2,1)} %pack_sum.1), calls=%async_computation.1 | async-start | bytes 1179648 | tf_op jit(solution)/shard_map/all_to_all | solution.py:584
  93.0 14.8 %collective-permute-start.6 = (bf16[32,4096]{1,0:T(8,128)(2,1)S(1)}, bf16[32,4096]{1,0:T(8,128)(2,1)S(1)}, u32[]{:S(2)}, u32[]{:S(2)}) collective-permute-start(bf16[32,4096]{1,0:T(8,128)(2,1)S(1)} %link.4.later_ref), channel_id=1, source_target_pairs={{0,8},{2,10},{4,12},{6,14},{8,16},{10,18},{12,20},{14,22},{16,24},... | collective-permute-start | bytes 786440 | tf_op jit(solution)/shard_map/ppermute | solution.py:566
  107.9 10.9 %collective-permute-start.8 = (bf16[16,4096]{1,0:T(8,128)(2,1)S(1)}, bf16[16,4096]{1,0:T(8,128)(2,1)S(1)}, u32[]{:S(2)}, u32[]{:S(2)}) collective-permute-start(bf16[16,4096]{1,0:T(8,128)(2,1)S(1)} %slice.8), channel_id=1, source_target_pairs={{0,16},{2,18},{4,20},{6,22},{8,24},{10,26},{12,28},{14,30},{1,17},... | collective-permute-start | bytes 393224 | tf_op jit(solution)/shard_map/ppermute | solution.py:566

commit v7 on v6

--- a/solution.py
+++ b/solution.py
@@ -485,26 +485,45 @@
     )
 
 
-def link_kernel(later_ref, earlier_ref, out_ref):
-    states = out_ref.shape[0] // 2
-    decay = later_ref[states:].astype(F32)
-    end = later_ref[:states].astype(F32) + decay * earlier_ref[:states].astype(F32)
-    out_ref[:states] = end.astype(BF16)
-    out_ref[states:] = (decay * earlier_ref[states:].astype(F32)).astype(BF16)
-
-
-def link(later, earlier):
-    return pl.pallas_call(
-        link_kernel,
-        out_shape=jax.ShapeDtypeStruct(later.shape, BF16),
+def upper_half(step):
+    return (lax.axis_index("seq") >> step) % 2 == 1
+
+
+def linked(later, earlier):
+    states = later.shape[0] // 2
+    decay = later[states:]
+    return jnp.concatenate([later[:states] + decay * earlier[:states], decay * earlier[states:]], 0)
+
+
+def link_kernel(step, *refs):
+    total_ref, received_ref, prefix_ref = refs[:3] if step else (*refs[:2], None)
+    total_out, prefix_out = refs[-2:]
+    upper = upper_half(step)
+    own, received = total_ref[...].astype(F32), received_ref[...].astype(F32)
+    later, earlier = jnp.where(upper, own, received), jnp.where(upper, received, own)
+    total_out[...] = linked(later, earlier).astype(BF16)
+    if step:
+        prefix = prefix_ref[...].astype(F32)
+    else:
+        states = own.shape[0] // 2
+        prefix = (iota(own.shape, 0) >= states).astype(F32)
+    prefix_out[...] = jnp.where(upper, linked(prefix, received), prefix).astype(BF16)
+
+
+def link(step, total, received, prefix):
+    shape = jax.ShapeDtypeStruct(total.shape, BF16)
+    args = [total, received] + ([prefix] if step else [])
+    return pl.pallas_call(
+        functools.partial(link_kernel, step),
+        out_shape=(shape, shape),
         compiler_params=params(16),
-        cost_estimate=cost(later.size * 2, later.size * 6),
+        cost_estimate=cost(total.size * 2, total.size * 6),
         name="link",
-    )(later, earlier)
+    )(*args)
 
 
 def finish_kernel(
-    read_ref, cum_ref, z_ref, later_ref, earlier_ref, alog_ref, bc_ref, out_ref, sum_ref, c_ref
+    step, read_ref, cum_ref, z_ref, prefix_ref, received_ref, alog_ref, bc_ref, out_ref, sum_ref, c_ref
 ):
     tokens, lanes = z_ref.shape
     states = alog_ref.shape[0]
@@ -514,8 +533,9 @@
         spread_states(bc_ref[1], c_ref)
 
     rates = -jnp.exp(alog_ref[...]) * LOG2E
-    entering = later_ref[:states].astype(F32)
-    entering = entering + later_ref[states:].astype(F32) * earlier_ref[...].astype(F32)
+    entering = prefix_ref[:states].astype(F32)
+    further = entering + prefix_ref[states:].astype(F32) * received_ref[:states].astype(F32)
+    entering = jnp.where(upper_half(step), further, entering)
 
     def eight(g, carry):
         at = pl.multiple_of(g * 8, 8)
@@ -532,7 +552,7 @@
     out_ref[...] = ((read_ref[...] + sum_ref[...]) * (z * jax.nn.sigmoid(z))).astype(BF16)
 
 
-def finish(read, cum, z_gate, later, earlier, a_log, b_and_c):
+def finish(step, read, cum, z_gate, prefix, received, a_log, b_and_c):
     tokens, channels = z_gate.shape
     states = a_log.shape[0]
     lanes = math.gcd(512, channels)
@@ -541,10 +561,10 @@
         return pl.BlockSpec((rows, lanes), lambda i: (0, i))
 
     return pl.pallas_call(
-        finish_kernel,
+        functools.partial(finish_kernel, step),
         grid=(channels // lanes,),
         in_specs=[
-            cut(tokens), cut(tokens), cut(tokens), cut(2 * states), cut(states), cut(states),
+            cut(tokens), cut(tokens), cut(tokens), cut(2 * states), cut(2 * states), cut(states),
             pl.BlockSpec(b_and_c.shape, lambda i: (0, 0, 0)),
         ],
         out_specs=cut(tokens),
@@ -558,12 +578,12 @@
             tokens * channels * states * 5, tokens * channels * 12, tokens * channels * states
         ),
         name="finish",
-    )(*in_hbm(read, cum, z_gate), later, earlier, *in_hbm(a_log, b_and_c))
-
-
-def shifted(value, by):
+    )(*in_hbm(read, cum, z_gate), prefix, received, *in_hbm(a_log, b_and_c))
+
+
+def swapped(value, by):
     count = lax.axis_size("seq")
-    return lax.ppermute(value, "seq", [(i, i + by) for i in range(count - by)])
+    return lax.ppermute(value, "seq", [(i, i ^ by) for i in range(count)])
 
 
 def turned(value, axis, by):
@@ -615,7 +635,8 @@
     pack = packing(features)
     ids = expert_ids.T
 
-    edge = shifted(x_in[tokens - (conv_weight.shape[0] - 1) :], 1)
+    edge = x_in[tokens - (conv_weight.shape[0] - 1) :]
+    edge = lax.ppermute(edge, "seq", [(i, i + 1) for i in range(blocks - 1)])
     outgoing, logits = route(ids, hidden, router.T, 1, pack)
     outgoing = after(outgoing, edge)
     arrived = exchanged(outgoing.reshape((experts,) + outgoing.shape[2:]), copies)
@@ -625,50 +646,49 @@
     )
     arrived = after(arrived, ends)
 
-    spans = [1, 2]
-    while spans[-1] * 2 < blocks:
-        spans.append(spans[-1] * 2)
-    state = ends
-    pending = [shifted(ends, by) for by in spans[:2]]
-    spans = spans[1:]
-
-    def linked(state, pending, spans, *marks):
-        if pending is None or not spans:
-            return state, pending, spans
-        state = link(*after(tuple(pending), *marks))
-        span, spans = spans[0], spans[1:]
-        if not spans:
-            return state, [shifted(state[: state.shape[0] // 2], span)], spans
-        return state, [state, shifted(state, span)], spans
+    steps = blocks.bit_length() - 1
+    total, prefix, received = ends, None, swapped(ends, 1)
+    step = 0
+
+    def advance(*marks):
+        nonlocal total, prefix, received, step
+        if step < steps - 1:
+            total, prefix = link(step, total, after(received, *marks), prefix)
+            step += 1
+            received = swapped(total, 1 << step)
+        return prefix
 
     rows = [unpack(arrived, features, pack)]
     for d in range(1, copies):
         rows.append(turned_within(rows[0], copies, d))
     gated = []
     for part in rows:
-        if gated:
-            state, pending, spans = linked(state, pending, spans, gated[-1][0])
-            part = after(part, gated[-1][0], state)
+        if len(gated) < 2:
+            part = after(part, advance(gated[-1][0] if gated else rows[0]))
+        else:
+            part = after(part, gated[-1][0])
         own = gate(part, w_gate)
         gated.append([own] + [turned(own, "exp", d) for d in range(1, feature_parts)])
     made = []
     for parts in gated[1:] + gated[:1]:
-        parts = lax.optimization_barrier((*parts, state))[:-1]
+        if made:
+            parts = lax.optimization_barrier((*parts, advance(made[-1])))[:-1]
         made.append(down(parts, w_down, BF16 if len(made) < copies - 1 else F32))
-        state, pending, spans = linked(state, pending, spans, made[-1])
-    while spans:
-        state, pending, spans = linked(state, pending, spans)
+    while step < steps - 1:
+        advance()
+    received = after(received, made[-1])
 
     logits = after(logits, made[0])
     logits = [logits] + [turned(logits, "exp", d) for d in range(1, feature_parts)]
     weights = blend_weights(ids, logits, 1, pack)
-    sums = [after(made[-1], weights[2])]
+    sums = [after(made[-1], weights[2], received)]
     for d in range(1, copies):
         sums.append(turned_within(made[d - 1], copies, -d))
     packed = pack_sum(sums, experts, pack)
     back = exchanged(packed, copies)
 
-    mamba_out = finish(read, cum, z_gate, state, after(pending[0], packed), a_log, b_and_c)
+    received = after(received, packed)
+    mamba_out = finish(step, read, cum, z_gate, prefix, received, a_log, b_and_c)
     back = after(back, mamba_out)
     moe_out = combine(back, weights, tokens, features, pack)
     return mamba_out, moe_out

time: 129 us -> 110 us (0.85)
  starting transfers between devices: 42.5 us -> 24.6 us
    ppermute x6 -> x5, starting transfers between devices: 29.1 us -> 11.5 us  [the longest x4 6.62 us: swapped(): return lax.ppermute(value, 'seq', [(i, i ^ by) for i in range(count)])]
    all_to_all x2, waiting for transfers between devices: 3.24 us -> 10.5 us  [exchanged(): lax.all_to_all(value, 'seq', split_axis=0, concat_axis=0, tiled=True, axi...]
    ppermute x6 -> x5, waiting for transfers between devices: 13.8 us -> 7.72 us  [the longest x4 7.71 us: swapped(): return lax.ppermute(value, 'seq', [(i, i ^ by) for i in range(count)])]
    ppermute x2, waiting for transfers between devices: 3.88 us -> 0.01 us  [turned_within(): lax.ppermute(value, 'seq', [(i, i // copies * copies + (i + by) % copies)...]
    ppermute x3, waiting for transfers between devices: 0.01 us -> 1.72 us  [turned(): lax.ppermute(value, axis, [(i, (i + by) % count) for i in range(count)])]
  transfers between devices with their start and end apart: 13 -> 12, of which waited for: 5 -> 5; matrix products, arithmetic and copies ran while one was open for 0% -> 0% of each run, Pallas kernels for 40% -> 47%
where the time goes in v7:
time: 110 us
  Pallas kernels  63.4 us (58%)
  starting transfers between devices  24.6 us (22%)
  waiting for transfers between devices  19.9 us (18%)
    pallas_call x2, Pallas kernels, down(): pl.pallas_call(functools.partial(down_kernel, chunk), in_specs=[INSIDE] *...  18.7 us
    pallas_call x2, Pallas kernels, gate(): pl.pallas_call(functools.partial(gate_kernel, chunk), in_specs=[INSIDE, A...  18.4 us
    pallas_call x1, Pallas kernels, scan(): pl.pallas_call(scan_kernel, grid=(channels // lanes,), in_specs=[cut(toke...  11.5 us
    all_to_all x2, starting transfers between devices, exchanged(): lax.all_to_all(value, 'seq', split_axis=0, concat_axis=0, tiled=True, axi...  11.3 us
    all_to_all x2, waiting for transfers between devices, exchanged(): lax.all_to_all(value, 'seq', split_axis=0, concat_axis=0, tiled=True, axi...  10.5 us
    pallas_call x1, Pallas kernels, finish(): pl.pallas_call(functools.partial(finish_kernel, step), grid=(channels //...  8.22 us
    ppermute x4, waiting for transfers between devices, swapped(): return lax.ppermute(value, 'seq', [(i, i ^ by) for i in range(count)])  7.71 us
    ppermute x4, starting transfers between devices, swapped(): return lax.ppermute(value, 'seq', [(i, i ^ by) for i in range(count)])  6.62 us
  transfers between devices with their start and end apart: 12, of which 5 were waited for; matrix products, arithmetic and copies ran while one was open for 0% of the time, Pallas kernels for 47%

profile of v7, /device:TPU:0, one launch (start us, length us, event | category | flops | bytes accessed | tf_op | source)
XLA Modules:
  0.0 109.5 jit_solution(45123227315181550)
XLA Ops:
  0.6 0.9 slice.3
  1.5 4.8 %collective-permute-start = (bf16[3,4096]{1,0:T(4,128)(2,1)S(1)}, bf16[3,4096]{1,0:T(4,128)(2,1)S(1)}, u32[]{:S(2)}, u32[]{:S(2)}) collective-permute-start(bf16[3,4096]{1,0:T(4,128)(2,1)S(1)} %slice.3), channel_id=1, source_target_pairs={{0,2},{2,4},{4,6},{6,8},{8,10},{10,12},{12,14},{14,16},{16,18},{18... | collective-permute-start | bytes 73736 | tf_op jit(solution)/shard_map/ppermute | solution.py:639
  6.3 2.4 %route.1 = (bf16[8,1,16,2304]{3,2,1,0:T(8,128)(2,1)}, f32[64,8]{1,0:T(8,128)S(1)}) custom-call(s32[2,64]{1,0:T(2,128)} %bitcast.7, bf16[64,2048]{1,0:T(8,128)(2,1)} %hidden_ref.1, bf16[8,2048]{1,0:T(8,128)(2,1)} %bitcast.6), custom_call_target="tpu_custom_call" | custom-call | flops 67108864 | bytes 1048576 | tf_op jit(solution)/shard_map/route/pallas_call | solution.py:102
  8.7 6.7 %all-to-all-start = ((bf16[8,16,2304]{2,1,0:T(8,128)(2,1)}), bf16[8,16,2304]{2,1,0:T(8,128)(2,1)S(1)}, u32[]{:S(2)}, u32[]{:S(2)}) async-start(bf16[8,16,2304]{2,1,0:T(8,128)(2,1)} %bitcast.5), calls=%async_computation | async-start | bytes 1179648 | tf_op jit(solution)/shard_map/all_to_all | solution.py:604
  15.5 11.5 %scan.1 = (f32[64,4096]{1,0:T(8,128)}, f32[64,4096]{1,0:T(8,128)}, bf16[32,4096]{1,0:T(8,128)(2,1)S(1)}) custom-call(bf16[64,4096]{1,0:T(8,128)(2,1)} %x_ref.1, bf16[3,4096]{1,0:T(4,128)(2,1)S(1)} %collective-permute-done.edge_ref, bf16[64,256]{1,0:T(8,128)(2,1)} %low_ref.1, bf16[256,4096]{1,0:T(8,128)(2,1)} %dtw_ref.1, f32[1,4096]{1,0:T(1,128)} %bitcast.9, ...), custom_call_target="tpu_custom_call" | custom-call | flops 33554432 | bytes 3145728 | tf_op jit(solution)/shard_map/scan/pallas_call | solution.py:453
  27.6 2.6 %all-to-all-done.arrived_ref = bf16[8,16,2304]{2,1,0:T(8,128)(2,1)S(1)} async-done(((bf16[8,16,2304]{2,1,0:T(8,128)(2,1)}), bf16[8,16,2304]{2,1,0:T(8,128)(2,1)S(1)}, u32[]{:S(2)}, u32[]{:S(2)}) %all-to-all-start) | async-done | bytes 589856 | tf_op jit(solution)/shard_map/all_to_all | solution.py:604
  30.4 0.6 collective-permute-start.4
  31.0 5.3 %collective-permute-done.1.refs_1_ = bf16[32,4096]{1,0:T(8,128)(2,1)S(1)} collective-permute-done((bf16[32,4096]{1,0:T(8,128)(2,1)S(1)}, bf16[32,4096]{1,0:T(8,128)(2,1)S(1)}, u32[]{:S(2)}, u32[]{:S(2)}) %collective-permute-start.1) | collective-permute-done | bytes 262176 | tf_op jit(solution)/shard_map/ppermute | solution.py:586
  36.5 2.1 %collective-permute-start.2 = (bf16[32,4096]{1,0:T(8,128)(2,1)S(1)}, bf16[32,4096]{1,0:T(8,128)(2,1)S(1)}, u32[]{:S(2)}, u32[]{:S(2)}) collective-permute-start(bf16[32,4096]{1,0:T(8,128)(2,1)S(1)} %get-tuple-element.37.refs_0_), channel_id=1, source_target_pairs={{0,4},{2,6},{4,0},{6,2},{8,12},{10,14},{12,8},{14,10},{16,20},{18,... | collective-permute-start | bytes 786440 | tf_op jit(solution)/shard_map/ppermute | solution.py:586
  38.5 9.2 %gate.2.refs_0_ = bf16[144,6144]{1,0:T(8,128)(2,1)S(1)} custom-call(bf16[144,2048]{1,0:T(8,128)(2,1)S(1)} %unpack.1.x_ref, bf16[2048,6144]{1,0:T(8,128)(2,1)} %w_ref.3), custom_call_target="tpu_custom_call" | custom-call | flops 3623878656 | bytes 25165824 | tf_op jit(solution)/shard_map/gate/pallas_call | solution.py:203
  48.0 9.2 %gate.3.refs_0_ = bf16[144,6144]{1,0:T(8,128)(2,1)S(1)} custom-call(bf16[144,2048]{1,0:T(8,128)(2,1)S(1)} %collective-permute-done.4.x_ref, bf16[2048,6144]{1,0:T(8,128)(2,1)} %w_ref.3), custom_call_target="tpu_custom_call" | custom-call | flops 3623878656 | bytes 25165824 | tf_op jit(solution)/shard_map/gate/pallas_call | solution.py:203
  57.8 1.5 %collective-permute-start.3 = (bf16[32,4096]{1,0:T(8,128)(2,1)S(1)}, bf16[32,4096]{1,0:T(8,128)(2,1)S(1)}, u32[]{:S(2)}, u32[]{:S(2)}) collective-permute-start(bf16[32,4096]{1,0:T(8,128)(2,1)S(1)} %get-tuple-element.41.refs_0_), channel_id=1, source_target_pairs={{0,8},{2,10},{4,12},{6,14},{8,0},{10,2},{12,4},{14,6},{16,24},{18,... | collective-permute-start | bytes 786440 | tf_op jit(solution)/shard_map/ppermute | solution.py:586
  59.2 1.7 %collective-permute-done.5.refs_1_ = bf16[144,6144]{1,0:T(8,128)(2,1)S(1)} collective-permute-done((bf16[144,6144]{1,0:T(8,128)(2,1)S(1)}, bf16[144,6144]{1,0:T(8,128)(2,1)S(1)}, u32[]{:S(2)}, u32[]{:S(2)}) %collective-permute-start.5) | collective-permute-done | bytes 1769504 | tf_op jit(solution)/shard_map/ppermute | solution.py:591
  61.0 9.3 %down.2 = bf16[144,2048]{1,0:T(8,128)(2,1)S(1)} custom-call(bf16[144,6144]{1,0:T(8,128)(2,1)S(1)} %gate.3.refs_0_, bf16[144,6144]{1,0:T(8,128)(2,1)S(1)} %collective-permute-done.5.refs_1_, bf16[6144,2048]{1,0:T(8,128)(2,1)} %refs_2_.3), custom_call_target="tpu_custom_call" | custom-call | flops 3623878656 | bytes 25165824 | tf_op jit(solution)/shard_map/down/pallas_call | solution.py:246
  70.3 0.7 collective-permute-start.9
  71.2 2.4 %collective-permute-start.6 = (bf16[32,4096]{1,0:T(8,128)(2,1)S(1)}, bf16[32,4096]{1,0:T(8,128)(2,1)S(1)}, u32[]{:S(2)}, u32[]{:S(2)}) collective-permute-start(bf16[32,4096]{1,0:T(8,128)(2,1)S(1)} %get-tuple-element.46), channel_id=1, source_target_pairs={{0,16},{2,18},{4,20},{6,22},{8,24},{10,26},{12,28},{14,30},{16,0},... | collective-permute-start | bytes 786440 | tf_op jit(solution)/shard_map/ppermute | solution.py:586
  73.6 9.3 %down.3.refs_0_ = f32[144,2048]{1,0:T(8,128)S(1)} custom-call(bf16[144,6144]{1,0:T(8,128)(2,1)S(1)} %gate.2.refs_0_, bf16[144,6144]{1,0:T(8,128)(2,1)S(1)} %collective-permute-done.7.refs_1_, bf16[6144,2048]{1,0:T(8,128)(2,1)} %refs_2_.3), custom_call_target="tpu_custom_call" | custom-call | flops 3623878656 | bytes 25165824 | tf_op jit(solution)/shard_map/down/pallas_call | solution.py:246
  83.0 1.1 blend_weights.1
  84.0 2.5 %collective-permute-done.6.received_ref = bf16[32,4096]{1,0:T(8,128)(2,1)S(1)} collective-permute-done((bf16[32,4096]{1,0:T(8,128)(2,1)S(1)}, bf16[32,4096]{1,0:T(8,128)(2,1)S(1)}, u32[]{:S(2)}, u32[]{:S(2)}) %collective-permute-start.6) | collective-permute-done | bytes 262176 | tf_op jit(solution)/shard_map/ppermute | solution.py:586
  86.5 1.2 %pack_sum.1 = bf16[8,16,2304]{2,1,0:T(8,128)(2,1)} custom-call(f32[144,2048]{1,0:T(8,128)S(1)} %down.3.refs_0_, bf16[144,2048]{1,0:T(8,128)(2,1)S(1)} %collective-permute-done.9.refs_1_), custom_call_target="tpu_custom_call" | custom-call | flops 4718592 | bytes 2359296 | tf_op jit(solution)/shard_map/pack_sum/pallas_call | solution.py:316
  87.7 4.5 %all-to-all-start.1 = ((bf16[8,16,2304]{2,1,0:T(8,128)(2,1)}), bf16[8,16,2304]{2,1,0:T(8,128)(2,1)S(1)}, u32[]{:S(2)}, u32[]{:S(2)}) async-start(bf16[8,16,2304]{2,1,0:T(8,128)(2,1)} %pack_sum.1), calls=%async_computation.1 | async-start | bytes 1179648 | tf_op jit(solution)/shard_map/all_to_all | solution.py:604
  92.3 8.2 %finish.1 = bf16[64,4096]{1,0:T(8,128)(2,1)} custom-call(f32[64,4096]{1,0:T(8,128)} %get-tuple-element.30.read_ref, f32[64,4096]{1,0:T(8,128)} %get-tuple-element.31.cum_ref, bf16[64,4096]{1,0:T(8,128)(2,1)} %z_ref.1, bf16[32,4096]{1,0:T(8,128)(2,1)S(1)} %get-tuple-element.45.prefix_ref, bf16[32,4096]{1,0:T(8,128)(2,1)S(1)} %collective-permute-done.6.received_ref, ...), custom_call_target="tpu_custom_call" | custom-call | flops 20971520 | bytes 3145728 | tf_op jit(solution)/shard_map/finish/pallas_call | solution.py:563
  100.5 7.9 %all-to-all-done.1.back_ref = bf16[8,16,2304]{2,1,0:T(8,128)(2,1)S(1)} async-done(((bf16[8,16,2304]{2,1,0:T(8,128)(2,1)}), bf16[8,16,2304]{2,1,0:T(8,128)(2,1)S(1)}, u32[]{:S(2)}, u32[]{:S(2)}) %all-to-all-start.1) | async-done | bytes 589856 | tf_op jit(solution)/shard_map/all_to_all | solution.py:604
  108.4 1.1 %combine.1 = bf16[64,2048]{1,0:T(8,128)(2,1)} custom-call(bf16[8,16,2304]{2,1,0:T(8,128)(2,1)S(1)} %all-to-all-done.1.back_ref, bf16[2,64,128]{2,1,0:T(8,128)(2,1)S(1)} %get-tuple-element.56.main_ref, bf16[2,64,128]{2,1,0:T(8,128)(2,1)S(1)} %get-tuple-element.57.extra_ref, f32[2,64,128]{2,1,0:T(8,128)S(1)} %get-tuple-element.52.gates_ref), custom_call_target="tpu_custom_call" | custom-call | flops 75497472 | bytes 589824 | tf_op jit(solution)/shard_map/combine/pallas_call | solution.py:347
  (15 shorter events, 2.0 us)
Async XLA Ops:
  1.5 7.3 %collective-permute-start = (bf16[3,4096]{1,0:T(4,128)(2,1)S(1)}, bf16[3,4096]{1,0:T(4,128)(2,1)S(1)}, u32[]{:S(2)}, u32[]{:S(2)}) collective-permute-start(bf16[3,4096]{1,0:T(4,128)(2,1)S(1)} %slice.3), channel_id=1, source_target_pairs={{0,2},{2,4},{4,6},{6,8},{8,10},{10,12},{12,14},{14,16},{16,18},{18... | collective-permute-start | bytes 73736 | tf_op jit(solution)/shard_map/ppermute | solution.py:639
  8.7 21.5 %all-to-all-start = ((bf16[8,16,2304]{2,1,0:T(8,128)(2,1)}), bf16[8,16,2304]{2,1,0:T(8,128)(2,1)S(1)}, u32[]{:S(2)}, u32[]{:S(2)}) async-start(bf16[8,16,2304]{2,1,0:T(8,128)(2,1)} %bitcast.5), calls=%async_computation | async-start | bytes 1179648 | tf_op jit(solution)/shard_map/all_to_all | solution.py:604
  27.0 9.3 %collective-permute-start.1 = (bf16[32,4096]{1,0:T(8,128)(2,1)S(1)}, bf16[32,4096]{1,0:T(8,128)(2,1)S(1)}, u32[]{:S(2)}, u32[]{:S(2)}) collective-permute-start(bf16[32,4096]{1,0:T(8,128)(2,1)S(1)} %get-tuple-element.32.refs_0_), channel_id=1, source_target_pairs={{0,2},{2,0},{4,6},{6,4},{8,10},{10,8},{12,14},{14,12},{16,18},{18,... | collective-permute-start | bytes 786440 | tf_op jit(solution)/shard_map/ppermute | solution.py:586
  30.4 17.6 %collective-permute-start.4 = (bf16[144,2048]{1,0:T(8,128)(2,1)S(1)}, bf16[144,2048]{1,0:T(8,128)(2,1)S(1)}, u32[]{:S(2)}, u32[]{:S(2)}) collective-permute-start(bf16[144,2048]{1,0:T(8,128)(2,1)S(1)} %unpack.1.x_ref), channel_id=1, source_target_pairs={{0,2},{2,0},{4,6},{6,4},{8,10},{10,8},{12,14},{14,12},{16,18},{18,... | collective-permute-start | bytes 1769480 | tf_op jit(solution)/shard_map/ppermute | solution.py:596
  36.5 11.3 %collective-permute-start.2 = (bf16[32,4096]{1,0:T(8,128)(2,1)S(1)}, bf16[32,4096]{1,0:T(8,128)(2,1)S(1)}, u32[]{:S(2)}, u32[]{:S(2)}) collective-permute-start(bf16[32,4096]{1,0:T(8,128)(2,1)S(1)} %get-tuple-element.37.refs_0_), channel_id=1, source_target_pairs={{0,4},{2,6},{4,0},{6,2},{8,12},{10,14},{12,8},{14,10},{16,20},{18,... | collective-permute-start | bytes 786440 | tf_op jit(solution)/shard_map/ppermute | solution.py:586
  57.2 3.8 %collective-permute-start.5 = (bf16[144,6144]{1,0:T(8,128)(2,1)S(1)}, bf16[144,6144]{1,0:T(8,128)(2,1)S(1)}, u32[]{:S(2)}, u32[]{:S(2)}) collective-permute-start(bf16[144,6144]{1,0:T(8,128)(2,1)S(1)} %gate.3.refs_0_), channel_id=1, source_target_pairs={{0,1},{1,0},{2,3},{3,2},{4,5},{5,4},{6,7},{7,6},{8,9},{9,8},{10,11... | collective-permute-start | bytes 5308424 | tf_op jit(solution)/shard_map/ppermute | solution.py:591
  57.3 13.9 %collective-permute-start.7 = (bf16[144,6144]{1,0:T(8,128)(2,1)S(1)}, bf16[144,6144]{1,0:T(8,128)(2,1)S(1)}, u32[]{:S(2)}, u32[]{:S(2)}) collective-permute-start(bf16[144,6144]{1,0:T(8,128)(2,1)S(1)} %gate.2.refs_0_), channel_id=1, source_target_pairs={{0,1},{1,0},{2,3},{3,2},{4,5},{5,4},{6,7},{7,6},{8,9},{9,8},{10,11... | collective-permute-start | bytes 5308424 | tf_op jit(solution)/shard_map/ppermute | solution.py:591
  57.8 13.2 %collective-permute-start.3 = (bf16[32,4096]{1,0:T(8,128)(2,1)S(1)}, bf16[32,4096]{1,0:T(8,128)(2,1)S(1)}, u32[]{:S(2)}, u32[]{:S(2)}) collective-permute-start(bf16[32,4096]{1,0:T(8,128)(2,1)S(1)} %get-tuple-element.41.refs_0_), channel_id=1, source_target_pairs={{0,8},{2,10},{4,12},{6,14},{8,0},{10,2},{12,4},{14,6},{16,24},{18,... | collective-permute-start | bytes 786440 | tf_op jit(solution)/shard_map/ppermute | solution.py:586
  70.3 16.2 %collective-permute-start.9 = (bf16[144,2048]{1,0:T(8,128)(2,1)S(1)}, bf16[144,2048]{1,0:T(8,128)(2,1)S(1)}, u32[]{:S(2)}, u32[]{:S(2)}) collective-permute-start(bf16[144,2048]{1,0:T(8,128)(2,1)S(1)} %down.2), channel_id=1, source_target_pairs={{0,2},{2,0},{4,6},{6,4},{8,10},{10,8},{12,14},{14,12},{16,18},{18,... | collective-permute-start | bytes 1769480 | tf_op jit(solution)/shard_map/ppermute | solution.py:596
  71.0 12.0 %collective-permute-start.8 = (f32[64,8]{1,0:T(8,128)S(1)}, f32[64,8]{1,0:T(8,128)S(1)}, u32[]{:S(2)}, u32[]{:S(2)}) collective-permute-start(f32[64,8]{1,0:T(8,128)S(1)} %get-tuple-element.51.refs_0_), channel_id=1, source_target_pairs={{0,1},{1,0},{2,3},{3,2},{4,5},{5,4},{6,7},{7,6},{8,9},{9,8},{10,11... | collective-permute-start | bytes 6152 | tf_op jit(solution)/shard_map/ppermute | solution.py:591
  71.2 15.3 %collective-permute-start.6 = (bf16[32,4096]{1,0:T(8,128)(2,1)S(1)}, bf16[32,4096]{1,0:T(8,128)(2,1)S(1)}, u32[]{:S(2)}, u32[]{:S(2)}) collective-permute-start(bf16[32,4096]{1,0:T(8,128)(2,1)S(1)} %get-tuple-element.46), channel_id=1, source_target_pairs={{0,16},{2,18},{4,20},{6,22},{8,24},{10,26},{12,28},{14,30},{16,0},... | collective-permute-start | bytes 786440 | tf_op jit(solution)/shard_map/ppermute | solution.py:586
  87.7 20.7 %all-to-all-start.1 = ((bf16[8,16,2304]{2,1,0:T(8,128)(2,1)}), bf16[8,16,2304]{2,1,0:T(8,128)(2,1)S(1)}, u32[]{:S(2)}, u32[]{:S(2)}) async-start(bf16[8,16,2304]{2,1,0:T(8,128)(2,1)} %pack_sum.1), calls=%async_computation.1 | async-start | bytes 1179648 | tf_op jit(solution)/shard_map/all_to_all | solution.py:604

commit v8 on v7

--- a/solution.py
+++ b/solution.py
@@ -663,30 +663,29 @@
         rows.append(turned_within(rows[0], copies, d))
     gated = []
     for part in rows:
-        if len(gated) < 2:
-            part = after(part, advance(gated[-1][0] if gated else rows[0]))
-        else:
+        if len(gated) == 1:
+            part = after(part, advance(gated[-1][0]))
+        elif gated:
             part = after(part, gated[-1][0])
         own = gate(part, w_gate)
         gated.append([own] + [turned(own, "exp", d) for d in range(1, feature_parts)])
+    logits = after(logits, gated[-1][0])
+    logits = [logits] + [turned(logits, "exp", d) for d in range(1, feature_parts)]
     made = []
     for parts in gated[1:] + gated[:1]:
         if made:
             parts = lax.optimization_barrier((*parts, advance(made[-1])))[:-1]
         made.append(down(parts, w_down, BF16 if len(made) < copies - 1 else F32))
+    advance(made[-1])
     while step < steps - 1:
         advance()
-    received = after(received, made[-1])
-
-    logits = after(logits, made[0])
-    logits = [logits] + [turned(logits, "exp", d) for d in range(1, feature_parts)]
-    weights = blend_weights(ids, logits, 1, pack)
-    sums = [after(made[-1], weights[2], received)]
+    sums = [after(made[-1], prefix)]
     for d in range(1, copies):
         sums.append(turned_within(made[d - 1], copies, -d))
     packed = pack_sum(sums, experts, pack)
     back = exchanged(packed, copies)
 
+    weights = blend_weights(ids, after(tuple(logits), packed), 1, pack)
     received = after(received, packed)
     mamba_out = finish(step, read, cum, z_gate, prefix, received, a_log, b_and_c)
     back = after(back, mamba_out)

time: 110 us -> 130 us (1.18)
  waiting for transfers between devices: 19.9 us -> 40.1 us
    ppermute x4, waiting for transfers between devices: 7.71 us -> 29 us  [swapped(): return lax.ppermute(value, 'seq', [(i, i ^ by) for i in range(count)])]
    all_to_all x2, waiting for transfers between devices: 10.5 us -> 3.22 us  [exchanged(): lax.all_to_all(value, 'seq', split_axis=0, concat_axis=0, tiled=True, axi...]
    ppermute x2, waiting for transfers between devices: 0.01 us -> 4.91 us  [turned_within(): lax.ppermute(value, 'seq', [(i, i // copies * copies + (i + by) % copies)...]
  transfers between devices with their start and end apart: 12 -> 12, of which waited for: 5 -> 6; matrix products, arithmetic and copies ran while one was open for 0% -> 0% of each run, Pallas kernels for 47% -> 40%
where the time goes in v8:
time: 130 us; the launch traced here: 129 us
  Pallas kernels  63.4 us (49%)
  waiting for transfers between devices  40.1 us (31%)
  starting transfers between devices  24.1 us (19%)
    ppermute x4, waiting for transfers between devices, swapped(): return lax.ppermute(value, 'seq', [(i, i ^ by) for i in range(count)])  29 us
    pallas_call x2, Pallas kernels, down(): pl.pallas_call(functools.partial(down_kernel, chunk), in_specs=[INSIDE] *...  18.7 us
    pallas_call x2, Pallas kernels, gate(): pl.pallas_call(functools.partial(gate_kernel, chunk), in_specs=[INSIDE, A...  18.4 us
    pallas_call x1, Pallas kernels, scan(): pl.pallas_call(scan_kernel, grid=(channels // lanes,), in_specs=[cut(toke...  11.5 us
    all_to_all x2, starting transfers between devices, exchanged(): lax.all_to_all(value, 'seq', split_axis=0, concat_axis=0, tiled=True, axi...  11.5 us
    pallas_call x1, Pallas kernels, finish(): pl.pallas_call(functools.partial(finish_kernel, step), grid=(channels //...  8.21 us
    ppermute x4, starting transfers between devices, swapped(): return lax.ppermute(value, 'seq', [(i, i ^ by) for i in range(count)])  5.91 us
    ppermute x2, waiting for transfers between devices, turned_within(): lax.ppermute(value, 'seq', [(i, i // copies * copies + (i + by) % copies)...  4.91 us
  transfers between devices with their start and end apart: 12, of which 6 were waited for; matrix products, arithmetic and copies ran while one was open for 0% of the time, Pallas kernels for 40%

profile of v8, /device:TPU:0, one launch (start us, length us, event | category | flops | bytes accessed | tf_op | source)
XLA Modules:
  0.0 129.1 jit_solution(14966469249636623279)
XLA Ops:
  0.6 0.9 slice.3
  1.5 4.8 %collective-permute-start = (bf16[3,4096]{1,0:T(4,128)(2,1)S(1)}, bf16[3,4096]{1,0:T(4,128)(2,1)S(1)}, u32[]{:S(2)}, u32[]{:S(2)}) collective-permute-start(bf16[3,4096]{1,0:T(4,128)(2,1)S(1)} %slice.3), channel_id=1, source_target_pairs={{0,2},{2,4},{4,6},{6,8},{8,10},{10,12},{12,14},{14,16},{16,18},{18... | collective-permute-start | bytes 73736 | tf_op jit(solution)/shard_map/ppermute | solution.py:639
  6.3 2.4 %route.1 = (bf16[8,1,16,2304]{3,2,1,0:T(8,128)(2,1)}, f32[64,8]{1,0:T(8,128)S(1)}) custom-call(s32[2,64]{1,0:T(2,128)} %bitcast.7, bf16[64,2048]{1,0:T(8,128)(2,1)} %hidden_ref.1, bf16[8,2048]{1,0:T(8,128)(2,1)} %bitcast.6), custom_call_target="tpu_custom_call" | custom-call | flops 67108864 | bytes 1048576 | tf_op jit(solution)/shard_map/route/pallas_call | solution.py:102
  8.7 6.7 %all-to-all-start = ((bf16[8,16,2304]{2,1,0:T(8,128)(2,1)}), bf16[8,16,2304]{2,1,0:T(8,128)(2,1)S(1)}, u32[]{:S(2)}, u32[]{:S(2)}) async-start(bf16[8,16,2304]{2,1,0:T(8,128)(2,1)} %bitcast.5), calls=%async_computation | async-start | bytes 1179648 | tf_op jit(solution)/shard_map/all_to_all | solution.py:604
  15.5 11.5 %scan.1 = (f32[64,4096]{1,0:T(8,128)}, f32[64,4096]{1,0:T(8,128)}, bf16[32,4096]{1,0:T(8,128)(2,1)S(1)}) custom-call(bf16[64,4096]{1,0:T(8,128)(2,1)} %x_ref.1, bf16[3,4096]{1,0:T(4,128)(2,1)S(1)} %collective-permute-done.edge_ref, bf16[64,256]{1,0:T(8,128)(2,1)} %low_ref.1, bf16[256,4096]{1,0:T(8,128)(2,1)} %dtw_ref.1, f32[1,4096]{1,0:T(1,128)} %bitcast.9, ...), custom_call_target="tpu_custom_call" | custom-call | flops 33554432 | bytes 3145728 | tf_op jit(solution)/shard_map/scan/pallas_call | solution.py:453
  27.0 3.2 %all-to-all-done.arrived_ref = bf16[8,16,2304]{2,1,0:T(8,128)(2,1)S(1)} async-done(((bf16[8,16,2304]{2,1,0:T(8,128)(2,1)}), bf16[8,16,2304]{2,1,0:T(8,128)(2,1)S(1)}, u32[]{:S(2)}, u32[]{:S(2)}) %all-to-all-start) | async-done | bytes 589856 | tf_op jit(solution)/shard_map/all_to_all | solution.py:604
  31.0 1.4 %collective-permute-start.1 = (bf16[32,4096]{1,0:T(8,128)(2,1)S(1)}, bf16[32,4096]{1,0:T(8,128)(2,1)S(1)}, u32[]{:S(2)}, u32[]{:S(2)}) collective-permute-start(bf16[32,4096]{1,0:T(8,128)(2,1)S(1)} %get-tuple-element.32.refs_0_), channel_id=1, source_target_pairs={{0,2},{2,0},{4,6},{6,4},{8,10},{10,8},{12,14},{14,12},{16,18},{18,... | collective-permute-start | bytes 786440 | tf_op jit(solution)/shard_map/ppermute | solution.py:586
  32.5 9.2 %gate.2.refs_0_ = bf16[144,6144]{1,0:T(8,128)(2,1)S(1)} custom-call(bf16[144,2048]{1,0:T(8,128)(2,1)S(1)} %unpack.1.x_ref, bf16[2048,6144]{1,0:T(8,128)(2,1)} %w_ref.3), custom_call_target="tpu_custom_call" | custom-call | flops 3623878656 | bytes 25165824 | tf_op jit(solution)/shard_map/gate/pallas_call | solution.py:203
  41.7 7.6 %collective-permute-done.1.refs_1_ = bf16[32,4096]{1,0:T(8,128)(2,1)S(1)} collective-permute-done((bf16[32,4096]{1,0:T(8,128)(2,1)S(1)}, bf16[32,4096]{1,0:T(8,128)(2,1)S(1)}, u32[]{:S(2)}, u32[]{:S(2)}) %collective-permute-start.1) | collective-permute-done | bytes 262176 | tf_op jit(solution)/shard_map/ppermute | solution.py:586
  49.4 9.2 %gate.3.refs_0_ = bf16[144,6144]{1,0:T(8,128)(2,1)S(1)} custom-call(bf16[144,2048]{1,0:T(8,128)(2,1)S(1)} %collective-permute-done.3.x_ref, bf16[2048,6144]{1,0:T(8,128)(2,1)} %w_ref.3), custom_call_target="tpu_custom_call" | custom-call | flops 3623878656 | bytes 25165824 | tf_op jit(solution)/shard_map/gate/pallas_call | solution.py:203
  59.2 1.5 %collective-permute-start.2 = (bf16[32,4096]{1,0:T(8,128)(2,1)S(1)}, bf16[32,4096]{1,0:T(8,128)(2,1)S(1)}, u32[]{:S(2)}, u32[]{:S(2)}) collective-permute-start(bf16[32,4096]{1,0:T(8,128)(2,1)S(1)} %get-tuple-element.37.refs_0_), channel_id=1, source_target_pairs={{0,4},{2,6},{4,0},{6,2},{8,12},{10,14},{12,8},{14,10},{16,20},{18,... | collective-permute-start | bytes 786440 | tf_op jit(solution)/shard_map/ppermute | solution.py:586
  60.7 1.7 %collective-permute-done.4.refs_1_ = bf16[144,6144]{1,0:T(8,128)(2,1)S(1)} collective-permute-done((bf16[144,6144]{1,0:T(8,128)(2,1)S(1)}, bf16[144,6144]{1,0:T(8,128)(2,1)S(1)}, u32[]{:S(2)}, u32[]{:S(2)}) %collective-permute-start.4) | collective-permute-done | bytes 1769504 | tf_op jit(solution)/shard_map/ppermute | solution.py:591
  62.4 9.3 %down.2 = bf16[144,2048]{1,0:T(8,128)(2,1)S(1)} custom-call(bf16[144,6144]{1,0:T(8,128)(2,1)S(1)} %gate.3.refs_0_, bf16[144,6144]{1,0:T(8,128)(2,1)S(1)} %collective-permute-done.4.refs_1_, bf16[6144,2048]{1,0:T(8,128)(2,1)} %refs_2_.3), custom_call_target="tpu_custom_call" | custom-call | flops 3623878656 | bytes 25165824 | tf_op jit(solution)/shard_map/down/pallas_call | solution.py:246
  71.8 0.6 collective-permute-start.8
  72.7 9.3 %down.3.refs_0_ = f32[144,2048]{1,0:T(8,128)S(1)} custom-call(bf16[144,6144]{1,0:T(8,128)(2,1)S(1)} %gate.2.refs_0_, bf16[144,6144]{1,0:T(8,128)(2,1)S(1)} %collective-permute-done.6.refs_1_, bf16[6144,2048]{1,0:T(8,128)(2,1)} %refs_2_.3), custom_call_target="tpu_custom_call" | custom-call | flops 3623878656 | bytes 25165824 | tf_op jit(solution)/shard_map/down/pallas_call | solution.py:246
  82.3 4.9 %collective-permute-done.8.refs_1_ = bf16[144,2048]{1,0:T(8,128)(2,1)S(1)} collective-permute-done((bf16[144,2048]{1,0:T(8,128)(2,1)S(1)}, bf16[144,2048]{1,0:T(8,128)(2,1)S(1)}, u32[]{:S(2)}, u32[]{:S(2)}) %collective-permute-start.8) | collective-permute-done | bytes 589856 | tf_op jit(solution)/shard_map/ppermute | solution.py:596
  87.2 1.2 pack_sum.1
  88.4 4.7 %all-to-all-start.1 = ((bf16[8,16,2304]{2,1,0:T(8,128)(2,1)}), bf16[8,16,2304]{2,1,0:T(8,128)(2,1)S(1)}, u32[]{:S(2)}, u32[]{:S(2)}) async-start(bf16[8,16,2304]{2,1,0:T(8,128)(2,1)} %pack_sum.1), calls=%async_computation.1 | async-start | bytes 1179648 | tf_op jit(solution)/shard_map/all_to_all | solution.py:604
  93.1 2.9 %collective-permute-start.7 = (bf16[32,4096]{1,0:T(8,128)(2,1)S(1)}, bf16[32,4096]{1,0:T(8,128)(2,1)S(1)}, u32[]{:S(2)}, u32[]{:S(2)}) collective-permute-start(bf16[32,4096]{1,0:T(8,128)(2,1)S(1)} %get-tuple-element.47), channel_id=1, source_target_pairs={{0,16},{2,18},{4,20},{6,22},{8,24},{10,26},{12,28},{14,30},{16,0},... | collective-permute-start | bytes 786440 | tf_op jit(solution)/shard_map/ppermute | solution.py:586
  96.1 1.2 collective-permute-done.9.refs_1_
  97.3 1.0 blend_weights.1
  98.3 21.4 %collective-permute-done.7.received_ref = bf16[32,4096]{1,0:T(8,128)(2,1)S(1)} collective-permute-done((bf16[32,4096]{1,0:T(8,128)(2,1)S(1)}, bf16[32,4096]{1,0:T(8,128)(2,1)S(1)}, u32[]{:S(2)}, u32[]{:S(2)}) %collective-permute-start.7) | collective-permute-done | bytes 262176 | tf_op jit(solution)/shard_map/ppermute | solution.py:586
  119.8 8.2 %finish.1 = bf16[64,4096]{1,0:T(8,128)(2,1)} custom-call(f32[64,4096]{1,0:T(8,128)} %get-tuple-element.30.read_ref, f32[64,4096]{1,0:T(8,128)} %get-tuple-element.31.cum_ref, bf16[64,4096]{1,0:T(8,128)(2,1)} %z_ref.1, bf16[32,4096]{1,0:T(8,128)(2,1)S(1)} %get-tuple-element.46.prefix_ref, bf16[32,4096]{1,0:T(8,128)(2,1)S(1)} %collective-permute-done.7.received_ref, ...), custom_call_target="tpu_custom_call" | custom-call | flops 20971520 | bytes 3145728 | tf_op jit(solution)/shard_map/finish/pallas_call | solution.py:563
  128.0 1.1 combine.1
  (15 shorter events, 2.0 us)
Async XLA Ops:
  1.5 7.3 %collective-permute-start = (bf16[3,4096]{1,0:T(4,128)(2,1)S(1)}, bf16[3,4096]{1,0:T(4,128)(2,1)S(1)}, u32[]{:S(2)}, u32[]{:S(2)}) collective-permute-start(bf16[3,4096]{1,0:T(4,128)(2,1)S(1)} %slice.3), channel_id=1, source_target_pairs={{0,2},{2,4},{4,6},{6,8},{8,10},{10,12},{12,14},{14,16},{16,18},{18... | collective-permute-start | bytes 73736 | tf_op jit(solution)/shard_map/ppermute | solution.py:639
  8.7 21.5 %all-to-all-start = ((bf16[8,16,2304]{2,1,0:T(8,128)(2,1)}), bf16[8,16,2304]{2,1,0:T(8,128)(2,1)S(1)}, u32[]{:S(2)}, u32[]{:S(2)}) async-start(bf16[8,16,2304]{2,1,0:T(8,128)(2,1)} %bitcast.5), calls=%async_computation | async-start | bytes 1179648 | tf_op jit(solution)/shard_map/all_to_all | solution.py:604
  30.4 19.0 %collective-permute-start.3 = (bf16[144,2048]{1,0:T(8,128)(2,1)S(1)}, bf16[144,2048]{1,0:T(8,128)(2,1)S(1)}, u32[]{:S(2)}, u32[]{:S(2)}) collective-permute-start(bf16[144,2048]{1,0:T(8,128)(2,1)S(1)} %unpack.1.x_ref), channel_id=1, source_target_pairs={{0,2},{2,0},{4,6},{6,4},{8,10},{10,8},{12,14},{14,12},{16,18},{18,... | collective-permute-start | bytes 1769480 | tf_op jit(solution)/shard_map/ppermute | solution.py:596
  31.0 18.2 %collective-permute-start.1 = (bf16[32,4096]{1,0:T(8,128)(2,1)S(1)}, bf16[32,4096]{1,0:T(8,128)(2,1)S(1)}, u32[]{:S(2)}, u32[]{:S(2)}) collective-permute-start(bf16[32,4096]{1,0:T(8,128)(2,1)S(1)} %get-tuple-element.32.refs_0_), channel_id=1, source_target_pairs={{0,2},{2,0},{4,6},{6,4},{8,10},{10,8},{12,14},{14,12},{16,18},{18,... | collective-permute-start | bytes 786440 | tf_op jit(solution)/shard_map/ppermute | solution.py:586
  58.6 3.8 %collective-permute-start.4 = (bf16[144,6144]{1,0:T(8,128)(2,1)S(1)}, bf16[144,6144]{1,0:T(8,128)(2,1)S(1)}, u32[]{:S(2)}, u32[]{:S(2)}) collective-permute-start(bf16[144,6144]{1,0:T(8,128)(2,1)S(1)} %gate.3.refs_0_), channel_id=1, source_target_pairs={{0,1},{1,0},{2,3},{3,2},{4,5},{5,4},{6,7},{7,6},{8,9},{9,8},{10,11... | collective-permute-start | bytes 5308424 | tf_op jit(solution)/shard_map/ppermute | solution.py:591
  58.7 14.0 %collective-permute-start.6 = (bf16[144,6144]{1,0:T(8,128)(2,1)S(1)}, bf16[144,6144]{1,0:T(8,128)(2,1)S(1)}, u32[]{:S(2)}, u32[]{:S(2)}) collective-permute-start(bf16[144,6144]{1,0:T(8,128)(2,1)S(1)} %gate.2.refs_0_), channel_id=1, source_target_pairs={{0,1},{1,0},{2,3},{3,2},{4,5},{5,4},{6,7},{7,6},{8,9},{9,8},{10,11... | collective-permute-start | bytes 5308424 | tf_op jit(solution)/shard_map/ppermute | solution.py:591
  59.2 13.2 %collective-permute-start.2 = (bf16[32,4096]{1,0:T(8,128)(2,1)S(1)}, bf16[32,4096]{1,0:T(8,128)(2,1)S(1)}, u32[]{:S(2)}, u32[]{:S(2)}) collective-permute-start(bf16[32,4096]{1,0:T(8,128)(2,1)S(1)} %get-tuple-element.37.refs_0_), channel_id=1, source_target_pairs={{0,4},{2,6},{4,0},{6,2},{8,12},{10,14},{12,8},{14,10},{16,20},{18,... | collective-permute-start | bytes 786440 | tf_op jit(solution)/shard_map/ppermute | solution.py:586
  71.8 15.4 %collective-permute-start.8 = (bf16[144,2048]{1,0:T(8,128)(2,1)S(1)}, bf16[144,2048]{1,0:T(8,128)(2,1)S(1)}, u32[]{:S(2)}, u32[]{:S(2)}) collective-permute-start(bf16[144,2048]{1,0:T(8,128)(2,1)S(1)} %down.2), channel_id=1, source_target_pairs={{0,2},{2,0},{4,6},{6,4},{8,10},{10,8},{12,14},{14,12},{16,18},{18,... | collective-permute-start | bytes 1769480 | tf_op jit(solution)/shard_map/ppermute | solution.py:596
  72.6 9.4 %collective-permute-start.5 = (bf16[32,4096]{1,0:T(8,128)(2,1)S(1)}, bf16[32,4096]{1,0:T(8,128)(2,1)S(1)}, u32[]{:S(2)}, u32[]{:S(2)}) collective-permute-start(bf16[32,4096]{1,0:T(8,128)(2,1)S(1)} %get-tuple-element.41.refs_0_), channel_id=1, source_target_pairs={{0,8},{2,10},{4,12},{6,14},{8,0},{10,2},{12,4},{14,6},{16,24},{18,... | collective-permute-start | bytes 786440 | tf_op jit(solution)/shard_map/ppermute | solution.py:586
  88.4 39.6 %all-to-all-start.1 = ((bf16[8,16,2304]{2,1,0:T(8,128)(2,1)}), bf16[8,16,2304]{2,1,0:T(8,128)(2,1)S(1)}, u32[]{:S(2)}, u32[]{:S(2)}) async-start(bf16[8,16,2304]{2,1,0:T(8,128)(2,1)} %pack_sum.1), calls=%async_computation.1 | async-start | bytes 1179648 | tf_op jit(solution)/shard_map/all_to_all | solution.py:604
  93.1 26.6 %collective-permute-start.7 = (bf16[32,4096]{1,0:T(8,128)(2,1)S(1)}, bf16[32,4096]{1,0:T(8,128)(2,1)S(1)}, u32[]{:S(2)}, u32[]{:S(2)}) collective-permute-start(bf16[32,4096]{1,0:T(8,128)(2,1)S(1)} %get-tuple-element.47), channel_id=1, source_target_pairs={{0,16},{2,18},{4,20},{6,22},{8,24},{10,26},{12,28},{14,30},{16,0},... | collective-permute-start | bytes 786440 | tf_op jit(solution)/shard_map/ppermute | solution.py:586
  96.1 1.2 collective-permute-start.9

commit v9 on v8

--- a/solution.py
+++ b/solution.py
@@ -389,7 +389,7 @@
 
 def scan_kernel(
     x_ref, edge_ref, low_ref, dtw_ref, dtb_ref, alog_ref, cw_ref, cb_ref, skip_ref, bc_ref,
-    read_ref, cum_ref, ends_ref, padded, delta_ref, fed_ref, b_ref, c_ref,
+    read_ref, cum_ref, ends_ref, padded, delta_ref, fed_ref, totals_ref, b_ref, c_ref,
 ):
     tokens, lanes = x_ref.shape
     taps = cw_ref.shape[0]
@@ -399,6 +399,7 @@
     def _():
         spread_states(bc_ref[0], b_ref)
         spread_states(bc_ref[1], c_ref)
+        totals_ref[...] = jnp.zeros_like(totals_ref)
 
     padded[8:] = x_ref[...].astype(F32)
     padded[8 - (taps - 1) : 8] = edge_ref[...].astype(F32)
@@ -434,8 +435,15 @@
     state, running = lax.fori_loop(
         0, tokens // 8, eight, (jnp.zeros((states, lanes), F32), jnp.zeros((1, lanes), F32))
     )
-    ends_ref[:states] = state.astype(BF16)
-    ends_ref[states:] = jnp.exp2(rates * running).astype(BF16)
+    step, steps = pl.program_id(0), pl.num_programs(0)
+    ends_ref[:, pl.ds(pl.multiple_of(step * lanes, lanes), lanes)] = state.astype(BF16)
+    high = running.astype(BF16).astype(F32)
+    totals_ref[pl.ds(step, 1)] = high
+    totals_ref[pl.ds(steps + step, 1)] = running - high
+
+    @pl.when(step == steps - 1)
+    def _():
+        ends_ref[:, ends_ref.shape[1] - lanes :] = totals_ref[...].astype(BF16)
 
 
 def scan(x_in, edge, dt_low, dt_weight, dt_bias, a_log, conv_weight, conv_bias, d_skip, b_and_c):
@@ -457,16 +465,21 @@
             cut(tokens), cut(edge.shape[0]), whole(dt_low), cut(dt_weight.shape[0]), cut(1),
             cut(states), cut(conv_weight.shape[0]), cut(1), cut(1), whole(b_and_c),
         ],
-        out_specs=(cut(tokens), cut(tokens), cut(2 * states)),
+        out_specs=(
+            cut(tokens),
+            cut(tokens),
+            pl.BlockSpec((states, channels + lanes), lambda i: (0, 0)),
+        ),
         out_shape=(
             pltpu.HBM((tokens, channels), F32),
             pltpu.HBM((tokens, channels), F32),
-            jax.ShapeDtypeStruct((2 * states, channels), BF16),
+            jax.ShapeDtypeStruct((states, channels + lanes), BF16),
         ),
         scratch_shapes=[
             pltpu.VMEM((tokens + 8, lanes), F32),
             pltpu.VMEM((tokens, lanes), F32),
             pltpu.VMEM((tokens, lanes), F32),
+            pltpu.VMEM((states, lanes), F32),
             pltpu.VMEM((tokens, states, 128), F32),
             pltpu.VMEM((tokens, states, 128), F32),
         ],
@@ -489,30 +502,46 @@
     return (lax.axis_index("seq") >> step) % 2 == 1
 
 
-def linked(later, earlier):
-    states = later.shape[0] // 2
-    decay = later[states:]
-    return jnp.concatenate([later[:states] + decay * earlier[:states], decay * earlier[states:]], 0)
-
-
 def link_kernel(step, *refs):
-    total_ref, received_ref, prefix_ref = refs[:3] if step else (*refs[:2], None)
+    total_ref, received_ref, alog_ref, prefix_ref = refs[:4] if step else (*refs[:3], None)
     total_out, prefix_out = refs[-2:]
+    channels = alog_ref.shape[1]
+    lanes = total_ref.shape[1] - channels
+    steps = channels // lanes
     upper = upper_half(step)
-    own, received = total_ref[...].astype(F32), received_ref[...].astype(F32)
-    later, earlier = jnp.where(upper, own, received), jnp.where(upper, received, own)
-    total_out[...] = linked(later, earlier).astype(BF16)
-    if step:
-        prefix = prefix_ref[...].astype(F32)
-    else:
-        states = own.shape[0] // 2
-        prefix = (iota(own.shape, 0) >= states).astype(F32)
-    prefix_out[...] = jnp.where(upper, linked(prefix, received), prefix).astype(BF16)
-
-
-def link(step, total, received, prefix):
+
+    def sizes(ref):
+        value = ref[:, channels:].astype(F32)
+        return value[:steps] + value[steps : 2 * steps]
+
+    def put_sizes(ref, value):
+        high = value.astype(BF16).astype(F32)
+        rest = jnp.zeros((ref.shape[0] - 2 * steps, lanes), F32)
+        parts = [high, value - high] + ([rest] if rest.shape[0] else [])
+        ref[:, channels:] = jnp.concatenate(parts, axis=0).astype(BF16)
+
+    own, received = sizes(total_ref), sizes(received_ref)
+    before = sizes(prefix_ref) if step else jnp.zeros_like(own)
+    later = jnp.where(upper, own, received)
+    put_sizes(total_out, own + received)
+    put_sizes(prefix_out, before + jnp.where(upper, received, 0.0))
+    for i in range(steps):
+        at = slice(i * lanes, (i + 1) * lanes)
+        rates = -jnp.exp(alog_ref[:, at]) * LOG2E
+        mine, theirs = total_ref[:, at].astype(F32), received_ref[:, at].astype(F32)
+        last, first = jnp.where(upper, mine, theirs), jnp.where(upper, theirs, mine)
+        total_out[:, at] = (last + jnp.exp2(rates * later[i : i + 1]) * first).astype(BF16)
+        if step:
+            prefix = prefix_ref[:, at].astype(F32)
+            further = prefix + jnp.exp2(rates * before[i : i + 1]) * theirs
+        else:
+            prefix, further = jnp.zeros_like(theirs), theirs
+        prefix_out[:, at] = jnp.where(upper, further, prefix).astype(BF16)
+
+
+def link(step, total, received, a_log, prefix):
     shape = jax.ShapeDtypeStruct(total.shape, BF16)
-    args = [total, received] + ([prefix] if step else [])
+    args = [total, received, a_log] + ([prefix] if step else [])
     return pl.pallas_call(
         functools.partial(link_kernel, step),
         out_shape=(shape, shape),
@@ -523,18 +552,21 @@
 
 
 def finish_kernel(
-    step, read_ref, cum_ref, z_ref, prefix_ref, received_ref, alog_ref, bc_ref, out_ref, sum_ref, c_ref
+    step, read_ref, cum_ref, z_ref, prefix_ref, sizes_ref, received_ref, alog_ref, bc_ref,
+    out_ref, sum_ref, wide_ref, c_ref,
 ):
     tokens, lanes = z_ref.shape
-    states = alog_ref.shape[0]
-
-    @pl.when(pl.program_id(0) == 0)
+    at, steps = pl.program_id(0), pl.num_programs(0)
+
+    @pl.when(at == 0)
     def _():
         spread_states(bc_ref[1], c_ref)
+        wide_ref[...] = sizes_ref[...].astype(F32)
 
     rates = -jnp.exp(alog_ref[...]) * LOG2E
-    entering = prefix_ref[:states].astype(F32)
-    further = entering + prefix_ref[states:].astype(F32) * received_ref[:states].astype(F32)
+    entering = prefix_ref[...].astype(F32)
+    size = wide_ref[pl.ds(at, 1)] + wide_ref[pl.ds(steps + at, 1)]
+    further = entering + jnp.exp2(rates * size) * received_ref[...].astype(F32)
     entering = jnp.where(upper_half(step), further, entering)
 
     def eight(g, carry):
@@ -564,13 +596,15 @@
         functools.partial(finish_kernel, step),
         grid=(channels // lanes,),
         in_specs=[
-            cut(tokens), cut(tokens), cut(tokens), cut(2 * states), cut(2 * states), cut(states),
+            cut(tokens), cut(tokens), cut(tokens), cut(states),
+            pl.BlockSpec((states, lanes), lambda i: (0, channels // lanes)), cut(states), cut(states),
             pl.BlockSpec(b_and_c.shape, lambda i: (0, 0, 0)),
         ],
         out_specs=cut(tokens),
         out_shape=jax.ShapeDtypeStruct((tokens, channels), BF16),
         scratch_shapes=[
             pltpu.VMEM((tokens, lanes), F32),
+            pltpu.VMEM((states, lanes), F32),
             pltpu.VMEM((tokens, states, 128), F32),
         ],
         compiler_params=params(40),
@@ -578,7 +612,7 @@
             tokens * channels * states * 5, tokens * channels * 12, tokens * channels * states
         ),
         name="finish",
-    )(*in_hbm(read, cum, z_gate), prefix, received, *in_hbm(a_log, b_and_c))
+    )(*in_hbm(read, cum, z_gate), prefix, prefix, received, *in_hbm(a_log, b_and_c))
 
 
 def swapped(value, by):
@@ -644,7 +678,8 @@
     read, cum, ends = scan(
         x_in, edge, dt_low, dt_weight, dt_bias, a_log, conv_weight, conv_bias, d_skip, b_and_c
     )
-    arrived = after(arrived, ends)
+    logits = [logits] + [turned(logits, "exp", d) for d in range(1, feature_parts)]
+    arrived = after(arrived, ends, *logits)
 
     steps = blocks.bit_length() - 1
     total, prefix, received = ends, None, swapped(ends, 1)
@@ -653,7 +688,7 @@
     def advance(*marks):
         nonlocal total, prefix, received, step
         if step < steps - 1:
-            total, prefix = link(step, total, after(received, *marks), prefix)
+            total, prefix = link(step, total, after(received, *marks), a_log, prefix)
             step += 1
             received = swapped(total, 1 << step)
         return prefix
@@ -668,18 +703,18 @@
         elif gated:
             part = after(part, gated[-1][0])
         own = gate(part, w_gate)
+        if len(gated) == copies - 1:
+            own = after(own, advance(own), *(p for parts in gated for p in parts[1:]))
         gated.append([own] + [turned(own, "exp", d) for d in range(1, feature_parts)])
-    logits = after(logits, gated[-1][0])
-    logits = [logits] + [turned(logits, "exp", d) for d in range(1, feature_parts)]
     made = []
     for parts in gated[1:] + gated[:1]:
-        if made:
-            parts = lax.optimization_barrier((*parts, advance(made[-1])))[:-1]
-        made.append(down(parts, w_down, BF16 if len(made) < copies - 1 else F32))
-    advance(made[-1])
+        product = down(parts, w_down, BF16 if len(made) < copies - 1 else F32)
+        if not made:
+            product = after(product, advance(product))
+        made.append(product)
     while step < steps - 1:
         advance()
-    sums = [after(made[-1], prefix)]
+    sums = [after(made[-1], received)]
     for d in range(1, copies):
         sums.append(turned_within(made[d - 1], copies, -d))
     packed = pack_sum(sums, experts, pack)

time: 130 us -> 121 us (0.931)
  waiting for transfers between devices: 40.1 us -> 35.3 us
  starting transfers between devices: 24.1 us -> 19.6 us
    ppermute x4, waiting for transfers between devices: 29 us -> 16.8 us  [swapped(): return lax.ppermute(value, 'seq', [(i, i ^ by) for i in range(count)])]
    all_to_all x2, waiting for transfers between devices: 3.22 us -> 9.5 us  [exchanged(): lax.all_to_all(value, 'seq', split_axis=0, concat_axis=0, tiled=True, axi...]
    ppermute x4, starting transfers between devices: 5.91 us -> 3.04 us  [swapped(): return lax.ppermute(value, 'seq', [(i, i ^ by) for i in range(count)])]
  transfers between devices with their start and end apart: 12 -> 12, of which waited for: 6 -> 5; matrix products, arithmetic and copies ran while one was open for 0% -> 0% of each run, Pallas kernels for 40% -> 43%
where the time goes in v9:
time: 121 us; the launch traced here: 120 us
  Pallas kernels  63.4 us (52%)
  waiting for transfers between devices  35.3 us (29%)
  starting transfers between devices  19.6 us (16%)
    pallas_call x2, Pallas kernels, down(): pl.pallas_call(functools.partial(down_kernel, chunk), in_specs=[INSIDE] *...  18.7 us
    pallas_call x2, Pallas kernels, gate(): pl.pallas_call(functools.partial(gate_kernel, chunk), in_specs=[INSIDE, A...  18.5 us
    ppermute x4, waiting for transfers between devices, swapped(): return lax.ppermute(value, 'seq', [(i, i ^ by) for i in range(count)])  16.8 us
    pallas_call x1, Pallas kernels, scan(): pl.pallas_call(scan_kernel, grid=(channels // lanes,), in_specs=[cut(toke...  11.5 us
    all_to_all x2, starting transfers between devices, exchanged(): lax.all_to_all(value, 'seq', split_axis=0, concat_axis=0, tiled=True, axi...  10.3 us
    all_to_all x2, waiting for transfers between devices, exchanged(): lax.all_to_all(value, 'seq', split_axis=0, concat_axis=0, tiled=True, axi...  9.5 us
    pallas_call x1, Pallas kernels, finish(): pl.pallas_call(functools.partial(finish_kernel, step), grid=(channels //...  8.27 us
    ppermute x2, waiting for transfers between devices, turned_within(): lax.ppermute(value, 'seq', [(i, i // copies * copies + (i + by) % copies)...  5.42 us
  transfers between devices with their start and end apart: 12, of which 5 were waited for; matrix products, arithmetic and copies ran while one was open for 0% of the time, Pallas kernels for 43%

profile of v9, /device:TPU:0, one launch (start us, length us, event | category | flops | bytes accessed | tf_op | source)
XLA Modules:
  0.0 120.0 jit_solution(7791118813187232554)
XLA Ops:
  0.6 0.9 slice.3
  1.5 4.8 %collective-permute-start = (bf16[3,4096]{1,0:T(4,128)(2,1)S(1)}, bf16[3,4096]{1,0:T(4,128)(2,1)S(1)}, u32[]{:S(2)}, u32[]{:S(2)}) collective-permute-start(bf16[3,4096]{1,0:T(4,128)(2,1)S(1)} %slice.3), channel_id=1, source_target_pairs={{0,2},{2,4},{4,6},{6,8},{8,10},{10,12},{12,14},{14,16},{16,18},{18... | collective-permute-start | bytes 73736 | tf_op jit(solution)/shard_map/ppermute | solution.py:673
  6.3 2.4 %route.1 = (bf16[8,1,16,2304]{3,2,1,0:T(8,128)(2,1)}, f32[64,8]{1,0:T(8,128)S(1)}) custom-call(s32[2,64]{1,0:T(2,128)} %bitcast.7, bf16[64,2048]{1,0:T(8,128)(2,1)} %hidden_ref.1, bf16[8,2048]{1,0:T(8,128)(2,1)} %bitcast.6), custom_call_target="tpu_custom_call" | custom-call | flops 67108864 | bytes 1048576 | tf_op jit(solution)/shard_map/route/pallas_call | solution.py:102
  8.8 6.7 %all-to-all-start = ((bf16[8,16,2304]{2,1,0:T(8,128)(2,1)}), bf16[8,16,2304]{2,1,0:T(8,128)(2,1)S(1)}, u32[]{:S(2)}, u32[]{:S(2)}) async-start(bf16[8,16,2304]{2,1,0:T(8,128)(2,1)} %bitcast.5), calls=%async_computation | async-start | bytes 1179648 | tf_op jit(solution)/shard_map/all_to_all | solution.py:638
  15.5 11.5 %scan.1 = (f32[64,4096]{1,0:T(8,128)}, f32[64,4096]{1,0:T(8,128)}, bf16[16,4608]{1,0:T(8,128)(2,1)S(1)}) custom-call(bf16[64,4096]{1,0:T(8,128)(2,1)} %x_ref.1, bf16[3,4096]{1,0:T(4,128)(2,1)S(1)} %collective-permute-done.edge_ref, bf16[64,256]{1,0:T(8,128)(2,1)} %low_ref.1, bf16[256,4096]{1,0:T(8,128)(2,1)} %dtw_ref.1, f32[1,4096]{1,0:T(1,128)} %bitcast.9, ...), custom_call_target="tpu_custom_call" | custom-call | flops 33554432 | bytes 3145728 | tf_op jit(solution)/shard_map/scan/pallas_call | solution.py:461
  27.0 3.3 %all-to-all-done.arrived_ref = bf16[8,16,2304]{2,1,0:T(8,128)(2,1)S(1)} async-done(((bf16[8,16,2304]{2,1,0:T(8,128)(2,1)}), bf16[8,16,2304]{2,1,0:T(8,128)(2,1)S(1)}, u32[]{:S(2)}, u32[]{:S(2)}) %all-to-all-start) | async-done | bytes 589856 | tf_op jit(solution)/shard_map/all_to_all | solution.py:638
  30.4 9.3 %gate.2.refs_0_ = bf16[144,6144]{1,0:T(8,128)(2,1)S(1)} custom-call(bf16[144,2048]{1,0:T(8,128)(2,1)S(1)} %unpack.1.x_ref, bf16[2048,6144]{1,0:T(8,128)(2,1)} %w_ref.3), custom_call_target="tpu_custom_call" | custom-call | flops 3623878656 | bytes 25165824 | tf_op jit(solution)/shard_map/gate/pallas_call | solution.py:203
  39.7 0.7 collective-permute-start.4
  40.4 1.4 %collective-permute-start.1 = (bf16[16,4608]{1,0:T(8,128)(2,1)S(1)}, bf16[16,4608]{1,0:T(8,128)(2,1)S(1)}, u32[]{:S(2)}, u32[]{:S(2)}) collective-permute-start(bf16[16,4608]{1,0:T(8,128)(2,1)S(1)} %get-tuple-element.31.refs_0_), channel_id=1, source_target_pairs={{0,2},{2,0},{4,6},{6,4},{8,10},{10,8},{12,14},{14,12},{16,18},{18,... | collective-permute-start | bytes 442376 | tf_op jit(solution)/shard_map/ppermute | solution.py:620
  41.8 16.8 %collective-permute-done.1.refs_1_ = bf16[16,4608]{1,0:T(8,128)(2,1)S(1)} collective-permute-done((bf16[16,4608]{1,0:T(8,128)(2,1)S(1)}, bf16[16,4608]{1,0:T(8,128)(2,1)S(1)}, u32[]{:S(2)}, u32[]{:S(2)}) %collective-permute-start.1) | collective-permute-done | bytes 147488 | tf_op jit(solution)/shard_map/ppermute | solution.py:620
  58.8 1.5 %collective-permute-start.3 = (bf16[16,4608]{1,0:T(8,128)(2,1)S(1)}, bf16[16,4608]{1,0:T(8,128)(2,1)S(1)}, u32[]{:S(2)}, u32[]{:S(2)}) collective-permute-start(bf16[16,4608]{1,0:T(8,128)(2,1)S(1)} %get-tuple-element.37.refs_0_), channel_id=1, source_target_pairs={{0,4},{2,6},{4,0},{6,2},{8,12},{10,14},{12,8},{14,10},{16,20},{18,... | collective-permute-start | bytes 442376 | tf_op jit(solution)/shard_map/ppermute | solution.py:620
  60.3 9.2 %gate.3.refs_0_ = bf16[144,6144]{1,0:T(8,128)(2,1)S(1)} custom-call(bf16[144,2048]{1,0:T(8,128)(2,1)S(1)} %collective-permute-done.4.x_ref, bf16[2048,6144]{1,0:T(8,128)(2,1)} %w_ref.3), custom_call_target="tpu_custom_call" | custom-call | flops 3623878656 | bytes 25165824 | tf_op jit(solution)/shard_map/gate/pallas_call | solution.py:203
  69.6 0.2 link.4
  69.9 3.6 %collective-permute-done.7.refs_1_ = bf16[144,6144]{1,0:T(8,128)(2,1)S(1)} collective-permute-done((bf16[144,6144]{1,0:T(8,128)(2,1)S(1)}, bf16[144,6144]{1,0:T(8,128)(2,1)S(1)}, u32[]{:S(2)}, u32[]{:S(2)}) %collective-permute-start.7) | collective-permute-done | bytes 1769504 | tf_op jit(solution)/shard_map/ppermute | solution.py:625
  73.5 9.3 %down.2 = bf16[144,2048]{1,0:T(8,128)(2,1)S(1)} custom-call(bf16[144,6144]{1,0:T(8,128)(2,1)S(1)} %gate.3.refs_0_, bf16[144,6144]{1,0:T(8,128)(2,1)S(1)} %collective-permute-done.7.refs_1_, bf16[6144,2048]{1,0:T(8,128)(2,1)} %refs_2_.9), custom_call_target="tpu_custom_call" | custom-call | flops 3623878656 | bytes 25165824 | tf_op jit(solution)/shard_map/down/pallas_call | solution.py:246
  83.1 0.7 collective-permute-start.9
  83.7 9.3 %down.3.refs_0_ = f32[144,2048]{1,0:T(8,128)S(1)} custom-call(bf16[144,6144]{1,0:T(8,128)(2,1)S(1)} %gate.2.refs_0_, bf16[144,6144]{1,0:T(8,128)(2,1)S(1)} %collective-permute-done.6.refs_1_, bf16[6144,2048]{1,0:T(8,128)(2,1)} %refs_2_.9), custom_call_target="tpu_custom_call" | custom-call | flops 3623878656 | bytes 25165824 | tf_op jit(solution)/shard_map/down/pallas_call | solution.py:246
  93.1 5.4 %collective-permute-done.9.refs_1_ = bf16[144,2048]{1,0:T(8,128)(2,1)S(1)} collective-permute-done((bf16[144,2048]{1,0:T(8,128)(2,1)S(1)}, bf16[144,2048]{1,0:T(8,128)(2,1)S(1)}, u32[]{:S(2)}, u32[]{:S(2)}) %collective-permute-start.9) | collective-permute-done | bytes 589856 | tf_op jit(solution)/shard_map/ppermute | solution.py:630
  98.5 1.2 %pack_sum.1 = bf16[8,16,2304]{2,1,0:T(8,128)(2,1)} custom-call(f32[144,2048]{1,0:T(8,128)S(1)} %down.3.refs_0_, bf16[144,2048]{1,0:T(8,128)(2,1)S(1)} %collective-permute-done.9.refs_1_), custom_call_target="tpu_custom_call" | custom-call | flops 4718592 | bytes 2359296 | tf_op jit(solution)/shard_map/pack_sum/pallas_call | solution.py:316
  99.8 3.5 %all-to-all-start.1 = ((bf16[8,16,2304]{2,1,0:T(8,128)(2,1)}), bf16[8,16,2304]{2,1,0:T(8,128)(2,1)S(1)}, u32[]{:S(2)}, u32[]{:S(2)}) async-start(bf16[8,16,2304]{2,1,0:T(8,128)(2,1)} %pack_sum.1), calls=%async_computation.1 | async-start | bytes 1179648 | tf_op jit(solution)/shard_map/all_to_all | solution.py:638
  103.3 1.1 blend_weights.1
  104.4 8.3 %finish.1 = bf16[64,4096]{1,0:T(8,128)(2,1)} custom-call(f32[64,4096]{1,0:T(8,128)} %get-tuple-element.29.read_ref, f32[64,4096]{1,0:T(8,128)} %get-tuple-element.30.cum_ref, bf16[64,4096]{1,0:T(8,128)(2,1)} %z_ref.1, bf16[16,4608]{1,0:T(8,128)(2,1)S(1)} %get-tuple-element.45.prefix_ref.sizes_ref, ...), custom_call_target="tpu_custom_call" | custom-call | flops 20971520 | bytes 3145728 | tf_op jit(solution)/shard_map/finish/pallas_call | solution.py:595
  112.6 6.2 %all-to-all-done.1.back_ref = bf16[8,16,2304]{2,1,0:T(8,128)(2,1)S(1)} async-done(((bf16[8,16,2304]{2,1,0:T(8,128)(2,1)}), bf16[8,16,2304]{2,1,0:T(8,128)(2,1)S(1)}, u32[]{:S(2)}, u32[]{:S(2)}) %all-to-all-start.1) | async-done | bytes 589856 | tf_op jit(solution)/shard_map/all_to_all | solution.py:638
  118.9 1.1 combine.1
  (17 shorter events, 0.8 us)
Async XLA Ops:
  1.5 7.3 %collective-permute-start = (bf16[3,4096]{1,0:T(4,128)(2,1)S(1)}, bf16[3,4096]{1,0:T(4,128)(2,1)S(1)}, u32[]{:S(2)}, u32[]{:S(2)}) collective-permute-start(bf16[3,4096]{1,0:T(4,128)(2,1)S(1)} %slice.3), channel_id=1, source_target_pairs={{0,2},{2,4},{4,6},{6,8},{8,10},{10,12},{12,14},{14,16},{16,18},{18... | collective-permute-start | bytes 73736 | tf_op jit(solution)/shard_map/ppermute | solution.py:673
  8.8 21.5 %all-to-all-start = ((bf16[8,16,2304]{2,1,0:T(8,128)(2,1)}), bf16[8,16,2304]{2,1,0:T(8,128)(2,1)S(1)}, u32[]{:S(2)}, u32[]{:S(2)}) async-start(bf16[8,16,2304]{2,1,0:T(8,128)(2,1)} %bitcast.5), calls=%async_computation | async-start | bytes 1179648 | tf_op jit(solution)/shard_map/all_to_all | solution.py:638
  15.5 11.5 %collective-permute-start.2 = (f32[64,8]{1,0:T(8,128)S(1)}, f32[64,8]{1,0:T(8,128)S(1)}, u32[]{:S(2)}, u32[]{:S(2)}) collective-permute-start(f32[64,8]{1,0:T(8,128)S(1)} %get-tuple-element.51.refs_0_), channel_id=1, source_target_pairs={{0,1},{1,0},{2,3},{3,2},{4,5},{5,4},{6,7},{7,6},{8,9},{9,8},{10,11... | collective-permute-start | bytes 6152 | tf_op jit(solution)/shard_map/ppermute | solution.py:625
  30.4 28.3 %copy-start = (f32[16,4096]{1,0:T(8,128)S(1)}, f32[16,4096]{1,0:T(8,128)}, u32[]{:S(2)}) copy-start(f32[16,4096]{1,0:T(8,128)} %alog_ref.3) | copy-start | bytes 786436
  39.7 30.1 %collective-permute-start.6 = (bf16[144,6144]{1,0:T(8,128)(2,1)S(1)}, bf16[144,6144]{1,0:T(8,128)(2,1)S(1)}, u32[]{:S(2)}, u32[]{:S(2)}) collective-permute-start(bf16[144,6144]{1,0:T(8,128)(2,1)S(1)} %gate.2.refs_0_), channel_id=1, source_target_pairs={{0,1},{1,0},{2,3},{3,2},{4,5},{5,4},{6,7},{7,6},{8,9},{9,8},{10,11... | collective-permute-start | bytes 5308424 | tf_op jit(solution)/shard_map/ppermute | solution.py:625
  39.7 20.6 %collective-permute-start.4 = (bf16[144,2048]{1,0:T(8,128)(2,1)S(1)}, bf16[144,2048]{1,0:T(8,128)(2,1)S(1)}, u32[]{:S(2)}, u32[]{:S(2)}) collective-permute-start(bf16[144,2048]{1,0:T(8,128)(2,1)S(1)} %unpack.1.x_ref), channel_id=1, source_target_pairs={{0,2},{2,0},{4,6},{6,4},{8,10},{10,8},{12,14},{14,12},{16,18},{18,... | collective-permute-start | bytes 1769480 | tf_op jit(solution)/shard_map/ppermute | solution.py:630
  40.4 18.2 %collective-permute-start.1 = (bf16[16,4608]{1,0:T(8,128)(2,1)S(1)}, bf16[16,4608]{1,0:T(8,128)(2,1)S(1)}, u32[]{:S(2)}, u32[]{:S(2)}) collective-permute-start(bf16[16,4608]{1,0:T(8,128)(2,1)S(1)} %get-tuple-element.31.refs_0_), channel_id=1, source_target_pairs={{0,2},{2,0},{4,6},{6,4},{8,10},{10,8},{12,14},{14,12},{16,18},{18,... | collective-permute-start | bytes 442376 | tf_op jit(solution)/shard_map/ppermute | solution.py:620
  58.8 10.8 %collective-permute-start.3 = (bf16[16,4608]{1,0:T(8,128)(2,1)S(1)}, bf16[16,4608]{1,0:T(8,128)(2,1)S(1)}, u32[]{:S(2)}, u32[]{:S(2)}) collective-permute-start(bf16[16,4608]{1,0:T(8,128)(2,1)S(1)} %get-tuple-element.37.refs_0_), channel_id=1, source_target_pairs={{0,4},{2,6},{4,0},{6,2},{8,12},{10,14},{12,8},{14,10},{16,20},{18,... | collective-permute-start | bytes 442376 | tf_op jit(solution)/shard_map/ppermute | solution.py:620
  69.8 3.8 %collective-permute-start.7 = (bf16[144,6144]{1,0:T(8,128)(2,1)S(1)}, bf16[144,6144]{1,0:T(8,128)(2,1)S(1)}, u32[]{:S(2)}, u32[]{:S(2)}) collective-permute-start(bf16[144,6144]{1,0:T(8,128)(2,1)S(1)} %gate.3.refs_0_), channel_id=1, source_target_pairs={{0,1},{1,0},{2,3},{3,2},{4,5},{5,4},{6,7},{7,6},{8,9},{9,8},{10,11... | collective-permute-start | bytes 5308424 | tf_op jit(solution)/shard_map/ppermute | solution.py:625
  69.8 13.0 %collective-permute-start.5 = (bf16[16,4608]{1,0:T(8,128)(2,1)S(1)}, bf16[16,4608]{1,0:T(8,128)(2,1)S(1)}, u32[]{:S(2)}, u32[]{:S(2)}) collective-permute-start(bf16[16,4608]{1,0:T(8,128)(2,1)S(1)} %get-tuple-element.41.refs_0_), channel_id=1, source_target_pairs={{0,8},{2,10},{4,12},{6,14},{8,0},{10,2},{12,4},{14,6},{16,24},{18,... | collective-permute-start | bytes 442376 | tf_op jit(solution)/shard_map/ppermute | solution.py:620
  83.1 15.4 %collective-permute-start.9 = (bf16[144,2048]{1,0:T(8,128)(2,1)S(1)}, bf16[144,2048]{1,0:T(8,128)(2,1)S(1)}, u32[]{:S(2)}, u32[]{:S(2)}) collective-permute-start(bf16[144,2048]{1,0:T(8,128)(2,1)S(1)} %down.2), channel_id=1, source_target_pairs={{0,2},{2,0},{4,6},{6,4},{8,10},{10,8},{12,14},{14,12},{16,18},{18,... | collective-permute-start | bytes 1769480 | tf_op jit(solution)/shard_map/ppermute | solution.py:630
  83.7 9.4 %collective-permute-start.8 = (bf16[16,4608]{1,0:T(8,128)(2,1)S(1)}, bf16[16,4608]{1,0:T(8,128)(2,1)S(1)}, u32[]{:S(2)}, u32[]{:S(2)}) collective-permute-start(bf16[16,4608]{1,0:T(8,128)(2,1)S(1)} %get-tuple-element.46), channel_id=1, source_target_pairs={{0,16},{2,18},{4,20},{6,22},{8,24},{10,26},{12,28},{14,30},{16,0},... | collective-permute-start | bytes 442376 | tf_op jit(solution)/shard_map/ppermute | solution.py:620
  99.8 19.1 %all-to-all-start.1 = ((bf16[8,16,2304]{2,1,0:T(8,128)(2,1)}), bf16[8,16,2304]{2,1,0:T(8,128)(2,1)S(1)}, u32[]{:S(2)}, u32[]{:S(2)}) async-start(bf16[8,16,2304]{2,1,0:T(8,128)(2,1)} %pack_sum.1), calls=%async_computation.1 | async-start | bytes 1179648 | tf_op jit(solution)/shard_map/all_to_all | solution.py:638

commit v10 on v9

--- a/solution.py
+++ b/solution.py
@@ -698,13 +698,11 @@
         rows.append(turned_within(rows[0], copies, d))
     gated = []
     for part in rows:
-        if len(gated) == 1:
-            part = after(part, advance(gated[-1][0]))
-        elif gated:
+        if gated:
             part = after(part, gated[-1][0])
         own = gate(part, w_gate)
-        if len(gated) == copies - 1:
-            own = after(own, advance(own), *(p for parts in gated for p in parts[1:]))
+        if len(gated) in (0, copies - 1):
+            own = after(own, advance(own, *rows[1:]), *(p for parts in gated for p in parts[1:]))
         gated.append([own] + [turned(own, "exp", d) for d in range(1, feature_parts)])
     made = []
     for parts in gated[1:] + gated[:1]:

time: 121 us -> 110 us (0.909)
  waiting for transfers between devices: 35.3 us -> 20.1 us
  starting transfers between devices: 19.6 us -> 23.9 us
    ppermute x4, waiting for transfers between devices: 16.8 us -> 5.12 us  [swapped(): return lax.ppermute(value, 'seq', [(i, i ^ by) for i in range(count)])]
    ppermute x4, starting transfers between devices: 3.04 us -> 6.39 us  [swapped(): return lax.ppermute(value, 'seq', [(i, i ^ by) for i in range(count)])]
    ppermute x2, waiting for transfers between devices: 5.42 us -> 3.29 us  [turned_within(): lax.ppermute(value, 'seq', [(i, i // copies * copies + (i + by) % copies)...]
    ppermute x3, waiting for transfers between devices: 3.6 us -> 2.28 us  [turned(): lax.ppermute(value, axis, [(i, (i + by) % count) for i in range(count)])]
  transfers between devices with their start and end apart: 12 -> 12, of which waited for: 5 -> 5; matrix products, arithmetic and copies ran while one was open for 0% -> 0% of each run, Pallas kernels for 43% -> 55%
where the time goes in v10:
time: 110 us; the launch traced here: 109 us
  Pallas kernels  63.4 us (58%)
  starting transfers between devices  23.9 us (22%)
  waiting for transfers between devices  20.1 us (18%)
    pallas_call x2, Pallas kernels, down(): pl.pallas_call(functools.partial(down_kernel, chunk), in_specs=[INSIDE] *...  18.7 us
    pallas_call x2, Pallas kernels, gate(): pl.pallas_call(functools.partial(gate_kernel, chunk), in_specs=[INSIDE, A...  18.4 us
    pallas_call x1, Pallas kernels, scan(): pl.pallas_call(scan_kernel, grid=(channels // lanes,), in_specs=[cut(toke...  11.5 us
    all_to_all x2, starting transfers between devices, exchanged(): lax.all_to_all(value, 'seq', split_axis=0, concat_axis=0, tiled=True, axi...  11.1 us
    all_to_all x2, waiting for transfers between devices, exchanged(): lax.all_to_all(value, 'seq', split_axis=0, concat_axis=0, tiled=True, axi...  9.37 us
    pallas_call x1, Pallas kernels, finish(): pl.pallas_call(functools.partial(finish_kernel, step), grid=(channels //...  8.27 us
    ppermute x4, starting transfers between devices, swapped(): return lax.ppermute(value, 'seq', [(i, i ^ by) for i in range(count)])  6.39 us
    ppermute x4, waiting for transfers between devices, swapped(): return lax.ppermute(value, 'seq', [(i, i ^ by) for i in range(count)])  5.12 us
  transfers between devices with their start and end apart: 12, of which 5 were waited for; matrix products, arithmetic and copies ran while one was open for 0% of the time, Pallas kernels for 55%

profile of v10, /device:TPU:0, one launch (start us, length us, event | category | flops | bytes accessed | tf_op | source)
XLA Modules:
  0.0 109.0 jit_solution(10851148798430473428)
XLA Ops:
  0.6 0.9 slice.3
  1.5 4.8 %collective-permute-start = (bf16[3,4096]{1,0:T(4,128)(2,1)S(1)}, bf16[3,4096]{1,0:T(4,128)(2,1)S(1)}, u32[]{:S(2)}, u32[]{:S(2)}) collective-permute-start(bf16[3,4096]{1,0:T(4,128)(2,1)S(1)} %slice.3), channel_id=1, source_target_pairs={{0,2},{2,4},{4,6},{6,8},{8,10},{10,12},{12,14},{14,16},{16,18},{18... | collective-permute-start | bytes 73736 | tf_op jit(solution)/shard_map/ppermute | solution.py:673
  6.3 2.4 %route.1 = (bf16[8,1,16,2304]{3,2,1,0:T(8,128)(2,1)}, f32[64,8]{1,0:T(8,128)S(1)}) custom-call(s32[2,64]{1,0:T(2,128)} %bitcast.7, bf16[64,2048]{1,0:T(8,128)(2,1)} %hidden_ref.1, bf16[8,2048]{1,0:T(8,128)(2,1)} %bitcast.6), custom_call_target="tpu_custom_call" | custom-call | flops 67108864 | bytes 1048576 | tf_op jit(solution)/shard_map/route/pallas_call | solution.py:102
  8.8 6.7 %all-to-all-start = ((bf16[8,16,2304]{2,1,0:T(8,128)(2,1)}), bf16[8,16,2304]{2,1,0:T(8,128)(2,1)S(1)}, u32[]{:S(2)}, u32[]{:S(2)}) async-start(bf16[8,16,2304]{2,1,0:T(8,128)(2,1)} %bitcast.5), calls=%async_computation | async-start | bytes 1179648 | tf_op jit(solution)/shard_map/all_to_all | solution.py:638
  15.5 11.5 %scan.1 = (f32[64,4096]{1,0:T(8,128)}, f32[64,4096]{1,0:T(8,128)}, bf16[16,4608]{1,0:T(8,128)(2,1)S(1)}) custom-call(bf16[64,4096]{1,0:T(8,128)(2,1)} %x_ref.1, bf16[3,4096]{1,0:T(4,128)(2,1)S(1)} %collective-permute-done.edge_ref, bf16[64,256]{1,0:T(8,128)(2,1)} %low_ref.1, bf16[256,4096]{1,0:T(8,128)(2,1)} %dtw_ref.1, f32[1,4096]{1,0:T(1,128)} %bitcast.9, ...), custom_call_target="tpu_custom_call" | custom-call | flops 33554432 | bytes 3145728 | tf_op jit(solution)/shard_map/scan/pallas_call | solution.py:461
  27.0 3.3 %all-to-all-done.arrived_ref = bf16[8,16,2304]{2,1,0:T(8,128)(2,1)S(1)} async-done(((bf16[8,16,2304]{2,1,0:T(8,128)(2,1)}), bf16[8,16,2304]{2,1,0:T(8,128)(2,1)S(1)}, u32[]{:S(2)}, u32[]{:S(2)}) %all-to-all-start) | async-done | bytes 589856 | tf_op jit(solution)/shard_map/all_to_all | solution.py:638
  31.0 1.4 %collective-permute-start.1 = (bf16[16,4608]{1,0:T(8,128)(2,1)S(1)}, bf16[16,4608]{1,0:T(8,128)(2,1)S(1)}, u32[]{:S(2)}, u32[]{:S(2)}) collective-permute-start(bf16[16,4608]{1,0:T(8,128)(2,1)S(1)} %get-tuple-element.32.refs_0_), channel_id=1, source_target_pairs={{0,2},{2,0},{4,6},{6,4},{8,10},{10,8},{12,14},{14,12},{16,18},{18,... | collective-permute-start | bytes 442376 | tf_op jit(solution)/shard_map/ppermute | solution.py:620
  32.5 9.2 %gate.2.refs_0_ = bf16[144,6144]{1,0:T(8,128)(2,1)S(1)} custom-call(bf16[144,2048]{1,0:T(8,128)(2,1)S(1)} %unpack.1.x_ref, bf16[2048,6144]{1,0:T(8,128)(2,1)} %w_ref.3), custom_call_target="tpu_custom_call" | custom-call | flops 3623878656 | bytes 25165824 | tf_op jit(solution)/shard_map/gate/pallas_call | solution.py:203
  41.7 5.1 %collective-permute-done.1.refs_1_ = bf16[16,4608]{1,0:T(8,128)(2,1)S(1)} collective-permute-done((bf16[16,4608]{1,0:T(8,128)(2,1)S(1)}, bf16[16,4608]{1,0:T(8,128)(2,1)S(1)}, u32[]{:S(2)}, u32[]{:S(2)}) %collective-permute-start.1) | collective-permute-done | bytes 147488 | tf_op jit(solution)/shard_map/ppermute | solution.py:620
  47.0 1.6 %collective-permute-start.4 = (bf16[16,4608]{1,0:T(8,128)(2,1)S(1)}, bf16[16,4608]{1,0:T(8,128)(2,1)S(1)}, u32[]{:S(2)}, u32[]{:S(2)}) collective-permute-start(bf16[16,4608]{1,0:T(8,128)(2,1)S(1)} %get-tuple-element.38.refs_0_), channel_id=1, source_target_pairs={{0,4},{2,6},{4,0},{6,2},{8,12},{10,14},{12,8},{14,10},{16,20},{18,... | collective-permute-start | bytes 442376 | tf_op jit(solution)/shard_map/ppermute | solution.py:620
  48.6 9.2 %gate.3.refs_0_ = bf16[144,6144]{1,0:T(8,128)(2,1)S(1)} custom-call(bf16[144,2048]{1,0:T(8,128)(2,1)S(1)} %collective-permute-done.3.x_ref, bf16[2048,6144]{1,0:T(8,128)(2,1)} %w_ref.3), custom_call_target="tpu_custom_call" | custom-call | flops 3623878656 | bytes 25165824 | tf_op jit(solution)/shard_map/gate/pallas_call | solution.py:203
  58.3 1.2 %collective-permute-start.5 = (bf16[16,4608]{1,0:T(8,128)(2,1)S(1)}, bf16[16,4608]{1,0:T(8,128)(2,1)S(1)}, u32[]{:S(2)}, u32[]{:S(2)}) collective-permute-start(bf16[16,4608]{1,0:T(8,128)(2,1)S(1)} %get-tuple-element.43.refs_0_), channel_id=1, source_target_pairs={{0,8},{2,10},{4,12},{6,14},{8,0},{10,2},{12,4},{14,6},{16,24},{18,... | collective-permute-start | bytes 442376 | tf_op jit(solution)/shard_map/ppermute | solution.py:620
  59.5 2.3 %collective-permute-done.7.refs_1_ = bf16[144,6144]{1,0:T(8,128)(2,1)S(1)} collective-permute-done((bf16[144,6144]{1,0:T(8,128)(2,1)S(1)}, bf16[144,6144]{1,0:T(8,128)(2,1)S(1)}, u32[]{:S(2)}, u32[]{:S(2)}) %collective-permute-start.7) | collective-permute-done | bytes 1769504 | tf_op jit(solution)/shard_map/ppermute | solution.py:625
  61.8 9.3 %down.2 = bf16[144,2048]{1,0:T(8,128)(2,1)S(1)} custom-call(bf16[144,6144]{1,0:T(8,128)(2,1)S(1)} %gate.3.refs_0_, bf16[144,6144]{1,0:T(8,128)(2,1)S(1)} %collective-permute-done.7.refs_1_, bf16[6144,2048]{1,0:T(8,128)(2,1)} %refs_2_.9), custom_call_target="tpu_custom_call" | custom-call | flops 3623878656 | bytes 25165824 | tf_op jit(solution)/shard_map/down/pallas_call | solution.py:246
  71.3 0.7 collective-permute-start.9
  72.0 2.2 %collective-permute-start.8 = (bf16[16,4608]{1,0:T(8,128)(2,1)S(1)}, bf16[16,4608]{1,0:T(8,128)(2,1)S(1)}, u32[]{:S(2)}, u32[]{:S(2)}) collective-permute-start(bf16[16,4608]{1,0:T(8,128)(2,1)S(1)} %get-tuple-element.48), channel_id=1, source_target_pairs={{0,16},{2,18},{4,20},{6,22},{8,24},{10,26},{12,28},{14,30},{16,0},... | collective-permute-start | bytes 442376 | tf_op jit(solution)/shard_map/ppermute | solution.py:620
  74.2 9.3 %down.3.refs_0_ = f32[144,2048]{1,0:T(8,128)S(1)} custom-call(bf16[144,6144]{1,0:T(8,128)(2,1)S(1)} %gate.2.refs_0_, bf16[144,6144]{1,0:T(8,128)(2,1)S(1)} %collective-permute-done.6.refs_1_, bf16[6144,2048]{1,0:T(8,128)(2,1)} %refs_2_.9), custom_call_target="tpu_custom_call" | custom-call | flops 3623878656 | bytes 25165824 | tf_op jit(solution)/shard_map/down/pallas_call | solution.py:246
  83.5 3.3 %collective-permute-done.9.refs_1_ = bf16[144,2048]{1,0:T(8,128)(2,1)S(1)} collective-permute-done((bf16[144,2048]{1,0:T(8,128)(2,1)S(1)}, bf16[144,2048]{1,0:T(8,128)(2,1)S(1)}, u32[]{:S(2)}, u32[]{:S(2)}) %collective-permute-start.9) | collective-permute-done | bytes 589856 | tf_op jit(solution)/shard_map/ppermute | solution.py:630
  86.8 1.2 %pack_sum.1 = bf16[8,16,2304]{2,1,0:T(8,128)(2,1)} custom-call(f32[144,2048]{1,0:T(8,128)S(1)} %down.3.refs_0_, bf16[144,2048]{1,0:T(8,128)(2,1)S(1)} %collective-permute-done.9.refs_1_), custom_call_target="tpu_custom_call" | custom-call | flops 4718592 | bytes 2359296 | tf_op jit(solution)/shard_map/pack_sum/pallas_call | solution.py:316
  88.1 4.3 %all-to-all-start.1 = ((bf16[8,16,2304]{2,1,0:T(8,128)(2,1)}), bf16[8,16,2304]{2,1,0:T(8,128)(2,1)S(1)}, u32[]{:S(2)}, u32[]{:S(2)}) async-start(bf16[8,16,2304]{2,1,0:T(8,128)(2,1)} %pack_sum.1), calls=%async_computation.1 | async-start | bytes 1179648 | tf_op jit(solution)/shard_map/all_to_all | solution.py:638
  92.4 1.0 blend_weights.1
  93.4 8.3 %finish.1 = bf16[64,4096]{1,0:T(8,128)(2,1)} custom-call(f32[64,4096]{1,0:T(8,128)} %get-tuple-element.30.read_ref, f32[64,4096]{1,0:T(8,128)} %get-tuple-element.31.cum_ref, bf16[64,4096]{1,0:T(8,128)(2,1)} %z_ref.1, bf16[16,4608]{1,0:T(8,128)(2,1)S(1)} %get-tuple-element.47.prefix_ref.sizes_ref, ...), custom_call_target="tpu_custom_call" | custom-call | flops 20971520 | bytes 3145728 | tf_op jit(solution)/shard_map/finish/pallas_call | solution.py:595
  101.7 6.1 %all-to-all-done.1.back_ref = bf16[8,16,2304]{2,1,0:T(8,128)(2,1)S(1)} async-done(((bf16[8,16,2304]{2,1,0:T(8,128)(2,1)}), bf16[8,16,2304]{2,1,0:T(8,128)(2,1)S(1)}, u32[]{:S(2)}, u32[]{:S(2)}) %all-to-all-start.1) | async-done | bytes 589856 | tf_op jit(solution)/shard_map/all_to_all | solution.py:638
  107.8 1.1 %combine.1 = bf16[64,2048]{1,0:T(8,128)(2,1)} custom-call(bf16[8,16,2304]{2,1,0:T(8,128)(2,1)S(1)} %all-to-all-done.1.back_ref, bf16[2,64,128]{2,1,0:T(8,128)(2,1)S(1)} %get-tuple-element.55.main_ref, bf16[2,64,128]{2,1,0:T(8,128)(2,1)S(1)} %get-tuple-element.56.extra_ref, f32[2,64,128]{2,1,0:T(8,128)S(1)} %get-tuple-element.57.gates_ref), custom_call_target="tpu_custom_call" | custom-call | flops 75497472 | bytes 589824 | tf_op jit(solution)/shard_map/combine/pallas_call | solution.py:347
  (17 shorter events, 1.7 us)
Async XLA Ops:
  1.5 7.3 %collective-permute-start = (bf16[3,4096]{1,0:T(4,128)(2,1)S(1)}, bf16[3,4096]{1,0:T(4,128)(2,1)S(1)}, u32[]{:S(2)}, u32[]{:S(2)}) collective-permute-start(bf16[3,4096]{1,0:T(4,128)(2,1)S(1)} %slice.3), channel_id=1, source_target_pairs={{0,2},{2,4},{4,6},{6,8},{8,10},{10,12},{12,14},{14,16},{16,18},{18... | collective-permute-start | bytes 73736 | tf_op jit(solution)/shard_map/ppermute | solution.py:673
  8.8 21.5 %all-to-all-start = ((bf16[8,16,2304]{2,1,0:T(8,128)(2,1)}), bf16[8,16,2304]{2,1,0:T(8,128)(2,1)S(1)}, u32[]{:S(2)}, u32[]{:S(2)}) async-start(bf16[8,16,2304]{2,1,0:T(8,128)(2,1)} %bitcast.5), calls=%async_computation | async-start | bytes 1179648 | tf_op jit(solution)/shard_map/all_to_all | solution.py:638
  15.5 11.5 %collective-permute-start.2 = (f32[64,8]{1,0:T(8,128)S(1)}, f32[64,8]{1,0:T(8,128)S(1)}, u32[]{:S(2)}, u32[]{:S(2)}) collective-permute-start(f32[64,8]{1,0:T(8,128)S(1)} %get-tuple-element.53.refs_0_), channel_id=1, source_target_pairs={{0,1},{1,0},{2,3},{3,2},{4,5},{5,4},{6,7},{7,6},{8,9},{9,8},{10,11... | collective-permute-start | bytes 6152 | tf_op jit(solution)/shard_map/ppermute | solution.py:625
  30.4 16.4 %copy-start = (f32[16,4096]{1,0:T(8,128)S(1)}, f32[16,4096]{1,0:T(8,128)}, u32[]{:S(2)}) copy-start(f32[16,4096]{1,0:T(8,128)} %alog_ref.3) | copy-start | bytes 786436
  30.4 16.4 %collective-permute-start.3 = (bf16[144,2048]{1,0:T(8,128)(2,1)S(1)}, bf16[144,2048]{1,0:T(8,128)(2,1)S(1)}, u32[]{:S(2)}, u32[]{:S(2)}) collective-permute-start(bf16[144,2048]{1,0:T(8,128)(2,1)S(1)} %unpack.1.x_ref), channel_id=1, source_target_pairs={{0,2},{2,0},{4,6},{6,4},{8,10},{10,8},{12,14},{14,12},{16,18},{18,... | collective-permute-start | bytes 1769480 | tf_op jit(solution)/shard_map/ppermute | solution.py:630
  31.0 15.8 %collective-permute-start.1 = (bf16[16,4608]{1,0:T(8,128)(2,1)S(1)}, bf16[16,4608]{1,0:T(8,128)(2,1)S(1)}, u32[]{:S(2)}, u32[]{:S(2)}) collective-permute-start(bf16[16,4608]{1,0:T(8,128)(2,1)S(1)} %get-tuple-element.32.refs_0_), channel_id=1, source_target_pairs={{0,2},{2,0},{4,6},{6,4},{8,10},{10,8},{12,14},{14,12},{16,18},{18,... | collective-permute-start | bytes 442376 | tf_op jit(solution)/shard_map/ppermute | solution.py:620
  47.0 11.1 %collective-permute-start.6 = (bf16[144,6144]{1,0:T(8,128)(2,1)S(1)}, bf16[144,6144]{1,0:T(8,128)(2,1)S(1)}, u32[]{:S(2)}, u32[]{:S(2)}) collective-permute-start(bf16[144,6144]{1,0:T(8,128)(2,1)S(1)} %gate.2.refs_0_), channel_id=1, source_target_pairs={{0,1},{1,0},{2,3},{3,2},{4,5},{5,4},{6,7},{7,6},{8,9},{9,8},{10,11... | collective-permute-start | bytes 5308424 | tf_op jit(solution)/shard_map/ppermute | solution.py:625
  47.0 10.8 %collective-permute-start.4 = (bf16[16,4608]{1,0:T(8,128)(2,1)S(1)}, bf16[16,4608]{1,0:T(8,128)(2,1)S(1)}, u32[]{:S(2)}, u32[]{:S(2)}) collective-permute-start(bf16[16,4608]{1,0:T(8,128)(2,1)S(1)} %get-tuple-element.38.refs_0_), channel_id=1, source_target_pairs={{0,4},{2,6},{4,0},{6,2},{8,12},{10,14},{12,8},{14,10},{16,20},{18,... | collective-permute-start | bytes 442376 | tf_op jit(solution)/shard_map/ppermute | solution.py:620
  58.0 3.8 %collective-permute-start.7 = (bf16[144,6144]{1,0:T(8,128)(2,1)S(1)}, bf16[144,6144]{1,0:T(8,128)(2,1)S(1)}, u32[]{:S(2)}, u32[]{:S(2)}) collective-permute-start(bf16[144,6144]{1,0:T(8,128)(2,1)S(1)} %gate.3.refs_0_), channel_id=1, source_target_pairs={{0,1},{1,0},{2,3},{3,2},{4,5},{5,4},{6,7},{7,6},{8,9},{9,8},{10,11... | collective-permute-start | bytes 5308424 | tf_op jit(solution)/shard_map/ppermute | solution.py:625
  58.3 12.9 %collective-permute-start.5 = (bf16[16,4608]{1,0:T(8,128)(2,1)S(1)}, bf16[16,4608]{1,0:T(8,128)(2,1)S(1)}, u32[]{:S(2)}, u32[]{:S(2)}) collective-permute-start(bf16[16,4608]{1,0:T(8,128)(2,1)S(1)} %get-tuple-element.43.refs_0_), channel_id=1, source_target_pairs={{0,8},{2,10},{4,12},{6,14},{8,0},{10,2},{12,4},{14,6},{16,24},{18,... | collective-permute-start | bytes 442376 | tf_op jit(solution)/shard_map/ppermute | solution.py:620
  71.3 15.5 %collective-permute-start.9 = (bf16[144,2048]{1,0:T(8,128)(2,1)S(1)}, bf16[144,2048]{1,0:T(8,128)(2,1)S(1)}, u32[]{:S(2)}, u32[]{:S(2)}) collective-permute-start(bf16[144,2048]{1,0:T(8,128)(2,1)S(1)} %down.2), channel_id=1, source_target_pairs={{0,2},{2,0},{4,6},{6,4},{8,10},{10,8},{12,14},{14,12},{16,18},{18,... | collective-permute-start | bytes 1769480 | tf_op jit(solution)/shard_map/ppermute | solution.py:630
  72.0 11.5 %collective-permute-start.8 = (bf16[16,4608]{1,0:T(8,128)(2,1)S(1)}, bf16[16,4608]{1,0:T(8,128)(2,1)S(1)}, u32[]{:S(2)}, u32[]{:S(2)}) collective-permute-start(bf16[16,4608]{1,0:T(8,128)(2,1)S(1)} %get-tuple-element.48), channel_id=1, source_target_pairs={{0,16},{2,18},{4,20},{6,22},{8,24},{10,26},{12,28},{14,30},{16,0},... | collective-permute-start | bytes 442376 | tf_op jit(solution)/shard_map/ppermute | solution.py:620
  88.1 19.8 %all-to-all-start.1 = ((bf16[8,16,2304]{2,1,0:T(8,128)(2,1)}), bf16[8,16,2304]{2,1,0:T(8,128)(2,1)S(1)}, u32[]{:S(2)}, u32[]{:S(2)}) async-start(bf16[8,16,2304]{2,1,0:T(8,128)(2,1)} %pack_sum.1), calls=%async_computation.1 | async-start | bytes 1179648 | tf_op jit(solution)/shard_map/all_to_all | solution.py:638

commit v11 on v10

--- a/solution.py
+++ b/solution.py
@@ -682,8 +682,7 @@
     arrived = after(arrived, ends, *logits)
 
     steps = blocks.bit_length() - 1
-    total, prefix, received = ends, None, swapped(ends, 1)
-    step = 0
+    total, prefix, received, step = ends, None, None, 0
 
     def advance(*marks):
         nonlocal total, prefix, received, step
@@ -701,8 +700,11 @@
         if gated:
             part = after(part, gated[-1][0])
         own = gate(part, w_gate)
-        if len(gated) in (0, copies - 1):
-            own = after(own, advance(own, *rows[1:]), *(p for parts in gated for p in parts[1:]))
+        if not gated:
+            own, received = after((own, ends), *rows[1:])
+            received = swapped(received, 1)
+        if len(gated) == copies - 1:
+            own = after(own, advance(own), *(p for parts in gated for p in parts[1:]))
         gated.append([own] + [turned(own, "exp", d) for d in range(1, feature_parts)])
     made = []
     for parts in gated[1:] + gated[:1]:
@@ -710,12 +712,13 @@
         if not made:
             product = after(product, advance(product))
         made.append(product)
+    advance(made[-1])
     while step < steps - 1:
         advance()
-    sums = [after(made[-1], received)]
+    sums = made[-1:]
     for d in range(1, copies):
         sums.append(turned_within(made[d - 1], copies, -d))
-    packed = pack_sum(sums, experts, pack)
+    packed = after(pack_sum(sums, experts, pack), received)
     back = exchanged(packed, copies)
 
     weights = blend_weights(ids, after(tuple(logits), packed), 1, pack)

time: 110 us -> 110 us (level)
  transfers between devices with their start and end apart: 12 -> 12, of which waited for: 5 -> 6; matrix products, arithmetic and copies ran while one was open for 0% -> 0% of each run, Pallas kernels for 55% -> 56%
where the time goes in v11:
time: 110 us
  Pallas kernels  63.4 us (58%)
  starting transfers between devices  24.3 us (22%)
  waiting for transfers between devices  20.4 us (19%)
    pallas_call x2, Pallas kernels, down(): pl.pallas_call(functools.partial(down_kernel, chunk), in_specs=[INSIDE] *...  18.7 us
    pallas_call x2, Pallas kernels, gate(): pl.pallas_call(functools.partial(gate_kernel, chunk), in_specs=[INSIDE, A...  18.4 us
    pallas_call x1, Pallas kernels, scan(): pl.pallas_call(scan_kernel, grid=(channels // lanes,), in_specs=[cut(toke...  11.5 us
    all_to_all x2, starting transfers between devices, exchanged(): lax.all_to_all(value, 'seq', split_axis=0, concat_axis=0, tiled=True, axi...  11.3 us
    all_to_all x2, waiting for transfers between devices, exchanged(): lax.all_to_all(value, 'seq', split_axis=0, concat_axis=0, tiled=True, axi...  9.12 us
    pallas_call x1, Pallas kernels, finish(): pl.pallas_call(functools.partial(finish_kernel, step), grid=(channels //...  8.27 us
    ppermute x4, starting transfers between devices, swapped(): return lax.ppermute(value, 'seq', [(i, i ^ by) for i in range(count)])  5.79 us
    ppermute x4, waiting for transfers between devices, swapped(): return lax.ppermute(value, 'seq', [(i, i ^ by) for i in range(count)])  5.13 us
  transfers between devices with their start and end apart: 12, of which 6 were waited for; matrix products, arithmetic and copies ran while one was open for 0% of the time, Pallas kernels for 56%

profile of v11, /device:TPU:0, one launch (start us, length us, event | category | flops | bytes accessed | tf_op | source)
XLA Modules:
  0.0 109.7 jit_solution(8057340829891005486)
XLA Ops:
  0.6 0.9 slice.3
  1.5 4.8 %collective-permute-start = (bf16[3,4096]{1,0:T(4,128)(2,1)S(1)}, bf16[3,4096]{1,0:T(4,128)(2,1)S(1)}, u32[]{:S(2)}, u32[]{:S(2)}) collective-permute-start(bf16[3,4096]{1,0:T(4,128)(2,1)S(1)} %slice.3), channel_id=1, source_target_pairs={{0,2},{2,4},{4,6},{6,8},{8,10},{10,12},{12,14},{14,16},{16,18},{18... | collective-permute-start | bytes 73736 | tf_op jit(solution)/shard_map/ppermute | solution.py:673
  6.3 2.4 %route.1 = (bf16[8,1,16,2304]{3,2,1,0:T(8,128)(2,1)}, f32[64,8]{1,0:T(8,128)S(1)}) custom-call(s32[2,64]{1,0:T(2,128)} %bitcast.7, bf16[64,2048]{1,0:T(8,128)(2,1)} %hidden_ref.1, bf16[8,2048]{1,0:T(8,128)(2,1)} %bitcast.6), custom_call_target="tpu_custom_call" | custom-call | flops 67108864 | bytes 1048576 | tf_op jit(solution)/shard_map/route/pallas_call | solution.py:102
  8.8 6.7 %all-to-all-start = ((bf16[8,16,2304]{2,1,0:T(8,128)(2,1)}), bf16[8,16,2304]{2,1,0:T(8,128)(2,1)S(1)}, u32[]{:S(2)}, u32[]{:S(2)}) async-start(bf16[8,16,2304]{2,1,0:T(8,128)(2,1)} %bitcast.5), calls=%async_computation | async-start | bytes 1179648 | tf_op jit(solution)/shard_map/all_to_all | solution.py:638
  15.5 11.5 %scan.1 = (f32[64,4096]{1,0:T(8,128)}, f32[64,4096]{1,0:T(8,128)}, bf16[16,4608]{1,0:T(8,128)(2,1)S(1)}) custom-call(bf16[64,4096]{1,0:T(8,128)(2,1)} %x_ref.1, bf16[3,4096]{1,0:T(4,128)(2,1)S(1)} %collective-permute-done.edge_ref, bf16[64,256]{1,0:T(8,128)(2,1)} %low_ref.1, bf16[256,4096]{1,0:T(8,128)(2,1)} %dtw_ref.1, f32[1,4096]{1,0:T(1,128)} %bitcast.9, ...), custom_call_target="tpu_custom_call" | custom-call | flops 33554432 | bytes 3145728 | tf_op jit(solution)/shard_map/scan/pallas_call | solution.py:461
  27.0 3.3 %all-to-all-done.arrived_ref = bf16[8,16,2304]{2,1,0:T(8,128)(2,1)S(1)} async-done(((bf16[8,16,2304]{2,1,0:T(8,128)(2,1)}), bf16[8,16,2304]{2,1,0:T(8,128)(2,1)S(1)}, u32[]{:S(2)}, u32[]{:S(2)}) %all-to-all-start) | async-done | bytes 589856 | tf_op jit(solution)/shard_map/all_to_all | solution.py:638
  31.0 9.2 %gate.2.refs_0_ = bf16[144,6144]{1,0:T(8,128)(2,1)S(1)} custom-call(bf16[144,2048]{1,0:T(8,128)(2,1)S(1)} %unpack.1.x_ref, bf16[2048,6144]{1,0:T(8,128)(2,1)} %w_ref.3), custom_call_target="tpu_custom_call" | custom-call | flops 3623878656 | bytes 25165824 | tf_op jit(solution)/shard_map/gate/pallas_call | solution.py:203
  40.3 3.4 %collective-permute-done.2.x_ref = bf16[144,2048]{1,0:T(8,128)(2,1)S(1)} collective-permute-done((bf16[144,2048]{1,0:T(8,128)(2,1)S(1)}, bf16[144,2048]{1,0:T(8,128)(2,1)S(1)}, u32[]{:S(2)}, u32[]{:S(2)}) %collective-permute-start.2) | collective-permute-done | bytes 589856 | tf_op jit(solution)/shard_map/ppermute | solution.py:630
  44.2 9.2 %gate.3.refs_0_ = bf16[144,6144]{1,0:T(8,128)(2,1)S(1)} custom-call(bf16[144,2048]{1,0:T(8,128)(2,1)S(1)} %collective-permute-done.2.x_ref, bf16[2048,6144]{1,0:T(8,128)(2,1)} %w_ref.3), custom_call_target="tpu_custom_call" | custom-call | flops 3623878656 | bytes 25165824 | tf_op jit(solution)/shard_map/gate/pallas_call | solution.py:203
  53.9 1.5 %collective-permute-start.4 = (bf16[16,4608]{1,0:T(8,128)(2,1)S(1)}, bf16[16,4608]{1,0:T(8,128)(2,1)S(1)}, u32[]{:S(2)}, u32[]{:S(2)}) collective-permute-start(bf16[16,4608]{1,0:T(8,128)(2,1)S(1)} %get-tuple-element.42.refs_0_), channel_id=1, source_target_pairs={{0,4},{2,6},{4,0},{6,2},{8,12},{10,14},{12,8},{14,10},{16,20},{18,... | collective-permute-start | bytes 442376 | tf_op jit(solution)/shard_map/ppermute | solution.py:620
  55.4 2.0 %collective-permute-done.6.refs_1_ = bf16[144,6144]{1,0:T(8,128)(2,1)S(1)} collective-permute-done((bf16[144,6144]{1,0:T(8,128)(2,1)S(1)}, bf16[144,6144]{1,0:T(8,128)(2,1)S(1)}, u32[]{:S(2)}, u32[]{:S(2)}) %collective-permute-start.6) | collective-permute-done | bytes 1769504 | tf_op jit(solution)/shard_map/ppermute | solution.py:625
  57.4 9.3 %down.2 = bf16[144,2048]{1,0:T(8,128)(2,1)S(1)} custom-call(bf16[144,6144]{1,0:T(8,128)(2,1)S(1)} %gate.3.refs_0_, bf16[144,6144]{1,0:T(8,128)(2,1)S(1)} %collective-permute-done.6.refs_1_, bf16[6144,2048]{1,0:T(8,128)(2,1)} %refs_2_.8), custom_call_target="tpu_custom_call" | custom-call | flops 3623878656 | bytes 25165824 | tf_op jit(solution)/shard_map/down/pallas_call | solution.py:246
  67.0 1.5 %collective-permute-start.9 = (bf16[144,2048]{1,0:T(8,128)(2,1)S(1)}, bf16[144,2048]{1,0:T(8,128)(2,1)S(1)}, u32[]{:S(2)}, u32[]{:S(2)}) collective-permute-start(bf16[144,2048]{1,0:T(8,128)(2,1)S(1)} %down.2), channel_id=1, source_target_pairs={{0,2},{2,0},{4,6},{6,4},{8,10},{10,8},{12,14},{14,12},{16,18},{18,... | collective-permute-start | bytes 1769480 | tf_op jit(solution)/shard_map/ppermute | solution.py:630
  68.4 1.3 %collective-permute-start.7 = (bf16[16,4608]{1,0:T(8,128)(2,1)S(1)}, bf16[16,4608]{1,0:T(8,128)(2,1)S(1)}, u32[]{:S(2)}, u32[]{:S(2)}) collective-permute-start(bf16[16,4608]{1,0:T(8,128)(2,1)S(1)} %get-tuple-element.46.refs_0_), channel_id=1, source_target_pairs={{0,8},{2,10},{4,12},{6,14},{8,0},{10,2},{12,4},{14,6},{16,24},{18,... | collective-permute-start | bytes 442376 | tf_op jit(solution)/shard_map/ppermute | solution.py:620
  69.7 9.3 %down.3.refs_0_ = f32[144,2048]{1,0:T(8,128)S(1)} custom-call(bf16[144,6144]{1,0:T(8,128)(2,1)S(1)} %gate.2.refs_0_, bf16[144,6144]{1,0:T(8,128)(2,1)S(1)} %collective-permute-done.5.refs_1_, bf16[6144,2048]{1,0:T(8,128)(2,1)} %refs_2_.8), custom_call_target="tpu_custom_call" | custom-call | flops 3623878656 | bytes 25165824 | tf_op jit(solution)/shard_map/down/pallas_call | solution.py:246
  79.3 2.4 %collective-permute-start.8 = (bf16[16,4608]{1,0:T(8,128)(2,1)S(1)}, bf16[16,4608]{1,0:T(8,128)(2,1)S(1)}, u32[]{:S(2)}, u32[]{:S(2)}) collective-permute-start(bf16[16,4608]{1,0:T(8,128)(2,1)S(1)} %get-tuple-element.50), channel_id=1, source_target_pairs={{0,16},{2,18},{4,20},{6,22},{8,24},{10,26},{12,28},{14,30},{16,0},... | collective-permute-start | bytes 442376 | tf_op jit(solution)/shard_map/ppermute | solution.py:620
  81.7 0.8 collective-permute-done.9.refs_1_
  82.5 1.2 %pack_sum.1 = bf16[8,16,2304]{2,1,0:T(8,128)(2,1)} custom-call(f32[144,2048]{1,0:T(8,128)S(1)} %down.3.refs_0_, bf16[144,2048]{1,0:T(8,128)(2,1)S(1)} %collective-permute-done.9.refs_1_), custom_call_target="tpu_custom_call" | custom-call | flops 4718592 | bytes 2359296 | tf_op jit(solution)/shard_map/pack_sum/pallas_call | solution.py:316
  83.7 5.1 %collective-permute-done.8.received_ref = bf16[16,4608]{1,0:T(8,128)(2,1)S(1)} collective-permute-done((bf16[16,4608]{1,0:T(8,128)(2,1)S(1)}, bf16[16,4608]{1,0:T(8,128)(2,1)S(1)}, u32[]{:S(2)}, u32[]{:S(2)}) %collective-permute-start.8) | collective-permute-done | bytes 147488 | tf_op jit(solution)/shard_map/ppermute | solution.py:620
  88.8 4.5 %all-to-all-start.1 = ((bf16[8,16,2304]{2,1,0:T(8,128)(2,1)}), bf16[8,16,2304]{2,1,0:T(8,128)(2,1)S(1)}, u32[]{:S(2)}, u32[]{:S(2)}) async-start(bf16[8,16,2304]{2,1,0:T(8,128)(2,1)} %pack_sum.1), calls=%async_computation.1 | async-start | bytes 1179648 | tf_op jit(solution)/shard_map/all_to_all | solution.py:638
  93.4 1.0 blend_weights.1
  94.4 8.3 %finish.1 = bf16[64,4096]{1,0:T(8,128)(2,1)} custom-call(f32[64,4096]{1,0:T(8,128)} %get-tuple-element.31.read_ref, f32[64,4096]{1,0:T(8,128)} %get-tuple-element.32.cum_ref, bf16[64,4096]{1,0:T(8,128)(2,1)} %z_ref.1, bf16[16,4608]{1,0:T(8,128)(2,1)S(1)} %get-tuple-element.49.prefix_ref.sizes_ref, ...), custom_call_target="tpu_custom_call" | custom-call | flops 20971520 | bytes 3145728 | tf_op jit(solution)/shard_map/finish/pallas_call | solution.py:595
  102.7 5.9 %all-to-all-done.1.back_ref = bf16[8,16,2304]{2,1,0:T(8,128)(2,1)S(1)} async-done(((bf16[8,16,2304]{2,1,0:T(8,128)(2,1)}), bf16[8,16,2304]{2,1,0:T(8,128)(2,1)S(1)}, u32[]{:S(2)}, u32[]{:S(2)}) %all-to-all-start.1) | async-done | bytes 589856 | tf_op jit(solution)/shard_map/all_to_all | solution.py:638
  108.6 1.1 %combine.1 = bf16[64,2048]{1,0:T(8,128)(2,1)} custom-call(bf16[8,16,2304]{2,1,0:T(8,128)(2,1)S(1)} %all-to-all-done.1.back_ref, bf16[2,64,128]{2,1,0:T(8,128)(2,1)S(1)} %get-tuple-element.57.main_ref, bf16[2,64,128]{2,1,0:T(8,128)(2,1)S(1)} %get-tuple-element.58.extra_ref, f32[2,64,128]{2,1,0:T(8,128)S(1)} %get-tuple-element.59.gates_ref), custom_call_target="tpu_custom_call" | custom-call | flops 75497472 | bytes 589824 | tf_op jit(solution)/shard_map/combine/pallas_call | solution.py:347
  (17 shorter events, 2.2 us)
Async XLA Ops:
  1.5 7.3 %collective-permute-start = (bf16[3,4096]{1,0:T(4,128)(2,1)S(1)}, bf16[3,4096]{1,0:T(4,128)(2,1)S(1)}, u32[]{:S(2)}, u32[]{:S(2)}) collective-permute-start(bf16[3,4096]{1,0:T(4,128)(2,1)S(1)} %slice.3), channel_id=1, source_target_pairs={{0,2},{2,4},{4,6},{6,8},{8,10},{10,12},{12,14},{14,16},{16,18},{18... | collective-permute-start | bytes 73736 | tf_op jit(solution)/shard_map/ppermute | solution.py:673
  8.8 21.5 %all-to-all-start = ((bf16[8,16,2304]{2,1,0:T(8,128)(2,1)}), bf16[8,16,2304]{2,1,0:T(8,128)(2,1)S(1)}, u32[]{:S(2)}, u32[]{:S(2)}) async-start(bf16[8,16,2304]{2,1,0:T(8,128)(2,1)} %bitcast.5), calls=%async_computation | async-start | bytes 1179648 | tf_op jit(solution)/shard_map/all_to_all | solution.py:638
  15.5 11.5 %collective-permute-start.1 = (f32[64,8]{1,0:T(8,128)S(1)}, f32[64,8]{1,0:T(8,128)S(1)}, u32[]{:S(2)}, u32[]{:S(2)}) collective-permute-start(f32[64,8]{1,0:T(8,128)S(1)} %get-tuple-element.55.refs_0_), channel_id=1, source_target_pairs={{0,1},{1,0},{2,3},{3,2},{4,5},{5,4},{6,7},{7,6},{8,9},{9,8},{10,11... | collective-permute-start | bytes 6152 | tf_op jit(solution)/shard_map/ppermute | solution.py:625
  30.4 13.2 %collective-permute-start.2 = (bf16[144,2048]{1,0:T(8,128)(2,1)S(1)}, bf16[144,2048]{1,0:T(8,128)(2,1)S(1)}, u32[]{:S(2)}, u32[]{:S(2)}) collective-permute-start(bf16[144,2048]{1,0:T(8,128)(2,1)S(1)} %unpack.1.x_ref), channel_id=1, source_target_pairs={{0,2},{2,0},{4,6},{6,4},{8,10},{10,8},{12,14},{14,12},{16,18},{18,... | collective-permute-start | bytes 1769480 | tf_op jit(solution)/shard_map/ppermute | solution.py:630
  40.2 13.2 %copy-start = (f32[16,4096]{1,0:T(8,128)S(1)}, f32[16,4096]{1,0:T(8,128)}, u32[]{:S(2)}) copy-start(f32[16,4096]{1,0:T(8,128)} %alog_ref.3) | copy-start | bytes 786436
  43.6 10.0 %collective-permute-start.5 = (bf16[144,6144]{1,0:T(8,128)(2,1)S(1)}, bf16[144,6144]{1,0:T(8,128)(2,1)S(1)}, u32[]{:S(2)}, u32[]{:S(2)}) collective-permute-start(bf16[144,6144]{1,0:T(8,128)(2,1)S(1)} %gate.2.refs_0_), channel_id=1, source_target_pairs={{0,1},{1,0},{2,3},{3,2},{4,5},{5,4},{6,7},{7,6},{8,9},{9,8},{10,11... | collective-permute-start | bytes 5308424 | tf_op jit(solution)/shard_map/ppermute | solution.py:625
  43.6 9.8 %collective-permute-start.3 = (bf16[16,4608]{1,0:T(8,128)(2,1)S(1)}, bf16[16,4608]{1,0:T(8,128)(2,1)S(1)}, u32[]{:S(2)}, u32[]{:S(2)}) collective-permute-start(bf16[16,4608]{1,0:T(8,128)(2,1)S(1)} %get-tuple-element.38.refs_0_), channel_id=1, source_target_pairs={{0,2},{2,0},{4,6},{6,4},{8,10},{10,8},{12,14},{14,12},{16,18},{18,... | collective-permute-start | bytes 442376 | tf_op jit(solution)/shard_map/ppermute | solution.py:620
  53.6 3.8 %collective-permute-start.6 = (bf16[144,6144]{1,0:T(8,128)(2,1)S(1)}, bf16[144,6144]{1,0:T(8,128)(2,1)S(1)}, u32[]{:S(2)}, u32[]{:S(2)}) collective-permute-start(bf16[144,6144]{1,0:T(8,128)(2,1)S(1)} %gate.3.refs_0_), channel_id=1, source_target_pairs={{0,1},{1,0},{2,3},{3,2},{4,5},{5,4},{6,7},{7,6},{8,9},{9,8},{10,11... | collective-permute-start | bytes 5308424 | tf_op jit(solution)/shard_map/ppermute | solution.py:625
  53.9 12.8 %collective-permute-start.4 = (bf16[16,4608]{1,0:T(8,128)(2,1)S(1)}, bf16[16,4608]{1,0:T(8,128)(2,1)S(1)}, u32[]{:S(2)}, u32[]{:S(2)}) collective-permute-start(bf16[16,4608]{1,0:T(8,128)(2,1)S(1)} %get-tuple-element.42.refs_0_), channel_id=1, source_target_pairs={{0,4},{2,6},{4,0},{6,2},{8,12},{10,14},{12,8},{14,10},{16,20},{18,... | collective-permute-start | bytes 442376 | tf_op jit(solution)/shard_map/ppermute | solution.py:620
  67.0 15.5 %collective-permute-start.9 = (bf16[144,2048]{1,0:T(8,128)(2,1)S(1)}, bf16[144,2048]{1,0:T(8,128)(2,1)S(1)}, u32[]{:S(2)}, u32[]{:S(2)}) collective-permute-start(bf16[144,2048]{1,0:T(8,128)(2,1)S(1)} %down.2), channel_id=1, source_target_pairs={{0,2},{2,0},{4,6},{6,4},{8,10},{10,8},{12,14},{14,12},{16,18},{18,... | collective-permute-start | bytes 1769480 | tf_op jit(solution)/shard_map/ppermute | solution.py:630
  68.4 10.6 %collective-permute-start.7 = (bf16[16,4608]{1,0:T(8,128)(2,1)S(1)}, bf16[16,4608]{1,0:T(8,128)(2,1)S(1)}, u32[]{:S(2)}, u32[]{:S(2)}) collective-permute-start(bf16[16,4608]{1,0:T(8,128)(2,1)S(1)} %get-tuple-element.46.refs_0_), channel_id=1, source_target_pairs={{0,8},{2,10},{4,12},{6,14},{8,0},{10,2},{12,4},{14,6},{16,24},{18,... | collective-permute-start | bytes 442376 | tf_op jit(solution)/shard_map/ppermute | solution.py:620
  79.3 9.6 %collective-permute-start.8 = (bf16[16,4608]{1,0:T(8,128)(2,1)S(1)}, bf16[16,4608]{1,0:T(8,128)(2,1)S(1)}, u32[]{:S(2)}, u32[]{:S(2)}) collective-permute-start(bf16[16,4608]{1,0:T(8,128)(2,1)S(1)} %get-tuple-element.50), channel_id=1, source_target_pairs={{0,16},{2,18},{4,20},{6,22},{8,24},{10,26},{12,28},{14,30},{16,0},... | collective-permute-start | bytes 442376 | tf_op jit(solution)/shard_map/ppermute | solution.py:620
  88.8 19.7 %all-to-all-start.1 = ((bf16[8,16,2304]{2,1,0:T(8,128)(2,1)}), bf16[8,16,2304]{2,1,0:T(8,128)(2,1)S(1)}, u32[]{:S(2)}, u32[]{:S(2)}) async-start(bf16[8,16,2304]{2,1,0:T(8,128)(2,1)} %pack_sum.1), calls=%async_computation.1 | async-start | bytes 1179648 | tf_op jit(solution)/shard_map/all_to_all | solution.py:638

commit v12 on v11

--- a/solution.py
+++ b/solution.py
@@ -552,22 +552,38 @@
 
 
 def finish_kernel(
-    step, read_ref, cum_ref, z_ref, prefix_ref, sizes_ref, received_ref, alog_ref, bc_ref,
-    out_ref, sum_ref, wide_ref, c_ref,
+    step, read_ref, cum_ref, z_ref, alog_ref, bc_ref, prefix_ref, *refs
 ):
+    others, sizes, (out_ref, sum_ref, wide_ref, c_ref) = refs[:3], refs[3:7], refs[7:]
     tokens, lanes = z_ref.shape
+    states = alog_ref.shape[0]
     at, steps = pl.program_id(0), pl.num_programs(0)
 
     @pl.when(at == 0)
     def _():
         spread_states(bc_ref[1], c_ref)
-        wide_ref[...] = sizes_ref[...].astype(F32)
+        for i, ref in enumerate(sizes):
+            wide_ref[i * states : (i + 1) * states] = ref[...].astype(F32)
 
     rates = -jnp.exp(alog_ref[...]) * LOG2E
-    entering = prefix_ref[...].astype(F32)
-    size = wide_ref[pl.ds(at, 1)] + wide_ref[pl.ds(steps + at, 1)]
-    further = entering + jnp.exp2(rates * size) * received_ref[...].astype(F32)
-    entering = jnp.where(upper_half(step), further, entering)
+
+    def decay(i):
+        row = i * states + at
+        return jnp.exp2(rates * (wide_ref[pl.ds(row, 1)] + wide_ref[pl.ds(row + steps, 1)]))
+
+    mine = lax.axis_index("seq") >> step
+    ends = [ref[...].astype(F32) for ref in others]
+    decays = [decay(i + 1) for i in range(3)]
+    entering = jnp.zeros((states, lanes), F32)
+    for group in range(3):
+        partner = mine ^ group
+
+        def chosen(values):
+            return jnp.where(partner == 1, values[0], jnp.where(partner == 2, values[1], values[2]))
+
+        further = chosen(decays) * entering + chosen(ends)
+        entering = jnp.where(group < mine, further, entering)
+    entering = prefix_ref[...].astype(F32) + decay(0) * entering
 
     def eight(g, carry):
         at = pl.multiple_of(g * 8, 8)
@@ -584,27 +600,29 @@
     out_ref[...] = ((read_ref[...] + sum_ref[...]) * (z * jax.nn.sigmoid(z))).astype(BF16)
 
 
-def finish(step, read, cum, z_gate, prefix, received, a_log, b_and_c):
+def finish(step, read, cum, z_gate, prefix, others, a_log, b_and_c):
     tokens, channels = z_gate.shape
     states = a_log.shape[0]
-    lanes = math.gcd(512, channels)
+    lanes = prefix.shape[1] - channels
 
     def cut(rows):
         return pl.BlockSpec((rows, lanes), lambda i: (0, i))
 
+    sizes = pl.BlockSpec((states, lanes), lambda i: (0, channels // lanes))
     return pl.pallas_call(
         functools.partial(finish_kernel, step),
         grid=(channels // lanes,),
         in_specs=[
             cut(tokens), cut(tokens), cut(tokens), cut(states),
-            pl.BlockSpec((states, lanes), lambda i: (0, channels // lanes)), cut(states), cut(states),
             pl.BlockSpec(b_and_c.shape, lambda i: (0, 0, 0)),
+            *[cut(states)] * 4,
+            *[sizes] * 4,
         ],
         out_specs=cut(tokens),
         out_shape=jax.ShapeDtypeStruct((tokens, channels), BF16),
         scratch_shapes=[
             pltpu.VMEM((tokens, lanes), F32),
-            pltpu.VMEM((states, lanes), F32),
+            pltpu.VMEM((4 * states, lanes), F32),
             pltpu.VMEM((tokens, states, 128), F32),
         ],
         compiler_params=params(40),
@@ -612,7 +630,7 @@
             tokens * channels * states * 5, tokens * channels * 12, tokens * channels * states
         ),
         name="finish",
-    )(*in_hbm(read, cum, z_gate), prefix, prefix, received, *in_hbm(a_log, b_and_c))
+    )(*in_hbm(read, cum, z_gate, a_log, b_and_c), *[prefix, *others] * 2)
 
 
 def swapped(value, by):
@@ -681,15 +699,18 @@
     logits = [logits] + [turned(logits, "exp", d) for d in range(1, feature_parts)]
     arrived = after(arrived, ends, *logits)
 
-    steps = blocks.bit_length() - 1
+    steps = blocks.bit_length() - 3
     total, prefix, received, step = ends, None, None, 0
 
     def advance(*marks):
         nonlocal total, prefix, received, step
-        if step < steps - 1:
+        if step < steps:
             total, prefix = link(step, total, after(received, *marks), a_log, prefix)
             step += 1
-            received = swapped(total, 1 << step)
+            if step < steps:
+                received = swapped(total, 1 << step)
+            else:
+                received = [swapped(total, q << step) for q in (1, 2, 3)]
         return prefix
 
     rows = [unpack(arrived, features, pack)]
@@ -712,17 +733,16 @@
         if not made:
             product = after(product, advance(product))
         made.append(product)
-    advance(made[-1])
-    while step < steps - 1:
+    while step < steps:
         advance()
     sums = made[-1:]
     for d in range(1, copies):
         sums.append(turned_within(made[d - 1], copies, -d))
-    packed = after(pack_sum(sums, experts, pack), received)
+    packed = after(pack_sum(sums, experts, pack), *received)
     back = exchanged(packed, copies)
 
     weights = blend_weights(ids, after(tuple(logits), packed), 1, pack)
-    received = after(received, packed)
+    received = after(tuple(received), packed)
     mamba_out = finish(step, read, cum, z_gate, prefix, received, a_log, b_and_c)
     back = after(back, mamba_out)
     moe_out = combine(back, weights, tokens, features, pack)

time: 110 us -> 106 us (0.964)
  waiting for transfers between devices: 20.4 us -> 15.6 us
    ppermute x4 -> x5, waiting for transfers between devices: 5.13 us -> 0.64 us  [swapped(): return lax.ppermute(value, 'seq', [(i, i ^ by) for i in range(count)])]
    ppermute x4 -> x5, starting transfers between devices: 5.79 us -> 6.46 us  [swapped(): return lax.ppermute(value, 'seq', [(i, i ^ by) for i in range(count)])]
  transfers between devices with their start and end apart: 12 -> 13, of which waited for: 6 -> 6; matrix products, arithmetic and copies ran while one was open for 0% -> 0% of each run, Pallas kernels for 56% -> 59%
where the time goes in v12:
time: 106 us
  Pallas kernels  63.4 us (60%)
  starting transfers between devices  25.1 us (24%)
  waiting for transfers between devices  15.6 us (15%)
    pallas_call x2, Pallas kernels, down(): pl.pallas_call(functools.partial(down_kernel, chunk), in_specs=[INSIDE] *...  18.7 us
    pallas_call x2, Pallas kernels, gate(): pl.pallas_call(functools.partial(gate_kernel, chunk), in_specs=[INSIDE, A...  18.4 us
    pallas_call x1, Pallas kernels, scan(): pl.pallas_call(scan_kernel, grid=(channels // lanes,), in_specs=[cut(toke...  11.5 us
    all_to_all x2, starting transfers between devices, exchanged(): lax.all_to_all(value, 'seq', split_axis=0, concat_axis=0, tiled=True, axi...  11.4 us
    all_to_all x2, waiting for transfers between devices, exchanged(): lax.all_to_all(value, 'seq', split_axis=0, concat_axis=0, tiled=True, axi...  9.27 us
    pallas_call x1, Pallas kernels, finish(): pl.pallas_call(functools.partial(finish_kernel, step), grid=(channels //...  8.45 us
    ppermute x5, starting transfers between devices, swapped(): return lax.ppermute(value, 'seq', [(i, i ^ by) for i in range(count)])  6.46 us
    ppermute x1, starting transfers between devices, local(): edge = lax.ppermute(edge, 'seq', [(i, i + 1) for i in range(blocks - 1)])  4.84 us
  transfers between devices with their start and end apart: 13, of which 6 were waited for; matrix products, arithmetic and copies ran while one was open for 0% of the time, Pallas kernels for 59%

profile of v12, /device:TPU:0, one launch (start us, length us, event | category | flops | bytes accessed | tf_op | source)
XLA Modules:
  0.0 105.7 jit_solution(5574215320419027791)
XLA Ops:
  0.6 0.9 slice.3
  1.5 4.8 %collective-permute-start = (bf16[3,4096]{1,0:T(4,128)(2,1)S(1)}, bf16[3,4096]{1,0:T(4,128)(2,1)S(1)}, u32[]{:S(2)}, u32[]{:S(2)}) collective-permute-start(bf16[3,4096]{1,0:T(4,128)(2,1)S(1)} %slice.3), channel_id=1, source_target_pairs={{0,2},{2,4},{4,6},{6,8},{8,10},{10,12},{12,14},{14,16},{16,18},{18... | collective-permute-start | bytes 73736 | tf_op jit(solution)/shard_map/ppermute | solution.py:691
  6.3 2.4 %route.1 = (bf16[8,1,16,2304]{3,2,1,0:T(8,128)(2,1)}, f32[64,8]{1,0:T(8,128)S(1)}) custom-call(s32[2,64]{1,0:T(2,128)} %bitcast.7, bf16[64,2048]{1,0:T(8,128)(2,1)} %hidden_ref.1, bf16[8,2048]{1,0:T(8,128)(2,1)} %bitcast.6), custom_call_target="tpu_custom_call" | custom-call | flops 67108864 | bytes 1048576 | tf_op jit(solution)/shard_map/route/pallas_call | solution.py:102
  8.8 6.7 %all-to-all-start = ((bf16[8,16,2304]{2,1,0:T(8,128)(2,1)}), bf16[8,16,2304]{2,1,0:T(8,128)(2,1)S(1)}, u32[]{:S(2)}, u32[]{:S(2)}) async-start(bf16[8,16,2304]{2,1,0:T(8,128)(2,1)} %bitcast.5), calls=%async_computation | async-start | bytes 1179648 | tf_op jit(solution)/shard_map/all_to_all | solution.py:656
  15.5 11.5 %scan.1 = (f32[64,4096]{1,0:T(8,128)}, f32[64,4096]{1,0:T(8,128)}, bf16[16,4608]{1,0:T(8,128)(2,1)S(1)}) custom-call(bf16[64,4096]{1,0:T(8,128)(2,1)} %x_ref.1, bf16[3,4096]{1,0:T(4,128)(2,1)S(1)} %collective-permute-done.edge_ref, bf16[64,256]{1,0:T(8,128)(2,1)} %low_ref.1, bf16[256,4096]{1,0:T(8,128)(2,1)} %dtw_ref.1, f32[1,4096]{1,0:T(1,128)} %bitcast.9, ...), custom_call_target="tpu_custom_call" | custom-call | flops 33554432 | bytes 3145728 | tf_op jit(solution)/shard_map/scan/pallas_call | solution.py:461
  27.0 3.3 %all-to-all-done.arrived_ref = bf16[8,16,2304]{2,1,0:T(8,128)(2,1)S(1)} async-done(((bf16[8,16,2304]{2,1,0:T(8,128)(2,1)}), bf16[8,16,2304]{2,1,0:T(8,128)(2,1)S(1)}, u32[]{:S(2)}, u32[]{:S(2)}) %all-to-all-start) | async-done | bytes 589856 | tf_op jit(solution)/shard_map/all_to_all | solution.py:656
  30.4 0.6 collective-permute-start.2
  31.0 9.2 %gate.2.refs_0_ = bf16[144,6144]{1,0:T(8,128)(2,1)S(1)} custom-call(bf16[144,2048]{1,0:T(8,128)(2,1)S(1)} %unpack.1.x_ref, bf16[2048,6144]{1,0:T(8,128)(2,1)} %w_ref.3), custom_call_target="tpu_custom_call" | custom-call | flops 3623878656 | bytes 25165824 | tf_op jit(solution)/shard_map/gate/pallas_call | solution.py:203
  40.3 3.4 %collective-permute-done.2.x_ref = bf16[144,2048]{1,0:T(8,128)(2,1)S(1)} collective-permute-done((bf16[144,2048]{1,0:T(8,128)(2,1)S(1)}, bf16[144,2048]{1,0:T(8,128)(2,1)S(1)}, u32[]{:S(2)}, u32[]{:S(2)}) %collective-permute-start.2) | collective-permute-done | bytes 589856 | tf_op jit(solution)/shard_map/ppermute | solution.py:648
  44.2 9.2 %gate.3.refs_0_ = bf16[144,6144]{1,0:T(8,128)(2,1)S(1)} custom-call(bf16[144,2048]{1,0:T(8,128)(2,1)S(1)} %collective-permute-done.2.x_ref, bf16[2048,6144]{1,0:T(8,128)(2,1)} %w_ref.3), custom_call_target="tpu_custom_call" | custom-call | flops 3623878656 | bytes 25165824 | tf_op jit(solution)/shard_map/gate/pallas_call | solution.py:203
  53.9 1.5 %collective-permute-start.4 = (bf16[16,4608]{1,0:T(8,128)(2,1)S(1)}, bf16[16,4608]{1,0:T(8,128)(2,1)S(1)}, u32[]{:S(2)}, u32[]{:S(2)}) collective-permute-start(bf16[16,4608]{1,0:T(8,128)(2,1)S(1)} %get-tuple-element.41.refs_0_), channel_id=1, source_target_pairs={{0,4},{2,6},{4,0},{6,2},{8,12},{10,14},{12,8},{14,10},{16,20},{18,... | collective-permute-start | bytes 442376 | tf_op jit(solution)/shard_map/ppermute | solution.py:638
  55.4 2.0 %collective-permute-done.6.refs_1_ = bf16[144,6144]{1,0:T(8,128)(2,1)S(1)} collective-permute-done((bf16[144,6144]{1,0:T(8,128)(2,1)S(1)}, bf16[144,6144]{1,0:T(8,128)(2,1)S(1)}, u32[]{:S(2)}, u32[]{:S(2)}) %collective-permute-start.6) | collective-permute-done | bytes 1769504 | tf_op jit(solution)/shard_map/ppermute | solution.py:643
  57.4 9.3 %down.2 = bf16[144,2048]{1,0:T(8,128)(2,1)S(1)} custom-call(bf16[144,6144]{1,0:T(8,128)(2,1)S(1)} %gate.3.refs_0_, bf16[144,6144]{1,0:T(8,128)(2,1)S(1)} %collective-permute-done.6.refs_1_, bf16[6144,2048]{1,0:T(8,128)(2,1)} %refs_2_.7), custom_call_target="tpu_custom_call" | custom-call | flops 3623878656 | bytes 25165824 | tf_op jit(solution)/shard_map/down/pallas_call | solution.py:246
  67.0 1.5 %collective-permute-start.10 = (bf16[144,2048]{1,0:T(8,128)(2,1)S(1)}, bf16[144,2048]{1,0:T(8,128)(2,1)S(1)}, u32[]{:S(2)}, u32[]{:S(2)}) collective-permute-start(bf16[144,2048]{1,0:T(8,128)(2,1)S(1)} %down.2), channel_id=1, source_target_pairs={{0,2},{2,0},{4,6},{6,4},{8,10},{10,8},{12,14},{14,12},{16,18},{18,... | collective-permute-start | bytes 1769480 | tf_op jit(solution)/shard_map/ppermute | solution.py:648
  68.4 3.1 %collective-permute-start.9 = (bf16[16,4608]{1,0:T(8,128)(2,1)S(1)}, bf16[16,4608]{1,0:T(8,128)(2,1)S(1)}, u32[]{:S(2)}, u32[]{:S(2)}) collective-permute-start(bf16[16,4608]{1,0:T(8,128)(2,1)S(1)} %get-tuple-element.46), channel_id=1, source_target_pairs={{0,24},{2,26},{4,28},{6,30},{8,16},{10,18},{12,20},{14,22},{16,8},... | collective-permute-start | bytes 442376 | tf_op jit(solution)/shard_map/ppermute | solution.py:638
  71.5 1.3 %collective-permute-start.7 = (bf16[16,4608]{1,0:T(8,128)(2,1)S(1)}, bf16[16,4608]{1,0:T(8,128)(2,1)S(1)}, u32[]{:S(2)}, u32[]{:S(2)}) collective-permute-start(bf16[16,4608]{1,0:T(8,128)(2,1)S(1)} %get-tuple-element.46), channel_id=1, source_target_pairs={{0,8},{2,10},{4,12},{6,14},{8,0},{10,2},{12,4},{14,6},{16,24},{18,... | collective-permute-start | bytes 442376 | tf_op jit(solution)/shard_map/ppermute | solution.py:638
  72.8 9.3 %down.3.refs_0_ = f32[144,2048]{1,0:T(8,128)S(1)} custom-call(bf16[144,6144]{1,0:T(8,128)(2,1)S(1)} %gate.2.refs_0_, bf16[144,6144]{1,0:T(8,128)(2,1)S(1)} %collective-permute-done.5.refs_1_, bf16[6144,2048]{1,0:T(8,128)(2,1)} %refs_2_.7), custom_call_target="tpu_custom_call" | custom-call | flops 3623878656 | bytes 25165824 | tf_op jit(solution)/shard_map/down/pallas_call | solution.py:246
  82.5 1.2 %pack_sum.1 = bf16[8,16,2304]{2,1,0:T(8,128)(2,1)} custom-call(f32[144,2048]{1,0:T(8,128)S(1)} %down.3.refs_0_, bf16[144,2048]{1,0:T(8,128)(2,1)S(1)} %collective-permute-done.10.refs_1_), custom_call_target="tpu_custom_call" | custom-call | flops 4718592 | bytes 2359296 | tf_op jit(solution)/shard_map/pack_sum/pallas_call | solution.py:316
  83.7 0.6 collective-permute-done.8.refs_1_.refs_5_
  84.4 4.7 %all-to-all-start.1 = ((bf16[8,16,2304]{2,1,0:T(8,128)(2,1)}), bf16[8,16,2304]{2,1,0:T(8,128)(2,1)S(1)}, u32[]{:S(2)}, u32[]{:S(2)}) async-start(bf16[8,16,2304]{2,1,0:T(8,128)(2,1)} %pack_sum.1), calls=%async_computation.1 | async-start | bytes 1179648 | tf_op jit(solution)/shard_map/all_to_all | solution.py:656
  89.0 1.0 blend_weights.1
  90.1 8.5 %finish.1 = bf16[64,4096]{1,0:T(8,128)(2,1)} custom-call(f32[64,4096]{1,0:T(8,128)} %get-tuple-element.30.read_ref, f32[64,4096]{1,0:T(8,128)} %get-tuple-element.31.cum_ref, bf16[64,4096]{1,0:T(8,128)(2,1)} %z_ref.1, f32[16,4096]{1,0:T(8,128)} %alog_ref.3, f32[2,16,64]{2,1,0:T(8,128)} %bc_ref.3, bf16[16,4608]{1,0:T(8,128)(2,1)S(1)} %get-tuple-element.45.prefix_ref.refs_3_, ...), custom_call_target="tpu_custom_call" | custom-call | flops 20971520 | bytes 3145728 | tf_op jit(solution)/shard_map/finish/pallas_call | solution.py:612
  98.5 6.0 %all-to-all-done.1.back_ref = bf16[8,16,2304]{2,1,0:T(8,128)(2,1)S(1)} async-done(((bf16[8,16,2304]{2,1,0:T(8,128)(2,1)}), bf16[8,16,2304]{2,1,0:T(8,128)(2,1)S(1)}, u32[]{:S(2)}, u32[]{:S(2)}) %all-to-all-start.1) | async-done | bytes 589856 | tf_op jit(solution)/shard_map/all_to_all | solution.py:656
  104.5 1.1 %combine.1 = bf16[64,2048]{1,0:T(8,128)(2,1)} custom-call(bf16[8,16,2304]{2,1,0:T(8,128)(2,1)S(1)} %all-to-all-done.1.back_ref, bf16[2,64,128]{2,1,0:T(8,128)(2,1)S(1)} %get-tuple-element.55.main_ref, bf16[2,64,128]{2,1,0:T(8,128)(2,1)S(1)} %get-tuple-element.56.extra_ref, f32[2,64,128]{2,1,0:T(8,128)S(1)} %get-tuple-element.57.gates_ref), custom_call_target="tpu_custom_call" | custom-call | flops 75497472 | bytes 589824 | tf_op jit(solution)/shard_map/combine/pallas_call | solution.py:347
  (18 shorter events, 1.7 us)
Async XLA Ops:
  1.5 7.3 %collective-permute-start = (bf16[3,4096]{1,0:T(4,128)(2,1)S(1)}, bf16[3,4096]{1,0:T(4,128)(2,1)S(1)}, u32[]{:S(2)}, u32[]{:S(2)}) collective-permute-start(bf16[3,4096]{1,0:T(4,128)(2,1)S(1)} %slice.3), channel_id=1, source_target_pairs={{0,2},{2,4},{4,6},{6,8},{8,10},{10,12},{12,14},{14,16},{16,18},{18... | collective-permute-start | bytes 73736 | tf_op jit(solution)/shard_map/ppermute | solution.py:691
  8.8 21.5 %all-to-all-start = ((bf16[8,16,2304]{2,1,0:T(8,128)(2,1)}), bf16[8,16,2304]{2,1,0:T(8,128)(2,1)S(1)}, u32[]{:S(2)}, u32[]{:S(2)}) async-start(bf16[8,16,2304]{2,1,0:T(8,128)(2,1)} %bitcast.5), calls=%async_computation | async-start | bytes 1179648 | tf_op jit(solution)/shard_map/all_to_all | solution.py:656
  15.5 11.5 %collective-permute-start.1 = (f32[64,8]{1,0:T(8,128)S(1)}, f32[64,8]{1,0:T(8,128)S(1)}, u32[]{:S(2)}, u32[]{:S(2)}) collective-permute-start(f32[64,8]{1,0:T(8,128)S(1)} %get-tuple-element.53.refs_0_), channel_id=1, source_target_pairs={{0,1},{1,0},{2,3},{3,2},{4,5},{5,4},{6,7},{7,6},{8,9},{9,8},{10,11... | collective-permute-start | bytes 6152 | tf_op jit(solution)/shard_map/ppermute | solution.py:643
  30.4 13.2 %collective-permute-start.2 = (bf16[144,2048]{1,0:T(8,128)(2,1)S(1)}, bf16[144,2048]{1,0:T(8,128)(2,1)S(1)}, u32[]{:S(2)}, u32[]{:S(2)}) collective-permute-start(bf16[144,2048]{1,0:T(8,128)(2,1)S(1)} %unpack.1.x_ref), channel_id=1, source_target_pairs={{0,2},{2,0},{4,6},{6,4},{8,10},{10,8},{12,14},{14,12},{16,18},{18,... | collective-permute-start | bytes 1769480 | tf_op jit(solution)/shard_map/ppermute | solution.py:648
  40.2 13.2 %copy-start = (f32[16,4096]{1,0:T(8,128)S(1)}, f32[16,4096]{1,0:T(8,128)}, u32[]{:S(2)}) copy-start(f32[16,4096]{1,0:T(8,128)} %alog_ref.3) | copy-start | bytes 786436
  43.6 10.0 %collective-permute-start.5 = (bf16[144,6144]{1,0:T(8,128)(2,1)S(1)}, bf16[144,6144]{1,0:T(8,128)(2,1)S(1)}, u32[]{:S(2)}, u32[]{:S(2)}) collective-permute-start(bf16[144,6144]{1,0:T(8,128)(2,1)S(1)} %gate.2.refs_0_), channel_id=1, source_target_pairs={{0,1},{1,0},{2,3},{3,2},{4,5},{5,4},{6,7},{7,6},{8,9},{9,8},{10,11... | collective-permute-start | bytes 5308424 | tf_op jit(solution)/shard_map/ppermute | solution.py:643
  43.6 9.8 %collective-permute-start.3 = (bf16[16,4608]{1,0:T(8,128)(2,1)S(1)}, bf16[16,4608]{1,0:T(8,128)(2,1)S(1)}, u32[]{:S(2)}, u32[]{:S(2)}) collective-permute-start(bf16[16,4608]{1,0:T(8,128)(2,1)S(1)} %get-tuple-element.37.refs_0_), channel_id=1, source_target_pairs={{0,2},{2,0},{4,6},{6,4},{8,10},{10,8},{12,14},{14,12},{16,18},{18,... | collective-permute-start | bytes 442376 | tf_op jit(solution)/shard_map/ppermute | solution.py:638
  53.6 3.8 %collective-permute-start.6 = (bf16[144,6144]{1,0:T(8,128)(2,1)S(1)}, bf16[144,6144]{1,0:T(8,128)(2,1)S(1)}, u32[]{:S(2)}, u32[]{:S(2)}) collective-permute-start(bf16[144,6144]{1,0:T(8,128)(2,1)S(1)} %gate.3.refs_0_), channel_id=1, source_target_pairs={{0,1},{1,0},{2,3},{3,2},{4,5},{5,4},{6,7},{7,6},{8,9},{9,8},{10,11... | collective-permute-start | bytes 5308424 | tf_op jit(solution)/shard_map/ppermute | solution.py:643
  53.9 12.8 %collective-permute-start.4 = (bf16[16,4608]{1,0:T(8,128)(2,1)S(1)}, bf16[16,4608]{1,0:T(8,128)(2,1)S(1)}, u32[]{:S(2)}, u32[]{:S(2)}) collective-permute-start(bf16[16,4608]{1,0:T(8,128)(2,1)S(1)} %get-tuple-element.41.refs_0_), channel_id=1, source_target_pairs={{0,4},{2,6},{4,0},{6,2},{8,12},{10,14},{12,8},{14,10},{16,20},{18,... | collective-permute-start | bytes 442376 | tf_op jit(solution)/shard_map/ppermute | solution.py:638
  67.0 15.5 %collective-permute-start.10 = (bf16[144,2048]{1,0:T(8,128)(2,1)S(1)}, bf16[144,2048]{1,0:T(8,128)(2,1)S(1)}, u32[]{:S(2)}, u32[]{:S(2)}) collective-permute-start(bf16[144,2048]{1,0:T(8,128)(2,1)S(1)} %down.2), channel_id=1, source_target_pairs={{0,2},{2,0},{4,6},{6,4},{8,10},{10,8},{12,14},{14,12},{16,18},{18,... | collective-permute-start | bytes 1769480 | tf_op jit(solution)/shard_map/ppermute | solution.py:648
  68.4 15.3 %collective-permute-start.9 = (bf16[16,4608]{1,0:T(8,128)(2,1)S(1)}, bf16[16,4608]{1,0:T(8,128)(2,1)S(1)}, u32[]{:S(2)}, u32[]{:S(2)}) collective-permute-start(bf16[16,4608]{1,0:T(8,128)(2,1)S(1)} %get-tuple-element.46), channel_id=1, source_target_pairs={{0,24},{2,26},{4,28},{6,30},{8,16},{10,18},{12,20},{14,22},{16,8},... | collective-permute-start | bytes 442376 | tf_op jit(solution)/shard_map/ppermute | solution.py:638
  71.5 12.8 %collective-permute-start.8 = (bf16[16,4608]{1,0:T(8,128)(2,1)S(1)}, bf16[16,4608]{1,0:T(8,128)(2,1)S(1)}, u32[]{:S(2)}, u32[]{:S(2)}) collective-permute-start(bf16[16,4608]{1,0:T(8,128)(2,1)S(1)} %get-tuple-element.46), channel_id=1, source_target_pairs={{0,16},{2,18},{4,20},{6,22},{8,24},{10,26},{12,28},{14,30},{16,0},... | collective-permute-start | bytes 442376 | tf_op jit(solution)/shard_map/ppermute | solution.py:638
  71.5 12.8 %collective-permute-start.7 = (bf16[16,4608]{1,0:T(8,128)(2,1)S(1)}, bf16[16,4608]{1,0:T(8,128)(2,1)S(1)}, u32[]{:S(2)}, u32[]{:S(2)}) collective-permute-start(bf16[16,4608]{1,0:T(8,128)(2,1)S(1)} %get-tuple-element.46), channel_id=1, source_target_pairs={{0,8},{2,10},{4,12},{6,14},{8,0},{10,2},{12,4},{14,6},{16,24},{18,... | collective-permute-start | bytes 442376 | tf_op jit(solution)/shard_map/ppermute | solution.py:638
  84.4 20.2 %all-to-all-start.1 = ((bf16[8,16,2304]{2,1,0:T(8,128)(2,1)}), bf16[8,16,2304]{2,1,0:T(8,128)(2,1)S(1)}, u32[]{:S(2)}, u32[]{:S(2)}) async-start(bf16[8,16,2304]{2,1,0:T(8,128)(2,1)} %pack_sum.1), calls=%async_computation.1 | async-start | bytes 1179648 | tf_op jit(solution)/shard_map/all_to_all | solution.py:656

commit v13 on v12

--- a/solution.py
+++ b/solution.py
@@ -162,16 +162,20 @@
 AHEAD = 6
 
 
-def streamed(from_ref, to_ref, sems, dim, chunk, use, begin=None):
-    count = from_ref.shape[dim] // chunk
-
+def chunk_copy(from_ref, to_ref, sems, dim, chunk):
     def copy(i):
         at = pl.ds(pl.multiple_of(i * chunk, chunk), chunk)
         part = (slice(None), at) if dim else (at, slice(None))
         return pltpu.make_async_copy(from_ref.at[part], to_ref.at[part], sems.at[i])
 
-    for i in range(min(AHEAD, count)):
-        copy(i).start()
+    return copy, from_ref.shape[dim] // chunk
+
+
+def streamed(stream, use, begin=None, begun=False, follow=None):
+    copy, count = stream
+    if not begun:
+        for i in range(min(AHEAD, count)):
+            copy(i).start()
     if begin is not None:
         begin()
 
@@ -182,36 +186,77 @@
         def _():
             copy(i + AHEAD).start()
 
+        if follow is not None:
+            later = i - max(count - AHEAD, 0)
+
+            @pl.when((later >= 0) & (later < follow[1]))
+            def _():
+                follow[0](later).start()
+
         use(i)
         return carry
 
     lax.fori_loop(0, count, step, 0)
 
 
-def gate_kernel(chunk, x_ref, w_ref, out_ref, held_ref, sems):
+def gate_first_kernel(chunk, x_ref, w_ref, out_ref, kept_ref, held_ref, kept_sems, sems):
+    start = kept_ref.shape[1]
+    one = chunk_copy(w_ref.at[:, :start], kept_ref, kept_sems, 1, chunk)
+    two = chunk_copy(w_ref.at[:, start:], held_ref, sems, 1, chunk)
+    streamed(one, gate_product(chunk, x_ref, kept_ref, out_ref, 0), follow=two)
+    for i in range(min(AHEAD, one[1]), min(AHEAD, two[1])):
+        two[0](i).start()
+    streamed(two, gate_product(chunk, x_ref, held_ref, out_ref, start), begun=True)
+
+
+def gate_product(chunk, x_ref, from_ref, out_ref, offset):
     def use(i):
         at = pl.ds(pl.multiple_of(i * chunk, chunk), chunk)
-        out_ref[:, at] = dot(x_ref[...], held_ref[:, at]).astype(BF16)
-
-    streamed(w_ref, held_ref, sems, 1, chunk, use)
-
-
-def gate(x, w_gate):
+        to = pl.ds(pl.multiple_of(offset + i * chunk, chunk), chunk)
+        out_ref[:, to] = dot(x_ref[...], from_ref[:, at]).astype(BF16)
+
+    return use
+
+
+def gate_next_kernel(chunk, x_ref, w_ref, kept_ref, out_ref, held_ref, sems):
+    start = kept_ref.shape[1]
+    kept = gate_product(chunk, x_ref, kept_ref, out_ref, 0)
+    streamed(
+        chunk_copy(w_ref.at[:, start:], held_ref, sems, 1, chunk),
+        gate_product(chunk, x_ref, held_ref, out_ref, start),
+        lambda: pl.loop(0, start // chunk)(kept),
+    )
+
+
+def gate(x, w_gate, kept=None):
     rows, features = x.shape
     amount = w_gate.shape[1]
     chunk = math.gcd(512, amount)
-    return pl.pallas_call(
-        functools.partial(gate_kernel, chunk),
-        in_specs=[INSIDE, ANYWHERE],
-        out_specs=INSIDE,
-        out_shape=jax.ShapeDtypeStruct((rows, amount), BF16),
-        scratch_shapes=[
-            pltpu.VMEM(w_gate.shape, BF16),
-            pltpu.SemaphoreType.DMA((amount // chunk,)),
-        ],
-        compiler_params=params(44),
+    half = amount // chunk // 2 * chunk
+    out = jax.ShapeDtypeStruct((rows, amount), BF16)
+    rest = [pltpu.VMEM((features, amount - half), BF16)]
+    rest_sems = pltpu.SemaphoreType.DMA(((amount - half) // chunk,))
+    hints = dict(
+        compiler_params=params(32),
         cost_estimate=cost(2 * rows * features * amount, features * amount * 2),
         name="gate",
+    )
+    if kept is not None:
+        return pl.pallas_call(
+            functools.partial(gate_next_kernel, chunk),
+            in_specs=[INSIDE, ANYWHERE, INSIDE],
+            out_specs=INSIDE,
+            out_shape=out,
+            scratch_shapes=rest + [rest_sems],
+            **hints,
+        )(x, *in_hbm(w_gate), kept)
+    return pl.pallas_call(
+        functools.partial(gate_first_kernel, chunk),
+        in_specs=[INSIDE, ANYWHERE],
+        out_specs=(INSIDE, INSIDE),
+        out_shape=(out, jax.ShapeDtypeStruct((features, half), BF16)),
+        scratch_shapes=rest + [pltpu.SemaphoreType.DMA((half // chunk,)), rest_sems],
+        **hints,
     )(x, *in_hbm(w_gate))
 
 
@@ -236,7 +281,7 @@
     def begin():
         fill_acted(math.gcd(512, acted_ref.shape[1]), part_refs, acted_ref)
 
-    streamed(w_ref, held_ref, sems, 1, chunk, use, begin)
+    streamed(chunk_copy(w_ref, held_ref, sems, 1, chunk), use, begin)
 
 
 def down(parts, w_down, dtype):
@@ -720,8 +765,9 @@
     for part in rows:
         if gated:
             part = after(part, gated[-1][0])
-        own = gate(part, w_gate)
-        if not gated:
+            own = gate(part, w_gate, kept)
+        else:
+            own, kept = gate(part, w_gate)
             own, received = after((own, ends), *rows[1:])
             received = swapped(received, 1)
         if len(gated) == copies - 1:

time: 106 us -> 104 us (0.981)
  Pallas kernels: 63.4 us -> 60.3 us
  local copies, waits for them, and re-layouts: 0.87 us -> 2.43 us
    pallas_call x2, Pallas kernels: 18.4 us -> 15.3 us  [the longest x1 9.21 us: gate(): pl.pallas_call(functools.partial(gate_first_kernel, chunk), in_specs=[INS...]
    unnamed x2 -> x6, local copies, waits for them, and re-layouts: 0.01 us -> 1.57 us
  transfers between devices with their start and end apart: 13 -> 13, of which waited for: 6 -> 6; matrix products, arithmetic and copies ran while one was open for 0% -> 0% of each run, Pallas kernels for 59% -> 57%
where the time goes in v13:
time: 104 us; the launch traced here: 103 us
  Pallas kernels  60.3 us (58%)
  starting transfers between devices  25 us (24%)
  waiting for transfers between devices  14.7 us (14%)
  local copies, waits for them, and re-layouts  2.43 us (2%)
    pallas_call x2, Pallas kernels, down(): pl.pallas_call(functools.partial(down_kernel, chunk), in_specs=[INSIDE] *...  18.7 us
    pallas_call x1, Pallas kernels, scan(): pl.pallas_call(scan_kernel, grid=(channels // lanes,), in_specs=[cut(toke...  11.5 us
    all_to_all x2, starting transfers between devices, exchanged(): lax.all_to_all(value, 'seq', split_axis=0, concat_axis=0, tiled=True, axi...  11.4 us
    pallas_call x1, Pallas kernels, gate(): pl.pallas_call(functools.partial(gate_first_kernel, chunk), in_specs=[INS...  9.21 us
    pallas_call x1, Pallas kernels, finish(): pl.pallas_call(functools.partial(finish_kernel, step), grid=(channels //...  8.42 us
    all_to_all x2, waiting for transfers between devices, exchanged(): lax.all_to_all(value, 'seq', split_axis=0, concat_axis=0, tiled=True, axi...  8.32 us
    ppermute x5, starting transfers between devices, swapped(): return lax.ppermute(value, 'seq', [(i, i ^ by) for i in range(count)])  6.46 us
    pallas_call x1, Pallas kernels, gate(): pl.pallas_call(functools.partial(gate_next_kernel, chunk), in_specs=[INSI...  6.11 us
  transfers between devices with their start and end apart: 13, of which 6 were waited for; matrix products, arithmetic and copies ran while one was open for 0% of the time, Pallas kernels for 57%

profile of v13, /device:TPU:0, one launch (start us, length us, event | category | flops | bytes accessed | tf_op | source)
XLA Modules:
  0.0 103.2 jit_solution(16029444769001220274)
XLA Ops:
  0.6 0.9 slice.3
  1.5 4.8 %collective-permute-start = (bf16[3,4096]{1,0:T(4,128)(2,1)S(1)}, bf16[3,4096]{1,0:T(4,128)(2,1)S(1)}, u32[]{:S(2)}, u32[]{:S(2)}) collective-permute-start(bf16[3,4096]{1,0:T(4,128)(2,1)S(1)} %slice.3), channel_id=1, source_target_pairs={{0,2},{2,4},{4,6},{6,8},{8,10},{10,12},{12,14},{14,16},{16,18},{18... | collective-permute-start | bytes 73736 | tf_op jit(solution)/shard_map/ppermute | solution.py:736
  6.3 2.4 %route.1 = (bf16[8,1,16,2304]{3,2,1,0:T(8,128)(2,1)}, f32[64,8]{1,0:T(8,128)S(1)}) custom-call(s32[2,64]{1,0:T(2,128)} %bitcast.7, bf16[64,2048]{1,0:T(8,128)(2,1)} %hidden_ref.1, bf16[8,2048]{1,0:T(8,128)(2,1)} %bitcast.6), custom_call_target="tpu_custom_call" | custom-call | flops 67108864 | bytes 1048576 | tf_op jit(solution)/shard_map/route/pallas_call | solution.py:102
  8.8 6.7 %all-to-all-start = ((bf16[8,16,2304]{2,1,0:T(8,128)(2,1)}), bf16[8,16,2304]{2,1,0:T(8,128)(2,1)S(1)}, u32[]{:S(2)}, u32[]{:S(2)}) async-start(bf16[8,16,2304]{2,1,0:T(8,128)(2,1)} %bitcast.5), calls=%async_computation | async-start | bytes 1179648 | tf_op jit(solution)/shard_map/all_to_all | solution.py:701
  15.5 11.5 %scan.1 = (f32[64,4096]{1,0:T(8,128)}, f32[64,4096]{1,0:T(8,128)}, bf16[16,4608]{1,0:T(8,128)(2,1)S(1)}) custom-call(bf16[64,4096]{1,0:T(8,128)(2,1)} %x_ref.1, bf16[3,4096]{1,0:T(4,128)(2,1)S(1)} %collective-permute-done.edge_ref, bf16[64,256]{1,0:T(8,128)(2,1)} %low_ref.1, bf16[256,4096]{1,0:T(8,128)(2,1)} %dtw_ref.1, f32[1,4096]{1,0:T(1,128)} %bitcast.9, ...), custom_call_target="tpu_custom_call" | custom-call | flops 33554432 | bytes 3145728 | tf_op jit(solution)/shard_map/scan/pallas_call | solution.py:506
  27.0 3.2 %all-to-all-done.arrived_ref = bf16[8,16,2304]{2,1,0:T(8,128)(2,1)S(1)} async-done(((bf16[8,16,2304]{2,1,0:T(8,128)(2,1)}), bf16[8,16,2304]{2,1,0:T(8,128)(2,1)S(1)}, u32[]{:S(2)}, u32[]{:S(2)}) %all-to-all-start) | async-done | bytes 589856 | tf_op jit(solution)/shard_map/all_to_all | solution.py:701
  31.0 9.2 %gate.2 = (bf16[144,6144]{1,0:T(8,128)(2,1)S(1)}, bf16[2048,3072]{1,0:T(8,128)(2,1)S(1)}) custom-call(bf16[144,2048]{1,0:T(8,128)(2,1)S(1)} %unpack.1.x_ref, bf16[2048,6144]{1,0:T(8,128)(2,1)} %w_ref.3), custom_call_target="tpu_custom_call" | custom-call | flops 3623878656 | bytes 25165824 | tf_op jit(solution)/shard_map/gate/pallas_call | solution.py:253
  40.3 3.4 %collective-permute-done.2.x_ref = bf16[144,2048]{1,0:T(8,128)(2,1)S(1)} collective-permute-done((bf16[144,2048]{1,0:T(8,128)(2,1)S(1)}, bf16[144,2048]{1,0:T(8,128)(2,1)S(1)}, u32[]{:S(2)}, u32[]{:S(2)}) %collective-permute-start.2) | collective-permute-done | bytes 589856 | tf_op jit(solution)/shard_map/ppermute | solution.py:693
  44.2 6.1 %gate.3.refs_0_ = bf16[144,6144]{1,0:T(8,128)(2,1)S(1)} custom-call(bf16[144,2048]{1,0:T(8,128)(2,1)S(1)} %collective-permute-done.2.x_ref, bf16[2048,6144]{1,0:T(8,128)(2,1)} %w_ref.3, bf16[2048,3072]{1,0:T(8,128)(2,1)S(1)} %get-tuple-element.43.kept_ref), custom_call_target="tpu_custom_call" | custom-call | flops 3623878656 | bytes 25165824 | tf_op jit(solution)/shard_map/gate/pallas_call | solution.py:245
  50.8 1.5 %collective-permute-start.4 = (bf16[16,4608]{1,0:T(8,128)(2,1)S(1)}, bf16[16,4608]{1,0:T(8,128)(2,1)S(1)}, u32[]{:S(2)}, u32[]{:S(2)}) collective-permute-start(bf16[16,4608]{1,0:T(8,128)(2,1)S(1)} %get-tuple-element.45.refs_0_), channel_id=1, source_target_pairs={{0,4},{2,6},{4,0},{6,2},{8,12},{10,14},{12,8},{14,10},{16,20},{18,... | collective-permute-start | bytes 442376 | tf_op jit(solution)/shard_map/ppermute | solution.py:683
  52.3 2.0 %collective-permute-done.6.refs_1_ = bf16[144,6144]{1,0:T(8,128)(2,1)S(1)} collective-permute-done((bf16[144,6144]{1,0:T(8,128)(2,1)S(1)}, bf16[144,6144]{1,0:T(8,128)(2,1)S(1)}, u32[]{:S(2)}, u32[]{:S(2)}) %collective-permute-start.6) | collective-permute-done | bytes 1769504 | tf_op jit(solution)/shard_map/ppermute | solution.py:688
  54.3 9.3 %down.2 = bf16[144,2048]{1,0:T(8,128)(2,1)S(1)} custom-call(bf16[144,6144]{1,0:T(8,128)(2,1)S(1)} %gate.3.refs_0_, bf16[144,6144]{1,0:T(8,128)(2,1)S(1)} %collective-permute-done.6.refs_1_, bf16[6144,2048]{1,0:T(8,128)(2,1)} %refs_2_.7), custom_call_target="tpu_custom_call" | custom-call | flops 3623878656 | bytes 25165824 | tf_op jit(solution)/shard_map/down/pallas_call | solution.py:291
  63.9 1.5 %collective-permute-start.10 = (bf16[144,2048]{1,0:T(8,128)(2,1)S(1)}, bf16[144,2048]{1,0:T(8,128)(2,1)S(1)}, u32[]{:S(2)}, u32[]{:S(2)}) collective-permute-start(bf16[144,2048]{1,0:T(8,128)(2,1)S(1)} %down.2), channel_id=1, source_target_pairs={{0,2},{2,0},{4,6},{6,4},{8,10},{10,8},{12,14},{14,12},{16,18},{18,... | collective-permute-start | bytes 1769480 | tf_op jit(solution)/shard_map/ppermute | solution.py:693
  65.3 3.1 %collective-permute-start.9 = (bf16[16,4608]{1,0:T(8,128)(2,1)S(1)}, bf16[16,4608]{1,0:T(8,128)(2,1)S(1)}, u32[]{:S(2)}, u32[]{:S(2)}) collective-permute-start(bf16[16,4608]{1,0:T(8,128)(2,1)S(1)} %get-tuple-element.50), channel_id=1, source_target_pairs={{0,24},{2,26},{4,28},{6,30},{8,16},{10,18},{12,20},{14,22},{16,8},... | collective-permute-start | bytes 442376 | tf_op jit(solution)/shard_map/ppermute | solution.py:683
  68.4 1.3 %collective-permute-start.7 = (bf16[16,4608]{1,0:T(8,128)(2,1)S(1)}, bf16[16,4608]{1,0:T(8,128)(2,1)S(1)}, u32[]{:S(2)}, u32[]{:S(2)}) collective-permute-start(bf16[16,4608]{1,0:T(8,128)(2,1)S(1)} %get-tuple-element.50), channel_id=1, source_target_pairs={{0,8},{2,10},{4,12},{6,14},{8,0},{10,2},{12,4},{14,6},{16,24},{18,... | collective-permute-start | bytes 442376 | tf_op jit(solution)/shard_map/ppermute | solution.py:683
  69.7 9.3 %down.3.refs_0_ = f32[144,2048]{1,0:T(8,128)S(1)} custom-call(bf16[144,6144]{1,0:T(8,128)(2,1)S(1)} %get-tuple-element.41.refs_0_, bf16[144,6144]{1,0:T(8,128)(2,1)S(1)} %collective-permute-done.5.refs_1_, bf16[6144,2048]{1,0:T(8,128)(2,1)} %refs_2_.7), custom_call_target="tpu_custom_call" | custom-call | flops 3623878656 | bytes 25165824 | tf_op jit(solution)/shard_map/down/pallas_call | solution.py:291
  79.3 1.2 %pack_sum.1 = bf16[8,16,2304]{2,1,0:T(8,128)(2,1)} custom-call(f32[144,2048]{1,0:T(8,128)S(1)} %down.3.refs_0_, bf16[144,2048]{1,0:T(8,128)(2,1)S(1)} %collective-permute-done.10.refs_1_), custom_call_target="tpu_custom_call" | custom-call | flops 4718592 | bytes 2359296 | tf_op jit(solution)/shard_map/pack_sum/pallas_call | solution.py:361
  81.2 0.7 copy-done.1
  81.9 4.6 %all-to-all-start.1 = ((bf16[8,16,2304]{2,1,0:T(8,128)(2,1)}), bf16[8,16,2304]{2,1,0:T(8,128)(2,1)S(1)}, u32[]{:S(2)}, u32[]{:S(2)}) async-start(bf16[8,16,2304]{2,1,0:T(8,128)(2,1)} %pack_sum.1), calls=%async_computation.1 | async-start | bytes 1179648 | tf_op jit(solution)/shard_map/all_to_all | solution.py:701
  86.5 1.0 %blend_weights.1 = (bf16[2,64,128]{2,1,0:T(8,128)(2,1)S(1)}, bf16[2,64,128]{2,1,0:T(8,128)(2,1)S(1)}, f32[2,64,128]{2,1,0:T(8,128)S(1)}) custom-call(s32[2,64]{1,0:T(2,128)} %bitcast.8, f32[64,8]{1,0:T(8,128)S(1)} %get-tuple-element.57.refs_0_, f32[64,8]{1,0:T(8,128)S(1)} %collective-permute-done.1.refs_1_), custom_call_target="tpu_custom_call" | custom-call | flops 262144 | bytes 65536 | tf_op jit(solution)/shard_map/blend_weights/pallas_call | solution.py:147
  87.6 0.9 copy-done.2
  88.5 8.4 %finish.1 = bf16[64,4096]{1,0:T(8,128)(2,1)} custom-call(f32[64,4096]{1,0:T(8,128)} %get-tuple-element.32.read_ref, f32[64,4096]{1,0:T(8,128)} %get-tuple-element.33.cum_ref, bf16[64,4096]{1,0:T(8,128)(2,1)} %z_ref.1, f32[16,4096]{1,0:T(8,128)} %alog_ref.3, f32[2,16,64]{2,1,0:T(8,128)} %bc_ref.3, bf16[16,4608]{1,0:T(8,128)(2,1)S(1)} %get-tuple-element.49.prefix_ref.refs_3_, ...), custom_call_target="tpu_custom_call" | custom-call | flops 20971520 | bytes 3145728 | tf_op jit(solution)/shard_map/finish/pallas_call | solution.py:657
  96.9 5.1 %all-to-all-done.1.back_ref = bf16[8,16,2304]{2,1,0:T(8,128)(2,1)S(1)} async-done(((bf16[8,16,2304]{2,1,0:T(8,128)(2,1)}), bf16[8,16,2304]{2,1,0:T(8,128)(2,1)S(1)}, u32[]{:S(2)}, u32[]{:S(2)}) %all-to-all-start.1) | async-done | bytes 589856 | tf_op jit(solution)/shard_map/all_to_all | solution.py:701
  102.0 1.1 %combine.1 = bf16[64,2048]{1,0:T(8,128)(2,1)} custom-call(bf16[8,16,2304]{2,1,0:T(8,128)(2,1)S(1)} %all-to-all-done.1.back_ref, bf16[2,64,128]{2,1,0:T(8,128)(2,1)S(1)} %get-tuple-element.59.main_ref, bf16[2,64,128]{2,1,0:T(8,128)(2,1)S(1)} %get-tuple-element.60.extra_ref, f32[2,64,128]{2,1,0:T(8,128)S(1)} %get-tuple-element.61.gates_ref), custom_call_target="tpu_custom_call" | custom-call | flops 75497472 | bytes 589824 | tf_op jit(solution)/shard_map/combine/pallas_call | solution.py:392
  (22 shorter events, 2.9 us)
Async XLA Ops:
  1.5 7.3 %collective-permute-start = (bf16[3,4096]{1,0:T(4,128)(2,1)S(1)}, bf16[3,4096]{1,0:T(4,128)(2,1)S(1)}, u32[]{:S(2)}, u32[]{:S(2)}) collective-permute-start(bf16[3,4096]{1,0:T(4,128)(2,1)S(1)} %slice.3), channel_id=1, source_target_pairs={{0,2},{2,4},{4,6},{6,8},{8,10},{10,12},{12,14},{14,16},{16,18},{18... | collective-permute-start | bytes 73736 | tf_op jit(solution)/shard_map/ppermute | solution.py:736
  8.8 21.5 %all-to-all-start = ((bf16[8,16,2304]{2,1,0:T(8,128)(2,1)}), bf16[8,16,2304]{2,1,0:T(8,128)(2,1)S(1)}, u32[]{:S(2)}, u32[]{:S(2)}) async-start(bf16[8,16,2304]{2,1,0:T(8,128)(2,1)} %bitcast.5), calls=%async_computation | async-start | bytes 1179648 | tf_op jit(solution)/shard_map/all_to_all | solution.py:701
  15.5 11.5 %collective-permute-start.1 = (f32[64,8]{1,0:T(8,128)S(1)}, f32[64,8]{1,0:T(8,128)S(1)}, u32[]{:S(2)}, u32[]{:S(2)}) collective-permute-start(f32[64,8]{1,0:T(8,128)S(1)} %get-tuple-element.57.refs_0_), channel_id=1, source_target_pairs={{0,1},{1,0},{2,3},{3,2},{4,5},{5,4},{6,7},{7,6},{8,9},{9,8},{10,11... | collective-permute-start | bytes 6152 | tf_op jit(solution)/shard_map/ppermute | solution.py:688
  30.4 13.2 %collective-permute-start.2 = (bf16[144,2048]{1,0:T(8,128)(2,1)S(1)}, bf16[144,2048]{1,0:T(8,128)(2,1)S(1)}, u32[]{:S(2)}, u32[]{:S(2)}) collective-permute-start(bf16[144,2048]{1,0:T(8,128)(2,1)S(1)} %unpack.1.x_ref), channel_id=1, source_target_pairs={{0,2},{2,0},{4,6},{6,4},{8,10},{10,8},{12,14},{14,12},{16,18},{18,... | collective-permute-start | bytes 1769480 | tf_op jit(solution)/shard_map/ppermute | solution.py:693
  43.6 6.9 %collective-permute-start.5 = (bf16[144,6144]{1,0:T(8,128)(2,1)S(1)}, bf16[144,6144]{1,0:T(8,128)(2,1)S(1)}, u32[]{:S(2)}, u32[]{:S(2)}) collective-permute-start(bf16[144,6144]{1,0:T(8,128)(2,1)S(1)} %get-tuple-element.41.refs_0_), channel_id=1, source_target_pairs={{0,1},{1,0},{2,3},{3,2},{4,5},{5,4},{6,7},{7,6},{8,9},{9,8},{10,11... | collective-permute-start | bytes 5308424 | tf_op jit(solution)/shard_map/ppermute | solution.py:688
  43.6 6.7 %collective-permute-start.3 = (bf16[16,4608]{1,0:T(8,128)(2,1)S(1)}, bf16[16,4608]{1,0:T(8,128)(2,1)S(1)}, u32[]{:S(2)}, u32[]{:S(2)}) collective-permute-start(bf16[16,4608]{1,0:T(8,128)(2,1)S(1)} %get-tuple-element.40.refs_0_), channel_id=1, source_target_pairs={{0,2},{2,0},{4,6},{6,4},{8,10},{10,8},{12,14},{14,12},{16,18},{18,... | collective-permute-start | bytes 442376 | tf_op jit(solution)/shard_map/ppermute | solution.py:683
  44.2 6.1 %copy-start = (f32[16,4096]{1,0:T(8,128)S(1)}, f32[16,4096]{1,0:T(8,128)}, u32[]{:S(2)}) copy-start(f32[16,4096]{1,0:T(8,128)} %alog_ref.3) | copy-start | bytes 786436
  50.5 3.8 %collective-permute-start.6 = (bf16[144,6144]{1,0:T(8,128)(2,1)S(1)}, bf16[144,6144]{1,0:T(8,128)(2,1)S(1)}, u32[]{:S(2)}, u32[]{:S(2)}) collective-permute-start(bf16[144,6144]{1,0:T(8,128)(2,1)S(1)} %gate.3.refs_0_), channel_id=1, source_target_pairs={{0,1},{1,0},{2,3},{3,2},{4,5},{5,4},{6,7},{7,6},{8,9},{9,8},{10,11... | collective-permute-start | bytes 5308424 | tf_op jit(solution)/shard_map/ppermute | solution.py:688
  50.8 12.9 %collective-permute-start.4 = (bf16[16,4608]{1,0:T(8,128)(2,1)S(1)}, bf16[16,4608]{1,0:T(8,128)(2,1)S(1)}, u32[]{:S(2)}, u32[]{:S(2)}) collective-permute-start(bf16[16,4608]{1,0:T(8,128)(2,1)S(1)} %get-tuple-element.45.refs_0_), channel_id=1, source_target_pairs={{0,4},{2,6},{4,0},{6,2},{8,12},{10,14},{12,8},{14,10},{16,20},{18,... | collective-permute-start | bytes 442376 | tf_op jit(solution)/shard_map/ppermute | solution.py:683
  63.9 15.5 %collective-permute-start.10 = (bf16[144,2048]{1,0:T(8,128)(2,1)S(1)}, bf16[144,2048]{1,0:T(8,128)(2,1)S(1)}, u32[]{:S(2)}, u32[]{:S(2)}) collective-permute-start(bf16[144,2048]{1,0:T(8,128)(2,1)S(1)} %down.2), channel_id=1, source_target_pairs={{0,2},{2,0},{4,6},{6,4},{8,10},{10,8},{12,14},{14,12},{16,18},{18,... | collective-permute-start | bytes 1769480 | tf_op jit(solution)/shard_map/ppermute | solution.py:693
  65.3 15.3 %collective-permute-start.9 = (bf16[16,4608]{1,0:T(8,128)(2,1)S(1)}, bf16[16,4608]{1,0:T(8,128)(2,1)S(1)}, u32[]{:S(2)}, u32[]{:S(2)}) collective-permute-start(bf16[16,4608]{1,0:T(8,128)(2,1)S(1)} %get-tuple-element.50), channel_id=1, source_target_pairs={{0,24},{2,26},{4,28},{6,30},{8,16},{10,18},{12,20},{14,22},{16,8},... | collective-permute-start | bytes 442376 | tf_op jit(solution)/shard_map/ppermute | solution.py:683
  68.4 12.8 %collective-permute-start.8 = (bf16[16,4608]{1,0:T(8,128)(2,1)S(1)}, bf16[16,4608]{1,0:T(8,128)(2,1)S(1)}, u32[]{:S(2)}, u32[]{:S(2)}) collective-permute-start(bf16[16,4608]{1,0:T(8,128)(2,1)S(1)} %get-tuple-element.50), channel_id=1, source_target_pairs={{0,16},{2,18},{4,20},{6,22},{8,24},{10,26},{12,28},{14,30},{16,0},... | collective-permute-start | bytes 442376 | tf_op jit(solution)/shard_map/ppermute | solution.py:683
  68.4 12.8 %collective-permute-start.7 = (bf16[16,4608]{1,0:T(8,128)(2,1)S(1)}, bf16[16,4608]{1,0:T(8,128)(2,1)S(1)}, u32[]{:S(2)}, u32[]{:S(2)}) collective-permute-start(bf16[16,4608]{1,0:T(8,128)(2,1)S(1)} %get-tuple-element.50), channel_id=1, source_target_pairs={{0,8},{2,10},{4,12},{6,14},{8,0},{10,2},{12,4},{14,6},{16,24},{18,... | collective-permute-start | bytes 442376 | tf_op jit(solution)/shard_map/ppermute | solution.py:683
  81.2 0.7 copy-start.1
  81.9 20.1 %all-to-all-start.1 = ((bf16[8,16,2304]{2,1,0:T(8,128)(2,1)}), bf16[8,16,2304]{2,1,0:T(8,128)(2,1)S(1)}, u32[]{:S(2)}, u32[]{:S(2)}) async-start(bf16[8,16,2304]{2,1,0:T(8,128)(2,1)} %pack_sum.1), calls=%async_computation.1 | async-start | bytes 1179648 | tf_op jit(solution)/shard_map/all_to_all | solution.py:701
  87.6 0.9 copy-start.2

commit v14 on v13

--- a/solution.py
+++ b/solution.py
@@ -199,14 +199,24 @@
     lax.fori_loop(0, count, step, 0)
 
 
-def gate_first_kernel(chunk, x_ref, w_ref, out_ref, kept_ref, held_ref, kept_sems, sems):
-    start = kept_ref.shape[1]
+def gate_first_kernel(
+    chunk, x_ref, w_ref, down_ref, out_ref, kept_ref, kept_down_ref, held_ref, kept_sems, sems, down_sems
+):
+    start, columns = kept_ref.shape[1], kept_down_ref.shape[1]
     one = chunk_copy(w_ref.at[:, :start], kept_ref, kept_sems, 1, chunk)
     two = chunk_copy(w_ref.at[:, start:], held_ref, sems, 1, chunk)
+    copy, count = chunk_copy(
+        down_ref.at[:, :columns], kept_down_ref, down_sems, 0, kept_down_ref.shape[0] // down_sems.shape[0]
+    )
     streamed(one, gate_product(chunk, x_ref, kept_ref, out_ref, 0), follow=two)
-    for i in range(min(AHEAD, one[1]), min(AHEAD, two[1])):
+    started = min(AHEAD, one[1])
+    for i in range(started, min(AHEAD, two[1])):
         two[0](i).start()
+    for i in range(count):
+        copy(i).start()
     streamed(two, gate_product(chunk, x_ref, held_ref, out_ref, start), begun=True)
+    for i in range(count):
+        copy(i).wait()
 
 
 def gate_product(chunk, x_ref, from_ref, out_ref, offset):
@@ -228,7 +238,7 @@
     )
 
 
-def gate(x, w_gate, kept=None):
+def gate(x, w_gate, w_down, kept=None):
     rows, features = x.shape
     amount = w_gate.shape[1]
     chunk = math.gcd(512, amount)
@@ -237,7 +247,7 @@
     rest = [pltpu.VMEM((features, amount - half), BF16)]
     rest_sems = pltpu.SemaphoreType.DMA(((amount - half) // chunk,))
     hints = dict(
-        compiler_params=params(32),
+        compiler_params=params(20),
         cost_estimate=cost(2 * rows * features * amount, features * amount * 2),
         name="gate",
     )
@@ -252,12 +262,21 @@
         )(x, *in_hbm(w_gate), kept)
     return pl.pallas_call(
         functools.partial(gate_first_kernel, chunk),
-        in_specs=[INSIDE, ANYWHERE],
-        out_specs=(INSIDE, INSIDE),
-        out_shape=(out, jax.ShapeDtypeStruct((features, half), BF16)),
-        scratch_shapes=rest + [pltpu.SemaphoreType.DMA((half // chunk,)), rest_sems],
+        in_specs=[INSIDE, ANYWHERE, ANYWHERE],
+        out_specs=(INSIDE, INSIDE, INSIDE),
+        out_shape=(
+            out,
+            jax.ShapeDtypeStruct((features, half), BF16),
+            jax.ShapeDtypeStruct((w_down.shape[0], w_down.shape[1] // 2), BF16),
+        ),
+        scratch_shapes=rest
+        + [
+            pltpu.SemaphoreType.DMA((half // chunk,)),
+            rest_sems,
+            pltpu.SemaphoreType.DMA((4,)),
+        ],
         **hints,
-    )(x, *in_hbm(w_gate))
+    )(x, *in_hbm(w_gate, w_down))
 
 
 def fill_acted(chunk, part_refs, acted_ref):
@@ -272,36 +291,48 @@
 
 
 def down_kernel(chunk, *refs):
-    part_refs, w_ref, out_ref, acted_ref, held_ref, sems = refs[:-5], *refs[-5:]
-
-    def use(i):
-        at = pl.ds(pl.multiple_of(i * chunk, chunk), chunk)
-        out_ref[:, at] = dot(acted_ref[...], held_ref[:, at]).astype(out_ref.dtype)
+    part_refs, w_ref, kept_ref, out_ref, acted_ref, held_ref, sems = refs[:-6], *refs[-6:]
+    start = kept_ref.shape[1]
+    wide = math.gcd(512, start)
+
+    def product(from_ref, offset, width):
+        def use(i):
+            at = pl.ds(pl.multiple_of(i * width, width), width)
+            to = pl.ds(pl.multiple_of(offset + i * width, math.gcd(offset, width)), width)
+            out_ref[:, to] = dot(acted_ref[...], from_ref[:, at]).astype(out_ref.dtype)
+
+        return use
 
     def begin():
         fill_acted(math.gcd(512, acted_ref.shape[1]), part_refs, acted_ref)
-
-    streamed(chunk_copy(w_ref, held_ref, sems, 1, chunk), use, begin)
-
-
-def down(parts, w_down, dtype):
+        pl.loop(0, start // wide)(product(kept_ref, 0, wide))
+
+    streamed(
+        chunk_copy(w_ref.at[:, start:], held_ref, sems, 1, chunk),
+        product(held_ref, start, chunk),
+        begin,
+    )
+
+
+def down(parts, w_down, kept, dtype):
     rows, amount = parts[0].shape
     features = w_down.shape[1]
-    chunk = math.gcd(256, features)
+    rest = features - kept.shape[1]
+    chunk = math.gcd(256, rest)
     return pl.pallas_call(
         functools.partial(down_kernel, chunk),
-        in_specs=[INSIDE] * len(parts) + [ANYWHERE],
+        in_specs=[INSIDE] * len(parts) + [ANYWHERE, INSIDE],
         out_specs=INSIDE,
         out_shape=jax.ShapeDtypeStruct((rows, features), dtype),
         scratch_shapes=[
             pltpu.VMEM((rows, amount), BF16),
-            pltpu.VMEM(w_down.shape, BF16),
-            pltpu.SemaphoreType.DMA((features // chunk,)),
+            pltpu.VMEM((amount, rest), BF16),
+            pltpu.SemaphoreType.DMA((rest // chunk,)),
         ],
-        compiler_params=params(48),
+        compiler_params=params(22),
         cost_estimate=cost(2 * rows * features * amount, features * amount * 2),
         name="down",
-    )(*parts, *in_hbm(w_down))
+    )(*parts, *in_hbm(w_down), kept)
 
 
 def unpack_kernel(pack, arrived_ref, out_ref):
@@ -765,9 +796,9 @@
     for part in rows:
         if gated:
             part = after(part, gated[-1][0])
-            own = gate(part, w_gate, kept)
+            own = gate(part, w_gate, w_down, kept)
         else:
-            own, kept = gate(part, w_gate)
+            own, kept, kept_down = gate(part, w_gate, w_down)
             own, received = after((own, ends), *rows[1:])
             received = swapped(received, 1)
         if len(gated) == copies - 1:
@@ -775,7 +806,7 @@
         gated.append([own] + [turned(own, "exp", d) for d in range(1, feature_parts)])
     made = []
     for parts in gated[1:] + gated[:1]:
-        product = down(parts, w_down, BF16 if len(made) < copies - 1 else F32)
+        product = down(parts, w_down, kept_down, BF16 if len(made) < copies - 1 else F32)
         if not made:
             product = after(product, advance(product))
         made.append(product)

time: 104 us -> 99.6 us (0.958)
  Pallas kernels: 60.3 us -> 56.5 us
  local copies, waits for them, and re-layouts: 2.43 us -> 0.87 us
  waiting for transfers between devices: 14.7 us -> 16 us
    pallas_call x2, Pallas kernels: 18.7 us -> 11.8 us  [down(): pl.pallas_call(functools.partial(down_kernel, chunk), in_specs=[INSIDE] *...]
    pallas_call x1, Pallas kernels: 9.21 us -> 12.4 us  [gate(): pl.pallas_call(functools.partial(gate_first_kernel, chunk), in_specs=[INS...]
    unnamed x6 -> x2, local copies, waits for them, and re-layouts: 1.57 us -> 0.01 us
  transfers between devices with their start and end apart: 13 -> 13, of which waited for: 6 -> 5; matrix products, arithmetic and copies ran while one was open for 0% -> 0% of each run, Pallas kernels for 57% -> 56%
where the time goes in v14:
time: 99.6 us; the launch traced here: 99 us
  Pallas kernels  56.5 us (57%)
  starting transfers between devices  24.9 us (25%)
  waiting for transfers between devices  16 us (16%)
    pallas_call x1, Pallas kernels, gate(): pl.pallas_call(functools.partial(gate_first_kernel, chunk), in_specs=[INS...  12.4 us
    pallas_call x2, Pallas kernels, down(): pl.pallas_call(functools.partial(down_kernel, chunk), in_specs=[INSIDE] *...  11.8 us
    pallas_call x1, Pallas kernels, scan(): pl.pallas_call(scan_kernel, grid=(channels // lanes,), in_specs=[cut(toke...  11.5 us
    all_to_all x2, starting transfers between devices, exchanged(): lax.all_to_all(value, 'seq', split_axis=0, concat_axis=0, tiled=True, axi...  11.2 us
    all_to_all x2, waiting for transfers between devices, exchanged(): lax.all_to_all(value, 'seq', split_axis=0, concat_axis=0, tiled=True, axi...  9.22 us
    pallas_call x1, Pallas kernels, finish(): pl.pallas_call(functools.partial(finish_kernel, step), grid=(channels //...  8.45 us
    ppermute x5, starting transfers between devices, swapped(): return lax.ppermute(value, 'seq', [(i, i ^ by) for i in range(count)])  7.2 us
    pallas_call x1, Pallas kernels, gate(): pl.pallas_call(functools.partial(gate_next_kernel, chunk), in_specs=[INSI...  6.07 us
  transfers between devices with their start and end apart: 13, of which 5 were waited for; matrix products, arithmetic and copies ran while one was open for 0% of the time, Pallas kernels for 56%

profile of v14, /device:TPU:0, one launch (start us, length us, event | category | flops | bytes accessed | tf_op | source)
XLA Modules:
  0.0 99.0 jit_solution(1418147029189473419)
XLA Ops:
  0.6 0.9 slice.3
  1.5 4.8 %collective-permute-start = (bf16[3,4096]{1,0:T(4,128)(2,1)S(1)}, bf16[3,4096]{1,0:T(4,128)(2,1)S(1)}, u32[]{:S(2)}, u32[]{:S(2)}) collective-permute-start(bf16[3,4096]{1,0:T(4,128)(2,1)S(1)} %slice.3), channel_id=1, source_target_pairs={{0,2},{2,4},{4,6},{6,8},{8,10},{10,12},{12,14},{14,16},{16,18},{18... | collective-permute-start | bytes 73736 | tf_op jit(solution)/shard_map/ppermute | solution.py:767
  6.3 2.4 %route.1 = (bf16[8,1,16,2304]{3,2,1,0:T(8,128)(2,1)}, f32[64,8]{1,0:T(8,128)S(1)}) custom-call(s32[2,64]{1,0:T(2,128)} %bitcast.7, bf16[64,2048]{1,0:T(8,128)(2,1)} %hidden_ref.1, bf16[8,2048]{1,0:T(8,128)(2,1)} %bitcast.6), custom_call_target="tpu_custom_call" | custom-call | flops 67108864 | bytes 1048576 | tf_op jit(solution)/shard_map/route/pallas_call | solution.py:102
  8.8 6.7 %all-to-all-start = ((bf16[8,16,2304]{2,1,0:T(8,128)(2,1)}), bf16[8,16,2304]{2,1,0:T(8,128)(2,1)S(1)}, u32[]{:S(2)}, u32[]{:S(2)}) async-start(bf16[8,16,2304]{2,1,0:T(8,128)(2,1)} %bitcast.5), calls=%async_computation | async-start | bytes 1179648 | tf_op jit(solution)/shard_map/all_to_all | solution.py:732
  15.5 11.5 %scan.1 = (f32[64,4096]{1,0:T(8,128)}, f32[64,4096]{1,0:T(8,128)}, bf16[16,4608]{1,0:T(8,128)(2,1)S(1)}) custom-call(bf16[64,4096]{1,0:T(8,128)(2,1)} %x_ref.1, bf16[3,4096]{1,0:T(4,128)(2,1)S(1)} %collective-permute-done.edge_ref, bf16[64,256]{1,0:T(8,128)(2,1)} %low_ref.1, bf16[256,4096]{1,0:T(8,128)(2,1)} %dtw_ref.1, f32[1,4096]{1,0:T(1,128)} %bitcast.9, ...), custom_call_target="tpu_custom_call" | custom-call | flops 33554432 | bytes 3145728 | tf_op jit(solution)/shard_map/scan/pallas_call | solution.py:537
  27.0 3.2 %all-to-all-done.arrived_ref = bf16[8,16,2304]{2,1,0:T(8,128)(2,1)S(1)} async-done(((bf16[8,16,2304]{2,1,0:T(8,128)(2,1)}), bf16[8,16,2304]{2,1,0:T(8,128)(2,1)S(1)}, u32[]{:S(2)}, u32[]{:S(2)}) %all-to-all-start) | async-done | bytes 589856 | tf_op jit(solution)/shard_map/all_to_all | solution.py:732
  30.4 0.6 collective-permute-start.2
  31.0 12.4 %gate.2 = (bf16[144,6144]{1,0:T(8,128)(2,1)S(1)}, bf16[2048,3072]{1,0:T(8,128)(2,1)S(1)}, bf16[6144,1024]{1,0:T(8,128)(2,1)S(1)}) custom-call(bf16[144,2048]{1,0:T(8,128)(2,1)S(1)} %unpack.1.x_ref, bf16[2048,6144]{1,0:T(8,128)(2,1)} %w_ref.3, bf16[6144,2048]{1,0:T(8,128)(2,1)} %refs_2_.7), custom_call_target="tpu_custom_call" | custom-call | flops 3623878656 | bytes 25165824 | tf_op jit(solution)/shard_map/gate/pallas_call | solution.py:263
  43.6 1.4 %collective-permute-start.3 = (bf16[16,4608]{1,0:T(8,128)(2,1)S(1)}, bf16[16,4608]{1,0:T(8,128)(2,1)S(1)}, u32[]{:S(2)}, u32[]{:S(2)}) collective-permute-start(bf16[16,4608]{1,0:T(8,128)(2,1)S(1)} %get-tuple-element.41.refs_0_), channel_id=1, source_target_pairs={{0,2},{2,0},{4,6},{6,4},{8,10},{10,8},{12,14},{14,12},{16,18},{18,... | collective-permute-start | bytes 442376 | tf_op jit(solution)/shard_map/ppermute | solution.py:714
  45.0 6.1 %gate.3.refs_0_ = bf16[144,6144]{1,0:T(8,128)(2,1)S(1)} custom-call(bf16[144,2048]{1,0:T(8,128)(2,1)S(1)} %collective-permute-done.2.x_ref, bf16[2048,6144]{1,0:T(8,128)(2,1)} %w_ref.3, bf16[2048,3072]{1,0:T(8,128)(2,1)S(1)} %get-tuple-element.44.kept_ref), custom_call_target="tpu_custom_call" | custom-call | flops 3623878656 | bytes 25165824 | tf_op jit(solution)/shard_map/gate/pallas_call | solution.py:255
  51.5 1.4 %collective-permute-start.4 = (bf16[16,4608]{1,0:T(8,128)(2,1)S(1)}, bf16[16,4608]{1,0:T(8,128)(2,1)S(1)}, u32[]{:S(2)}, u32[]{:S(2)}) collective-permute-start(bf16[16,4608]{1,0:T(8,128)(2,1)S(1)} %get-tuple-element.46.refs_0_), channel_id=1, source_target_pairs={{0,4},{2,6},{4,0},{6,2},{8,12},{10,14},{12,8},{14,10},{16,20},{18,... | collective-permute-start | bytes 442376 | tf_op jit(solution)/shard_map/ppermute | solution.py:714
  53.0 2.1 %collective-permute-done.6.refs_1_ = bf16[144,6144]{1,0:T(8,128)(2,1)S(1)} collective-permute-done((bf16[144,6144]{1,0:T(8,128)(2,1)S(1)}, bf16[144,6144]{1,0:T(8,128)(2,1)S(1)}, u32[]{:S(2)}, u32[]{:S(2)}) %collective-permute-start.6) | collective-permute-done | bytes 1769504 | tf_op jit(solution)/shard_map/ppermute | solution.py:719
  55.0 5.9 %down.2 = bf16[144,2048]{1,0:T(8,128)(2,1)S(1)} custom-call(bf16[144,6144]{1,0:T(8,128)(2,1)S(1)} %gate.3.refs_0_, bf16[144,6144]{1,0:T(8,128)(2,1)S(1)} %collective-permute-done.6.refs_1_, bf16[6144,2048]{1,0:T(8,128)(2,1)} %refs_2_.7, bf16[6144,1024]{1,0:T(8,128)(2,1)S(1)} %get-tuple-element.49.refs_3_), custom_call_target="tpu_custom_call" | custom-call | flops 3623878656 | bytes 25165824 | tf_op jit(solution)/shard_map/down/pallas_call | solution.py:322
  61.1 0.7 collective-permute-start.10
  61.9 3.1 %collective-permute-start.9 = (bf16[16,4608]{1,0:T(8,128)(2,1)S(1)}, bf16[16,4608]{1,0:T(8,128)(2,1)S(1)}, u32[]{:S(2)}, u32[]{:S(2)}) collective-permute-start(bf16[16,4608]{1,0:T(8,128)(2,1)S(1)} %get-tuple-element.52), channel_id=1, source_target_pairs={{0,24},{2,26},{4,28},{6,30},{8,16},{10,18},{12,20},{14,22},{16,8},... | collective-permute-start | bytes 442376 | tf_op jit(solution)/shard_map/ppermute | solution.py:714
  65.0 1.3 %collective-permute-start.7 = (bf16[16,4608]{1,0:T(8,128)(2,1)S(1)}, bf16[16,4608]{1,0:T(8,128)(2,1)S(1)}, u32[]{:S(2)}, u32[]{:S(2)}) collective-permute-start(bf16[16,4608]{1,0:T(8,128)(2,1)S(1)} %get-tuple-element.52), channel_id=1, source_target_pairs={{0,8},{2,10},{4,12},{6,14},{8,0},{10,2},{12,4},{14,6},{16,24},{18,... | collective-permute-start | bytes 442376 | tf_op jit(solution)/shard_map/ppermute | solution.py:714
  66.2 5.9 %down.3.refs_0_ = f32[144,2048]{1,0:T(8,128)S(1)} custom-call(bf16[144,6144]{1,0:T(8,128)(2,1)S(1)} %get-tuple-element.42.refs_0_, bf16[144,6144]{1,0:T(8,128)(2,1)S(1)} %collective-permute-done.5.refs_1_, bf16[6144,2048]{1,0:T(8,128)(2,1)} %refs_2_.7, bf16[6144,1024]{1,0:T(8,128)(2,1)S(1)} %get-tuple-element.49.refs_3_), custom_call_target="tpu_custom_call" | custom-call | flops 3623878656 | bytes 25165824 | tf_op jit(solution)/shard_map/down/pallas_call | solution.py:322
  72.1 4.5 %collective-permute-done.10.refs_1_ = bf16[144,2048]{1,0:T(8,128)(2,1)S(1)} collective-permute-done((bf16[144,2048]{1,0:T(8,128)(2,1)S(1)}, bf16[144,2048]{1,0:T(8,128)(2,1)S(1)}, u32[]{:S(2)}, u32[]{:S(2)}) %collective-permute-start.10) | collective-permute-done | bytes 589856 | tf_op jit(solution)/shard_map/ppermute | solution.py:724
  76.6 1.2 %pack_sum.1 = bf16[8,16,2304]{2,1,0:T(8,128)(2,1)} custom-call(f32[144,2048]{1,0:T(8,128)S(1)} %down.3.refs_0_, bf16[144,2048]{1,0:T(8,128)(2,1)S(1)} %collective-permute-done.10.refs_1_), custom_call_target="tpu_custom_call" | custom-call | flops 4718592 | bytes 2359296 | tf_op jit(solution)/shard_map/pack_sum/pallas_call | solution.py:392
  77.9 4.5 %all-to-all-start.1 = ((bf16[8,16,2304]{2,1,0:T(8,128)(2,1)}), bf16[8,16,2304]{2,1,0:T(8,128)(2,1)S(1)}, u32[]{:S(2)}, u32[]{:S(2)}) async-start(bf16[8,16,2304]{2,1,0:T(8,128)(2,1)} %pack_sum.1), calls=%async_computation.1 | async-start | bytes 1179648 | tf_op jit(solution)/shard_map/all_to_all | solution.py:732
  82.4 1.0 %blend_weights.1 = (bf16[2,64,128]{2,1,0:T(8,128)(2,1)S(1)}, bf16[2,64,128]{2,1,0:T(8,128)(2,1)S(1)}, f32[2,64,128]{2,1,0:T(8,128)S(1)}) custom-call(s32[2,64]{1,0:T(2,128)} %bitcast.8, f32[64,8]{1,0:T(8,128)S(1)} %get-tuple-element.59.refs_0_, f32[64,8]{1,0:T(8,128)S(1)} %collective-permute-done.1.refs_1_), custom_call_target="tpu_custom_call" | custom-call | flops 262144 | bytes 65536 | tf_op jit(solution)/shard_map/blend_weights/pallas_call | solution.py:147
  83.4 8.5 %finish.1 = bf16[64,4096]{1,0:T(8,128)(2,1)} custom-call(f32[64,4096]{1,0:T(8,128)} %get-tuple-element.33.read_ref, f32[64,4096]{1,0:T(8,128)} %get-tuple-element.34.cum_ref, bf16[64,4096]{1,0:T(8,128)(2,1)} %z_ref.1, f32[16,4096]{1,0:T(8,128)} %alog_ref.3, f32[2,16,64]{2,1,0:T(8,128)} %bc_ref.3, bf16[16,4608]{1,0:T(8,128)(2,1)S(1)} %get-tuple-element.51.prefix_ref.refs_3_, ...), custom_call_target="tpu_custom_call" | custom-call | flops 20971520 | bytes 3145728 | tf_op jit(solution)/shard_map/finish/pallas_call | solution.py:688
  91.9 6.0 %all-to-all-done.1.back_ref = bf16[8,16,2304]{2,1,0:T(8,128)(2,1)S(1)} async-done(((bf16[8,16,2304]{2,1,0:T(8,128)(2,1)}), bf16[8,16,2304]{2,1,0:T(8,128)(2,1)S(1)}, u32[]{:S(2)}, u32[]{:S(2)}) %all-to-all-start.1) | async-done | bytes 589856 | tf_op jit(solution)/shard_map/all_to_all | solution.py:732
  97.9 1.1 %combine.1 = bf16[64,2048]{1,0:T(8,128)(2,1)} custom-call(bf16[8,16,2304]{2,1,0:T(8,128)(2,1)S(1)} %all-to-all-done.1.back_ref, bf16[2,64,128]{2,1,0:T(8,128)(2,1)S(1)} %get-tuple-element.61.main_ref, bf16[2,64,128]{2,1,0:T(8,128)(2,1)S(1)} %get-tuple-element.62.extra_ref, f32[2,64,128]{2,1,0:T(8,128)S(1)} %get-tuple-element.63.gates_ref), custom_call_target="tpu_custom_call" | custom-call | flops 75497472 | bytes 589824 | tf_op jit(solution)/shard_map/combine/pallas_call | solution.py:423
  (18 shorter events, 1.0 us)
Async XLA Ops:
  1.5 7.3 %collective-permute-start = (bf16[3,4096]{1,0:T(4,128)(2,1)S(1)}, bf16[3,4096]{1,0:T(4,128)(2,1)S(1)}, u32[]{:S(2)}, u32[]{:S(2)}) collective-permute-start(bf16[3,4096]{1,0:T(4,128)(2,1)S(1)} %slice.3), channel_id=1, source_target_pairs={{0,2},{2,4},{4,6},{6,8},{8,10},{10,12},{12,14},{14,16},{16,18},{18... | collective-permute-start | bytes 73736 | tf_op jit(solution)/shard_map/ppermute | solution.py:767
  8.8 21.5 %all-to-all-start = ((bf16[8,16,2304]{2,1,0:T(8,128)(2,1)}), bf16[8,16,2304]{2,1,0:T(8,128)(2,1)S(1)}, u32[]{:S(2)}, u32[]{:S(2)}) async-start(bf16[8,16,2304]{2,1,0:T(8,128)(2,1)} %bitcast.5), calls=%async_computation | async-start | bytes 1179648 | tf_op jit(solution)/shard_map/all_to_all | solution.py:732
  15.5 11.5 %collective-permute-start.1 = (f32[64,8]{1,0:T(8,128)S(1)}, f32[64,8]{1,0:T(8,128)S(1)}, u32[]{:S(2)}, u32[]{:S(2)}) collective-permute-start(f32[64,8]{1,0:T(8,128)S(1)} %get-tuple-element.59.refs_0_), channel_id=1, source_target_pairs={{0,1},{1,0},{2,3},{3,2},{4,5},{5,4},{6,7},{7,6},{8,9},{9,8},{10,11... | collective-permute-start | bytes 6152 | tf_op jit(solution)/shard_map/ppermute | solution.py:719
  30.4 13.2 %collective-permute-start.2 = (bf16[144,2048]{1,0:T(8,128)(2,1)S(1)}, bf16[144,2048]{1,0:T(8,128)(2,1)S(1)}, u32[]{:S(2)}, u32[]{:S(2)}) collective-permute-start(bf16[144,2048]{1,0:T(8,128)(2,1)S(1)} %unpack.1.x_ref), channel_id=1, source_target_pairs={{0,2},{2,0},{4,6},{6,4},{8,10},{10,8},{12,14},{14,12},{16,18},{18,... | collective-permute-start | bytes 1769480 | tf_op jit(solution)/shard_map/ppermute | solution.py:724
  43.6 7.6 %collective-permute-start.5 = (bf16[144,6144]{1,0:T(8,128)(2,1)S(1)}, bf16[144,6144]{1,0:T(8,128)(2,1)S(1)}, u32[]{:S(2)}, u32[]{:S(2)}) collective-permute-start(bf16[144,6144]{1,0:T(8,128)(2,1)S(1)} %get-tuple-element.42.refs_0_), channel_id=1, source_target_pairs={{0,1},{1,0},{2,3},{3,2},{4,5},{5,4},{6,7},{7,6},{8,9},{9,8},{10,11... | collective-permute-start | bytes 5308424 | tf_op jit(solution)/shard_map/ppermute | solution.py:719
  43.6 7.5 %collective-permute-start.3 = (bf16[16,4608]{1,0:T(8,128)(2,1)S(1)}, bf16[16,4608]{1,0:T(8,128)(2,1)S(1)}, u32[]{:S(2)}, u32[]{:S(2)}) collective-permute-start(bf16[16,4608]{1,0:T(8,128)(2,1)S(1)} %get-tuple-element.41.refs_0_), channel_id=1, source_target_pairs={{0,2},{2,0},{4,6},{6,4},{8,10},{10,8},{12,14},{14,12},{16,18},{18,... | collective-permute-start | bytes 442376 | tf_op jit(solution)/shard_map/ppermute | solution.py:714
  45.0 6.1 %copy-start = (f32[16,4096]{1,0:T(8,128)S(1)}, f32[16,4096]{1,0:T(8,128)}, u32[]{:S(2)}) copy-start(f32[16,4096]{1,0:T(8,128)} %alog_ref.3) | copy-start | bytes 786436
  51.3 3.8 %collective-permute-start.6 = (bf16[144,6144]{1,0:T(8,128)(2,1)S(1)}, bf16[144,6144]{1,0:T(8,128)(2,1)S(1)}, u32[]{:S(2)}, u32[]{:S(2)}) collective-permute-start(bf16[144,6144]{1,0:T(8,128)(2,1)S(1)} %gate.3.refs_0_), channel_id=1, source_target_pairs={{0,1},{1,0},{2,3},{3,2},{4,5},{5,4},{6,7},{7,6},{8,9},{9,8},{10,11... | collective-permute-start | bytes 5308424 | tf_op jit(solution)/shard_map/ppermute | solution.py:719
  51.5 9.4 %collective-permute-start.4 = (bf16[16,4608]{1,0:T(8,128)(2,1)S(1)}, bf16[16,4608]{1,0:T(8,128)(2,1)S(1)}, u32[]{:S(2)}, u32[]{:S(2)}) collective-permute-start(bf16[16,4608]{1,0:T(8,128)(2,1)S(1)} %get-tuple-element.46.refs_0_), channel_id=1, source_target_pairs={{0,4},{2,6},{4,0},{6,2},{8,12},{10,14},{12,8},{14,10},{16,20},{18,... | collective-permute-start | bytes 442376 | tf_op jit(solution)/shard_map/ppermute | solution.py:714
  61.1 15.5 %collective-permute-start.10 = (bf16[144,2048]{1,0:T(8,128)(2,1)S(1)}, bf16[144,2048]{1,0:T(8,128)(2,1)S(1)}, u32[]{:S(2)}, u32[]{:S(2)}) collective-permute-start(bf16[144,2048]{1,0:T(8,128)(2,1)S(1)} %down.2), channel_id=1, source_target_pairs={{0,2},{2,0},{4,6},{6,4},{8,10},{10,8},{12,14},{14,12},{16,18},{18,... | collective-permute-start | bytes 1769480 | tf_op jit(solution)/shard_map/ppermute | solution.py:724
  61.9 16.0 %collective-permute-start.9 = (bf16[16,4608]{1,0:T(8,128)(2,1)S(1)}, bf16[16,4608]{1,0:T(8,128)(2,1)S(1)}, u32[]{:S(2)}, u32[]{:S(2)}) collective-permute-start(bf16[16,4608]{1,0:T(8,128)(2,1)S(1)} %get-tuple-element.52), channel_id=1, source_target_pairs={{0,24},{2,26},{4,28},{6,30},{8,16},{10,18},{12,20},{14,22},{16,8},... | collective-permute-start | bytes 442376 | tf_op jit(solution)/shard_map/ppermute | solution.py:714
  65.0 12.9 %collective-permute-start.8 = (bf16[16,4608]{1,0:T(8,128)(2,1)S(1)}, bf16[16,4608]{1,0:T(8,128)(2,1)S(1)}, u32[]{:S(2)}, u32[]{:S(2)}) collective-permute-start(bf16[16,4608]{1,0:T(8,128)(2,1)S(1)} %get-tuple-element.52), channel_id=1, source_target_pairs={{0,16},{2,18},{4,20},{6,22},{8,24},{10,26},{12,28},{14,30},{16,0},... | collective-permute-start | bytes 442376 | tf_op jit(solution)/shard_map/ppermute | solution.py:714
  65.0 12.9 %collective-permute-start.7 = (bf16[16,4608]{1,0:T(8,128)(2,1)S(1)}, bf16[16,4608]{1,0:T(8,128)(2,1)S(1)}, u32[]{:S(2)}, u32[]{:S(2)}) collective-permute-start(bf16[16,4608]{1,0:T(8,128)(2,1)S(1)} %get-tuple-element.52), channel_id=1, source_target_pairs={{0,8},{2,10},{4,12},{6,14},{8,0},{10,2},{12,4},{14,6},{16,24},{18,... | collective-permute-start | bytes 442376 | tf_op jit(solution)/shard_map/ppermute | solution.py:714
  77.9 20.0 %all-to-all-start.1 = ((bf16[8,16,2304]{2,1,0:T(8,128)(2,1)}), bf16[8,16,2304]{2,1,0:T(8,128)(2,1)S(1)}, u32[]{:S(2)}, u32[]{:S(2)}) async-start(bf16[8,16,2304]{2,1,0:T(8,128)(2,1)} %pack_sum.1), calls=%async_computation.1 | async-start | bytes 1179648 | tf_op jit(solution)/shard_map/all_to_all | solution.py:732

commit v15 on v14

--- a/solution.py
+++ b/solution.py
@@ -772,8 +772,7 @@
     read, cum, ends = scan(
         x_in, edge, dt_low, dt_weight, dt_bias, a_log, conv_weight, conv_bias, d_skip, b_and_c
     )
-    logits = [logits] + [turned(logits, "exp", d) for d in range(1, feature_parts)]
-    arrived = after(arrived, ends, *logits)
+    arrived = after(arrived, ends)
 
     steps = blocks.bit_length() - 3
     total, prefix, received, step = ends, None, None, 0
@@ -799,10 +798,12 @@
             own = gate(part, w_gate, w_down, kept)
         else:
             own, kept, kept_down = gate(part, w_gate, w_down)
-            own, received = after((own, ends), *rows[1:])
+            own, received, logits = after((own, ends, logits), *rows[1:])
             received = swapped(received, 1)
+            logits = [logits] + [turned(logits, "exp", d) for d in range(1, feature_parts)]
         if len(gated) == copies - 1:
-            own = after(own, advance(own), *(p for parts in gated for p in parts[1:]))
+            marks = [p for parts in gated for p in parts[1:]] + logits
+            own = after(own, advance(own), *marks)
         gated.append([own] + [turned(own, "exp", d) for d in range(1, feature_parts)])
     made = []
     for parts in gated[1:] + gated[:1]:

time: 99.6 us -> 99.4 us (level)
  no operation moved by 1% of the time
where the time goes in v15:
time: 99.4 us; the launch traced here: 98.8 us
  Pallas kernels  56.6 us (57%)
  starting transfers between devices  24.6 us (25%)
  waiting for transfers between devices  16 us (16%)
    pallas_call x1, Pallas kernels, gate(): pl.pallas_call(functools.partial(gate_first_kernel, chunk), in_specs=[INS...  12.4 us
    pallas_call x2, Pallas kernels, down(): pl.pallas_call(functools.partial(down_kernel, chunk), in_specs=[INSIDE] *...  11.8 us
    pallas_call x1, Pallas kernels, scan(): pl.pallas_call(scan_kernel, grid=(channels // lanes,), in_specs=[cut(toke...  11.5 us
    all_to_all x2, starting transfers between devices, exchanged(): lax.all_to_all(value, 'seq', split_axis=0, concat_axis=0, tiled=True, axi...  10.7 us
    all_to_all x2, waiting for transfers between devices, exchanged(): lax.all_to_all(value, 'seq', split_axis=0, concat_axis=0, tiled=True, axi...  9.16 us
    pallas_call x1, Pallas kernels, finish(): pl.pallas_call(functools.partial(finish_kernel, step), grid=(channels //...  8.45 us
    ppermute x5, starting transfers between devices, swapped(): return lax.ppermute(value, 'seq', [(i, i ^ by) for i in range(count)])  7.14 us
    pallas_call x1, Pallas kernels, gate(): pl.pallas_call(functools.partial(gate_next_kernel, chunk), in_specs=[INSI...  6.13 us
  transfers between devices with their start and end apart: 13, of which 5 were waited for; matrix products, arithmetic and copies ran while one was open for 0% of the time, Pallas kernels for 56%

profile of v15, /device:TPU:0, one launch (start us, length us, event | category | flops | bytes accessed | tf_op | source)
XLA Modules:
  0.0 98.8 jit_solution(2303218547251865819)
XLA Ops:
  0.6 0.9 slice.3
  1.5 4.8 %collective-permute-start = (bf16[3,4096]{1,0:T(4,128)(2,1)S(1)}, bf16[3,4096]{1,0:T(4,128)(2,1)S(1)}, u32[]{:S(2)}, u32[]{:S(2)}) collective-permute-start(bf16[3,4096]{1,0:T(4,128)(2,1)S(1)} %slice.3), channel_id=1, source_target_pairs={{0,2},{2,4},{4,6},{6,8},{8,10},{10,12},{12,14},{14,16},{16,18},{18... | collective-permute-start | bytes 73736 | tf_op jit(solution)/shard_map/ppermute | solution.py:767
  6.3 2.4 %route.1 = (bf16[8,1,16,2304]{3,2,1,0:T(8,128)(2,1)}, f32[64,8]{1,0:T(8,128)S(1)}) custom-call(s32[2,64]{1,0:T(2,128)} %bitcast.7, bf16[64,2048]{1,0:T(8,128)(2,1)} %hidden_ref.1, bf16[8,2048]{1,0:T(8,128)(2,1)} %bitcast.6), custom_call_target="tpu_custom_call" | custom-call | flops 67108864 | bytes 1048576 | tf_op jit(solution)/shard_map/route/pallas_call | solution.py:102
  8.8 6.7 %all-to-all-start = ((bf16[8,16,2304]{2,1,0:T(8,128)(2,1)}), bf16[8,16,2304]{2,1,0:T(8,128)(2,1)S(1)}, u32[]{:S(2)}, u32[]{:S(2)}) async-start(bf16[8,16,2304]{2,1,0:T(8,128)(2,1)} %bitcast.5), calls=%async_computation | async-start | bytes 1179648 | tf_op jit(solution)/shard_map/all_to_all | solution.py:732
  15.5 11.5 %scan.1 = (f32[64,4096]{1,0:T(8,128)}, f32[64,4096]{1,0:T(8,128)}, bf16[16,4608]{1,0:T(8,128)(2,1)S(1)}) custom-call(bf16[64,4096]{1,0:T(8,128)(2,1)} %x_ref.1, bf16[3,4096]{1,0:T(4,128)(2,1)S(1)} %collective-permute-done.edge_ref, bf16[64,256]{1,0:T(8,128)(2,1)} %low_ref.1, bf16[256,4096]{1,0:T(8,128)(2,1)} %dtw_ref.1, f32[1,4096]{1,0:T(1,128)} %bitcast.9, ...), custom_call_target="tpu_custom_call" | custom-call | flops 33554432 | bytes 3145728 | tf_op jit(solution)/shard_map/scan/pallas_call | solution.py:537
  26.9 3.3 %all-to-all-done.arrived_ref = bf16[8,16,2304]{2,1,0:T(8,128)(2,1)S(1)} async-done(((bf16[8,16,2304]{2,1,0:T(8,128)(2,1)}), bf16[8,16,2304]{2,1,0:T(8,128)(2,1)S(1)}, u32[]{:S(2)}, u32[]{:S(2)}) %all-to-all-start) | async-done | bytes 589856 | tf_op jit(solution)/shard_map/all_to_all | solution.py:732
  30.4 0.6 collective-permute-start.1
  31.0 12.4 %gate.2 = (bf16[144,6144]{1,0:T(8,128)(2,1)S(1)}, bf16[2048,3072]{1,0:T(8,128)(2,1)S(1)}, bf16[6144,1024]{1,0:T(8,128)(2,1)S(1)}) custom-call(bf16[144,2048]{1,0:T(8,128)(2,1)S(1)} %unpack.1.x_ref, bf16[2048,6144]{1,0:T(8,128)(2,1)} %w_ref.3, bf16[6144,2048]{1,0:T(8,128)(2,1)} %refs_2_.7), custom_call_target="tpu_custom_call" | custom-call | flops 3623878656 | bytes 25165824 | tf_op jit(solution)/shard_map/gate/pallas_call | solution.py:263
  44.2 1.3 %collective-permute-start.2 = (bf16[16,4608]{1,0:T(8,128)(2,1)S(1)}, bf16[16,4608]{1,0:T(8,128)(2,1)S(1)}, u32[]{:S(2)}, u32[]{:S(2)}) collective-permute-start(bf16[16,4608]{1,0:T(8,128)(2,1)S(1)} %get-tuple-element.42.refs_0_), channel_id=1, source_target_pairs={{0,2},{2,0},{4,6},{6,4},{8,10},{10,8},{12,14},{14,12},{16,18},{18,... | collective-permute-start | bytes 442376 | tf_op jit(solution)/shard_map/ppermute | solution.py:714
  45.5 6.1 %gate.3.refs_0_ = bf16[144,6144]{1,0:T(8,128)(2,1)S(1)} custom-call(bf16[144,2048]{1,0:T(8,128)(2,1)S(1)} %collective-permute-done.1.x_ref, bf16[2048,6144]{1,0:T(8,128)(2,1)} %w_ref.3, bf16[2048,3072]{1,0:T(8,128)(2,1)S(1)} %get-tuple-element.45.kept_ref), custom_call_target="tpu_custom_call" | custom-call | flops 3623878656 | bytes 25165824 | tf_op jit(solution)/shard_map/gate/pallas_call | solution.py:255
  51.9 1.5 %collective-permute-start.3 = (bf16[16,4608]{1,0:T(8,128)(2,1)S(1)}, bf16[16,4608]{1,0:T(8,128)(2,1)S(1)}, u32[]{:S(2)}, u32[]{:S(2)}) collective-permute-start(bf16[16,4608]{1,0:T(8,128)(2,1)S(1)} %get-tuple-element.47.refs_0_), channel_id=1, source_target_pairs={{0,4},{2,6},{4,0},{6,2},{8,12},{10,14},{12,8},{14,10},{16,20},{18,... | collective-permute-start | bytes 442376 | tf_op jit(solution)/shard_map/ppermute | solution.py:714
  53.3 2.2 %collective-permute-done.6.refs_1_ = bf16[144,6144]{1,0:T(8,128)(2,1)S(1)} collective-permute-done((bf16[144,6144]{1,0:T(8,128)(2,1)S(1)}, bf16[144,6144]{1,0:T(8,128)(2,1)S(1)}, u32[]{:S(2)}, u32[]{:S(2)}) %collective-permute-start.6) | collective-permute-done | bytes 1769504 | tf_op jit(solution)/shard_map/ppermute | solution.py:719
  55.5 5.9 %down.2 = bf16[144,2048]{1,0:T(8,128)(2,1)S(1)} custom-call(bf16[144,6144]{1,0:T(8,128)(2,1)S(1)} %gate.3.refs_0_, bf16[144,6144]{1,0:T(8,128)(2,1)S(1)} %collective-permute-done.6.refs_1_, bf16[6144,2048]{1,0:T(8,128)(2,1)} %refs_2_.7, bf16[6144,1024]{1,0:T(8,128)(2,1)S(1)} %get-tuple-element.51.refs_3_), custom_call_target="tpu_custom_call" | custom-call | flops 3623878656 | bytes 25165824 | tf_op jit(solution)/shard_map/down/pallas_call | solution.py:322
  61.7 0.7 collective-permute-start.10
  62.4 2.0 %collective-permute-start.9 = (bf16[16,4608]{1,0:T(8,128)(2,1)S(1)}, bf16[16,4608]{1,0:T(8,128)(2,1)S(1)}, u32[]{:S(2)}, u32[]{:S(2)}) collective-permute-start(bf16[16,4608]{1,0:T(8,128)(2,1)S(1)} %get-tuple-element.54), channel_id=1, source_target_pairs={{0,24},{2,26},{4,28},{6,30},{8,16},{10,18},{12,20},{14,22},{16,8},... | collective-permute-start | bytes 442376 | tf_op jit(solution)/shard_map/ppermute | solution.py:714
  64.4 2.4 %collective-permute-start.7 = (bf16[16,4608]{1,0:T(8,128)(2,1)S(1)}, bf16[16,4608]{1,0:T(8,128)(2,1)S(1)}, u32[]{:S(2)}, u32[]{:S(2)}) collective-permute-start(bf16[16,4608]{1,0:T(8,128)(2,1)S(1)} %get-tuple-element.54), channel_id=1, source_target_pairs={{0,8},{2,10},{4,12},{6,14},{8,0},{10,2},{12,4},{14,6},{16,24},{18,... | collective-permute-start | bytes 442376 | tf_op jit(solution)/shard_map/ppermute | solution.py:714
  66.8 5.9 %down.3.refs_0_ = f32[144,2048]{1,0:T(8,128)S(1)} custom-call(bf16[144,6144]{1,0:T(8,128)(2,1)S(1)} %get-tuple-element.43.refs_0_, bf16[144,6144]{1,0:T(8,128)(2,1)S(1)} %collective-permute-done.4.refs_1_, bf16[6144,2048]{1,0:T(8,128)(2,1)} %refs_2_.7, bf16[6144,1024]{1,0:T(8,128)(2,1)S(1)} %get-tuple-element.51.refs_3_), custom_call_target="tpu_custom_call" | custom-call | flops 3623878656 | bytes 25165824 | tf_op jit(solution)/shard_map/down/pallas_call | solution.py:322
  72.7 4.4 %collective-permute-done.10.refs_1_ = bf16[144,2048]{1,0:T(8,128)(2,1)S(1)} collective-permute-done((bf16[144,2048]{1,0:T(8,128)(2,1)S(1)}, bf16[144,2048]{1,0:T(8,128)(2,1)S(1)}, u32[]{:S(2)}, u32[]{:S(2)}) %collective-permute-start.10) | collective-permute-done | bytes 589856 | tf_op jit(solution)/shard_map/ppermute | solution.py:724
  77.1 1.2 %pack_sum.1 = bf16[8,16,2304]{2,1,0:T(8,128)(2,1)} custom-call(f32[144,2048]{1,0:T(8,128)S(1)} %down.3.refs_0_, bf16[144,2048]{1,0:T(8,128)(2,1)S(1)} %collective-permute-done.10.refs_1_), custom_call_target="tpu_custom_call" | custom-call | flops 4718592 | bytes 2359296 | tf_op jit(solution)/shard_map/pack_sum/pallas_call | solution.py:392
  78.3 4.0 %all-to-all-start.1 = ((bf16[8,16,2304]{2,1,0:T(8,128)(2,1)}), bf16[8,16,2304]{2,1,0:T(8,128)(2,1)S(1)}, u32[]{:S(2)}, u32[]{:S(2)}) async-start(bf16[8,16,2304]{2,1,0:T(8,128)(2,1)} %pack_sum.1), calls=%async_computation.1 | async-start | bytes 1179648 | tf_op jit(solution)/shard_map/all_to_all | solution.py:732
  82.3 1.0 %blend_weights.1 = (bf16[2,64,128]{2,1,0:T(8,128)(2,1)S(1)}, bf16[2,64,128]{2,1,0:T(8,128)(2,1)S(1)}, f32[2,64,128]{2,1,0:T(8,128)S(1)}) custom-call(s32[2,64]{1,0:T(2,128)} %bitcast.8, f32[64,8]{1,0:T(8,128)S(1)} %get-tuple-element.61.refs_0_, f32[64,8]{1,0:T(8,128)S(1)} %collective-permute-done.5.refs_1_), custom_call_target="tpu_custom_call" | custom-call | flops 262144 | bytes 65536 | tf_op jit(solution)/shard_map/blend_weights/pallas_call | solution.py:147
  83.3 8.5 %finish.1 = bf16[64,4096]{1,0:T(8,128)(2,1)} custom-call(f32[64,4096]{1,0:T(8,128)} %get-tuple-element.34.read_ref, f32[64,4096]{1,0:T(8,128)} %get-tuple-element.35.cum_ref, bf16[64,4096]{1,0:T(8,128)(2,1)} %z_ref.1, f32[16,4096]{1,0:T(8,128)} %alog_ref.3, f32[2,16,64]{2,1,0:T(8,128)} %bc_ref.3, bf16[16,4608]{1,0:T(8,128)(2,1)S(1)} %get-tuple-element.53.prefix_ref.refs_3_, ...), custom_call_target="tpu_custom_call" | custom-call | flops 20971520 | bytes 3145728 | tf_op jit(solution)/shard_map/finish/pallas_call | solution.py:688
  91.8 5.9 %all-to-all-done.1.back_ref = bf16[8,16,2304]{2,1,0:T(8,128)(2,1)S(1)} async-done(((bf16[8,16,2304]{2,1,0:T(8,128)(2,1)}), bf16[8,16,2304]{2,1,0:T(8,128)(2,1)S(1)}, u32[]{:S(2)}, u32[]{:S(2)}) %all-to-all-start.1) | async-done | bytes 589856 | tf_op jit(solution)/shard_map/all_to_all | solution.py:732
  97.7 1.1 %combine.1 = bf16[64,2048]{1,0:T(8,128)(2,1)} custom-call(bf16[8,16,2304]{2,1,0:T(8,128)(2,1)S(1)} %all-to-all-done.1.back_ref, bf16[2,64,128]{2,1,0:T(8,128)(2,1)S(1)} %get-tuple-element.63.main_ref, bf16[2,64,128]{2,1,0:T(8,128)(2,1)S(1)} %get-tuple-element.64.extra_ref, f32[2,64,128]{2,1,0:T(8,128)S(1)} %get-tuple-element.65.gates_ref), custom_call_target="tpu_custom_call" | custom-call | flops 75497472 | bytes 589824 | tf_op jit(solution)/shard_map/combine/pallas_call | solution.py:423
  (18 shorter events, 1.4 us)
Async XLA Ops:
  1.5 7.3 %collective-permute-start = (bf16[3,4096]{1,0:T(4,128)(2,1)S(1)}, bf16[3,4096]{1,0:T(4,128)(2,1)S(1)}, u32[]{:S(2)}, u32[]{:S(2)}) collective-permute-start(bf16[3,4096]{1,0:T(4,128)(2,1)S(1)} %slice.3), channel_id=1, source_target_pairs={{0,2},{2,4},{4,6},{6,8},{8,10},{10,12},{12,14},{14,16},{16,18},{18... | collective-permute-start | bytes 73736 | tf_op jit(solution)/shard_map/ppermute | solution.py:767
  8.8 21.5 %all-to-all-start = ((bf16[8,16,2304]{2,1,0:T(8,128)(2,1)}), bf16[8,16,2304]{2,1,0:T(8,128)(2,1)S(1)}, u32[]{:S(2)}, u32[]{:S(2)}) async-start(bf16[8,16,2304]{2,1,0:T(8,128)(2,1)} %bitcast.5), calls=%async_computation | async-start | bytes 1179648 | tf_op jit(solution)/shard_map/all_to_all | solution.py:732
  30.4 13.2 %collective-permute-start.1 = (bf16[144,2048]{1,0:T(8,128)(2,1)S(1)}, bf16[144,2048]{1,0:T(8,128)(2,1)S(1)}, u32[]{:S(2)}, u32[]{:S(2)}) collective-permute-start(bf16[144,2048]{1,0:T(8,128)(2,1)S(1)} %unpack.1.x_ref), channel_id=1, source_target_pairs={{0,2},{2,0},{4,6},{6,4},{8,10},{10,8},{12,14},{14,12},{16,18},{18,... | collective-permute-start | bytes 1769480 | tf_op jit(solution)/shard_map/ppermute | solution.py:724
  43.6 8.1 %collective-permute-start.4 = (bf16[144,6144]{1,0:T(8,128)(2,1)S(1)}, bf16[144,6144]{1,0:T(8,128)(2,1)S(1)}, u32[]{:S(2)}, u32[]{:S(2)}) collective-permute-start(bf16[144,6144]{1,0:T(8,128)(2,1)S(1)} %get-tuple-element.43.refs_0_), channel_id=1, source_target_pairs={{0,1},{1,0},{2,3},{3,2},{4,5},{5,4},{6,7},{7,6},{8,9},{9,8},{10,11... | collective-permute-start | bytes 5308424 | tf_op jit(solution)/shard_map/ppermute | solution.py:719
  43.6 8.1 %collective-permute-start.5 = (f32[64,8]{1,0:T(8,128)S(1)}, f32[64,8]{1,0:T(8,128)S(1)}, u32[]{:S(2)}, u32[]{:S(2)}) collective-permute-start(f32[64,8]{1,0:T(8,128)S(1)} %get-tuple-element.61.refs_0_), channel_id=1, source_target_pairs={{0,1},{1,0},{2,3},{3,2},{4,5},{5,4},{6,7},{7,6},{8,9},{9,8},{10,11... | collective-permute-start | bytes 6152 | tf_op jit(solution)/shard_map/ppermute | solution.py:719
  44.2 7.4 %collective-permute-start.2 = (bf16[16,4608]{1,0:T(8,128)(2,1)S(1)}, bf16[16,4608]{1,0:T(8,128)(2,1)S(1)}, u32[]{:S(2)}, u32[]{:S(2)}) collective-permute-start(bf16[16,4608]{1,0:T(8,128)(2,1)S(1)} %get-tuple-element.42.refs_0_), channel_id=1, source_target_pairs={{0,2},{2,0},{4,6},{6,4},{8,10},{10,8},{12,14},{14,12},{16,18},{18,... | collective-permute-start | bytes 442376 | tf_op jit(solution)/shard_map/ppermute | solution.py:714
  45.5 6.2 %copy-start = (f32[16,4096]{1,0:T(8,128)S(1)}, f32[16,4096]{1,0:T(8,128)}, u32[]{:S(2)}) copy-start(f32[16,4096]{1,0:T(8,128)} %alog_ref.3) | copy-start | bytes 786436
  51.8 3.8 %collective-permute-start.6 = (bf16[144,6144]{1,0:T(8,128)(2,1)S(1)}, bf16[144,6144]{1,0:T(8,128)(2,1)S(1)}, u32[]{:S(2)}, u32[]{:S(2)}) collective-permute-start(bf16[144,6144]{1,0:T(8,128)(2,1)S(1)} %gate.3.refs_0_), channel_id=1, source_target_pairs={{0,1},{1,0},{2,3},{3,2},{4,5},{5,4},{6,7},{7,6},{8,9},{9,8},{10,11... | collective-permute-start | bytes 5308424 | tf_op jit(solution)/shard_map/ppermute | solution.py:719
  51.9 9.6 %collective-permute-start.3 = (bf16[16,4608]{1,0:T(8,128)(2,1)S(1)}, bf16[16,4608]{1,0:T(8,128)(2,1)S(1)}, u32[]{:S(2)}, u32[]{:S(2)}) collective-permute-start(bf16[16,4608]{1,0:T(8,128)(2,1)S(1)} %get-tuple-element.47.refs_0_), channel_id=1, source_target_pairs={{0,4},{2,6},{4,0},{6,2},{8,12},{10,14},{12,8},{14,10},{16,20},{18,... | collective-permute-start | bytes 442376 | tf_op jit(solution)/shard_map/ppermute | solution.py:714
  61.7 15.4 %collective-permute-start.10 = (bf16[144,2048]{1,0:T(8,128)(2,1)S(1)}, bf16[144,2048]{1,0:T(8,128)(2,1)S(1)}, u32[]{:S(2)}, u32[]{:S(2)}) collective-permute-start(bf16[144,2048]{1,0:T(8,128)(2,1)S(1)} %down.2), channel_id=1, source_target_pairs={{0,2},{2,0},{4,6},{6,4},{8,10},{10,8},{12,14},{14,12},{16,18},{18,... | collective-permute-start | bytes 1769480 | tf_op jit(solution)/shard_map/ppermute | solution.py:724
  62.4 16.0 %collective-permute-start.9 = (bf16[16,4608]{1,0:T(8,128)(2,1)S(1)}, bf16[16,4608]{1,0:T(8,128)(2,1)S(1)}, u32[]{:S(2)}, u32[]{:S(2)}) collective-permute-start(bf16[16,4608]{1,0:T(8,128)(2,1)S(1)} %get-tuple-element.54), channel_id=1, source_target_pairs={{0,24},{2,26},{4,28},{6,30},{8,16},{10,18},{12,20},{14,22},{16,8},... | collective-permute-start | bytes 442376 | tf_op jit(solution)/shard_map/ppermute | solution.py:714
  64.3 14.0 %collective-permute-start.8 = (bf16[16,4608]{1,0:T(8,128)(2,1)S(1)}, bf16[16,4608]{1,0:T(8,128)(2,1)S(1)}, u32[]{:S(2)}, u32[]{:S(2)}) collective-permute-start(bf16[16,4608]{1,0:T(8,128)(2,1)S(1)} %get-tuple-element.54), channel_id=1, source_target_pairs={{0,16},{2,18},{4,20},{6,22},{8,24},{10,26},{12,28},{14,30},{16,0},... | collective-permute-start | bytes 442376 | tf_op jit(solution)/shard_map/ppermute | solution.py:714
  64.4 13.9 %collective-permute-start.7 = (bf16[16,4608]{1,0:T(8,128)(2,1)S(1)}, bf16[16,4608]{1,0:T(8,128)(2,1)S(1)}, u32[]{:S(2)}, u32[]{:S(2)}) collective-permute-start(bf16[16,4608]{1,0:T(8,128)(2,1)S(1)} %get-tuple-element.54), channel_id=1, source_target_pairs={{0,8},{2,10},{4,12},{6,14},{8,0},{10,2},{12,4},{14,6},{16,24},{18,... | collective-permute-start | bytes 442376 | tf_op jit(solution)/shard_map/ppermute | solution.py:714
  78.3 19.3 %all-to-all-start.1 = ((bf16[8,16,2304]{2,1,0:T(8,128)(2,1)}), bf16[8,16,2304]{2,1,0:T(8,128)(2,1)S(1)}, u32[]{:S(2)}, u32[]{:S(2)}) async-start(bf16[8,16,2304]{2,1,0:T(8,128)(2,1)} %pack_sum.1), calls=%async_computation.1 | async-start | bytes 1179648 | tf_op jit(solution)/shard_map/all_to_all | solution.py:732

commit v16 on v15

--- a/solution.py
+++ b/solution.py
@@ -124,7 +124,7 @@
     columns = [dot_nt(eye, h.astype(BF16)) for h in hits]
     picked = [jnp.sum(c * logits, axis=1, keepdims=True) for c in columns]
     expert = iota((tokens, experts), 1).astype(F32)
-    total = experts * copies * main
+    total = experts * main
     col = iota((tokens, total), 1)
     for k in range(2):
         gate = jax.nn.sigmoid(picked[k] - picked[1 - k])
@@ -132,7 +132,7 @@
         named = jnp.sum(columns[k] * expert, axis=1, keepdims=True).astype(jnp.int32)
         wide = jnp.broadcast_to(slots[k].astype(F32), (8, tokens)).astype(BF16)
         slot = dot_nt(eye, wide)[:, :1].astype(jnp.int32)
-        mine = col // (copies * main) == named
+        mine = (col // main) ^ own_expert(copies) == named
         main_ref[k] = (mine & (col % main == slot)).astype(BF16)
         if extra:
             place = (col % main) // cuts + main
@@ -143,7 +143,7 @@
 
 def blend_weights(ids, logits, copies, pack):
     tokens, experts = logits[0].shape
-    total = experts * copies * pack[0]
+    total = experts * pack[0]
     return pl.pallas_call(
         functools.partial(weights_kernel, pack, copies),
         out_shape=(
@@ -360,10 +360,16 @@
     )(arrived)
 
 
-def pack_kernel(pack, *refs):
+def own_expert(copies):
+    return lax.axis_index("seq") // copies
+
+
+def pack_kernel(pack, copies, count, *refs):
     main, extra, cuts, width = pack
-    part_refs, out_ref = refs[:-1], refs[-1]
-    sources = out_ref.shape[0]
+    part_refs, out_refs = refs[:count], refs[count:]
+    if extra:
+        out_refs, folded_ref = out_refs[:-1], out_refs[-1]
+    sources = len(out_refs)
     features = part_refs[0].shape[1]
     first = sources * main
 
@@ -373,8 +379,6 @@
             value = value + ref[rows, columns].astype(F32)
         return value.astype(BF16)
 
-    made = total(slice(0, first), slice(0, features))
-    out_ref[:, :, :features] = made.reshape(sources, main, features)
     if extra:
         shape = (sources * main, sources * extra)
         folded = None
@@ -383,27 +387,34 @@
             pick = (iota(shape, 0) == iota(shape, 1) * cuts + c).astype(BF16)
             part = dot(pick, piece)
             folded = part if folded is None else folded + part
-        out_ref[:, :, features:] = folded.astype(BF16).reshape(sources, main, width)
-
-
-def pack_sum(parts, sources, pack):
-    main, _, _, width = pack
+        folded_ref[...] = folded
+    own = own_expert(copies)
+    for q, out_ref in enumerate(out_refs):
+        rows = pl.ds(pl.multiple_of((own ^ q) * main, main), main)
+        out_ref[:, :features] = total(rows, slice(0, features))
+        if extra:
+            out_ref[:, features:] = folded_ref[rows].astype(BF16)
+
+
+def pack_sum(parts, sources, copies, pack):
+    main, extra, _, width = pack
     features = parts[0].shape[1]
     return pl.pallas_call(
-        functools.partial(pack_kernel, pack),
-        out_shape=jax.ShapeDtypeStruct((sources, main, features + width), BF16),
+        functools.partial(pack_kernel, pack, copies, len(parts)),
+        out_shape=[jax.ShapeDtypeStruct((main, features + width), BF16)] * sources,
+        scratch_shapes=[pltpu.VMEM((sources * main, width), F32)] if extra else [],
         compiler_params=params(24),
         cost_estimate=cost(parts[0].size * 16, parts[0].size * 8),
         name="pack_sum",
     )(*parts)
 
 
-def combine_kernel(pack, back_ref, main_ref, extra_ref, gates_ref, out_ref):
+def combine_kernel(pack, *refs):
+    back_refs, (main_ref, extra_ref, gates_ref, out_ref) = refs[:-4], refs[-4:]
     main, extra, cuts, width = pack
-    sources = back_ref.shape[0]
-    tokens, features = out_ref.shape
-    back = back_ref[:, :, :features].reshape(sources * main, features)
-    folded = back_ref[:, :, features:].reshape(sources * main, width) if extra else None
+    features = out_ref.shape[1]
+    back = jnp.concatenate([ref[:, :features] for ref in back_refs], axis=0)
+    folded = jnp.concatenate([ref[:, features:] for ref in back_refs], axis=0) if extra else None
     total = None
     for k in range(2):
         rows = dot(main_ref[k], back)
@@ -420,13 +431,14 @@
 
 
 def combine(back, weights, tokens, features, pack):
+    size = sum(b.size for b in back)
     return pl.pallas_call(
         functools.partial(combine_kernel, pack),
         out_shape=jax.ShapeDtypeStruct((tokens, features), BF16),
         compiler_params=params(40),
-        cost_estimate=cost(4 * tokens * back.size, back.size * 2),
+        cost_estimate=cost(4 * tokens * size, size * 2),
         name="combine",
-    )(back, *weights)
+    )(*back, *weights)
 
 
 def spread_states(values, spread_ref):
@@ -816,13 +828,13 @@
     sums = made[-1:]
     for d in range(1, copies):
         sums.append(turned_within(made[d - 1], copies, -d))
-    packed = after(pack_sum(sums, experts, pack), *received)
-    back = exchanged(packed, copies)
-
-    weights = blend_weights(ids, after(tuple(logits), packed), 1, pack)
-    received = after(tuple(received), packed)
+    packed = after(tuple(pack_sum(sums, experts, copies, pack)), *received)
+    back = [packed[0]] + [swapped(packed[q], q * copies) for q in range(1, experts)]
+
+    weights = blend_weights(ids, after(tuple(logits), *packed), copies, pack)
+    received = after(tuple(received), *packed)
     mamba_out = finish(step, read, cum, z_gate, prefix, received, a_log, b_and_c)
-    back = after(back, mamba_out)
+    back = after(tuple(back), mamba_out)
     moe_out = combine(back, weights, tokens, features, pack)
     return mamba_out, moe_out
 

time: 99.4 us -> 99.8 us (level)
  starting transfers between devices: 24.6 us -> 31.8 us
  waiting for transfers between devices: 16 us -> 10.2 us
    ppermute x5 -> x12, starting transfers between devices: 7.14 us -> 18.3 us  [swapped(): return lax.ppermute(value, 'seq', [(i, i ^ by) for i in range(count)])]
    all_to_all x2 -> x1, waiting for transfers between devices: 9.16 us -> 3.27 us  [exchanged(): lax.all_to_all(value, 'seq', split_axis=0, concat_axis=0, tiled=True, axi...]
    all_to_all x2 -> x1, starting transfers between devices: 10.7 us -> 6.7 us  [exchanged(): lax.all_to_all(value, 'seq', split_axis=0, concat_axis=0, tiled=True, axi...]
  transfers between devices with their start and end apart: 13 -> 19, of which waited for: 5 -> 4; matrix products, arithmetic and copies ran while one was open for 0% -> 0% of each run, Pallas kernels for 56% -> 55%
where the time goes in v16:
time: 99.8 us; the launch traced here: 99.3 us
  Pallas kernels  55.7 us (56%)
  starting transfers between devices  31.8 us (32%)
  waiting for transfers between devices  10.2 us (10%)
    ppermute x12, starting transfers between devices, swapped(): return lax.ppermute(value, 'seq', [(i, i ^ by) for i in range(count)])  18.3 us
    pallas_call x1, Pallas kernels, gate(): pl.pallas_call(functools.partial(gate_first_kernel, chunk), in_specs=[INS...  12.4 us
    pallas_call x2, Pallas kernels, down(): pl.pallas_call(functools.partial(down_kernel, chunk), in_specs=[INSIDE] *...  11.8 us
    pallas_call x1, Pallas kernels, scan(): pl.pallas_call(scan_kernel, grid=(channels // lanes,), in_specs=[cut(toke...  11.5 us
    pallas_call x1, Pallas kernels, finish(): pl.pallas_call(functools.partial(finish_kernel, step), grid=(channels //...  8.45 us
    all_to_all x1, starting transfers between devices, exchanged(): lax.all_to_all(value, 'seq', split_axis=0, concat_axis=0, tiled=True, axi...  6.7 us
    pallas_call x1, Pallas kernels, gate(): pl.pallas_call(functools.partial(gate_next_kernel, chunk), in_specs=[INSI...  6.13 us
    ppermute x1, starting transfers between devices, local(): edge = lax.ppermute(edge, 'seq', [(i, i + 1) for i in range(blocks - 1)])  4.84 us
  transfers between devices with their start and end apart: 19, of which 4 were waited for; matrix products, arithmetic and copies ran while one was open for 0% of the time, Pallas kernels for 55%

profile of v16, /device:TPU:0, one launch (start us, length us, event | category | flops | bytes accessed | tf_op | source)
XLA Modules:
  0.0 99.3 jit_solution(3590895402820008820)
XLA Ops:
  0.6 0.9 slice.3
  1.5 4.8 %collective-permute-start = (bf16[3,4096]{1,0:T(4,128)(2,1)S(1)}, bf16[3,4096]{1,0:T(4,128)(2,1)S(1)}, u32[]{:S(2)}, u32[]{:S(2)}) collective-permute-start(bf16[3,4096]{1,0:T(4,128)(2,1)S(1)} %slice.3), channel_id=1, source_target_pairs={{0,2},{2,4},{4,6},{6,8},{8,10},{10,12},{12,14},{14,16},{16,18},{18... | collective-permute-start | bytes 73736 | tf_op jit(solution)/shard_map/ppermute | solution.py:779
  6.3 2.4 %route.1 = (bf16[8,1,16,2304]{3,2,1,0:T(8,128)(2,1)}, f32[64,8]{1,0:T(8,128)S(1)}) custom-call(s32[2,64]{1,0:T(2,128)} %bitcast.7, bf16[64,2048]{1,0:T(8,128)(2,1)} %hidden_ref.1, bf16[8,2048]{1,0:T(8,128)(2,1)} %bitcast.6), custom_call_target="tpu_custom_call" | custom-call | flops 67108864 | bytes 1048576 | tf_op jit(solution)/shard_map/route/pallas_call | solution.py:102
  8.8 6.7 %all-to-all-start = ((bf16[8,16,2304]{2,1,0:T(8,128)(2,1)}), bf16[8,16,2304]{2,1,0:T(8,128)(2,1)S(1)}, u32[]{:S(2)}, u32[]{:S(2)}) async-start(bf16[8,16,2304]{2,1,0:T(8,128)(2,1)} %bitcast.5), calls=%async_computation | async-start | bytes 1179648 | tf_op jit(solution)/shard_map/all_to_all | solution.py:744
  15.5 11.5 %scan.1 = (f32[64,4096]{1,0:T(8,128)}, f32[64,4096]{1,0:T(8,128)}, bf16[16,4608]{1,0:T(8,128)(2,1)S(1)}) custom-call(bf16[64,4096]{1,0:T(8,128)(2,1)} %x_ref.1, bf16[3,4096]{1,0:T(4,128)(2,1)S(1)} %collective-permute-done.edge_ref, bf16[64,256]{1,0:T(8,128)(2,1)} %low_ref.1, bf16[256,4096]{1,0:T(8,128)(2,1)} %dtw_ref.1, f32[1,4096]{1,0:T(1,128)} %bitcast.9, ...), custom_call_target="tpu_custom_call" | custom-call | flops 33554432 | bytes 3145728 | tf_op jit(solution)/shard_map/scan/pallas_call | solution.py:549
  27.0 3.3 %all-to-all-done.arrived_ref = bf16[8,16,2304]{2,1,0:T(8,128)(2,1)S(1)} async-done(((bf16[8,16,2304]{2,1,0:T(8,128)(2,1)}), bf16[8,16,2304]{2,1,0:T(8,128)(2,1)S(1)}, u32[]{:S(2)}, u32[]{:S(2)}) %all-to-all-start) | async-done | bytes 589856 | tf_op jit(solution)/shard_map/all_to_all | solution.py:744
  31.0 12.4 %gate.2 = (bf16[144,6144]{1,0:T(8,128)(2,1)S(1)}, bf16[2048,3072]{1,0:T(8,128)(2,1)S(1)}, bf16[6144,1024]{1,0:T(8,128)(2,1)S(1)}) custom-call(bf16[144,2048]{1,0:T(8,128)(2,1)S(1)} %unpack.1.x_ref, bf16[2048,6144]{1,0:T(8,128)(2,1)} %w_ref.3, bf16[6144,2048]{1,0:T(8,128)(2,1)} %refs_2_.7), custom_call_target="tpu_custom_call" | custom-call | flops 3623878656 | bytes 25165824 | tf_op jit(solution)/shard_map/gate/pallas_call | solution.py:263
  44.2 1.3 %collective-permute-start.2 = (bf16[16,4608]{1,0:T(8,128)(2,1)S(1)}, bf16[16,4608]{1,0:T(8,128)(2,1)S(1)}, u32[]{:S(2)}, u32[]{:S(2)}) collective-permute-start(bf16[16,4608]{1,0:T(8,128)(2,1)S(1)} %get-tuple-element.64.refs_0_), channel_id=1, source_target_pairs={{0,2},{2,0},{4,6},{6,4},{8,10},{10,8},{12,14},{14,12},{16,18},{18,... | collective-permute-start | bytes 442376 | tf_op jit(solution)/shard_map/ppermute | solution.py:726
  45.5 6.1 %gate.3.refs_0_ = bf16[144,6144]{1,0:T(8,128)(2,1)S(1)} custom-call(bf16[144,2048]{1,0:T(8,128)(2,1)S(1)} %collective-permute-done.1.x_ref, bf16[2048,6144]{1,0:T(8,128)(2,1)} %w_ref.3, bf16[2048,3072]{1,0:T(8,128)(2,1)S(1)} %get-tuple-element.67.kept_ref), custom_call_target="tpu_custom_call" | custom-call | flops 3623878656 | bytes 25165824 | tf_op jit(solution)/shard_map/gate/pallas_call | solution.py:255
  51.9 1.5 %collective-permute-start.3 = (bf16[16,4608]{1,0:T(8,128)(2,1)S(1)}, bf16[16,4608]{1,0:T(8,128)(2,1)S(1)}, u32[]{:S(2)}, u32[]{:S(2)}) collective-permute-start(bf16[16,4608]{1,0:T(8,128)(2,1)S(1)} %get-tuple-element.69.refs_0_), channel_id=1, source_target_pairs={{0,4},{2,6},{4,0},{6,2},{8,12},{10,14},{12,8},{14,10},{16,20},{18,... | collective-permute-start | bytes 442376 | tf_op jit(solution)/shard_map/ppermute | solution.py:726
  53.3 2.2 %collective-permute-done.6.refs_1_ = bf16[144,6144]{1,0:T(8,128)(2,1)S(1)} collective-permute-done((bf16[144,6144]{1,0:T(8,128)(2,1)S(1)}, bf16[144,6144]{1,0:T(8,128)(2,1)S(1)}, u32[]{:S(2)}, u32[]{:S(2)}) %collective-permute-start.6) | collective-permute-done | bytes 1769504 | tf_op jit(solution)/shard_map/ppermute | solution.py:731
  55.5 5.9 %down.2 = bf16[144,2048]{1,0:T(8,128)(2,1)S(1)} custom-call(bf16[144,6144]{1,0:T(8,128)(2,1)S(1)} %gate.3.refs_0_, bf16[144,6144]{1,0:T(8,128)(2,1)S(1)} %collective-permute-done.6.refs_1_, bf16[6144,2048]{1,0:T(8,128)(2,1)} %refs_2_.7, bf16[6144,1024]{1,0:T(8,128)(2,1)S(1)} %get-tuple-element.73.refs_3_), custom_call_target="tpu_custom_call" | custom-call | flops 3623878656 | bytes 25165824 | tf_op jit(solution)/shard_map/down/pallas_call | solution.py:322
  62.4 2.0 %collective-permute-start.9 = (bf16[16,4608]{1,0:T(8,128)(2,1)S(1)}, bf16[16,4608]{1,0:T(8,128)(2,1)S(1)}, u32[]{:S(2)}, u32[]{:S(2)}) collective-permute-start(bf16[16,4608]{1,0:T(8,128)(2,1)S(1)} %get-tuple-element.76), channel_id=1, source_target_pairs={{0,24},{2,26},{4,28},{6,30},{8,16},{10,18},{12,20},{14,22},{16,8},... | collective-permute-start | bytes 442376 | tf_op jit(solution)/shard_map/ppermute | solution.py:726
  64.4 2.4 %collective-permute-start.7 = (bf16[16,4608]{1,0:T(8,128)(2,1)S(1)}, bf16[16,4608]{1,0:T(8,128)(2,1)S(1)}, u32[]{:S(2)}, u32[]{:S(2)}) collective-permute-start(bf16[16,4608]{1,0:T(8,128)(2,1)S(1)} %get-tuple-element.76), channel_id=1, source_target_pairs={{0,8},{2,10},{4,12},{6,14},{8,0},{10,2},{12,4},{14,6},{16,24},{18,... | collective-permute-start | bytes 442376 | tf_op jit(solution)/shard_map/ppermute | solution.py:726
  66.8 5.9 %down.3.refs_0_ = f32[144,2048]{1,0:T(8,128)S(1)} custom-call(bf16[144,6144]{1,0:T(8,128)(2,1)S(1)} %get-tuple-element.65.refs_0_, bf16[144,6144]{1,0:T(8,128)(2,1)S(1)} %collective-permute-done.4.refs_1_, bf16[6144,2048]{1,0:T(8,128)(2,1)} %refs_2_.7, bf16[6144,1024]{1,0:T(8,128)(2,1)S(1)} %get-tuple-element.73.refs_3_), custom_call_target="tpu_custom_call" | custom-call | flops 3623878656 | bytes 25165824 | tf_op jit(solution)/shard_map/down/pallas_call | solution.py:322
  72.7 4.4 %collective-permute-done.10.refs_1_ = bf16[144,2048]{1,0:T(8,128)(2,1)S(1)} collective-permute-done((bf16[144,2048]{1,0:T(8,128)(2,1)S(1)}, bf16[144,2048]{1,0:T(8,128)(2,1)S(1)}, u32[]{:S(2)}, u32[]{:S(2)}) %collective-permute-start.10) | collective-permute-done | bytes 589856 | tf_op jit(solution)/shard_map/ppermute | solution.py:736
  77.4 1.4 %collective-permute-start.11 = (bf16[16,2304]{1,0:T(8,128)(2,1)S(1)}, bf16[16,2304]{1,0:T(8,128)(2,1)S(1)}, u32[]{:S(2)}, u32[]{:S(2)}) collective-permute-start(bf16[16,2304]{1,0:T(8,128)(2,1)S(1)} %get-tuple-element.87), channel_id=1, source_target_pairs={{0,4},{2,6},{4,0},{6,2},{8,12},{10,14},{12,8},{14,10},{16,20},{18,... | collective-permute-start | bytes 221192 | tf_op jit(solution)/shard_map/ppermute | solution.py:726
  78.9 2.1 %collective-permute-start.13 = (bf16[16,2304]{1,0:T(8,128)(2,1)S(1)}, bf16[16,2304]{1,0:T(8,128)(2,1)S(1)}, u32[]{:S(2)}, u32[]{:S(2)}) collective-permute-start(bf16[16,2304]{1,0:T(8,128)(2,1)S(1)} %get-tuple-element.89), channel_id=1, source_target_pairs={{0,12},{2,14},{4,8},{6,10},{8,4},{10,6},{12,0},{14,2},{16,28},{18,... | collective-permute-start | bytes 221192 | tf_op jit(solution)/shard_map/ppermute | solution.py:726
  81.6 3.1 %collective-permute-start.15 = (bf16[16,2304]{1,0:T(8,128)(2,1)S(1)}, bf16[16,2304]{1,0:T(8,128)(2,1)S(1)}, u32[]{:S(2)}, u32[]{:S(2)}) collective-permute-start(bf16[16,2304]{1,0:T(8,128)(2,1)S(1)} %get-tuple-element.91), channel_id=1, source_target_pairs={{0,20},{2,22},{4,16},{6,18},{8,28},{10,30},{12,24},{14,26},{16,4},... | collective-permute-start | bytes 221192 | tf_op jit(solution)/shard_map/ppermute | solution.py:726
  84.8 1.8 %collective-permute-start.16 = (bf16[16,2304]{1,0:T(8,128)(2,1)S(1)}, bf16[16,2304]{1,0:T(8,128)(2,1)S(1)}, u32[]{:S(2)}, u32[]{:S(2)}) collective-permute-start(bf16[16,2304]{1,0:T(8,128)(2,1)S(1)} %get-tuple-element.92), channel_id=1, source_target_pairs={{0,24},{2,26},{4,28},{6,30},{8,16},{10,18},{12,20},{14,22},{16,8},... | collective-permute-start | bytes 221192 | tf_op jit(solution)/shard_map/ppermute | solution.py:726
  86.6 2.1 %collective-permute-start.17 = (bf16[16,2304]{1,0:T(8,128)(2,1)S(1)}, bf16[16,2304]{1,0:T(8,128)(2,1)S(1)}, u32[]{:S(2)}, u32[]{:S(2)}) collective-permute-start(bf16[16,2304]{1,0:T(8,128)(2,1)S(1)} %get-tuple-element.93), channel_id=1, source_target_pairs={{0,28},{2,30},{4,24},{6,26},{8,20},{10,22},{12,16},{14,18},{16,12}... | collective-permute-start | bytes 221192 | tf_op jit(solution)/shard_map/ppermute | solution.py:726
  88.6 1.1 %blend_weights.1 = (bf16[2,64,128]{2,1,0:T(8,128)(2,1)S(1)}, bf16[2,64,128]{2,1,0:T(8,128)(2,1)S(1)}, f32[2,64,128]{2,1,0:T(8,128)S(1)}) custom-call(s32[2,64]{1,0:T(2,128)} %bitcast.8, f32[64,8]{1,0:T(8,128)S(1)} %get-tuple-element.105.refs_0_, f32[64,8]{1,0:T(8,128)S(1)} %collective-permute-done.5.refs_1_), custom_call_target="tpu_custom_call" | custom-call | flops 262144 | bytes 65536 | tf_op jit(solution)/shard_map/blend_weights/pallas_call | solution.py:147
  89.7 8.5 %finish.1 = bf16[64,4096]{1,0:T(8,128)(2,1)} custom-call(f32[64,4096]{1,0:T(8,128)} %get-tuple-element.56.read_ref, f32[64,4096]{1,0:T(8,128)} %get-tuple-element.57.cum_ref, bf16[64,4096]{1,0:T(8,128)(2,1)} %z_ref.1, f32[16,4096]{1,0:T(8,128)} %alog_ref.3, f32[2,16,64]{2,1,0:T(8,128)} %bc_ref.3, bf16[16,4608]{1,0:T(8,128)(2,1)S(1)} %get-tuple-element.75.prefix_ref.refs_3_, ...), custom_call_target="tpu_custom_call" | custom-call | flops 20971520 | bytes 3145728 | tf_op jit(solution)/shard_map/finish/pallas_call | solution.py:700
  98.2 1.1 %combine.1 = bf16[64,2048]{1,0:T(8,128)(2,1)} custom-call(bf16[16,2304]{1,0:T(8,128)(2,1)S(1)} %get-tuple-element.97.refs_0_, bf16[16,2304]{1,0:T(8,128)(2,1)S(1)} %collective-permute-done.11.refs_1_, bf16[16,2304]{1,0:T(8,128)(2,1)S(1)} %collective-permute-done.12.refs_2_, bf16[16,2304]{1,0:T(8,128)(2,1)S(1)} %collective-permute-done.13.refs_3_, ...), custom_call_target="tpu_custom_call" | custom-call | flops 75497472 | bytes 589824 | tf_op jit(solution)/shard_map/combine/pallas_call | solution.py:435
  (30 shorter events, 3.8 us)
Async XLA Ops:
  1.5 7.3 %collective-permute-start = (bf16[3,4096]{1,0:T(4,128)(2,1)S(1)}, bf16[3,4096]{1,0:T(4,128)(2,1)S(1)}, u32[]{:S(2)}, u32[]{:S(2)}) collective-permute-start(bf16[3,4096]{1,0:T(4,128)(2,1)S(1)} %slice.3), channel_id=1, source_target_pairs={{0,2},{2,4},{4,6},{6,8},{8,10},{10,12},{12,14},{14,16},{16,18},{18... | collective-permute-start | bytes 73736 | tf_op jit(solution)/shard_map/ppermute | solution.py:779
  8.8 21.4 %all-to-all-start = ((bf16[8,16,2304]{2,1,0:T(8,128)(2,1)}), bf16[8,16,2304]{2,1,0:T(8,128)(2,1)S(1)}, u32[]{:S(2)}, u32[]{:S(2)}) async-start(bf16[8,16,2304]{2,1,0:T(8,128)(2,1)} %bitcast.5), calls=%async_computation | async-start | bytes 1179648 | tf_op jit(solution)/shard_map/all_to_all | solution.py:744
  30.4 13.2 %collective-permute-start.1 = (bf16[144,2048]{1,0:T(8,128)(2,1)S(1)}, bf16[144,2048]{1,0:T(8,128)(2,1)S(1)}, u32[]{:S(2)}, u32[]{:S(2)}) collective-permute-start(bf16[144,2048]{1,0:T(8,128)(2,1)S(1)} %unpack.1.x_ref), channel_id=1, source_target_pairs={{0,2},{2,0},{4,6},{6,4},{8,10},{10,8},{12,14},{14,12},{16,18},{18,... | collective-permute-start | bytes 1769480 | tf_op jit(solution)/shard_map/ppermute | solution.py:736
  43.6 8.1 %collective-permute-start.4 = (bf16[144,6144]{1,0:T(8,128)(2,1)S(1)}, bf16[144,6144]{1,0:T(8,128)(2,1)S(1)}, u32[]{:S(2)}, u32[]{:S(2)}) collective-permute-start(bf16[144,6144]{1,0:T(8,128)(2,1)S(1)} %get-tuple-element.65.refs_0_), channel_id=1, source_target_pairs={{0,1},{1,0},{2,3},{3,2},{4,5},{5,4},{6,7},{7,6},{8,9},{9,8},{10,11... | collective-permute-start | bytes 5308424 | tf_op jit(solution)/shard_map/ppermute | solution.py:731
  43.6 8.1 %collective-permute-start.5 = (f32[64,8]{1,0:T(8,128)S(1)}, f32[64,8]{1,0:T(8,128)S(1)}, u32[]{:S(2)}, u32[]{:S(2)}) collective-permute-start(f32[64,8]{1,0:T(8,128)S(1)} %get-tuple-element.105.refs_0_), channel_id=1, source_target_pairs={{0,1},{1,0},{2,3},{3,2},{4,5},{5,4},{6,7},{7,6},{8,9},{9,8},{10,11... | collective-permute-start | bytes 6152 | tf_op jit(solution)/shard_map/ppermute | solution.py:731
  44.2 7.4 %collective-permute-start.2 = (bf16[16,4608]{1,0:T(8,128)(2,1)S(1)}, bf16[16,4608]{1,0:T(8,128)(2,1)S(1)}, u32[]{:S(2)}, u32[]{:S(2)}) collective-permute-start(bf16[16,4608]{1,0:T(8,128)(2,1)S(1)} %get-tuple-element.64.refs_0_), channel_id=1, source_target_pairs={{0,2},{2,0},{4,6},{6,4},{8,10},{10,8},{12,14},{14,12},{16,18},{18,... | collective-permute-start | bytes 442376 | tf_op jit(solution)/shard_map/ppermute | solution.py:726
  45.5 6.2 %copy-start = (f32[16,4096]{1,0:T(8,128)S(1)}, f32[16,4096]{1,0:T(8,128)}, u32[]{:S(2)}) copy-start(f32[16,4096]{1,0:T(8,128)} %alog_ref.3) | copy-start | bytes 786436
  51.8 3.8 %collective-permute-start.6 = (bf16[144,6144]{1,0:T(8,128)(2,1)S(1)}, bf16[144,6144]{1,0:T(8,128)(2,1)S(1)}, u32[]{:S(2)}, u32[]{:S(2)}) collective-permute-start(bf16[144,6144]{1,0:T(8,128)(2,1)S(1)} %gate.3.refs_0_), channel_id=1, source_target_pairs={{0,1},{1,0},{2,3},{3,2},{4,5},{5,4},{6,7},{7,6},{8,9},{9,8},{10,11... | collective-permute-start | bytes 5308424 | tf_op jit(solution)/shard_map/ppermute | solution.py:731
  51.9 9.6 %collective-permute-start.3 = (bf16[16,4608]{1,0:T(8,128)(2,1)S(1)}, bf16[16,4608]{1,0:T(8,128)(2,1)S(1)}, u32[]{:S(2)}, u32[]{:S(2)}) collective-permute-start(bf16[16,4608]{1,0:T(8,128)(2,1)S(1)} %get-tuple-element.69.refs_0_), channel_id=1, source_target_pairs={{0,4},{2,6},{4,0},{6,2},{8,12},{10,14},{12,8},{14,10},{16,20},{18,... | collective-permute-start | bytes 442376 | tf_op jit(solution)/shard_map/ppermute | solution.py:726
  61.7 15.4 %collective-permute-start.10 = (bf16[144,2048]{1,0:T(8,128)(2,1)S(1)}, bf16[144,2048]{1,0:T(8,128)(2,1)S(1)}, u32[]{:S(2)}, u32[]{:S(2)}) collective-permute-start(bf16[144,2048]{1,0:T(8,128)(2,1)S(1)} %down.2), channel_id=1, source_target_pairs={{0,2},{2,0},{4,6},{6,4},{8,10},{10,8},{12,14},{14,12},{16,18},{18,... | collective-permute-start | bytes 1769480 | tf_op jit(solution)/shard_map/ppermute | solution.py:736
  62.4 15.0 %collective-permute-start.9 = (bf16[16,4608]{1,0:T(8,128)(2,1)S(1)}, bf16[16,4608]{1,0:T(8,128)(2,1)S(1)}, u32[]{:S(2)}, u32[]{:S(2)}) collective-permute-start(bf16[16,4608]{1,0:T(8,128)(2,1)S(1)} %get-tuple-element.76), channel_id=1, source_target_pairs={{0,24},{2,26},{4,28},{6,30},{8,16},{10,18},{12,20},{14,22},{16,8},... | collective-permute-start | bytes 442376 | tf_op jit(solution)/shard_map/ppermute | solution.py:726
  64.3 13.1 %collective-permute-start.8 = (bf16[16,4608]{1,0:T(8,128)(2,1)S(1)}, bf16[16,4608]{1,0:T(8,128)(2,1)S(1)}, u32[]{:S(2)}, u32[]{:S(2)}) collective-permute-start(bf16[16,4608]{1,0:T(8,128)(2,1)S(1)} %get-tuple-element.76), channel_id=1, source_target_pairs={{0,16},{2,18},{4,20},{6,22},{8,24},{10,26},{12,28},{14,30},{16,0},... | collective-permute-start | bytes 442376 | tf_op jit(solution)/shard_map/ppermute | solution.py:726
  64.4 13.0 %collective-permute-start.7 = (bf16[16,4608]{1,0:T(8,128)(2,1)S(1)}, bf16[16,4608]{1,0:T(8,128)(2,1)S(1)}, u32[]{:S(2)}, u32[]{:S(2)}) collective-permute-start(bf16[16,4608]{1,0:T(8,128)(2,1)S(1)} %get-tuple-element.76), channel_id=1, source_target_pairs={{0,8},{2,10},{4,12},{6,14},{8,0},{10,2},{12,4},{14,6},{16,24},{18,... | collective-permute-start | bytes 442376 | tf_op jit(solution)/shard_map/ppermute | solution.py:726
  77.4 7.3 %collective-permute-start.11 = (bf16[16,2304]{1,0:T(8,128)(2,1)S(1)}, bf16[16,2304]{1,0:T(8,128)(2,1)S(1)}, u32[]{:S(2)}, u32[]{:S(2)}) collective-permute-start(bf16[16,2304]{1,0:T(8,128)(2,1)S(1)} %get-tuple-element.87), channel_id=1, source_target_pairs={{0,4},{2,6},{4,0},{6,2},{8,12},{10,14},{12,8},{14,10},{16,20},{18,... | collective-permute-start | bytes 221192 | tf_op jit(solution)/shard_map/ppermute | solution.py:726
  78.9 7.7 %collective-permute-start.12 = (bf16[16,2304]{1,0:T(8,128)(2,1)S(1)}, bf16[16,2304]{1,0:T(8,128)(2,1)S(1)}, u32[]{:S(2)}, u32[]{:S(2)}) collective-permute-start(bf16[16,2304]{1,0:T(8,128)(2,1)S(1)} %get-tuple-element.88), channel_id=1, source_target_pairs={{0,8},{2,10},{4,12},{6,14},{8,0},{10,2},{12,4},{14,6},{16,24},{18,... | collective-permute-start | bytes 221192 | tf_op jit(solution)/shard_map/ppermute | solution.py:726
  78.9 19.3 %collective-permute-start.13 = (bf16[16,2304]{1,0:T(8,128)(2,1)S(1)}, bf16[16,2304]{1,0:T(8,128)(2,1)S(1)}, u32[]{:S(2)}, u32[]{:S(2)}) collective-permute-start(bf16[16,2304]{1,0:T(8,128)(2,1)S(1)} %get-tuple-element.89), channel_id=1, source_target_pairs={{0,12},{2,14},{4,8},{6,10},{8,4},{10,6},{12,0},{14,2},{16,28},{18,... | collective-permute-start | bytes 221192 | tf_op jit(solution)/shard_map/ppermute | solution.py:726
  81.0 17.2 %collective-permute-start.14 = (bf16[16,2304]{1,0:T(8,128)(2,1)S(1)}, bf16[16,2304]{1,0:T(8,128)(2,1)S(1)}, u32[]{:S(2)}, u32[]{:S(2)}) collective-permute-start(bf16[16,2304]{1,0:T(8,128)(2,1)S(1)} %get-tuple-element.90), channel_id=1, source_target_pairs={{0,16},{2,18},{4,20},{6,22},{8,24},{10,26},{12,28},{14,30},{16,0},... | collective-permute-start | bytes 221192 | tf_op jit(solution)/shard_map/ppermute | solution.py:726
  81.6 16.5 %collective-permute-start.15 = (bf16[16,2304]{1,0:T(8,128)(2,1)S(1)}, bf16[16,2304]{1,0:T(8,128)(2,1)S(1)}, u32[]{:S(2)}, u32[]{:S(2)}) collective-permute-start(bf16[16,2304]{1,0:T(8,128)(2,1)S(1)} %get-tuple-element.91), channel_id=1, source_target_pairs={{0,20},{2,22},{4,16},{6,18},{8,28},{10,30},{12,24},{14,26},{16,4},... | collective-permute-start | bytes 221192 | tf_op jit(solution)/shard_map/ppermute | solution.py:726
  84.8 13.4 %collective-permute-start.16 = (bf16[16,2304]{1,0:T(8,128)(2,1)S(1)}, bf16[16,2304]{1,0:T(8,128)(2,1)S(1)}, u32[]{:S(2)}, u32[]{:S(2)}) collective-permute-start(bf16[16,2304]{1,0:T(8,128)(2,1)S(1)} %get-tuple-element.92), channel_id=1, source_target_pairs={{0,24},{2,26},{4,28},{6,30},{8,16},{10,18},{12,20},{14,22},{16,8},... | collective-permute-start | bytes 221192 | tf_op jit(solution)/shard_map/ppermute | solution.py:726
  86.6 11.6 %collective-permute-start.17 = (bf16[16,2304]{1,0:T(8,128)(2,1)S(1)}, bf16[16,2304]{1,0:T(8,128)(2,1)S(1)}, u32[]{:S(2)}, u32[]{:S(2)}) collective-permute-start(bf16[16,2304]{1,0:T(8,128)(2,1)S(1)} %get-tuple-element.93), channel_id=1, source_target_pairs={{0,28},{2,30},{4,24},{6,26},{8,20},{10,22},{12,16},{14,18},{16,12}... | collective-permute-start | bytes 221192 | tf_op jit(solution)/shard_map/ppermute | solution.py:726

commit v17 on v16

--- a/solution.py
+++ b/solution.py
@@ -825,13 +825,13 @@
         made.append(product)
     while step < steps:
         advance()
-    sums = made[-1:]
+    weights = blend_weights(ids, after(tuple(logits), made[-1]), copies, pack)
+    sums = [after(made[-1], *weights)]
     for d in range(1, copies):
         sums.append(turned_within(made[d - 1], copies, -d))
     packed = after(tuple(pack_sum(sums, experts, copies, pack)), *received)
     back = [packed[0]] + [swapped(packed[q], q * copies) for q in range(1, experts)]
 
-    weights = blend_weights(ids, after(tuple(logits), *packed), copies, pack)
     received = after(tuple(received), *packed)
     mamba_out = finish(step, read, cum, z_gate, prefix, received, a_log, b_and_c)
     back = after(tuple(back), mamba_out)

time: 99.8 us -> 98.7 us (0.989)
  waiting for transfers between devices: 10.2 us -> 9.12 us
    ppermute x2, waiting for transfers between devices: 4.62 us -> 3.56 us  [turned_within(): lax.ppermute(value, 'seq', [(i, i // copies * copies + (i + by) % copies)...]
where the time goes in v17:
time: 98.7 us; the launch traced here: 98.2 us
  Pallas kernels  55.7 us (56%)
  starting transfers between devices  31.8 us (32%)
  waiting for transfers between devices  9.12 us (9%)
    ppermute x12, starting transfers between devices, swapped(): return lax.ppermute(value, 'seq', [(i, i ^ by) for i in range(count)])  18.3 us
    pallas_call x1, Pallas kernels, gate(): pl.pallas_call(functools.partial(gate_first_kernel, chunk), in_specs=[INS...  12.4 us
    pallas_call x2, Pallas kernels, down(): pl.pallas_call(functools.partial(down_kernel, chunk), in_specs=[INSIDE] *...  11.8 us
    pallas_call x1, Pallas kernels, scan(): pl.pallas_call(scan_kernel, grid=(channels // lanes,), in_specs=[cut(toke...  11.5 us
    pallas_call x1, Pallas kernels, finish(): pl.pallas_call(functools.partial(finish_kernel, step), grid=(channels //...  8.42 us
    all_to_all x1, starting transfers between devices, exchanged(): lax.all_to_all(value, 'seq', split_axis=0, concat_axis=0, tiled=True, axi...  6.7 us
    pallas_call x1, Pallas kernels, gate(): pl.pallas_call(functools.partial(gate_next_kernel, chunk), in_specs=[INSI...  6.13 us
    ppermute x1, starting transfers between devices, local(): edge = lax.ppermute(edge, 'seq', [(i, i + 1) for i in range(blocks - 1)])  4.84 us
  transfers between devices with their start and end apart: 19, of which 4 were waited for; matrix products, arithmetic and copies ran while one was open for 0% of the time, Pallas kernels for 55%

profile of v17, /device:TPU:0, one launch (start us, length us, event | category | flops | bytes accessed | tf_op | source)
XLA Modules:
  0.0 98.2 jit_solution(12352040745565730759)
XLA Ops:
  0.6 0.9 slice.3
  1.5 4.8 %collective-permute-start = (bf16[3,4096]{1,0:T(4,128)(2,1)S(1)}, bf16[3,4096]{1,0:T(4,128)(2,1)S(1)}, u32[]{:S(2)}, u32[]{:S(2)}) collective-permute-start(bf16[3,4096]{1,0:T(4,128)(2,1)S(1)} %slice.3), channel_id=1, source_target_pairs={{0,2},{2,4},{4,6},{6,8},{8,10},{10,12},{12,14},{14,16},{16,18},{18... | collective-permute-start | bytes 73736 | tf_op jit(solution)/shard_map/ppermute | solution.py:779
  6.3 2.4 %route.1 = (bf16[8,1,16,2304]{3,2,1,0:T(8,128)(2,1)}, f32[64,8]{1,0:T(8,128)S(1)}) custom-call(s32[2,64]{1,0:T(2,128)} %bitcast.7, bf16[64,2048]{1,0:T(8,128)(2,1)} %hidden_ref.1, bf16[8,2048]{1,0:T(8,128)(2,1)} %bitcast.6), custom_call_target="tpu_custom_call" | custom-call | flops 67108864 | bytes 1048576 | tf_op jit(solution)/shard_map/route/pallas_call | solution.py:102
  8.8 6.7 %all-to-all-start = ((bf16[8,16,2304]{2,1,0:T(8,128)(2,1)}), bf16[8,16,2304]{2,1,0:T(8,128)(2,1)S(1)}, u32[]{:S(2)}, u32[]{:S(2)}) async-start(bf16[8,16,2304]{2,1,0:T(8,128)(2,1)} %bitcast.5), calls=%async_computation | async-start | bytes 1179648 | tf_op jit(solution)/shard_map/all_to_all | solution.py:744
  15.5 11.5 %scan.1 = (f32[64,4096]{1,0:T(8,128)}, f32[64,4096]{1,0:T(8,128)}, bf16[16,4608]{1,0:T(8,128)(2,1)S(1)}) custom-call(bf16[64,4096]{1,0:T(8,128)(2,1)} %x_ref.1, bf16[3,4096]{1,0:T(4,128)(2,1)S(1)} %collective-permute-done.edge_ref, bf16[64,256]{1,0:T(8,128)(2,1)} %low_ref.1, bf16[256,4096]{1,0:T(8,128)(2,1)} %dtw_ref.1, f32[1,4096]{1,0:T(1,128)} %bitcast.9, ...), custom_call_target="tpu_custom_call" | custom-call | flops 33554432 | bytes 3145728 | tf_op jit(solution)/shard_map/scan/pallas_call | solution.py:549
  27.0 3.3 %all-to-all-done.arrived_ref = bf16[8,16,2304]{2,1,0:T(8,128)(2,1)S(1)} async-done(((bf16[8,16,2304]{2,1,0:T(8,128)(2,1)}), bf16[8,16,2304]{2,1,0:T(8,128)(2,1)S(1)}, u32[]{:S(2)}, u32[]{:S(2)}) %all-to-all-start) | async-done | bytes 589856 | tf_op jit(solution)/shard_map/all_to_all | solution.py:744
  31.0 12.4 %gate.2 = (bf16[144,6144]{1,0:T(8,128)(2,1)S(1)}, bf16[2048,3072]{1,0:T(8,128)(2,1)S(1)}, bf16[6144,1024]{1,0:T(8,128)(2,1)S(1)}) custom-call(bf16[144,2048]{1,0:T(8,128)(2,1)S(1)} %unpack.1.x_ref, bf16[2048,6144]{1,0:T(8,128)(2,1)} %w_ref.3, bf16[6144,2048]{1,0:T(8,128)(2,1)} %refs_2_.7), custom_call_target="tpu_custom_call" | custom-call | flops 3623878656 | bytes 25165824 | tf_op jit(solution)/shard_map/gate/pallas_call | solution.py:263
  44.2 1.3 %collective-permute-start.2 = (bf16[16,4608]{1,0:T(8,128)(2,1)S(1)}, bf16[16,4608]{1,0:T(8,128)(2,1)S(1)}, u32[]{:S(2)}, u32[]{:S(2)}) collective-permute-start(bf16[16,4608]{1,0:T(8,128)(2,1)S(1)} %get-tuple-element.65.refs_0_), channel_id=1, source_target_pairs={{0,2},{2,0},{4,6},{6,4},{8,10},{10,8},{12,14},{14,12},{16,18},{18,... | collective-permute-start | bytes 442376 | tf_op jit(solution)/shard_map/ppermute | solution.py:726
  45.5 6.1 %gate.3.refs_0_ = bf16[144,6144]{1,0:T(8,128)(2,1)S(1)} custom-call(bf16[144,2048]{1,0:T(8,128)(2,1)S(1)} %collective-permute-done.1.x_ref, bf16[2048,6144]{1,0:T(8,128)(2,1)} %w_ref.3, bf16[2048,3072]{1,0:T(8,128)(2,1)S(1)} %get-tuple-element.68.kept_ref), custom_call_target="tpu_custom_call" | custom-call | flops 3623878656 | bytes 25165824 | tf_op jit(solution)/shard_map/gate/pallas_call | solution.py:255
  51.9 1.5 %collective-permute-start.3 = (bf16[16,4608]{1,0:T(8,128)(2,1)S(1)}, bf16[16,4608]{1,0:T(8,128)(2,1)S(1)}, u32[]{:S(2)}, u32[]{:S(2)}) collective-permute-start(bf16[16,4608]{1,0:T(8,128)(2,1)S(1)} %get-tuple-element.70.refs_0_), channel_id=1, source_target_pairs={{0,4},{2,6},{4,0},{6,2},{8,12},{10,14},{12,8},{14,10},{16,20},{18,... | collective-permute-start | bytes 442376 | tf_op jit(solution)/shard_map/ppermute | solution.py:726
  53.3 2.2 %collective-permute-done.6.refs_1_ = bf16[144,6144]{1,0:T(8,128)(2,1)S(1)} collective-permute-done((bf16[144,6144]{1,0:T(8,128)(2,1)S(1)}, bf16[144,6144]{1,0:T(8,128)(2,1)S(1)}, u32[]{:S(2)}, u32[]{:S(2)}) %collective-permute-start.6) | collective-permute-done | bytes 1769504 | tf_op jit(solution)/shard_map/ppermute | solution.py:731
  55.5 5.9 %down.2 = bf16[144,2048]{1,0:T(8,128)(2,1)S(1)} custom-call(bf16[144,6144]{1,0:T(8,128)(2,1)S(1)} %gate.3.refs_0_, bf16[144,6144]{1,0:T(8,128)(2,1)S(1)} %collective-permute-done.6.refs_1_, bf16[6144,2048]{1,0:T(8,128)(2,1)} %refs_2_.7, bf16[6144,1024]{1,0:T(8,128)(2,1)S(1)} %get-tuple-element.74.refs_3_), custom_call_target="tpu_custom_call" | custom-call | flops 3623878656 | bytes 25165824 | tf_op jit(solution)/shard_map/down/pallas_call | solution.py:322
  62.4 2.0 %collective-permute-start.9 = (bf16[16,4608]{1,0:T(8,128)(2,1)S(1)}, bf16[16,4608]{1,0:T(8,128)(2,1)S(1)}, u32[]{:S(2)}, u32[]{:S(2)}) collective-permute-start(bf16[16,4608]{1,0:T(8,128)(2,1)S(1)} %get-tuple-element.77), channel_id=1, source_target_pairs={{0,24},{2,26},{4,28},{6,30},{8,16},{10,18},{12,20},{14,22},{16,8},... | collective-permute-start | bytes 442376 | tf_op jit(solution)/shard_map/ppermute | solution.py:726
  64.4 2.4 %collective-permute-start.7 = (bf16[16,4608]{1,0:T(8,128)(2,1)S(1)}, bf16[16,4608]{1,0:T(8,128)(2,1)S(1)}, u32[]{:S(2)}, u32[]{:S(2)}) collective-permute-start(bf16[16,4608]{1,0:T(8,128)(2,1)S(1)} %get-tuple-element.77), channel_id=1, source_target_pairs={{0,8},{2,10},{4,12},{6,14},{8,0},{10,2},{12,4},{14,6},{16,24},{18,... | collective-permute-start | bytes 442376 | tf_op jit(solution)/shard_map/ppermute | solution.py:726
  66.8 5.9 %down.3.refs_0_ = f32[144,2048]{1,0:T(8,128)S(1)} custom-call(bf16[144,6144]{1,0:T(8,128)(2,1)S(1)} %get-tuple-element.66.refs_0_, bf16[144,6144]{1,0:T(8,128)(2,1)S(1)} %collective-permute-done.4.refs_1_, bf16[6144,2048]{1,0:T(8,128)(2,1)} %refs_2_.7, bf16[6144,1024]{1,0:T(8,128)(2,1)S(1)} %get-tuple-element.74.refs_3_), custom_call_target="tpu_custom_call" | custom-call | flops 3623878656 | bytes 25165824 | tf_op jit(solution)/shard_map/down/pallas_call | solution.py:322
  72.7 1.1 %blend_weights.1 = (bf16[2,64,128]{2,1,0:T(8,128)(2,1)S(1)}, bf16[2,64,128]{2,1,0:T(8,128)(2,1)S(1)}, f32[2,64,128]{2,1,0:T(8,128)S(1)}) custom-call(s32[2,64]{1,0:T(2,128)} %bitcast.8, f32[64,8]{1,0:T(8,128)S(1)} %get-tuple-element.78.refs_0_, f32[64,8]{1,0:T(8,128)S(1)} %collective-permute-done.5.refs_1_), custom_call_target="tpu_custom_call" | custom-call | flops 262144 | bytes 65536 | tf_op jit(solution)/shard_map/blend_weights/pallas_call | solution.py:147
  73.7 3.4 %collective-permute-done.10.refs_1_ = bf16[144,2048]{1,0:T(8,128)(2,1)S(1)} collective-permute-done((bf16[144,2048]{1,0:T(8,128)(2,1)S(1)}, bf16[144,2048]{1,0:T(8,128)(2,1)S(1)}, u32[]{:S(2)}, u32[]{:S(2)}) %collective-permute-start.10) | collective-permute-done | bytes 589856 | tf_op jit(solution)/shard_map/ppermute | solution.py:736
  77.4 1.4 %collective-permute-start.11 = (bf16[16,2304]{1,0:T(8,128)(2,1)S(1)}, bf16[16,2304]{1,0:T(8,128)(2,1)S(1)}, u32[]{:S(2)}, u32[]{:S(2)}) collective-permute-start(bf16[16,2304]{1,0:T(8,128)(2,1)S(1)} %get-tuple-element.94), channel_id=1, source_target_pairs={{0,4},{2,6},{4,0},{6,2},{8,12},{10,14},{12,8},{14,10},{16,20},{18,... | collective-permute-start | bytes 221192 | tf_op jit(solution)/shard_map/ppermute | solution.py:726
  78.9 2.1 %collective-permute-start.13 = (bf16[16,2304]{1,0:T(8,128)(2,1)S(1)}, bf16[16,2304]{1,0:T(8,128)(2,1)S(1)}, u32[]{:S(2)}, u32[]{:S(2)}) collective-permute-start(bf16[16,2304]{1,0:T(8,128)(2,1)S(1)} %get-tuple-element.96), channel_id=1, source_target_pairs={{0,12},{2,14},{4,8},{6,10},{8,4},{10,6},{12,0},{14,2},{16,28},{18,... | collective-permute-start | bytes 221192 | tf_op jit(solution)/shard_map/ppermute | solution.py:726
  81.6 3.1 %collective-permute-start.15 = (bf16[16,2304]{1,0:T(8,128)(2,1)S(1)}, bf16[16,2304]{1,0:T(8,128)(2,1)S(1)}, u32[]{:S(2)}, u32[]{:S(2)}) collective-permute-start(bf16[16,2304]{1,0:T(8,128)(2,1)S(1)} %get-tuple-element.98), channel_id=1, source_target_pairs={{0,20},{2,22},{4,16},{6,18},{8,28},{10,30},{12,24},{14,26},{16,4},... | collective-permute-start | bytes 221192 | tf_op jit(solution)/shard_map/ppermute | solution.py:726
  84.8 1.8 %collective-permute-start.16 = (bf16[16,2304]{1,0:T(8,128)(2,1)S(1)}, bf16[16,2304]{1,0:T(8,128)(2,1)S(1)}, u32[]{:S(2)}, u32[]{:S(2)}) collective-permute-start(bf16[16,2304]{1,0:T(8,128)(2,1)S(1)} %get-tuple-element.99), channel_id=1, source_target_pairs={{0,24},{2,26},{4,28},{6,30},{8,16},{10,18},{12,20},{14,22},{16,8},... | collective-permute-start | bytes 221192 | tf_op jit(solution)/shard_map/ppermute | solution.py:726
  86.6 2.1 %collective-permute-start.17 = (bf16[16,2304]{1,0:T(8,128)(2,1)S(1)}, bf16[16,2304]{1,0:T(8,128)(2,1)S(1)}, u32[]{:S(2)}, u32[]{:S(2)}) collective-permute-start(bf16[16,2304]{1,0:T(8,128)(2,1)S(1)} %get-tuple-element.100), channel_id=1, source_target_pairs={{0,28},{2,30},{4,24},{6,26},{8,20},{10,22},{12,16},{14,18},{16,12}... | collective-permute-start | bytes 221192 | tf_op jit(solution)/shard_map/ppermute | solution.py:726
  88.6 8.4 %finish.1 = bf16[64,4096]{1,0:T(8,128)(2,1)} custom-call(f32[64,4096]{1,0:T(8,128)} %get-tuple-element.57.read_ref, f32[64,4096]{1,0:T(8,128)} %get-tuple-element.58.cum_ref, bf16[64,4096]{1,0:T(8,128)(2,1)} %z_ref.1, f32[16,4096]{1,0:T(8,128)} %alog_ref.3, f32[2,16,64]{2,1,0:T(8,128)} %bc_ref.3, bf16[16,4608]{1,0:T(8,128)(2,1)S(1)} %get-tuple-element.76.prefix_ref.refs_3_, ...), custom_call_target="tpu_custom_call" | custom-call | flops 20971520 | bytes 3145728 | tf_op jit(solution)/shard_map/finish/pallas_call | solution.py:700
  97.1 1.1 %combine.1 = bf16[64,2048]{1,0:T(8,128)(2,1)} custom-call(bf16[16,2304]{1,0:T(8,128)(2,1)S(1)} %get-tuple-element.104.refs_0_, bf16[16,2304]{1,0:T(8,128)(2,1)S(1)} %collective-permute-done.11.refs_1_, bf16[16,2304]{1,0:T(8,128)(2,1)S(1)} %collective-permute-done.12.refs_2_, bf16[16,2304]{1,0:T(8,128)(2,1)S(1)} %collective-permute-done.13.refs_3_, ...), custom_call_target="tpu_custom_call" | custom-call | flops 75497472 | bytes 589824 | tf_op jit(solution)/shard_map/combine/pallas_call | solution.py:435
  (30 shorter events, 3.8 us)
Async XLA Ops:
  1.5 7.3 %collective-permute-start = (bf16[3,4096]{1,0:T(4,128)(2,1)S(1)}, bf16[3,4096]{1,0:T(4,128)(2,1)S(1)}, u32[]{:S(2)}, u32[]{:S(2)}) collective-permute-start(bf16[3,4096]{1,0:T(4,128)(2,1)S(1)} %slice.3), channel_id=1, source_target_pairs={{0,2},{2,4},{4,6},{6,8},{8,10},{10,12},{12,14},{14,16},{16,18},{18... | collective-permute-start | bytes 73736 | tf_op jit(solution)/shard_map/ppermute | solution.py:779
  8.8 21.4 %all-to-all-start = ((bf16[8,16,2304]{2,1,0:T(8,128)(2,1)}), bf16[8,16,2304]{2,1,0:T(8,128)(2,1)S(1)}, u32[]{:S(2)}, u32[]{:S(2)}) async-start(bf16[8,16,2304]{2,1,0:T(8,128)(2,1)} %bitcast.5), calls=%async_computation | async-start | bytes 1179648 | tf_op jit(solution)/shard_map/all_to_all | solution.py:744
  30.4 13.2 %collective-permute-start.1 = (bf16[144,2048]{1,0:T(8,128)(2,1)S(1)}, bf16[144,2048]{1,0:T(8,128)(2,1)S(1)}, u32[]{:S(2)}, u32[]{:S(2)}) collective-permute-start(bf16[144,2048]{1,0:T(8,128)(2,1)S(1)} %unpack.1.x_ref), channel_id=1, source_target_pairs={{0,2},{2,0},{4,6},{6,4},{8,10},{10,8},{12,14},{14,12},{16,18},{18,... | collective-permute-start | bytes 1769480 | tf_op jit(solution)/shard_map/ppermute | solution.py:736
  43.6 8.1 %collective-permute-start.4 = (bf16[144,6144]{1,0:T(8,128)(2,1)S(1)}, bf16[144,6144]{1,0:T(8,128)(2,1)S(1)}, u32[]{:S(2)}, u32[]{:S(2)}) collective-permute-start(bf16[144,6144]{1,0:T(8,128)(2,1)S(1)} %get-tuple-element.66.refs_0_), channel_id=1, source_target_pairs={{0,1},{1,0},{2,3},{3,2},{4,5},{5,4},{6,7},{7,6},{8,9},{9,8},{10,11... | collective-permute-start | bytes 5308424 | tf_op jit(solution)/shard_map/ppermute | solution.py:731
  43.6 8.1 %collective-permute-start.5 = (f32[64,8]{1,0:T(8,128)S(1)}, f32[64,8]{1,0:T(8,128)S(1)}, u32[]{:S(2)}, u32[]{:S(2)}) collective-permute-start(f32[64,8]{1,0:T(8,128)S(1)} %get-tuple-element.78.refs_0_), channel_id=1, source_target_pairs={{0,1},{1,0},{2,3},{3,2},{4,5},{5,4},{6,7},{7,6},{8,9},{9,8},{10,11... | collective-permute-start | bytes 6152 | tf_op jit(solution)/shard_map/ppermute | solution.py:731
  44.2 7.4 %collective-permute-start.2 = (bf16[16,4608]{1,0:T(8,128)(2,1)S(1)}, bf16[16,4608]{1,0:T(8,128)(2,1)S(1)}, u32[]{:S(2)}, u32[]{:S(2)}) collective-permute-start(bf16[16,4608]{1,0:T(8,128)(2,1)S(1)} %get-tuple-element.65.refs_0_), channel_id=1, source_target_pairs={{0,2},{2,0},{4,6},{6,4},{8,10},{10,8},{12,14},{14,12},{16,18},{18,... | collective-permute-start | bytes 442376 | tf_op jit(solution)/shard_map/ppermute | solution.py:726
  45.5 6.2 %copy-start = (f32[16,4096]{1,0:T(8,128)S(1)}, f32[16,4096]{1,0:T(8,128)}, u32[]{:S(2)}) copy-start(f32[16,4096]{1,0:T(8,128)} %alog_ref.3) | copy-start | bytes 786436
  51.8 3.8 %collective-permute-start.6 = (bf16[144,6144]{1,0:T(8,128)(2,1)S(1)}, bf16[144,6144]{1,0:T(8,128)(2,1)S(1)}, u32[]{:S(2)}, u32[]{:S(2)}) collective-permute-start(bf16[144,6144]{1,0:T(8,128)(2,1)S(1)} %gate.3.refs_0_), channel_id=1, source_target_pairs={{0,1},{1,0},{2,3},{3,2},{4,5},{5,4},{6,7},{7,6},{8,9},{9,8},{10,11... | collective-permute-start | bytes 5308424 | tf_op jit(solution)/shard_map/ppermute | solution.py:731
  51.9 9.6 %collective-permute-start.3 = (bf16[16,4608]{1,0:T(8,128)(2,1)S(1)}, bf16[16,4608]{1,0:T(8,128)(2,1)S(1)}, u32[]{:S(2)}, u32[]{:S(2)}) collective-permute-start(bf16[16,4608]{1,0:T(8,128)(2,1)S(1)} %get-tuple-element.70.refs_0_), channel_id=1, source_target_pairs={{0,4},{2,6},{4,0},{6,2},{8,12},{10,14},{12,8},{14,10},{16,20},{18,... | collective-permute-start | bytes 442376 | tf_op jit(solution)/shard_map/ppermute | solution.py:726
  61.7 15.4 %collective-permute-start.10 = (bf16[144,2048]{1,0:T(8,128)(2,1)S(1)}, bf16[144,2048]{1,0:T(8,128)(2,1)S(1)}, u32[]{:S(2)}, u32[]{:S(2)}) collective-permute-start(bf16[144,2048]{1,0:T(8,128)(2,1)S(1)} %down.2), channel_id=1, source_target_pairs={{0,2},{2,0},{4,6},{6,4},{8,10},{10,8},{12,14},{14,12},{16,18},{18,... | collective-permute-start | bytes 1769480 | tf_op jit(solution)/shard_map/ppermute | solution.py:736
  62.4 15.0 %collective-permute-start.9 = (bf16[16,4608]{1,0:T(8,128)(2,1)S(1)}, bf16[16,4608]{1,0:T(8,128)(2,1)S(1)}, u32[]{:S(2)}, u32[]{:S(2)}) collective-permute-start(bf16[16,4608]{1,0:T(8,128)(2,1)S(1)} %get-tuple-element.77), channel_id=1, source_target_pairs={{0,24},{2,26},{4,28},{6,30},{8,16},{10,18},{12,20},{14,22},{16,8},... | collective-permute-start | bytes 442376 | tf_op jit(solution)/shard_map/ppermute | solution.py:726
  64.3 13.1 %collective-permute-start.8 = (bf16[16,4608]{1,0:T(8,128)(2,1)S(1)}, bf16[16,4608]{1,0:T(8,128)(2,1)S(1)}, u32[]{:S(2)}, u32[]{:S(2)}) collective-permute-start(bf16[16,4608]{1,0:T(8,128)(2,1)S(1)} %get-tuple-element.77), channel_id=1, source_target_pairs={{0,16},{2,18},{4,20},{6,22},{8,24},{10,26},{12,28},{14,30},{16,0},... | collective-permute-start | bytes 442376 | tf_op jit(solution)/shard_map/ppermute | solution.py:726
  64.4 13.0 %collective-permute-start.7 = (bf16[16,4608]{1,0:T(8,128)(2,1)S(1)}, bf16[16,4608]{1,0:T(8,128)(2,1)S(1)}, u32[]{:S(2)}, u32[]{:S(2)}) collective-permute-start(bf16[16,4608]{1,0:T(8,128)(2,1)S(1)} %get-tuple-element.77), channel_id=1, source_target_pairs={{0,8},{2,10},{4,12},{6,14},{8,0},{10,2},{12,4},{14,6},{16,24},{18,... | collective-permute-start | bytes 442376 | tf_op jit(solution)/shard_map/ppermute | solution.py:726
  77.4 7.3 %collective-permute-start.11 = (bf16[16,2304]{1,0:T(8,128)(2,1)S(1)}, bf16[16,2304]{1,0:T(8,128)(2,1)S(1)}, u32[]{:S(2)}, u32[]{:S(2)}) collective-permute-start(bf16[16,2304]{1,0:T(8,128)(2,1)S(1)} %get-tuple-element.94), channel_id=1, source_target_pairs={{0,4},{2,6},{4,0},{6,2},{8,12},{10,14},{12,8},{14,10},{16,20},{18,... | collective-permute-start | bytes 221192 | tf_op jit(solution)/shard_map/ppermute | solution.py:726
  78.9 7.7 %collective-permute-start.12 = (bf16[16,2304]{1,0:T(8,128)(2,1)S(1)}, bf16[16,2304]{1,0:T(8,128)(2,1)S(1)}, u32[]{:S(2)}, u32[]{:S(2)}) collective-permute-start(bf16[16,2304]{1,0:T(8,128)(2,1)S(1)} %get-tuple-element.95), channel_id=1, source_target_pairs={{0,8},{2,10},{4,12},{6,14},{8,0},{10,2},{12,4},{14,6},{16,24},{18,... | collective-permute-start | bytes 221192 | tf_op jit(solution)/shard_map/ppermute | solution.py:726
  78.9 18.2 %collective-permute-start.13 = (bf16[16,2304]{1,0:T(8,128)(2,1)S(1)}, bf16[16,2304]{1,0:T(8,128)(2,1)S(1)}, u32[]{:S(2)}, u32[]{:S(2)}) collective-permute-start(bf16[16,2304]{1,0:T(8,128)(2,1)S(1)} %get-tuple-element.96), channel_id=1, source_target_pairs={{0,12},{2,14},{4,8},{6,10},{8,4},{10,6},{12,0},{14,2},{16,28},{18,... | collective-permute-start | bytes 221192 | tf_op jit(solution)/shard_map/ppermute | solution.py:726
  81.0 16.1 %collective-permute-start.14 = (bf16[16,2304]{1,0:T(8,128)(2,1)S(1)}, bf16[16,2304]{1,0:T(8,128)(2,1)S(1)}, u32[]{:S(2)}, u32[]{:S(2)}) collective-permute-start(bf16[16,2304]{1,0:T(8,128)(2,1)S(1)} %get-tuple-element.97), channel_id=1, source_target_pairs={{0,16},{2,18},{4,20},{6,22},{8,24},{10,26},{12,28},{14,30},{16,0},... | collective-permute-start | bytes 221192 | tf_op jit(solution)/shard_map/ppermute | solution.py:726
  81.6 15.4 %collective-permute-start.15 = (bf16[16,2304]{1,0:T(8,128)(2,1)S(1)}, bf16[16,2304]{1,0:T(8,128)(2,1)S(1)}, u32[]{:S(2)}, u32[]{:S(2)}) collective-permute-start(bf16[16,2304]{1,0:T(8,128)(2,1)S(1)} %get-tuple-element.98), channel_id=1, source_target_pairs={{0,20},{2,22},{4,16},{6,18},{8,28},{10,30},{12,24},{14,26},{16,4},... | collective-permute-start | bytes 221192 | tf_op jit(solution)/shard_map/ppermute | solution.py:726
  84.8 12.3 %collective-permute-start.16 = (bf16[16,2304]{1,0:T(8,128)(2,1)S(1)}, bf16[16,2304]{1,0:T(8,128)(2,1)S(1)}, u32[]{:S(2)}, u32[]{:S(2)}) collective-permute-start(bf16[16,2304]{1,0:T(8,128)(2,1)S(1)} %get-tuple-element.99), channel_id=1, source_target_pairs={{0,24},{2,26},{4,28},{6,30},{8,16},{10,18},{12,20},{14,22},{16,8},... | collective-permute-start | bytes 221192 | tf_op jit(solution)/shard_map/ppermute | solution.py:726
  86.6 10.5 %collective-permute-start.17 = (bf16[16,2304]{1,0:T(8,128)(2,1)S(1)}, bf16[16,2304]{1,0:T(8,128)(2,1)S(1)}, u32[]{:S(2)}, u32[]{:S(2)}) collective-permute-start(bf16[16,2304]{1,0:T(8,128)(2,1)S(1)} %get-tuple-element.100), channel_id=1, source_target_pairs={{0,28},{2,30},{4,24},{6,26},{8,20},{10,22},{12,16},{14,18},{16,12}... | collective-permute-start | bytes 221192 | tf_op jit(solution)/shard_map/ppermute | solution.py:726
